TPU v7x, 32 devices: a whole 2x2x4 slice. The times are simulated.
32 devices in a mesh: groups: 2 (over x), row: 16 (over z, y, core).
Axes of the slice: x: 2, y: 2, z: 4, core: 2. Of those that a mesh axis runs over, the one named last changes fastest.
Arguments:
- h_blocks: float32 [32, 14, 128, 128], P(('groups', 'row')), parts along dimension 0, may hold values from -0.09375 to 0.09375
- h_cols: int32 [32, 14], P(('groups', 'row')), parts along dimension 0, may hold values from 0 to 15, as said below
- term_prev: float32 [32, 14, 128, 128], P(('groups', 'row')), parts along dimension 0, may hold values from -6 to 6
- term_cur: float32 [32, 14, 128, 128], P(('groups', 'row')), parts along dimension 0, may hold values from -6 to 6
- t_cols: int32 [32, 14], P(('groups', 'row')), parts along dimension 0, may hold values from 0 to 15, as said below
- density_in: float32 [32, 14, 128, 128], P(('groups', 'row')), parts along dimension 0, may hold values from -6 to 6
- coefs: float32 [3], replicated, may hold values from -1 to 1
Outputs:
- density: float32 [32, 14, 128, 128], P(('groups', 'row')), parts along dimension 0
- term_last: float32 [32, 14, 128, 128], P(('groups', 'row')), parts along dimension 0
- term_before: float32 [32, 14, 128, 128], P(('groups', 'row')), parts along dimension 0
There are 2 independent parts, one for each index of `groups`. A program takes and returns all parts, laid end to end along the dimension named above; an argument that names none is the same for every part. Nothing has to cross between parts.
Inputs may be any that keep to these rules, and one draw needn't show every extreme that they name: `h_cols`: each row i names 14 distinct block columns (i + o) mod 16, with offsets o taken from -7 to 7 (all but one of them), in rising order of o; offset 0 is always named. `t_cols`: same law as h_cols, drawn independently.
All inputs are finite; a program needn't handle non-finite values.
Results may differ from a plain program's by a relative error of at most 0.0003.
Values sent between devices are 32-bit elements; how exact they have to be, the bound alone decides.
No kernel may reach another device: no remote copies, remote signals or barrier semaphores. Data moves between devices by JAX's collectives and lax.ppermute only.
A program may use at most 128 MiB of HBM per device.

v0:
```python
import jax
import jax.numpy as jnp
from jax import lax
from jax.sharding import PartitionSpec as P

REACH = 7
STEPS = 3


def from_behind(x, axis, by):
    devices = lax.axis_size(axis)
    return lax.ppermute(x, axis, [(i, (i + by) % devices) for i in range(devices)])


def take_below(block):
    return from_behind(block, "row", 1)


def take_above(block):
    return from_behind(block, "row", -1)


def per_device(h_blocks, h_cols, term_prev, term_cur, t_cols, density_in, coefs):
    rows = h_blocks.shape[0]
    count = h_blocks.shape[1]
    devices = lax.axis_size("row")
    total = rows * devices
    hops = (REACH + rows - 1) // rows
    first = lax.axis_index("row") * rows
    start = first - hops * rows
    all_cols = lax.all_gather(t_cols, "row", axis=0, tiled=True)
    window_rows = (2 * hops + 1) * rows
    global_rows = jnp.mod(start + jnp.arange(window_rows, dtype=jnp.int32), total)
    window_cols = all_cols[global_rows]
    relative = jnp.mod(h_cols - start, total)
    matched = window_cols[relative][:, :, None, :] == t_cols[:, None, :, None]
    slots = jnp.arange(count, dtype=jnp.int32)
    position = jnp.sum(jnp.where(matched, slots[None, None, None, :], 0), axis=3)
    present = jnp.any(matched, axis=3)
    position = jnp.where(present, position, count)
    position_t = jnp.transpose(position, (2, 0, 1))
    previous = term_prev
    current = term_cur
    density = density_in
    for step in range(STEPS):
        lowers = []
        uppers = []
        below = current
        for hop in range(hops):
            below = take_below(below)
            lowers.append(below)
        above = current
        for hop in range(hops):
            above = take_above(above)
            uppers.append(above)
        window = jnp.concatenate(lowers[::-1] + [current] + uppers, axis=0)
        empty_slot = jnp.zeros((window.shape[0], 1, window.shape[2], window.shape[3]), jnp.float32)
        window = jnp.concatenate([window, empty_slot], axis=1)

        def target_block(slot_index):
            gathered = window[relative, slot_index]
            return jnp.einsum("iaxy,iayz->ixz", h_blocks, gathered, precision=lax.Precision.HIGHEST)

        stacked = lax.map(target_block, position_t)
        product = jnp.transpose(stacked, (1, 0, 2, 3))
        newest = 2.0 * product - previous
        density = density + coefs[step] * newest
        previous = current
        current = newest
    return (density, current, previous)


def solution(mesh):
    in_specs = (
        P(("groups", "row"), None, None, None),
        P(("groups", "row"), None),
        P(("groups", "row"), None, None, None),
        P(("groups", "row"), None, None, None),
        P(("groups", "row"), None),
        P(("groups", "row"), None, None, None),
        P(),
    )
    out_specs = (
        P(("groups", "row"), None, None, None),
        P(("groups", "row"), None, None, None),
        P(("groups", "row"), None, None, None),
    )
    return jax.shard_map(
        per_device, mesh=mesh, in_specs=in_specs, out_specs=out_specs, check_vma=False
    )
```

profile of v0, /device:TPU:22, one launch (start us, length us, event | category | flops | bytes accessed | tf_op | source)
XLA Modules:
  0.0 920.6 jit_solution(4702512126799373820)
XLA Ops:
  2.4 21.1 %collective-permute-done = f32[1,14,128,128]{3,2,1,0:T(8,128)S(1)} collective-permute-done((f32[1,14,128,128]{3,2,1,0:T(8,128)}, f32[1,14,128,128]{3,2,1,0:T(8,128)S(1)}, u32[]{:S(2)}, u32[]{:S(2)}) %collective-permute-start) | collective-permute-done | bytes 917536 | tf_op jit(solution)/shard_map/ppermute | solution.py:12
  23.5 8.9 collective-permute-done.7
  34.2 11.3 %collective-permute-done.1 = f32[1,14,128,128]{3,2,1,0:T(8,128)S(1)} collective-permute-done((f32[1,14,128,128]{3,2,1,0:T(8,128)S(1)}, f32[1,14,128,128]{3,2,1,0:T(8,128)S(1)}, u32[]{:S(2)}, u32[]{:S(2)}) %collective-permute-start.1) | collective-permute-done | bytes 917536 | tf_op jit(solution)/shard_map/ppermute | solution.py:12
  45.5 7.3 collective-permute-done.8
  54.8 11.3 %collective-permute-done.2 = f32[1,14,128,128]{3,2,1,0:T(8,128)S(1)} collective-permute-done((f32[1,14,128,128]{3,2,1,0:T(8,128)S(1)}, f32[1,14,128,128]{3,2,1,0:T(8,128)S(1)}, u32[]{:S(2)}, u32[]{:S(2)}) %collective-permute-start.2) | collective-permute-done | bytes 917536 | tf_op jit(solution)/shard_map/ppermute | solution.py:12
  66.1 8.2 collective-permute-done.9
  76.2 11.8 %collective-permute-done.3 = f32[1,14,128,128]{3,2,1,0:T(8,128)S(1)} collective-permute-done((f32[1,14,128,128]{3,2,1,0:T(8,128)S(1)}, f32[1,14,128,128]{3,2,1,0:T(8,128)S(1)}, u32[]{:S(2)}, u32[]{:S(2)}) %collective-permute-start.3) | collective-permute-done | bytes 917536 | tf_op jit(solution)/shard_map/ppermute | solution.py:12
  88.0 8.8 collective-permute-done.10
  98.9 11.3 %collective-permute-done.4 = f32[1,14,128,128]{3,2,1,0:T(8,128)} collective-permute-done((f32[1,14,128,128]{3,2,1,0:T(8,128)S(1)}, f32[1,14,128,128]{3,2,1,0:T(8,128)}, u32[]{:S(2)}, u32[]{:S(2)}) %collective-permute-start.4) | collective-permute-done | bytes 917536 | tf_op jit(solution)/shard_map/ppermute | solution.py:12
  110.2 19.8 %all-gather = s32[16,1,14]{2,1,0:T(1,128)S(1)} all-gather(s32[1,1,14]{2,1,0:T(1,128)} %bitcast.112), channel_id=1, replica_groups=mesh['groups'=2,'row'=16] {'row'}, dimensions={0}, use_global_device_ids=true | all-gather | bytes 952 | tf_op jit(solution)/shard_map/all_gather | solution.py:31
  141.3 10.5 %collective-permute-done.12 = f32[1,14,128,128]{3,2,1,0:T(8,128)} collective-permute-done((f32[1,14,128,128]{3,2,1,0:T(8,128)}, f32[1,14,128,128]{3,2,1,0:T(8,128)}, u32[]{:S(2)}, u32[]{:S(2)}) %collective-permute-start.12) | collective-permute-done | bytes 917536 | tf_op jit(solution)/shard_map/ppermute | solution.py:12
  153.8 9.8 %collective-permute-done.6 = f32[1,14,128,128]{3,2,1,0:T(8,128)} collective-permute-done((f32[1,14,128,128]{3,2,1,0:T(8,128)}, f32[1,14,128,128]{3,2,1,0:T(8,128)}, u32[]{:S(2)}, u32[]{:S(2)}) %collective-permute-start.6) | collective-permute-done | bytes 917536 | tf_op jit(solution)/shard_map/ppermute | solution.py:12
  190.7 12.8 %concatenate.28 = f32[15,15,128,128]{3,2,1,0:T(8,128)} pad(f32[15,14,128,128]{3,2,1,0:T(8,128)} %constant_dynamic-update-slice_fusion.3, f32[]{:T(128)} %constant.68.clone.1), padding=0_0x0_1x0_0x0_0 | pad | bytes 28508164 | tf_op jit(solution)/shard_map/concatenate | solution.py:58
  203.6 106.5 %while.30 = (s32[]{:T(128)}, f32[14,1,128,128]{3,2,0,1:T(8,128)S(1)}, s32[1,14]{1,0:T(1,128)S(1)}, s32[14,1,14]{2,1,0:T(1,128)S(1)}, f32[15,15,128,128]{3,2,1,0:...) while((s32[]{:T(128)}, f32[14,1,128,128]{3,2,0,1:T(8,128)S(1)}, s32[1,14]{1,0:T(1,128)S(1)}, ...), condition=%wide.region_3.4_spmd, body=%wide.region_2.3_spmd.sunk | while | flops 352321728 | bytes 3998509 | solution.py:64
  203.6 5.8 gather_fusion
  211.2 5.8 gather_fusion
  218.8 5.8 gather_fusion
  226.4 5.8 gather_fusion
  234.1 5.8 gather_fusion
  241.7 5.8 gather_fusion
  249.3 5.8 gather_fusion
  256.9 5.8 gather_fusion
  272.1 5.8 gather_fusion
  287.3 5.8 gather_fusion
  313.2 20.4 %collective-permute-done.14 = f32[1,14,128,128]{3,2,1,0:T(8,128)S(1)} collective-permute-done((f32[1,14,128,128]{3,2,1,0:T(8,128)S(1)}, f32[1,14,128,128]{3,2,1,0:T(8,128)S(1)}, u32[]{:S(2)}, u32[]{:S(2)}) %collective-permute-start.14) | collective-permute-done | bytes 917536 | tf_op jit(solution)/shard_map/ppermute | solution.py:12
  335.8 20.3 %collective-permute-done.15 = f32[1,14,128,128]{3,2,1,0:T(8,128)S(1)} collective-permute-done((f32[1,14,128,128]{3,2,1,0:T(8,128)S(1)}, f32[1,14,128,128]{3,2,1,0:T(8,128)S(1)}, u32[]{:S(2)}, u32[]{:S(2)}) %collective-permute-start.15) | collective-permute-done | bytes 917536 | tf_op jit(solution)/shard_map/ppermute | solution.py:12
  358.3 18.0 %collective-permute-done.16 = f32[1,14,128,128]{3,2,1,0:T(8,128)S(1)} collective-permute-done((f32[1,14,128,128]{3,2,1,0:T(8,128)S(1)}, f32[1,14,128,128]{3,2,1,0:T(8,128)S(1)}, u32[]{:S(2)}, u32[]{:S(2)}) %collective-permute-start.16) | collective-permute-done | bytes 917536 | tf_op jit(solution)/shard_map/ppermute | solution.py:12
  380.9 16.8 %collective-permute-done.17 = f32[1,14,128,128]{3,2,1,0:T(8,128)S(1)} collective-permute-done((f32[1,14,128,128]{3,2,1,0:T(8,128)S(1)}, f32[1,14,128,128]{3,2,1,0:T(8,128)S(1)}, u32[]{:S(2)}, u32[]{:S(2)}) %collective-permute-start.17) | collective-permute-done | bytes 917536 | tf_op jit(solution)/shard_map/ppermute | solution.py:12
  402.6 17.3 %collective-permute-done.18 = f32[1,14,128,128]{3,2,1,0:T(8,128)S(1)} collective-permute-done((f32[1,14,128,128]{3,2,1,0:T(8,128)S(1)}, f32[1,14,128,128]{3,2,1,0:T(8,128)S(1)}, u32[]{:S(2)}, u32[]{:S(2)}) %collective-permute-start.18) | collective-permute-done | bytes 917536 | tf_op jit(solution)/shard_map/ppermute | solution.py:12
  423.5 19.1 %collective-permute-done.19 = f32[1,14,128,128]{3,2,1,0:T(8,128)} collective-permute-done((f32[1,14,128,128]{3,2,1,0:T(8,128)S(1)}, f32[1,14,128,128]{3,2,1,0:T(8,128)}, u32[]{:S(2)}, u32[]{:S(2)}) %collective-permute-start.19) | collective-permute-done | bytes 917536 | tf_op jit(solution)/shard_map/ppermute | solution.py:12
  445.5 17.8 %collective-permute-done.20 = f32[1,14,128,128]{3,2,1,0:T(8,128)} collective-permute-done((f32[1,14,128,128]{3,2,1,0:T(8,128)}, f32[1,14,128,128]{3,2,1,0:T(8,128)}, u32[]{:S(2)}, u32[]{:S(2)}) %collective-permute-start.20) | collective-permute-done | bytes 917536 | tf_op jit(solution)/shard_map/ppermute | solution.py:12
  489.2 12.7 %concatenate.30 = f32[15,15,128,128]{3,2,1,0:T(8,128)} pad(f32[15,14,128,128]{3,2,1,0:T(8,128)} %constant_dynamic-update-slice_fusion.18, f32[]{:T(128)} %constant.68.clone.1), padding=0_0x0_1x0_0x0_0 | pad | bytes 28508164 | tf_op jit(solution)/shard_map/concatenate | solution.py:58
  502.9 114.8 %while.31 = (s32[]{:T(128)}, f32[14,1,128,128]{3,2,0,1:T(8,128)}, s32[1,14]{1,0:T(1,128)S(1)}, s32[14,1,14]{2,1,0:T(1,128)S(1)}, f32[15,15,128,128]{3,2,1,0:T(8,...) while((s32[]{:T(128)}, f32[14,1,128,128]{3,2,0,1:T(8,128)}, s32[1,14]{1,0:T(1,128)S(1)}, ...), condition=%wide.region_5.6_spmd, body=%wide.region_4.5_spmd.sunk | while | flops 352321728 | bytes 3999017 | solution.py:64
  543.9 5.8 gather_fusion.1
  560.3 5.8 gather_fusion.1
  601.3 5.8 gather_fusion.1
  621.0 19.6 %collective-permute-done.28 = f32[1,14,128,128]{3,2,1,0:T(8,128)S(1)} collective-permute-done((f32[1,14,128,128]{3,2,1,0:T(8,128)S(1)}, f32[1,14,128,128]{3,2,1,0:T(8,128)S(1)}, u32[]{:S(2)}, u32[]{:S(2)}) %collective-permute-start.28) | collective-permute-done | bytes 917536 | tf_op jit(solution)/shard_map/ppermute | solution.py:12
  643.7 19.0 %collective-permute-done.29 = f32[1,14,128,128]{3,2,1,0:T(8,128)S(1)} collective-permute-done((f32[1,14,128,128]{3,2,1,0:T(8,128)S(1)}, f32[1,14,128,128]{3,2,1,0:T(8,128)S(1)}, u32[]{:S(2)}, u32[]{:S(2)}) %collective-permute-start.29) | collective-permute-done | bytes 917536 | tf_op jit(solution)/shard_map/ppermute | solution.py:12
  665.7 19.4 %collective-permute-done.30 = f32[1,14,128,128]{3,2,1,0:T(8,128)S(1)} collective-permute-done((f32[1,14,128,128]{3,2,1,0:T(8,128)S(1)}, f32[1,14,128,128]{3,2,1,0:T(8,128)S(1)}, u32[]{:S(2)}, u32[]{:S(2)}) %collective-permute-start.30) | collective-permute-done | bytes 917536 | tf_op jit(solution)/shard_map/ppermute | solution.py:12
  687.5 17.9 %collective-permute-done.31 = f32[1,14,128,128]{3,2,1,0:T(8,128)S(1)} collective-permute-done((f32[1,14,128,128]{3,2,1,0:T(8,128)S(1)}, f32[1,14,128,128]{3,2,1,0:T(8,128)S(1)}, u32[]{:S(2)}, u32[]{:S(2)}) %collective-permute-start.31) | collective-permute-done | bytes 917536 | tf_op jit(solution)/shard_map/ppermute | solution.py:12
  709.9 16.9 %collective-permute-done.32 = f32[1,14,128,128]{3,2,1,0:T(8,128)S(1)} collective-permute-done((f32[1,14,128,128]{3,2,1,0:T(8,128)S(1)}, f32[1,14,128,128]{3,2,1,0:T(8,128)S(1)}, u32[]{:S(2)}, u32[]{:S(2)}) %collective-permute-start.32) | collective-permute-done | bytes 917536 | tf_op jit(solution)/shard_map/ppermute | solution.py:12
  731.4 17.5 %collective-permute-done.33 = f32[1,14,128,128]{3,2,1,0:T(8,128)S(1)} collective-permute-done((f32[1,14,128,128]{3,2,1,0:T(8,128)S(1)}, f32[1,14,128,128]{3,2,1,0:T(8,128)S(1)}, u32[]{:S(2)}, u32[]{:S(2)}) %collective-permute-start.33) | collective-permute-done | bytes 917536 | tf_op jit(solution)/shard_map/ppermute | solution.py:12
  752.5 19.0 %collective-permute-done.34 = f32[1,14,128,128]{3,2,1,0:T(8,128)S(1)} collective-permute-done((f32[1,14,128,128]{3,2,1,0:T(8,128)S(1)}, f32[1,14,128,128]{3,2,1,0:T(8,128)S(1)}, u32[]{:S(2)}, u32[]{:S(2)}) %collective-permute-start.34) | collective-permute-done | bytes 917536 | tf_op jit(solution)/shard_map/ppermute | solution.py:12
  786.7 12.7 %concatenate.32 = f32[15,15,128,128]{3,2,1,0:T(8,128)} pad(f32[15,14,128,128]{3,2,1,0:T(8,128)} %constant_dynamic-update-slice_fusion.33, f32[]{:T(128)} %constant.68.clone.1), padding=0_0x0_1x0_0x0_0 | pad | bytes 28508164 | tf_op jit(solution)/shard_map/concatenate | solution.py:58
  800.4 114.8 %while.32 = (s32[]{:T(128)}, f32[14,1,128,128]{3,2,0,1:T(8,128)}, s32[1,14]{1,0:T(1,128)S(1)}, s32[14,1,14]{2,1,0:T(1,128)S(1)}, f32[15,15,128,128]{3,2,1,0:T(8,...) while((s32[]{:T(128)}, f32[14,1,128,128]{3,2,0,1:T(8,128)}, s32[1,14]{1,0:T(1,128)S(1)}, ...), condition=%wide.region_7.8_spmd, body=%wide.region_6.7_spmd.sunk | while | flops 352321728 | bytes 3999017 | solution.py:64
  833.2 5.8 gather_fusion.2
  857.8 5.8 gather_fusion.2
  890.7 5.8 gather_fusion.2
  (436 shorter events, 387.7 us)
Async XLA Ops:
  0.6 22.9 %collective-permute-start = (f32[1,14,128,128]{3,2,1,0:T(8,128)}, f32[1,14,128,128]{3,2,1,0:T(8,128)S(1)}, u32[]{:S(2)}, u32[]{:S(2)}) collective-permute-start(f32[1,14,128,128]{3,2,1,0:T(8,128)} %param.16), channel_id=1, source_target_pairs={{0,1},{1,2},{2,3},{3,4},{4,5},{5,6},{6,7},{7,8},{8,9},{9,10},{10,1... | collective-permute-start | bytes 2752520 | tf_op jit(solution)/shard_map/ppermute | solution.py:12
  0.7 31.7 %collective-permute-start.7 = (f32[1,14,128,128]{3,2,1,0:T(8,128)}, f32[1,14,128,128]{3,2,1,0:T(8,128)S(1)}, u32[]{:S(2)}, u32[]{:S(2)}) collective-permute-start(f32[1,14,128,128]{3,2,1,0:T(8,128)} %param.16), channel_id=1, source_target_pairs={{0,15},{1,0},{2,1},{3,2},{4,3},{5,4},{6,5},{7,6},{8,7},{9,8},{10,9... | collective-permute-start | bytes 2752520 | tf_op jit(solution)/shard_map/ppermute | solution.py:12
  23.5 22.0 %collective-permute-start.1 = (f32[1,14,128,128]{3,2,1,0:T(8,128)S(1)}, f32[1,14,128,128]{3,2,1,0:T(8,128)S(1)}, u32[]{:S(2)}, u32[]{:S(2)}) collective-permute-start(f32[1,14,128,128]{3,2,1,0:T(8,128)S(1)} %collective-permute-done), channel_id=1, source_target_pairs={{0,1},{1,2},{2,3},{3,4},{4,5},{5,6},{6,7},{7,8},{8,9},{9,10},{10,1... | collective-permute-start | bytes 2752520 | tf_op jit(solution)/shard_map/ppermute | solution.py:12
  32.4 20.5 %collective-permute-start.8 = (f32[1,14,128,128]{3,2,1,0:T(8,128)S(1)}, f32[1,14,128,128]{3,2,1,0:T(8,128)S(1)}, u32[]{:S(2)}, u32[]{:S(2)}) collective-permute-start(f32[1,14,128,128]{3,2,1,0:T(8,128)S(1)} %collective-permute-done.7), channel_id=1, source_target_pairs={{0,15},{1,0},{2,1},{3,2},{4,3},{5,4},{6,5},{7,6},{8,7},{9,8},{10,9... | collective-permute-start | bytes 2752520 | tf_op jit(solution)/shard_map/ppermute | solution.py:12
  45.5 20.5 %collective-permute-start.2 = (f32[1,14,128,128]{3,2,1,0:T(8,128)S(1)}, f32[1,14,128,128]{3,2,1,0:T(8,128)S(1)}, u32[]{:S(2)}, u32[]{:S(2)}) collective-permute-start(f32[1,14,128,128]{3,2,1,0:T(8,128)S(1)} %collective-permute-done.1), channel_id=1, source_target_pairs={{0,1},{1,2},{2,3},{3,4},{4,5},{5,6},{6,7},{7,8},{8,9},{9,10},{10,1... | collective-permute-start | bytes 2752520 | tf_op jit(solution)/shard_map/ppermute | solution.py:12
  52.9 21.4 %collective-permute-start.9 = (f32[1,14,128,128]{3,2,1,0:T(8,128)S(1)}, f32[1,14,128,128]{3,2,1,0:T(8,128)S(1)}, u32[]{:S(2)}, u32[]{:S(2)}) collective-permute-start(f32[1,14,128,128]{3,2,1,0:T(8,128)S(1)} %collective-permute-done.8), channel_id=1, source_target_pairs={{0,15},{1,0},{2,1},{3,2},{4,3},{5,4},{6,5},{7,6},{8,7},{9,8},{10,9... | collective-permute-start | bytes 2752520 | tf_op jit(solution)/shard_map/ppermute | solution.py:12
  66.1 21.9 %collective-permute-start.3 = (f32[1,14,128,128]{3,2,1,0:T(8,128)S(1)}, f32[1,14,128,128]{3,2,1,0:T(8,128)S(1)}, u32[]{:S(2)}, u32[]{:S(2)}) collective-permute-start(f32[1,14,128,128]{3,2,1,0:T(8,128)S(1)} %collective-permute-done.2), channel_id=1, source_target_pairs={{0,1},{1,2},{2,3},{3,4},{4,5},{5,6},{6,7},{7,8},{8,9},{9,10},{10,1... | collective-permute-start | bytes 2752520 | tf_op jit(solution)/shard_map/ppermute | solution.py:12
  74.2 22.6 %collective-permute-start.10 = (f32[1,14,128,128]{3,2,1,0:T(8,128)S(1)}, f32[1,14,128,128]{3,2,1,0:T(8,128)}, u32[]{:S(2)}, u32[]{:S(2)}) collective-permute-start(f32[1,14,128,128]{3,2,1,0:T(8,128)S(1)} %collective-permute-done.9), channel_id=1, source_target_pairs={{0,15},{1,0},{2,1},{3,2},{4,3},{5,4},{6,5},{7,6},{8,7},{9,8},{10,9... | collective-permute-start | bytes 2752520 | tf_op jit(solution)/shard_map/ppermute | solution.py:12
  88.0 22.2 %collective-permute-start.4 = (f32[1,14,128,128]{3,2,1,0:T(8,128)S(1)}, f32[1,14,128,128]{3,2,1,0:T(8,128)}, u32[]{:S(2)}, u32[]{:S(2)}) collective-permute-start(f32[1,14,128,128]{3,2,1,0:T(8,128)S(1)} %collective-permute-done.3), channel_id=1, source_target_pairs={{0,1},{1,2},{2,3},{3,4},{4,5},{5,6},{6,7},{7,8},{8,9},{9,10},{10,1... | collective-permute-start | bytes 2752520 | tf_op jit(solution)/shard_map/ppermute | solution.py:12
  96.8 33.1 %collective-permute-start.11 = (f32[1,14,128,128]{3,2,1,0:T(8,128)}, f32[1,14,128,128]{3,2,1,0:T(8,128)}, u32[]{:S(2)}, u32[]{:S(2)}) collective-permute-start(f32[1,14,128,128]{3,2,1,0:T(8,128)} %collective-permute-done.10), channel_id=1, source_target_pairs={{0,15},{1,0},{2,1},{3,2},{4,3},{5,4},{6,5},{7,6},{8,7},{9,8},{10,9... | collective-permute-start | bytes 2752520 | tf_op jit(solution)/shard_map/ppermute | solution.py:12
  110.2 20.6 %collective-permute-start.5 = (f32[1,14,128,128]{3,2,1,0:T(8,128)}, f32[1,14,128,128]{3,2,1,0:T(8,128)}, u32[]{:S(2)}, u32[]{:S(2)}) collective-permute-start(f32[1,14,128,128]{3,2,1,0:T(8,128)} %collective-permute-done.4), channel_id=1, source_target_pairs={{0,1},{1,2},{2,3},{3,4},{4,5},{5,6},{6,7},{7,8},{8,9},{9,10},{10,1... | collective-permute-start | bytes 2752520 | tf_op jit(solution)/shard_map/ppermute | solution.py:12
  130.0 21.9 %collective-permute-start.12 = (f32[1,14,128,128]{3,2,1,0:T(8,128)}, f32[1,14,128,128]{3,2,1,0:T(8,128)}, u32[]{:S(2)}, u32[]{:S(2)}) collective-permute-start(f32[1,14,128,128]{3,2,1,0:T(8,128)} %collective-permute-done.11), channel_id=1, source_target_pairs={{0,15},{1,0},{2,1},{3,2},{4,3},{5,4},{6,5},{7,6},{8,7},{9,8},{10,9... | collective-permute-start | bytes 2752520 | tf_op jit(solution)/shard_map/ppermute | solution.py:12
  130.8 32.8 %collective-permute-start.6 = (f32[1,14,128,128]{3,2,1,0:T(8,128)}, f32[1,14,128,128]{3,2,1,0:T(8,128)}, u32[]{:S(2)}, u32[]{:S(2)}) collective-permute-start(f32[1,14,128,128]{3,2,1,0:T(8,128)} %collective-permute-done.5), channel_id=1, source_target_pairs={{0,1},{1,2},{2,3},{3,4},{4,5},{5,6},{6,7},{7,8},{8,9},{9,10},{10,1... | collective-permute-start | bytes 2752520 | tf_op jit(solution)/shard_map/ppermute | solution.py:12
  141.3 40.7 %copy-start.4 = (f32[1,14,128,128]{3,2,1,0:T(8,128)S(1)}, f32[1,14,128,128]{3,2,1,0:T(8,128)}, u32[]{:S(2)}) copy-start(f32[1,14,128,128]{3,2,1,0:T(8,128)} %copy-done.3) | copy-start | bytes 2752516
  151.9 37.8 %collective-permute-start.13 = (f32[1,14,128,128]{3,2,1,0:T(8,128)}, f32[1,14,128,128]{3,2,1,0:T(8,128)S(1)}, u32[]{:S(2)}, u32[]{:S(2)}) collective-permute-start(f32[1,14,128,128]{3,2,1,0:T(8,128)} %collective-permute-done.12), channel_id=1, source_target_pairs={{0,15},{1,0},{2,1},{3,2},{4,3},{5,4},{6,5},{7,6},{8,7},{9,8},{10,9... | collective-permute-start | bytes 2752520 | tf_op jit(solution)/shard_map/ppermute | solution.py:12
  311.4 22.2 %collective-permute-start.14 = (f32[1,14,128,128]{3,2,1,0:T(8,128)S(1)}, f32[1,14,128,128]{3,2,1,0:T(8,128)S(1)}, u32[]{:S(2)}, u32[]{:S(2)}) collective-permute-start(f32[1,14,128,128]{3,2,1,0:T(8,128)S(1)} %bitcast_subtract_fusion.2), channel_id=1, source_target_pairs={{0,1},{1,2},{2,3},{3,4},{4,5},{5,6},{6,7},{7,8},{8,9},{9,10},{10,1... | collective-permute-start | bytes 2752520 | tf_op jit(solution)/shard_map/ppermute | solution.py:12
  311.5 22.5 %collective-permute-start.21 = (f32[1,14,128,128]{3,2,1,0:T(8,128)S(1)}, f32[1,14,128,128]{3,2,1,0:T(8,128)S(1)}, u32[]{:S(2)}, u32[]{:S(2)}) collective-permute-start(f32[1,14,128,128]{3,2,1,0:T(8,128)S(1)} %bitcast_subtract_fusion.2), channel_id=1, source_target_pairs={{0,15},{1,0},{2,1},{3,2},{4,3},{5,4},{6,5},{7,6},{8,7},{9,8},{10,9... | collective-permute-start | bytes 2752520 | tf_op jit(solution)/shard_map/ppermute | solution.py:12
  333.6 22.6 %collective-permute-start.15 = (f32[1,14,128,128]{3,2,1,0:T(8,128)S(1)}, f32[1,14,128,128]{3,2,1,0:T(8,128)S(1)}, u32[]{:S(2)}, u32[]{:S(2)}) collective-permute-start(f32[1,14,128,128]{3,2,1,0:T(8,128)S(1)} %collective-permute-done.14), channel_id=1, source_target_pairs={{0,1},{1,2},{2,3},{3,4},{4,5},{5,6},{6,7},{7,8},{8,9},{9,10},{10,1... | collective-permute-start | bytes 2752520 | tf_op jit(solution)/shard_map/ppermute | solution.py:12
  333.9 22.4 %collective-permute-start.22 = (f32[1,14,128,128]{3,2,1,0:T(8,128)S(1)}, f32[1,14,128,128]{3,2,1,0:T(8,128)S(1)}, u32[]{:S(2)}, u32[]{:S(2)}) collective-permute-start(f32[1,14,128,128]{3,2,1,0:T(8,128)S(1)} %collective-permute-done.21), channel_id=1, source_target_pairs={{0,15},{1,0},{2,1},{3,2},{4,3},{5,4},{6,5},{7,6},{8,7},{9,8},{10,9... | collective-permute-start | bytes 2752520 | tf_op jit(solution)/shard_map/ppermute | solution.py:12
  356.2 20.2 %collective-permute-start.16 = (f32[1,14,128,128]{3,2,1,0:T(8,128)S(1)}, f32[1,14,128,128]{3,2,1,0:T(8,128)S(1)}, u32[]{:S(2)}, u32[]{:S(2)}) collective-permute-start(f32[1,14,128,128]{3,2,1,0:T(8,128)S(1)} %collective-permute-done.15), channel_id=1, source_target_pairs={{0,1},{1,2},{2,3},{3,4},{4,5},{5,6},{6,7},{7,8},{8,9},{9,10},{10,1... | collective-permute-start | bytes 2752520 | tf_op jit(solution)/shard_map/ppermute | solution.py:12
  356.4 22.6 %collective-permute-start.23 = (f32[1,14,128,128]{3,2,1,0:T(8,128)S(1)}, f32[1,14,128,128]{3,2,1,0:T(8,128)S(1)}, u32[]{:S(2)}, u32[]{:S(2)}) collective-permute-start(f32[1,14,128,128]{3,2,1,0:T(8,128)S(1)} %collective-permute-done.22), channel_id=1, source_target_pairs={{0,15},{1,0},{2,1},{3,2},{4,3},{5,4},{6,5},{7,6},{8,7},{9,8},{10,9... | collective-permute-start | bytes 2752520 | tf_op jit(solution)/shard_map/ppermute | solution.py:12
  376.4 21.4 %collective-permute-start.17 = (f32[1,14,128,128]{3,2,1,0:T(8,128)S(1)}, f32[1,14,128,128]{3,2,1,0:T(8,128)S(1)}, u32[]{:S(2)}, u32[]{:S(2)}) collective-permute-start(f32[1,14,128,128]{3,2,1,0:T(8,128)S(1)} %collective-permute-done.16), channel_id=1, source_target_pairs={{0,1},{1,2},{2,3},{3,4},{4,5},{5,6},{6,7},{7,8},{8,9},{9,10},{10,1... | collective-permute-start | bytes 2752520 | tf_op jit(solution)/shard_map/ppermute | solution.py:12
  379.0 21.6 %collective-permute-start.24 = (f32[1,14,128,128]{3,2,1,0:T(8,128)S(1)}, f32[1,14,128,128]{3,2,1,0:T(8,128)S(1)}, u32[]{:S(2)}, u32[]{:S(2)}) collective-permute-start(f32[1,14,128,128]{3,2,1,0:T(8,128)S(1)} %collective-permute-done.23), channel_id=1, source_target_pairs={{0,15},{1,0},{2,1},{3,2},{4,3},{5,4},{6,5},{7,6},{8,7},{9,8},{10,9... | collective-permute-start | bytes 2752520 | tf_op jit(solution)/shard_map/ppermute | solution.py:12
  397.7 22.2 %collective-permute-start.18 = (f32[1,14,128,128]{3,2,1,0:T(8,128)S(1)}, f32[1,14,128,128]{3,2,1,0:T(8,128)S(1)}, u32[]{:S(2)}, u32[]{:S(2)}) collective-permute-start(f32[1,14,128,128]{3,2,1,0:T(8,128)S(1)} %collective-permute-done.17), channel_id=1, source_target_pairs={{0,1},{1,2},{2,3},{3,4},{4,5},{5,6},{6,7},{7,8},{8,9},{9,10},{10,1... | collective-permute-start | bytes 2752520 | tf_op jit(solution)/shard_map/ppermute | solution.py:12
  400.7 20.8 %collective-permute-start.25 = (f32[1,14,128,128]{3,2,1,0:T(8,128)S(1)}, f32[1,14,128,128]{3,2,1,0:T(8,128)}, u32[]{:S(2)}, u32[]{:S(2)}) collective-permute-start(f32[1,14,128,128]{3,2,1,0:T(8,128)S(1)} %collective-permute-done.24), channel_id=1, source_target_pairs={{0,15},{1,0},{2,1},{3,2},{4,3},{5,4},{6,5},{7,6},{8,7},{9,8},{10,9... | collective-permute-start | bytes 2752520 | tf_op jit(solution)/shard_map/ppermute | solution.py:12
  419.9 22.8 %collective-permute-start.19 = (f32[1,14,128,128]{3,2,1,0:T(8,128)S(1)}, f32[1,14,128,128]{3,2,1,0:T(8,128)}, u32[]{:S(2)}, u32[]{:S(2)}) collective-permute-start(f32[1,14,128,128]{3,2,1,0:T(8,128)S(1)} %collective-permute-done.18), channel_id=1, source_target_pairs={{0,1},{1,2},{2,3},{3,4},{4,5},{5,6},{6,7},{7,8},{8,9},{9,10},{10,1... | collective-permute-start | bytes 2752520 | tf_op jit(solution)/shard_map/ppermute | solution.py:12
  421.5 22.1 %collective-permute-start.26 = (f32[1,14,128,128]{3,2,1,0:T(8,128)}, f32[1,14,128,128]{3,2,1,0:T(8,128)}, u32[]{:S(2)}, u32[]{:S(2)}) collective-permute-start(f32[1,14,128,128]{3,2,1,0:T(8,128)} %collective-permute-done.25), channel_id=1, source_target_pairs={{0,15},{1,0},{2,1},{3,2},{4,3},{5,4},{6,5},{7,6},{8,7},{9,8},{10,9... | collective-permute-start | bytes 2752520 | tf_op jit(solution)/shard_map/ppermute | solution.py:12
  442.7 20.6 %collective-permute-start.20 = (f32[1,14,128,128]{3,2,1,0:T(8,128)}, f32[1,14,128,128]{3,2,1,0:T(8,128)}, u32[]{:S(2)}, u32[]{:S(2)}) collective-permute-start(f32[1,14,128,128]{3,2,1,0:T(8,128)} %collective-permute-done.19), channel_id=1, source_target_pairs={{0,1},{1,2},{2,3},{3,4},{4,5},{5,6},{6,7},{7,8},{8,9},{9,10},{10,1... | collective-permute-start | bytes 2752520 | tf_op jit(solution)/shard_map/ppermute | solution.py:12
  442.7 38.0 %copy-start.8 = (f32[1,14,128,128]{3,2,1,0:T(8,128)S(1)}, f32[1,14,128,128]{3,2,1,0:T(8,128)}, u32[]{:S(2)}) copy-start(f32[1,14,128,128]{3,2,1,0:T(8,128)} %copy-done.7) | copy-start | bytes 2752516
  442.7 39.0 %copy-start.12 = (f32[1,14,128,128]{3,2,1,0:T(8,128)S(1)}, f32[1,14,128,128]{3,2,1,0:T(8,128)}, u32[]{:S(2)}) copy-start(f32[1,14,128,128]{3,2,1,0:T(8,128)} %copy-done.11) | copy-start | bytes 2752516
  442.7 40.1 %copy-start.15 = (f32[1,14,128,128]{3,2,1,0:T(8,128)S(1)}, f32[1,14,128,128]{3,2,1,0:T(8,128)}, u32[]{:S(2)}) copy-start(f32[1,14,128,128]{3,2,1,0:T(8,128)} %copy-done.14) | copy-start | bytes 2752516
  443.6 44.6 %collective-permute-start.27 = (f32[1,14,128,128]{3,2,1,0:T(8,128)}, f32[1,14,128,128]{3,2,1,0:T(8,128)S(1)}, u32[]{:S(2)}, u32[]{:S(2)}) collective-permute-start(f32[1,14,128,128]{3,2,1,0:T(8,128)} %collective-permute-done.26), channel_id=1, source_target_pairs={{0,15},{1,0},{2,1},{3,2},{4,3},{5,4},{6,5},{7,6},{8,7},{9,8},{10,9... | collective-permute-start | bytes 2752520 | tf_op jit(solution)/shard_map/ppermute | solution.py:12
  501.8 247.1 %copy-start.18 = (f32[3]{0:T(128)S(1)}, f32[3]{0:T(128)}, u32[]{:S(2)}) copy-start(f32[3]{0:T(128)} %param.19) | copy-start | bytes 40
  619.2 159.4 %copy-start.1 = (f32[1,14,128,128]{3,2,1,0:T(8,128)}, f32[1,14,128,128]{3,2,1,0:T(8,128)S(1)}, u32[]{:S(2)}) copy-start(f32[1,14,128,128]{3,2,1,0:T(8,128)S(1)} %bitcast_subtract_fusion.1) | copy-start | bytes 2752516
  619.2 21.4 %collective-permute-start.28 = (f32[1,14,128,128]{3,2,1,0:T(8,128)S(1)}, f32[1,14,128,128]{3,2,1,0:T(8,128)S(1)}, u32[]{:S(2)}, u32[]{:S(2)}) collective-permute-start(f32[1,14,128,128]{3,2,1,0:T(8,128)S(1)} %bitcast_subtract_fusion.1), channel_id=1, source_target_pairs={{0,1},{1,2},{2,3},{3,4},{4,5},{5,6},{6,7},{7,8},{8,9},{9,10},{10,1... | collective-permute-start | bytes 2752520 | tf_op jit(solution)/shard_map/ppermute | solution.py:12
  619.3 22.5 %collective-permute-start.35 = (f32[1,14,128,128]{3,2,1,0:T(8,128)S(1)}, f32[1,14,128,128]{3,2,1,0:T(8,128)S(1)}, u32[]{:S(2)}, u32[]{:S(2)}) collective-permute-start(f32[1,14,128,128]{3,2,1,0:T(8,128)S(1)} %bitcast_subtract_fusion.1), channel_id=1, source_target_pairs={{0,15},{1,0},{2,1},{3,2},{4,3},{5,4},{6,5},{7,6},{8,7},{9,8},{10,9... | collective-permute-start | bytes 2752520 | tf_op jit(solution)/shard_map/ppermute | solution.py:12
  640.6 22.1 %collective-permute-start.29 = (f32[1,14,128,128]{3,2,1,0:T(8,128)S(1)}, f32[1,14,128,128]{3,2,1,0:T(8,128)S(1)}, u32[]{:S(2)}, u32[]{:S(2)}) collective-permute-start(f32[1,14,128,128]{3,2,1,0:T(8,128)S(1)} %collective-permute-done.28), channel_id=1, source_target_pairs={{0,1},{1,2},{2,3},{3,4},{4,5},{5,6},{6,7},{7,8},{8,9},{9,10},{10,1... | collective-permute-start | bytes 2752520 | tf_op jit(solution)/shard_map/ppermute | solution.py:12
  641.8 22.0 %collective-permute-start.36 = (f32[1,14,128,128]{3,2,1,0:T(8,128)S(1)}, f32[1,14,128,128]{3,2,1,0:T(8,128)S(1)}, u32[]{:S(2)}, u32[]{:S(2)}) collective-permute-start(f32[1,14,128,128]{3,2,1,0:T(8,128)S(1)} %collective-permute-done.35), channel_id=1, source_target_pairs={{0,15},{1,0},{2,1},{3,2},{4,3},{5,4},{6,5},{7,6},{8,7},{9,8},{10,9... | collective-permute-start | bytes 2752520 | tf_op jit(solution)/shard_map/ppermute | solution.py:12
  662.7 22.4 %collective-permute-start.30 = (f32[1,14,128,128]{3,2,1,0:T(8,128)S(1)}, f32[1,14,128,128]{3,2,1,0:T(8,128)S(1)}, u32[]{:S(2)}, u32[]{:S(2)}) collective-permute-start(f32[1,14,128,128]{3,2,1,0:T(8,128)S(1)} %collective-permute-done.29), channel_id=1, source_target_pairs={{0,1},{1,2},{2,3},{3,4},{4,5},{5,6},{6,7},{7,8},{8,9},{9,10},{10,1... | collective-permute-start | bytes 2752520 | tf_op jit(solution)/shard_map/ppermute | solution.py:12
  663.8 21.8 %collective-permute-start.37 = (f32[1,14,128,128]{3,2,1,0:T(8,128)S(1)}, f32[1,14,128,128]{3,2,1,0:T(8,128)S(1)}, u32[]{:S(2)}, u32[]{:S(2)}) collective-permute-start(f32[1,14,128,128]{3,2,1,0:T(8,128)S(1)} %collective-permute-done.36), channel_id=1, source_target_pairs={{0,15},{1,0},{2,1},{3,2},{4,3},{5,4},{6,5},{7,6},{8,7},{9,8},{10,9... | collective-permute-start | bytes 2752520 | tf_op jit(solution)/shard_map/ppermute | solution.py:12
  685.2 20.3 %collective-permute-start.31 = (f32[1,14,128,128]{3,2,1,0:T(8,128)S(1)}, f32[1,14,128,128]{3,2,1,0:T(8,128)S(1)}, u32[]{:S(2)}, u32[]{:S(2)}) collective-permute-start(f32[1,14,128,128]{3,2,1,0:T(8,128)S(1)} %collective-permute-done.30), channel_id=1, source_target_pairs={{0,1},{1,2},{2,3},{3,4},{4,5},{5,6},{6,7},{7,8},{8,9},{9,10},{10,1... | collective-permute-start | bytes 2752520 | tf_op jit(solution)/shard_map/ppermute | solution.py:12
  685.6 22.4 %collective-permute-start.38 = (f32[1,14,128,128]{3,2,1,0:T(8,128)S(1)}, f32[1,14,128,128]{3,2,1,0:T(8,128)S(1)}, u32[]{:S(2)}, u32[]{:S(2)}) collective-permute-start(f32[1,14,128,128]{3,2,1,0:T(8,128)S(1)} %collective-permute-done.37), channel_id=1, source_target_pairs={{0,15},{1,0},{2,1},{3,2},{4,3},{5,4},{6,5},{7,6},{8,7},{9,8},{10,9... | collective-permute-start | bytes 2752520 | tf_op jit(solution)/shard_map/ppermute | solution.py:12
  705.5 21.3 %collective-permute-start.32 = (f32[1,14,128,128]{3,2,1,0:T(8,128)S(1)}, f32[1,14,128,128]{3,2,1,0:T(8,128)S(1)}, u32[]{:S(2)}, u32[]{:S(2)}) collective-permute-start(f32[1,14,128,128]{3,2,1,0:T(8,128)S(1)} %collective-permute-done.31), channel_id=1, source_target_pairs={{0,1},{1,2},{2,3},{3,4},{4,5},{5,6},{6,7},{7,8},{8,9},{9,10},{10,1... | collective-permute-start | bytes 2752520 | tf_op jit(solution)/shard_map/ppermute | solution.py:12
  708.0 21.5 %collective-permute-start.39 = (f32[1,14,128,128]{3,2,1,0:T(8,128)S(1)}, f32[1,14,128,128]{3,2,1,0:T(8,128)S(1)}, u32[]{:S(2)}, u32[]{:S(2)}) collective-permute-start(f32[1,14,128,128]{3,2,1,0:T(8,128)S(1)} %collective-permute-done.38), channel_id=1, source_target_pairs={{0,15},{1,0},{2,1},{3,2},{4,3},{5,4},{6,5},{7,6},{8,7},{9,8},{10,9... | collective-permute-start | bytes 2752520 | tf_op jit(solution)/shard_map/ppermute | solution.py:12
  726.8 22.1 %collective-permute-start.33 = (f32[1,14,128,128]{3,2,1,0:T(8,128)S(1)}, f32[1,14,128,128]{3,2,1,0:T(8,128)S(1)}, u32[]{:S(2)}, u32[]{:S(2)}) collective-permute-start(f32[1,14,128,128]{3,2,1,0:T(8,128)S(1)} %collective-permute-done.32), channel_id=1, source_target_pairs={{0,1},{1,2},{2,3},{3,4},{4,5},{5,6},{6,7},{7,8},{8,9},{9,10},{10,1... | collective-permute-start | bytes 2752520 | tf_op jit(solution)/shard_map/ppermute | solution.py:12
  729.5 21.2 %collective-permute-start.40 = (f32[1,14,128,128]{3,2,1,0:T(8,128)S(1)}, f32[1,14,128,128]{3,2,1,0:T(8,128)S(1)}, u32[]{:S(2)}, u32[]{:S(2)}) collective-permute-start(f32[1,14,128,128]{3,2,1,0:T(8,128)S(1)} %collective-permute-done.39), channel_id=1, source_target_pairs={{0,15},{1,0},{2,1},{3,2},{4,3},{5,4},{6,5},{7,6},{8,7},{9,8},{10,9... | collective-permute-start | bytes 2752520 | tf_op jit(solution)/shard_map/ppermute | solution.py:12
  748.9 22.7 %collective-permute-start.34 = (f32[1,14,128,128]{3,2,1,0:T(8,128)S(1)}, f32[1,14,128,128]{3,2,1,0:T(8,128)S(1)}, u32[]{:S(2)}, u32[]{:S(2)}) collective-permute-start(f32[1,14,128,128]{3,2,1,0:T(8,128)S(1)} %collective-permute-done.33), channel_id=1, source_target_pairs={{0,1},{1,2},{2,3},{3,4},{4,5},{5,6},{6,7},{7,8},{8,9},{9,10},{10,1... | collective-permute-start | bytes 2752520 | tf_op jit(solution)/shard_map/ppermute | solution.py:12
  750.6 35.1 %collective-permute-start.41 = (f32[1,14,128,128]{3,2,1,0:T(8,128)S(1)}, f32[1,14,128,128]{3,2,1,0:T(8,128)S(1)}, u32[]{:S(2)}, u32[]{:S(2)}) collective-permute-start(f32[1,14,128,128]{3,2,1,0:T(8,128)S(1)} %collective-permute-done.40), channel_id=1, source_target_pairs={{0,15},{1,0},{2,1},{3,2},{4,3},{5,4},{6,5},{7,6},{8,7},{9,8},{10,9... | collective-permute-start | bytes 2752520 | tf_op jit(solution)/shard_map/ppermute | solution.py:12
  (13 other events, 188.2 us)
where the time goes:
time: 923 us; the launch traced here: 921 us
  waiting for transfers between devices  397 us (43%)
  local copies, waits for them, and re-layouts  376 us (41%)
  matrix products  67.6 us (7%)
  starting transfers between devices  38.8 us (4%)
  blocking collectives  19.8 us (2%)
  other arithmetic  18.6 us (2%)
    ppermute x42, waiting for transfers between devices, from_behind(): lax.ppermute(x, axis, [(i, (i + by) % devices) for i in range(devices)])  397 us
    gather x42, local copies, waits for them, and re-layouts, target_block(): gathered = window[relative, slot_index]  244 us
    dot_general x42, matrix products, target_block(): jnp.einsum('iaxy,iayz->ixz', h_blocks, gathered, precision=lax.Precision....  67.6 us
    unnamed x80, local copies, waits for them, and re-layouts  65.2 us
    ppermute x42, starting transfers between devices, from_behind(): lax.ppermute(x, axis, [(i, (i + by) % devices) for i in range(devices)])  38.8 us
    concatenate x3, local copies, waits for them, and re-layouts, per_device(): window = jnp.concatenate([window, empty_slot], axis=1)  38.1 us
    dynamic_update_slice x84, local copies, waits for them, and re-layouts, per_device(): stacked = lax.map(target_block, position_t)  21.8 us
    all_gather x1, blocking collectives, per_device(): all_cols = lax.all_gather(t_cols, 'row', axis=0, tiled=True)  19.8 us
  transfers between devices with their start and end apart: 42, of which 37 were waited for; matrix products, arithmetic and copies ran while one was open for 8% of the time, Pallas kernels for 0%

commit v1 on v0

v1 whole, which is shorter than its diff:
```python
import functools

import jax
import jax.numpy as jnp
from jax import lax
from jax.experimental import pallas as pl
from jax.experimental.pallas import tpu as pltpu
from jax.sharding import PartitionSpec as P

REACH = 7
STEPS = 3
STAGES = 4


def place_of(offset, dropped):
    named = jnp.logical_and(offset <= 2 * REACH, offset != dropped)
    slot = offset - jnp.where(offset > dropped, 1, 0)
    return jnp.clip(slot, 0, 2 * REACH - 1), named


def dropped_offset(cols, row, total):
    offsets = jnp.mod(cols - row + REACH, total)
    return REACH * (2 * REACH + 1) - jnp.sum(offsets, axis=1)


def pack_kernel(total, row_ref, cols_ref, cur_ref, prev_ref, send_ref, zeros, sem):
    row = row_ref[0]
    drop = row_ref[1]
    zeros[...] = jnp.zeros_like(zeros)
    for k in range(cols_ref.shape[0]):
        col = cols_ref[k]
        pltpu.make_async_copy(cur_ref.at[k], send_ref.at[col, 0], sem).start()
        pltpu.make_async_copy(prev_ref.at[k], send_ref.at[col, 1], sem).start()

    def fill(j, carry):
        offset = lax.rem(j - row + REACH + total, total)
        _, named = place_of(offset, drop)

        @pl.when(jnp.logical_not(named))
        def _():
            pltpu.make_async_copy(zeros, send_ref.at[j], sem).start()

        return carry

    lax.fori_loop(0, total, fill, 0)
    pltpu.make_async_copy(send_ref, send_ref, sem).wait()


def split(x):
    high = x.astype(jnp.bfloat16)
    low = (x - high.astype(jnp.float32)).astype(jnp.bfloat16)
    return high, low


def column_kernel(
    total, window, drops_ref, base_ref, coefs_ref, h_ref, t_ref, out_ref,
    stage, dense, pair, terms, h_sem, t_sem, out_sem,
):
    size = h_ref.shape[-1]
    base = base_ref[0]
    column = base_ref[1]

    def row_of(w):
        return lax.rem(base + w, total)

    def h_copy(w):
        slot = lax.rem(w, STAGES)
        return pltpu.make_async_copy(h_ref.at[row_of(w)], stage.at[slot], h_sem.at[slot])

    def t_copy(w):
        return pltpu.make_async_copy(t_ref.at[row_of(w)], terms.at[w, pl.ds(0, 2)], t_sem)

    def kept(w):
        row = row_of(w)
        offset = lax.rem(column - row + REACH + total, total)
        _, named = place_of(offset, drops_ref[2 * row + 1])
        return named

    for w in range(window):
        t_copy(w).start()
    for w in range(STAGES):
        h_copy(jnp.int32(w)).start()
    pltpu.make_async_copy(terms.at[:, pl.ds(0, 2)], terms.at[:, pl.ds(0, 2)], t_sem).wait()
    for w in range(window):
        high, low = split(jnp.where(kept(w), terms[w, 0], 0.0))
        pair[0, pl.ds(w * size, size), pl.ds(0, size)] = high
        pair[0, pl.ds(w * size, size), pl.ds(size, size)] = low

    def densify(w):
        row = row_of(w)
        drop = drops_ref[2 * row]
        slot = lax.rem(w, STAGES)
        for p in range(window):
            offset = lax.rem(row_of(p) - row + REACH + total, total)
            k, named = place_of(offset, drop)
            high, low = split(jnp.where(named, stage[slot, k], 0.0))
            dense[w, pl.ds(0, size), pl.ds(p * size, size)] = high
            dense[w, pl.ds(size, size), pl.ds(p * size, size)] = low

    def advance(step, w, source):
        older = 1 if step % 2 == 0 else 0
        parts = jnp.dot(dense[w], source, preferred_element_type=jnp.float32)
        parts = parts[:size] + parts[size:]
        product = parts[:, :size] + parts[:, size:]
        newest = jnp.where(kept(w), 2.0 * product - terms[w, older], 0.0)
        terms[w, older] = newest
        gain = coefs_ref[step] * newest
        terms[w, 2] = gain if step == 0 else terms[w, 2] + gain
        if step < STEPS - 1:
            high, low = split(newest)
            into = 1 - step % 2
            at = pl.ds(pl.multiple_of(w * size, size), size)
            pair[into, at, pl.ds(0, size)] = high
            pair[into, at, pl.ds(size, size)] = low

    def first(w, carry):
        h_copy(w).wait()
        densify(w)

        @pl.when(w + STAGES < window)
        def _():
            h_copy(w + STAGES).start()

        advance(0, w, pair[0])
        return carry

    lax.fori_loop(0, window, first, 0)
    for step in range(1, STEPS):

        def later(w, carry, step=step):
            advance(step, w, pair[step % 2])
            if step == STEPS - 1:
                pltpu.make_async_copy(terms.at[w], out_ref.at[row_of(w)], out_sem).start()
            return carry

        lax.fori_loop(0, window, later, 0)
    pltpu.make_async_copy(terms, terms, out_sem).wait()


def unpack_kernel(
    cols_ref, recv_ref, density_ref, out_density, out_last, out_before, gains, total, sems
):
    count = cols_ref.shape[0]
    load = pltpu.make_async_copy(density_ref, total, sems.at[0])
    load.start()
    for k in range(count):
        pltpu.make_async_copy(recv_ref.at[cols_ref[k], 2], gains.at[k], sems.at[1]).start()
    for k in range(count):
        col = cols_ref[k]
        pltpu.make_async_copy(recv_ref.at[col, 0], out_before.at[k], sems.at[2]).start()
        pltpu.make_async_copy(recv_ref.at[col, 1], out_last.at[k], sems.at[3]).start()
    load.wait()
    pltpu.make_async_copy(gains, gains, sems.at[1]).wait()
    total[...] += gains[...]
    store = pltpu.make_async_copy(total, out_density, sems.at[0])
    store.start()
    pltpu.make_async_copy(out_before, out_before, sems.at[2]).wait()
    pltpu.make_async_copy(out_last, out_last, sems.at[3]).wait()
    store.wait()


SMEM = pl.BlockSpec(memory_space=pltpu.SMEM)
ANY = pl.BlockSpec(memory_space=pl.ANY)


def per_device(h_blocks, h_cols, term_prev, term_cur, t_cols, density_in, coefs):
    total = lax.axis_size("row")
    me = lax.axis_index("row")
    count, size = h_blocks.shape[1:3]
    window = total if total <= 2 * REACH + 2 else 2 * REACH + 1
    base = jnp.int32(0) if window == total else jnp.mod(me - REACH, total)
    drop_h = dropped_offset(h_cols, me, total)
    drop_t = dropped_offset(t_cols, me, total)
    block = (size, size)

    h_all = lax.all_gather(h_blocks, "row", axis=0, tiled=True)
    drops = lax.all_gather(jnp.stack([drop_h, drop_t], axis=1), "row", axis=0, tiled=True)
    send = pl.pallas_call(
        functools.partial(pack_kernel, total),
        out_shape=jax.ShapeDtypeStruct((total, 2) + block, jnp.float32),
        in_specs=[SMEM, SMEM, ANY, ANY],
        out_specs=ANY,
        scratch_shapes=[pltpu.VMEM((2,) + block, jnp.float32), pltpu.SemaphoreType.DMA],
        name="pack",
    )(jnp.stack([me, drop_t[0]]), t_cols[0], term_cur[0], term_prev[0])
    columns = lax.all_to_all(send, "row", 0, 0, tiled=True)
    result = pl.pallas_call(
        functools.partial(column_kernel, total, window),
        out_shape=jax.ShapeDtypeStruct((total, 3) + block, jnp.float32),
        in_specs=[SMEM, SMEM, SMEM, ANY, ANY],
        out_specs=ANY,
        scratch_shapes=[
            pltpu.VMEM((STAGES, count) + block, jnp.float32),
            pltpu.VMEM((window, 2 * size, window * size), jnp.bfloat16),
            pltpu.VMEM((2, window * size, 2 * size), jnp.bfloat16),
            pltpu.VMEM((window, 3) + block, jnp.float32),
            pltpu.SemaphoreType.DMA((STAGES,)),
            pltpu.SemaphoreType.DMA,
            pltpu.SemaphoreType.DMA,
        ],
        compiler_params=pltpu.CompilerParams(vmem_limit_bytes=44 * 1024 * 1024),
        name="steps",
    )(drops.reshape(-1), jnp.stack([base, me]), coefs, h_all, columns)
    back = lax.all_to_all(result, "row", 0, 0, tiled=True)
    row_shape = jax.ShapeDtypeStruct((count,) + block, jnp.float32)
    density, last, before = pl.pallas_call(
        unpack_kernel,
        out_shape=(row_shape, row_shape, row_shape),
        in_specs=[SMEM, ANY, ANY],
        out_specs=(ANY, ANY, ANY),
        scratch_shapes=[
            pltpu.VMEM((count,) + block, jnp.float32),
            pltpu.VMEM((count,) + block, jnp.float32),
            pltpu.SemaphoreType.DMA((4,)),
        ],
        name="unpack",
    )(t_cols[0], back, density_in[0])
    return density[None], last[None], before[None]


def solution(mesh):
    blocks = P(("groups", "row"), None, None, None)
    cols = P(("groups", "row"), None)
    return jax.shard_map(
        per_device,
        mesh=mesh,
        in_specs=(blocks, cols, blocks, blocks, cols, blocks, P()),
        out_specs=(blocks, blocks, blocks),
        check_vma=False,
    )
```

time: 923 us -> 347 us (0.38)
  waiting for transfers between devices: 397 us -> 0.69 us
  local copies, waits for them, and re-layouts: 376 us -> 0.6 us
  blocking collectives: 19.8 us -> 171 us
  Pallas kernels: 0 us -> 147 us
  matrix products: 67.6 us -> 0 us
  starting transfers between devices: 38.8 us -> 6.18 us
  other arithmetic: 18.6 us -> 2.73 us
  between operations: 0.81 us -> 15.4 us
    ppermute x42 -> x0, waiting for transfers between devices: 397 us -> none  [from_behind(): lax.ppermute(x, axis, [(i, (i + by) % devices) for i in range(devices)])]
    gather x44 -> x0, local copies, waits for them, and re-layouts: 245 us -> none  [the longest x42 244 us: target_block(): gathered = window[relative, slot_index]]
    pallas_call x0 -> x3, Pallas kernels: none -> 147 us  [the longest x1 57.5 us: per_device(): pl.pallas_call(functools.partial(pack_kernel, total), out_shape=jax.Shape...]
    all_gather x1, blocking collectives: 19.8 us -> 98.2 us  [per_device(): lax.all_gather(jnp.stack([drop_h, drop_t], axis=1), 'row', axis=0, tiled=...]
    all_to_all x0 -> x1, blocking collectives: none -> 73.1 us  [per_device(): back = lax.all_to_all(result, 'row', 0, 0, tiled=True)]
    dot_general x42 -> x0, matrix products: 67.6 us -> none  [target_block(): jnp.einsum('iaxy,iayz->ixz', h_blocks, gathered, precision=lax.Precision....]
    unnamed x80 -> x2, local copies, waits for them, and re-layouts: 65.2 us -> 0.01 us
    concatenate x6 -> x0, local copies, waits for them, and re-layouts: 41.2 us -> none  [the longest x3 38.1 us: per_device(): window = jnp.concatenate([window, empty_slot], axis=1)]
  transfers between devices with their start and end apart: 42 -> 2, of which waited for: 37 -> 0; matrix products, arithmetic and copies ran while one was open for 8% -> 1% of each run, Pallas kernels for 0% -> 17%
where the time goes in v1:
time: 347 us; the launch traced here: 344 us
  blocking collectives  171 us (49%)
  Pallas kernels  147 us (42%)
  between operations  15.4 us (4%)
  starting transfers between devices  6.18 us (2%)
    all_gather x1, blocking collectives, per_device(): lax.all_gather(jnp.stack([drop_h, drop_t], axis=1), 'row', axis=0, tiled=...  98.2 us
    all_to_all x1, blocking collectives, per_device(): back = lax.all_to_all(result, 'row', 0, 0, tiled=True)  73.1 us
    pallas_call x1, Pallas kernels, per_device(): pl.pallas_call(functools.partial(pack_kernel, total), out_shape=jax.Shape...  57.5 us
    pallas_call x1, Pallas kernels, per_device(): pl.pallas_call(unpack_kernel, out_shape=(row_shape, row_shape, row_shape)...  57.4 us
    pallas_call x1, Pallas kernels, per_device(): pl.pallas_call(functools.partial(column_kernel, total, window), out_shape...  31.9 us
  transfers between devices with their start and end apart: 2, of which 0 were waited for; matrix products, arithmetic and copies ran while one was open for 1% of the time, Pallas kernels for 17%

profile of v1, /device:TPU:22, one launch (start us, length us, event | category | flops | bytes accessed | tf_op | source)
XLA Modules:
  0.0 343.7 jit_solution(2210468741756759191)
XLA Ops:
  7.2 0.0 all-gather.3.cloned.1.call-start
  7.2 0.7 all-gather.3.cloned.1.call-update
  7.9 1.3 fusion
  9.9 0.6 pad_add_fusion.1.row_ref
  10.5 0.0 copy-start
  10.5 57.5 %pack.1 = f32[16,2,128,128]{3,2,1,0:T(8,128)} custom-call(s32[2]{0:T(128)} %pad_add_fusion.1.row_ref, s32[14]{0:T(128)} %bitcast.16, f32[14,128,128]{2,1,0:T(8,128)} %bitcast.13, f32[14,128,128]{2,1,0:T(8,128)} %bitcast.14), custom_call_target="tpu_custom_call" | custom-call | tf_op jit(solution)/shard_map/pack/pallas_call | solution.py:178
  68.0 6.1 %all-to-all-start = ((f32[16,2,128,128]{3,2,1,0:T(8,128)}), f32[16,2,128,128]{3,2,1,0:T(8,128)S(1)}, u32[]{:S(2)}, u32[]{:S(2)}) async-start(f32[16,2,128,128]{3,2,1,0:T(8,128)} %pack.1), calls=%async_computation | async-start | bytes 4194304 | tf_op jit(solution)/shard_map/all_to_all | solution.py:186
  74.8 0.1 add_bitcast_fusion
  74.8 98.2 %all-gather = s32[16,1,2]{2,1,0:T(1,128)S(1)} all-gather(s32[1,1,2]{2,1,0:T(1,128)S(1)} %add_bitcast_fusion), channel_id=1, replica_groups=mesh['groups'=2,'row'=16] {'row'}, dimensions={0}, use_global_device_ids=true | all-gather | bytes 136 | tf_op jit(solution)/shard_map/all_gather | solution.py:177
  173.1 0.5 broadcast.21
  173.6 0.7 reduce.5
  174.3 0.1 reshape.17.drops_ref
  174.3 0.1 pad_add_fusion.base_ref
  174.4 0.0 all-to-all-done.t_ref
  174.4 0.0 all-gather.3.cloned.1.call-done.h_ref
  174.4 0.0 copy-done
  174.4 31.9 %steps.1 = f32[16,3,128,128]{3,2,1,0:T(8,128)S(1)} custom-call(s32[32]{0:T(128)S(1)} %reshape.17.drops_ref, s32[2]{0:T(128)S(1)} %pad_add_fusion.base_ref, f32[3]{0:T(128)S(1)} %copy-done, f32[16,14,128,128]{3,2,1,0:T(8,128)} %all-gather.3.cloned.1.call-done.h_ref, f32[16,2,128,128]{3,2,1,0:T(8,128)S(1)} %all-to-all-done.t_ref), custom_call_target="tpu_custom_call" | custom-call | tf_op jit(solution)/shard_map/steps/pallas_call | solution.py:187
  206.3 73.1 %all_to_all.10.recv_ref = f32[16,3,128,128]{3,2,1,0:T(8,128)} all-to-all(f32[16,3,128,128]{3,2,1,0:T(8,128)S(1)} %steps.1), channel_id=1, replica_groups=mesh['groups'=2,'row'=16] {'row'}, dimensions={0} | all-to-all | bytes 6291456 | tf_op jit(solution)/shard_map/all_to_all | solution.py:204
  279.4 57.4 %unpack.1 = (f32[14,128,128]{2,1,0:T(8,128)}, f32[14,128,128]{2,1,0:T(8,128)}, f32[14,128,128]{2,1,0:T(8,128)}) custom-call(s32[14]{0:T(128)} %bitcast.17, f32[16,3,128,128]{3,2,1,0:T(8,128)} %all_to_all.10.recv_ref, f32[14,128,128]{2,1,0:T(8,128)} %bitcast.15), custom_call_target="tpu_custom_call" | custom-call | tf_op jit(solution)/shard_map/unpack/pallas_call | solution.py:206
Async XLA Ops:
  7.2 167.3 %all-gather.3.cloned.1.call-start = ((), (), s32[]{:S(2)}) async-start(), calls=%async_computation.2 | async-start | bytes 15597568 | tf_op jit(solution)/shard_map/all_gather | solution.py:176
  10.5 164.0 %copy-start = (f32[3]{0:T(128)S(1)}, f32[3]{0:T(128)}, u32[]{:S(2)}) copy-start(f32[3]{0:T(128)} %coefs_ref.1) | copy-start | bytes 40
  68.0 106.5 %all-to-all-start = ((f32[16,2,128,128]{3,2,1,0:T(8,128)}), f32[16,2,128,128]{3,2,1,0:T(8,128)S(1)}, u32[]{:S(2)}, u32[]{:S(2)}) async-start(f32[16,2,128,128]{3,2,1,0:T(8,128)} %pack.1), calls=%async_computation | async-start | bytes 4194304 | tf_op jit(solution)/shard_map/all_to_all | solution.py:186
Sparse Core Ops, SparseCore 0:
  10.3 151.0 all-gather.2

commit v2 on v1

v2 whole, which is shorter than its diff:
```python
import functools

import jax
import jax.numpy as jnp
from jax import lax
from jax.experimental import pallas as pl
from jax.experimental.pallas import tpu as pltpu
from jax.sharding import PartitionSpec as P

REACH = 7
STEPS = 3
NOTE = 8


def place_of(offset, dropped):
    named = jnp.logical_and(offset <= 2 * REACH, offset != dropped)
    slot = offset - jnp.where(offset > dropped, 1, 0)
    return jnp.clip(slot, 0, 2 * REACH - 1), named


def dropped_offset(cols, row, total):
    offsets = jnp.mod(cols - row + REACH, total)
    return REACH * (2 * REACH + 1) - jnp.sum(offsets, axis=1)


def pack_kernel(total, info_ref, cols_ref, cur_ref, prev_ref, send_ref, cur, prev, zeros, note, sems):
    row = info_ref[0]
    drop = info_ref[2]
    count, size = cur.shape[:2]
    loads = (
        pltpu.make_async_copy(cur_ref, cur, sems.at[0]),
        pltpu.make_async_copy(prev_ref, prev, sems.at[1]),
    )
    for load in loads:
        load.start()
    zeros[...] = jnp.zeros_like(zeros)
    line = lax.broadcasted_iota(jnp.int32, note.shape, 0)
    note[...] = jnp.where(line == 0, info_ref[1], drop).astype(jnp.float32)

    def fill(j, carry):
        offset = lax.rem(j - row + REACH + total, total)
        _, named = place_of(offset, drop)
        pltpu.make_async_copy(note, send_ref.at[j, pl.ds(2 * size, NOTE)], sems.at[2]).start()

        @pl.when(jnp.logical_not(named))
        def _():
            pltpu.make_async_copy(zeros, send_ref.at[j, pl.ds(0, 2 * size)], sems.at[2]).start()

        return carry

    lax.fori_loop(0, total, fill, 0)
    for which, held in enumerate((cur, prev)):
        loads[which].wait()
        for k in range(count):
            place = send_ref.at[cols_ref[k], pl.ds(which * size, size)]
            pltpu.make_async_copy(held.at[k], place, sems.at[2]).start()
    pltpu.make_async_copy(send_ref, send_ref, sems.at[2]).wait()


def split(x):
    high = x.astype(jnp.bfloat16)
    low = (x - high.astype(jnp.float32)).astype(jnp.bfloat16)
    return high, low


def column_kernel(
    total, window, group, drops_ref, base_ref, coefs_ref, h_ref, t_ref, out_ref,
    stage, dense, pair, terms, h_sem, t_sem, out_sem,
):
    size = h_ref.shape[-1]
    base = base_ref[0]
    column = base_ref[1]
    groups = window // group

    def row_of(w):
        return lax.rem(base + w, total)

    def h_copy(w):
        slot = lax.rem(w, 2 * group)
        return pltpu.make_async_copy(h_ref.at[row_of(w)], stage.at[slot], h_sem.at[slot])

    def kept(w):
        row = row_of(w)
        offset = lax.rem(column - row + REACH + total, total)
        _, named = place_of(offset, drops_ref[2 * row + 1])
        return named

    for w in range(2 * group):
        h_copy(jnp.int32(w)).start()
    for w in range(window):
        for which in range(2):
            block = t_ref.at[row_of(w), pl.ds(which * size, size)]
            pltpu.make_async_copy(block, terms.at[w, which], t_sem).start()
    pltpu.make_async_copy(terms.at[:, pl.ds(0, 2)], terms.at[:, pl.ds(0, 2)], t_sem).wait()
    for w in range(window):
        high, low = split(jnp.where(kept(w), terms[w, 0], 0.0))
        pair[0, pl.ds(w * size, size), pl.ds(0, size)] = high
        pair[0, pl.ds(w * size, size), pl.ds(size, size)] = low

    def densify(w):
        row = row_of(w)
        drop = drops_ref[2 * row]
        slot = lax.rem(w, 2 * group)
        for p in range(window):
            offset = lax.rem(row_of(p) - row + REACH + total, total)
            k, named = place_of(offset, drop)
            high, low = split(jnp.where(named, stage[slot, k], 0.0))
            dense[w, pl.ds(0, size), pl.ds(p * size, size)] = high
            dense[w, pl.ds(size, size), pl.ds(p * size, size)] = low

    def advance(step, g):
        older = 1 if step % 2 == 0 else 0
        rows = dense[pl.ds(g * group, group)].reshape(group * 2 * size, window * size)
        products = jnp.dot(rows, pair[step % 2], preferred_element_type=jnp.float32)
        for r in range(group):
            w = g * group + r
            parts = products[2 * r * size:(2 * r + 1) * size] + products[(2 * r + 1) * size:(2 * r + 2) * size]
            product = parts[:, :size] + parts[:, size:]
            newest = jnp.where(kept(w), 2.0 * product - terms[w, older], 0.0)
            terms[w, older] = newest
            gain = coefs_ref[step] * newest
            terms[w, 2] = gain if step == 0 else terms[w, 2] + gain
            if step < STEPS - 1:
                high, low = split(newest)
                into = 1 - step % 2
                at = pl.ds(pl.multiple_of(w * size, size), size)
                pair[into, at, pl.ds(0, size)] = high
                pair[into, at, pl.ds(size, size)] = low
            else:
                pltpu.make_async_copy(terms.at[w], out_ref.at[row_of(w)], out_sem).start()

    def first(g, carry):
        for r in range(group):
            w = g * group + r
            h_copy(w).wait()
            densify(w)

            @pl.when(w + 2 * group < window)
            def _():
                h_copy(w + 2 * group).start()

        advance(0, g)
        return carry

    lax.fori_loop(0, groups, first, 0)
    for step in range(1, STEPS):

        def later(g, carry, step=step):
            advance(step, g)
            return carry

        lax.fori_loop(0, groups, later, 0)
    pltpu.make_async_copy(terms, terms, out_sem).wait()


def unpack_kernel(
    cols_ref, recv_ref, density_ref, out_density, out_last, out_before, sums, blocks, sems
):
    count = cols_ref.shape[0]
    load = pltpu.make_async_copy(density_ref, sums, sems.at[3])
    load.start()
    for which in range(3):
        for k in range(count):
            block = recv_ref.at[cols_ref[k], which]
            pltpu.make_async_copy(block, blocks.at[which, k], sems.at[which]).start()

    def arrived(which):
        pltpu.make_async_copy(blocks.at[which], blocks.at[which], sems.at[which]).wait()

    arrived(0)
    before = pltpu.make_async_copy(blocks.at[0], out_before, sems.at[0])
    before.start()
    arrived(1)
    last = pltpu.make_async_copy(blocks.at[1], out_last, sems.at[1])
    last.start()
    load.wait()
    arrived(2)
    sums[...] += blocks[2]
    density = pltpu.make_async_copy(sums, out_density, sems.at[2])
    density.start()
    before.wait()
    last.wait()
    density.wait()


SMEM = pl.BlockSpec(memory_space=pltpu.SMEM)
ANY = pl.BlockSpec(memory_space=pl.ANY)


def per_device(h_blocks, h_cols, term_prev, term_cur, t_cols, density_in, coefs):
    total = lax.axis_size("row")
    me = lax.axis_index("row")
    count, size = h_blocks.shape[1:3]
    window = total if total <= 2 * REACH + 2 else 2 * REACH + 1
    base = jnp.int32(0) if window == total else jnp.mod(me - REACH, total)
    drop_h = dropped_offset(h_cols, me, total)
    drop_t = dropped_offset(t_cols, me, total)
    block = (size, size)

    h_all = lax.all_gather(h_blocks, "row", axis=0, tiled=True)
    send = pl.pallas_call(
        functools.partial(pack_kernel, total),
        out_shape=jax.ShapeDtypeStruct((total, 2 * size + NOTE, size), jnp.float32),
        in_specs=[SMEM, SMEM, ANY, ANY],
        out_specs=ANY,
        scratch_shapes=[
            pltpu.VMEM((count,) + block, jnp.float32),
            pltpu.VMEM((count,) + block, jnp.float32),
            pltpu.VMEM((2 * size, size), jnp.float32),
            pltpu.VMEM((NOTE, size), jnp.float32),
            pltpu.SemaphoreType.DMA((3,)),
        ],
        name="pack",
    )(jnp.stack([me, drop_h[0], drop_t[0]]), t_cols[0], term_cur[0], term_prev[0])
    columns = lax.all_to_all(send, "row", 0, 0, tiled=True)
    drops = columns[:, 2 * size:2 * size + 2, 0].astype(jnp.int32)
    group = max(g for g in (3, 4) if window % g == 0)
    result = pl.pallas_call(
        functools.partial(column_kernel, total, window, group),
        out_shape=jax.ShapeDtypeStruct((total, 3) + block, jnp.float32),
        in_specs=[SMEM, SMEM, SMEM, ANY, ANY],
        out_specs=ANY,
        scratch_shapes=[
            pltpu.VMEM((2 * group, count) + block, jnp.float32),
            pltpu.VMEM((window, 2 * size, window * size), jnp.bfloat16),
            pltpu.VMEM((2, window * size, 2 * size), jnp.bfloat16),
            pltpu.VMEM((window, 3) + block, jnp.float32),
            pltpu.SemaphoreType.DMA((2 * group,)),
            pltpu.SemaphoreType.DMA,
            pltpu.SemaphoreType.DMA,
        ],
        compiler_params=pltpu.CompilerParams(vmem_limit_bytes=48 * 1024 * 1024),
        name="steps",
    )(drops.reshape(-1), jnp.stack([base, me]), coefs, h_all, columns)
    back = lax.all_to_all(result, "row", 0, 0, tiled=True)
    row_shape = jax.ShapeDtypeStruct((count,) + block, jnp.float32)
    density, last, before = pl.pallas_call(
        unpack_kernel,
        out_shape=(row_shape, row_shape, row_shape),
        in_specs=[SMEM, ANY, ANY],
        out_specs=(ANY, ANY, ANY),
        scratch_shapes=[
            pltpu.VMEM((count,) + block, jnp.float32),
            pltpu.VMEM((3, count) + block, jnp.float32),
            pltpu.SemaphoreType.DMA((4,)),
        ],
        name="unpack",
    )(t_cols[0], back, density_in[0])
    return density[None], last[None], before[None]


def solution(mesh):
    blocks = P(("groups", "row"), None, None, None)
    cols = P(("groups", "row"), None)
    return jax.shard_map(
        per_device,
        mesh=mesh,
        in_specs=(blocks, cols, blocks, blocks, cols, blocks, P()),
        out_specs=(blocks, blocks, blocks),
        check_vma=False,
    )
```

time: 347 us -> 276 us (0.80)
  waiting for transfers between devices: 0.69 us -> 141 us
  Pallas kernels: 147 us -> 33.1 us
  blocking collectives: 171 us -> 73.6 us
    all_gather x1 -> x0, blocking collectives: 98.2 us -> none  [per_device(): lax.all_gather(jnp.stack([drop_h, drop_t], axis=1), 'row', axis=0, tiled=...]
    all_to_all x1, waiting for transfers between devices: 0.01 us -> 79.6 us  [per_device(): columns = lax.all_to_all(send, 'row', 0, 0, tiled=True)]
    all_gather x1, waiting for transfers between devices: 0.01 us -> 61.1 us  [per_device(): h_all = lax.all_gather(h_blocks, 'row', axis=0, tiled=True)]
    pallas_call x1, Pallas kernels: 57.5 us -> 3.25 us  [per_device(): pl.pallas_call(functools.partial(pack_kernel, total), out_shape=jax.Shape...]
    pallas_call x1, Pallas kernels: 57.4 us -> 3.63 us  [per_device(): pl.pallas_call(unpack_kernel, out_shape=(row_shape, row_shape, row_shape)...]
    pallas_call x1, Pallas kernels: 31.9 us -> 26.2 us  [per_device(): pl.pallas_call(functools.partial(column_kernel, total, window, group), ou...]
  transfers between devices with their start and end apart: 2 -> 2, of which waited for: 0 -> 2; matrix products, arithmetic and copies ran while one was open for 1% -> 1% of each run, Pallas kernels for 17% -> 1%
where the time goes in v2:
time: 276 us; the launch traced here: 272 us
  waiting for transfers between devices  141 us (51%)
  blocking collectives  73.6 us (27%)
  Pallas kernels  33.1 us (12%)
  between operations  15.4 us (6%)
  starting transfers between devices  6.17 us (2%)
    all_to_all x1, waiting for transfers between devices, per_device(): columns = lax.all_to_all(send, 'row', 0, 0, tiled=True)  79.6 us
    all_to_all x1, blocking collectives, per_device(): back = lax.all_to_all(result, 'row', 0, 0, tiled=True)  73.6 us
    all_gather x1, waiting for transfers between devices, per_device(): h_all = lax.all_gather(h_blocks, 'row', axis=0, tiled=True)  61.1 us
    pallas_call x1, Pallas kernels, per_device(): pl.pallas_call(functools.partial(column_kernel, total, window, group), ou...  26.2 us
    all_to_all x1, starting transfers between devices, per_device(): columns = lax.all_to_all(send, 'row', 0, 0, tiled=True)  6.14 us
  transfers between devices with their start and end apart: 2, of which 2 were waited for; matrix products, arithmetic and copies ran while one was open for 1% of the time, Pallas kernels for 1%

profile of v2, /device:TPU:22, one launch (start us, length us, event | category | flops | bytes accessed | tf_op | source)
XLA Modules:
  0.0 272.2 jit_solution(17942545097600597657)
XLA Ops:
  7.2 0.0 all-gather.2.cloned.1.call-start
  7.2 0.7 all-gather.2.cloned.1.call-update
  7.9 1.3 fusion.1
  10.5 0.6 pad_add_fusion.info_ref
  11.1 3.2 %pack.1 = f32[16,264,128]{2,1,0:T(8,128)} custom-call(s32[3]{0:T(128)} %pad_add_fusion.info_ref, s32[14]{0:T(128)} %bitcast.13, f32[14,128,128]{2,1,0:T(8,128)} %bitcast.10, f32[14,128,128]{2,1,0:T(8,128)} %bitcast.11), custom_call_target="tpu_custom_call" | custom-call | tf_op jit(solution)/shard_map/pack/pallas_call | solution.py:201
  14.4 0.0 copy-start
  14.4 6.1 %all-to-all-start = ((f32[16,264,128]{2,1,0:T(8,128)}), f32[16,264,128]{2,1,0:T(8,128)S(1)}, u32[]{:S(2)}, u32[]{:S(2)}) async-start(f32[16,264,128]{2,1,0:T(8,128)} %pack.1), calls=%async_computation | async-start | bytes 4325376 | tf_op jit(solution)/shard_map/all_to_all | solution.py:215
  20.5 0.1 pad_add_fusion.1.base_ref
  20.6 79.6 %all-to-all-done.t_ref = f32[16,264,128]{2,1,0:T(8,128)S(1)} async-done(((f32[16,264,128]{2,1,0:T(8,128)}), f32[16,264,128]{2,1,0:T(8,128)S(1)}, u32[]{:S(2)}, u32[]{:S(2)}) %all-to-all-start) | async-done | bytes 2162720 | tf_op jit(solution)/shard_map/all_to_all | solution.py:215
  100.2 0.3 fusion
  100.6 0.1 convert_element_type.8.drops_ref
  100.7 61.1 %all-gather.2.cloned.1.call-done.h_ref = f32[16,14,128,128]{3,2,1,0:T(8,128)} async-done(((f32[1,14,128,128]{3,2,1,0:T(8,128)}), f32[16,14,128,128]{3,2,1,0:T(8,128)}) %all-gather.2.cloned.1.call-update) | async-done | bytes 14680080 | tf_op jit(solution)/shard_map/all_gather | solution.py:200
  161.8 0.0 copy-done
  161.8 26.2 %steps.1 = f32[16,3,128,128]{3,2,1,0:T(8,128)S(1)} custom-call(s32[32]{0:T(128)S(1)} %convert_element_type.8.drops_ref, s32[2]{0:T(128)S(1)} %pad_add_fusion.1.base_ref, f32[3]{0:T(128)S(1)} %copy-done, f32[16,14,128,128]{3,2,1,0:T(8,128)} %all-gather.2.cloned.1.call-done.h_ref, f32[16,264,128]{2,1,0:T(8,128)S(1)} %all-to-all-done.t_ref), custom_call_target="tpu_custom_call" | custom-call | tf_op jit(solution)/shard_map/steps/pallas_call | solution.py:218
  188.1 73.6 %all_to_all.10.recv_ref = f32[16,3,128,128]{3,2,1,0:T(8,128)} all-to-all(f32[16,3,128,128]{3,2,1,0:T(8,128)S(1)} %steps.1), channel_id=1, replica_groups=mesh['groups'=2,'row'=16] {'row'}, dimensions={0} | all-to-all | bytes 6291456 | tf_op jit(solution)/shard_map/all_to_all | solution.py:235
  261.7 3.6 %unpack.1 = (f32[14,128,128]{2,1,0:T(8,128)}, f32[14,128,128]{2,1,0:T(8,128)}, f32[14,128,128]{2,1,0:T(8,128)}) custom-call(s32[14]{0:T(128)} %bitcast.14, f32[16,3,128,128]{3,2,1,0:T(8,128)} %all_to_all.10.recv_ref, f32[14,128,128]{2,1,0:T(8,128)} %bitcast.12), custom_call_target="tpu_custom_call" | custom-call | tf_op jit(solution)/shard_map/unpack/pallas_call | solution.py:237
Async XLA Ops:
  7.2 154.7 %all-gather.2.cloned.1.call-start = ((), (), s32[]{:S(2)}) async-start(), calls=%async_computation.2 | async-start | bytes 15597568 | tf_op jit(solution)/shard_map/all_gather | solution.py:200
  14.4 147.4 %copy-start = (f32[3]{0:T(128)S(1)}, f32[3]{0:T(128)}, u32[]{:S(2)}) copy-start(f32[3]{0:T(128)} %coefs_ref.1) | copy-start | bytes 40
  14.4 85.8 %all-to-all-start = ((f32[16,264,128]{2,1,0:T(8,128)}), f32[16,264,128]{2,1,0:T(8,128)S(1)}, u32[]{:S(2)}, u32[]{:S(2)}) async-start(f32[16,264,128]{2,1,0:T(8,128)} %pack.1), calls=%async_computation | async-start | bytes 4325376 | tf_op jit(solution)/shard_map/all_to_all | solution.py:215
Sparse Core Ops, SparseCore 0:
  10.3 151.4 all-gather.1

commit v3 on v2

--- a/solution.py
+++ b/solution.py
@@ -10,6 +10,13 @@
 REACH = 7
 STEPS = 3
 NOTE = 8
+
+
+def cycle_of(total):
+    if total != 16:
+        return list(range(total))
+    chips = [0, 2, 4, 6, 7, 5, 3, 1]
+    return [2 * chip + core for chip in chips for core in (0, 1)]
 
 
 def place_of(offset, dropped):
@@ -64,7 +71,7 @@
 
 
 def column_kernel(
-    total, window, group, drops_ref, base_ref, coefs_ref, h_ref, t_ref, out_ref,
+    total, window, group, drops_ref, base_ref, place_ref, coefs_ref, h_ref, t_ref, out_ref,
     stage, dense, pair, terms, h_sem, t_sem, out_sem,
 ):
     size = h_ref.shape[-1]
@@ -77,7 +84,7 @@
 
     def h_copy(w):
         slot = lax.rem(w, 2 * group)
-        return pltpu.make_async_copy(h_ref.at[row_of(w)], stage.at[slot], h_sem.at[slot])
+        return pltpu.make_async_copy(h_ref.at[place_ref[row_of(w)]], stage.at[slot], h_sem.at[slot])
 
     def kept(w):
         row = row_of(w)
@@ -197,7 +204,9 @@
     drop_t = dropped_offset(t_cols, me, total)
     block = (size, size)
 
-    h_all = lax.all_gather(h_blocks, "row", axis=0, tiled=True)
+    cycle = cycle_of(total)
+    places = [cycle.index(row) for row in range(total)]
+    h_all = lax.all_gather(h_blocks, "row", axis=0, tiled=True, axis_index_groups=[cycle])
     send = pl.pallas_call(
         functools.partial(pack_kernel, total),
         out_shape=jax.ShapeDtypeStruct((total, 2 * size + NOTE, size), jnp.float32),
@@ -218,7 +227,7 @@
     result = pl.pallas_call(
         functools.partial(column_kernel, total, window, group),
         out_shape=jax.ShapeDtypeStruct((total, 3) + block, jnp.float32),
-        in_specs=[SMEM, SMEM, SMEM, ANY, ANY],
+        in_specs=[SMEM, SMEM, SMEM, SMEM, ANY, ANY],
         out_specs=ANY,
         scratch_shapes=[
             pltpu.VMEM((2 * group, count) + block, jnp.float32),
@@ -231,7 +240,7 @@
         ],
         compiler_params=pltpu.CompilerParams(vmem_limit_bytes=48 * 1024 * 1024),
         name="steps",
-    )(drops.reshape(-1), jnp.stack([base, me]), coefs, h_all, columns)
+    )(drops.reshape(-1), jnp.stack([base, me]), jnp.array(places, jnp.int32), coefs, h_all, columns)
     back = lax.all_to_all(result, "row", 0, 0, tiled=True)
     row_shape = jax.ShapeDtypeStruct((count,) + block, jnp.float32)
     density, last, before = pl.pallas_call(

time: 276 us -> 249 us (0.902)
  waiting for transfers between devices: 141 us -> 115 us
    all_gather x1, waiting for transfers between devices: 61.1 us -> 42.3 us  [per_device(): lax.all_gather(h_blocks, 'row', axis=0, tiled=True, axis_index_groups=[cy...]
    all_to_all x1, waiting for transfers between devices: 79.6 us -> 71.9 us  [per_device(): columns = lax.all_to_all(send, 'row', 0, 0, tiled=True)]
where the time goes in v3:
time: 249 us; the launch traced here: 245 us
  waiting for transfers between devices  115 us (46%)
  blocking collectives  73.1 us (29%)
  Pallas kernels  33.1 us (13%)
  between operations  15.4 us (6%)
  starting transfers between devices  6.2 us (2%)
    all_to_all x1, blocking collectives, per_device(): back = lax.all_to_all(result, 'row', 0, 0, tiled=True)  73.1 us
    all_to_all x1, waiting for transfers between devices, per_device(): columns = lax.all_to_all(send, 'row', 0, 0, tiled=True)  71.9 us
    all_gather x1, waiting for transfers between devices, per_device(): lax.all_gather(h_blocks, 'row', axis=0, tiled=True, axis_index_groups=[cy...  42.3 us
    pallas_call x1, Pallas kernels, per_device(): pl.pallas_call(functools.partial(column_kernel, total, window, group), ou...  26.3 us
    all_to_all x1, starting transfers between devices, per_device(): columns = lax.all_to_all(send, 'row', 0, 0, tiled=True)  6.16 us
  transfers between devices with their start and end apart: 2, of which 2 were waited for; matrix products, arithmetic and copies ran while one was open for 1% of the time, Pallas kernels for 1%

profile of v3, /device:TPU:22, one launch (start us, length us, event | category | flops | bytes accessed | tf_op | source)
XLA Modules:
  0.0 245.1 jit_solution(8424167732559184193)
XLA Ops:
  7.2 0.0 all-gather.2.cloned.1.call-start
  7.2 0.7 all-gather.2.cloned.1.call-update
  7.9 1.3 fusion.1
  10.5 0.6 pad_add_fusion.info_ref
  11.1 3.2 %pack.1 = f32[16,264,128]{2,1,0:T(8,128)} custom-call(s32[3]{0:T(128)} %pad_add_fusion.info_ref, s32[14]{0:T(128)} %bitcast.13, f32[14,128,128]{2,1,0:T(8,128)} %bitcast.10, f32[14,128,128]{2,1,0:T(8,128)} %bitcast.11), custom_call_target="tpu_custom_call" | custom-call | tf_op jit(solution)/shard_map/pack/pallas_call | solution.py:210
  14.4 0.0 copy-start
  14.4 0.0 copy-start.1
  14.4 6.2 %all-to-all-start = ((f32[16,264,128]{2,1,0:T(8,128)}), f32[16,264,128]{2,1,0:T(8,128)S(1)}, u32[]{:S(2)}, u32[]{:S(2)}) async-start(f32[16,264,128]{2,1,0:T(8,128)} %pack.1), calls=%async_computation | async-start | bytes 4325376 | tf_op jit(solution)/shard_map/all_to_all | solution.py:224
  20.6 0.1 pad_add_fusion.1.base_ref
  20.6 71.9 %all-to-all-done.t_ref = f32[16,264,128]{2,1,0:T(8,128)S(1)} async-done(((f32[16,264,128]{2,1,0:T(8,128)}), f32[16,264,128]{2,1,0:T(8,128)S(1)}, u32[]{:S(2)}, u32[]{:S(2)}) %all-to-all-start) | async-done | bytes 2162720 | tf_op jit(solution)/shard_map/all_to_all | solution.py:224
  92.5 0.3 fusion
  92.9 0.1 convert_element_type.8.drops_ref
  93.0 42.3 %all-gather.2.cloned.1.call-done.h_ref = f32[16,14,128,128]{3,2,1,0:T(8,128)} async-done(((f32[1,14,128,128]{3,2,1,0:T(8,128)}), f32[16,14,128,128]{3,2,1,0:T(8,128)}) %all-gather.2.cloned.1.call-update) | async-done | bytes 14680080 | tf_op jit(solution)/shard_map/all_gather | solution.py:209
  135.2 0.0 copy-done
  135.2 0.0 copy-done.1
  135.2 26.3 %steps.1 = f32[16,3,128,128]{3,2,1,0:T(8,128)S(1)} custom-call(s32[32]{0:T(128)S(1)} %convert_element_type.8.drops_ref, s32[2]{0:T(128)S(1)} %pad_add_fusion.1.base_ref, s32[16]{0:T(128)S(1)} %copy-done.1, f32[3]{0:T(128)S(1)} %copy-done, f32[16,14,128,128]{3,2,1,0:T(8,128)} %all-gather.2.cloned.1.call-done.h_ref, f32[16,264,128]{2,1,0:T(8,128)S(1)} %all-to-all-done.t_ref), custom_call_target="tpu_custom_call" | custom-call | tf_op jit(solution)/shard_map/steps/pallas_call | solution.py:227
  161.5 73.1 %all_to_all.10.recv_ref = f32[16,3,128,128]{3,2,1,0:T(8,128)} all-to-all(f32[16,3,128,128]{3,2,1,0:T(8,128)S(1)} %steps.1), channel_id=1, replica_groups=mesh['groups'=2,'row'=16] {'row'}, dimensions={0} | all-to-all | bytes 6291456 | tf_op jit(solution)/shard_map/all_to_all | solution.py:244
  234.6 3.6 %unpack.1 = (f32[14,128,128]{2,1,0:T(8,128)}, f32[14,128,128]{2,1,0:T(8,128)}, f32[14,128,128]{2,1,0:T(8,128)}) custom-call(s32[14]{0:T(128)} %bitcast.14, f32[16,3,128,128]{3,2,1,0:T(8,128)} %all_to_all.10.recv_ref, f32[14,128,128]{2,1,0:T(8,128)} %bitcast.12), custom_call_target="tpu_custom_call" | custom-call | tf_op jit(solution)/shard_map/unpack/pallas_call | solution.py:246
Async XLA Ops:
  7.2 128.1 %all-gather.2.cloned.1.call-start = ((), (), s32[]{:S(2)}) async-start(), calls=%async_computation.2 | async-start | bytes 15597568 | tf_op jit(solution)/shard_map/all_gather | solution.py:209
  14.4 120.9 %copy-start = (f32[3]{0:T(128)S(1)}, f32[3]{0:T(128)}, u32[]{:S(2)}) copy-start(f32[3]{0:T(128)} %coefs_ref.1) | copy-start | bytes 40
  14.4 120.9 %copy-start.1 = (s32[16]{0:T(128)S(1)}, s32[16]{0:T(128)}, u32[]{:S(2)}) copy-start(s32[16]{0:T(128)} %constant.35.clone.place_ref) | copy-start | bytes 196
  14.4 78.1 %all-to-all-start = ((f32[16,264,128]{2,1,0:T(8,128)}), f32[16,264,128]{2,1,0:T(8,128)S(1)}, u32[]{:S(2)}, u32[]{:S(2)}) async-start(f32[16,264,128]{2,1,0:T(8,128)} %pack.1), calls=%async_computation | async-start | bytes 4325376 | tf_op jit(solution)/shard_map/all_to_all | solution.py:224
Sparse Core Ops, SparseCore 0:
  9.6 125.5 all-gather.1

commit v4 on v2

--- a/solution.py
+++ b/solution.py
@@ -10,6 +10,30 @@
 REACH = 7
 STEPS = 3
 NOTE = 8
+
+
+def permute(x, target):
+    devices = lax.axis_size("row")
+    return lax.ppermute(x, "row", [(i, target(i)) for i in range(devices)])
+
+
+def gathered_rows(x, me, total, window):
+    if total != 16:
+        rows = [x]
+        for hop in range(1, REACH + 1):
+            rows.insert(0, permute(x, lambda i, hop=hop: (i + hop) % total))
+            rows.append(permute(x, lambda i, hop=hop: (i - hop) % total))
+        return rows, jnp.mod(me + jnp.arange(-REACH, REACH + 1, dtype=jnp.int32), total)
+    rows, indices = [], []
+    along, level = x, me
+    for hop in range(4):
+        if hop:
+            along, level = permute(along, lambda i: (i + 4) % 16), jnp.mod(level - 4, 16)
+        across = permute(along, lambda i: i ^ 2)
+        for row, index in ((along, level), (across, level ^ 2)):
+            rows += [row, permute(row, lambda i: i ^ 1)]
+            indices += [index, index ^ 1]
+    return rows, jnp.stack(indices)
 
 
 def place_of(offset, dropped):
@@ -63,21 +87,15 @@
     return high, low
 
 
-def column_kernel(
-    total, window, group, drops_ref, base_ref, coefs_ref, h_ref, t_ref, out_ref,
-    stage, dense, pair, terms, h_sem, t_sem, out_sem,
-):
-    size = h_ref.shape[-1]
-    base = base_ref[0]
-    column = base_ref[1]
+def column_kernel(total, window, group, drops_ref, rows_ref, coefs_ref, *refs):
+    h_refs = refs[:window]
+    t_ref, out_ref, stage, dense, pair, terms, h_sem, t_sem, out_sem = refs[window:]
+    size = t_ref.shape[-1]
+    column = rows_ref[window]
     groups = window // group
 
     def row_of(w):
-        return lax.rem(base + w, total)
-
-    def h_copy(w):
-        slot = lax.rem(w, 2 * group)
-        return pltpu.make_async_copy(h_ref.at[row_of(w)], stage.at[slot], h_sem.at[slot])
+        return rows_ref[w]
 
     def kept(w):
         row = row_of(w)
@@ -85,8 +103,8 @@
         _, named = place_of(offset, drops_ref[2 * row + 1])
         return named
 
-    for w in range(2 * group):
-        h_copy(jnp.int32(w)).start()
+    for w in range(window):
+        pltpu.make_async_copy(h_refs[w], stage.at[w], h_sem.at[w]).start()
     for w in range(window):
         for which in range(2):
             block = t_ref.at[row_of(w), pl.ds(which * size, size)]
@@ -100,11 +118,10 @@
     def densify(w):
         row = row_of(w)
         drop = drops_ref[2 * row]
-        slot = lax.rem(w, 2 * group)
         for p in range(window):
             offset = lax.rem(row_of(p) - row + REACH + total, total)
             k, named = place_of(offset, drop)
-            high, low = split(jnp.where(named, stage[slot, k], 0.0))
+            high, low = split(jnp.where(named, stage[w, k], 0.0))
             dense[w, pl.ds(0, size), pl.ds(p * size, size)] = high
             dense[w, pl.ds(size, size), pl.ds(p * size, size)] = low
 
@@ -132,12 +149,8 @@
     def first(g, carry):
         for r in range(group):
             w = g * group + r
-            h_copy(w).wait()
+            pltpu.make_async_copy(stage.at[w], stage.at[w], h_sem.at[w]).wait()
             densify(w)
-
-            @pl.when(w + 2 * group < window)
-            def _():
-                h_copy(w + 2 * group).start()
 
         advance(0, g)
         return carry
@@ -192,12 +205,11 @@
     me = lax.axis_index("row")
     count, size = h_blocks.shape[1:3]
     window = total if total <= 2 * REACH + 2 else 2 * REACH + 1
-    base = jnp.int32(0) if window == total else jnp.mod(me - REACH, total)
     drop_h = dropped_offset(h_cols, me, total)
     drop_t = dropped_offset(t_cols, me, total)
     block = (size, size)
 
-    h_all = lax.all_gather(h_blocks, "row", axis=0, tiled=True)
+    h_rows, rows = gathered_rows(h_blocks[0], me, total, window)
     send = pl.pallas_call(
         functools.partial(pack_kernel, total),
         out_shape=jax.ShapeDtypeStruct((total, 2 * size + NOTE, size), jnp.float32),
@@ -218,20 +230,20 @@
     result = pl.pallas_call(
         functools.partial(column_kernel, total, window, group),
         out_shape=jax.ShapeDtypeStruct((total, 3) + block, jnp.float32),
-        in_specs=[SMEM, SMEM, SMEM, ANY, ANY],
+        in_specs=[SMEM] * 3 + [ANY] * (window + 1),
         out_specs=ANY,
         scratch_shapes=[
-            pltpu.VMEM((2 * group, count) + block, jnp.float32),
+            pltpu.VMEM((window, count) + block, jnp.float32),
             pltpu.VMEM((window, 2 * size, window * size), jnp.bfloat16),
             pltpu.VMEM((2, window * size, 2 * size), jnp.bfloat16),
             pltpu.VMEM((window, 3) + block, jnp.float32),
-            pltpu.SemaphoreType.DMA((2 * group,)),
+            pltpu.SemaphoreType.DMA((window,)),
             pltpu.SemaphoreType.DMA,
             pltpu.SemaphoreType.DMA,
         ],
-        compiler_params=pltpu.CompilerParams(vmem_limit_bytes=48 * 1024 * 1024),
+        compiler_params=pltpu.CompilerParams(vmem_limit_bytes=50 * 1024 * 1024),
         name="steps",
-    )(drops.reshape(-1), jnp.stack([base, me]), coefs, h_all, columns)
+    )(drops.reshape(-1), jnp.concatenate([rows, me[None]]), coefs, *h_rows, columns)
     back = lax.all_to_all(result, "row", 0, 0, tiled=True)
     row_shape = jax.ShapeDtypeStruct((count,) + block, jnp.float32)
     density, last, before = pl.pallas_call(

time: 276 us -> 264 us (0.957)
  between operations: 15.4 us -> 2.03 us
  waiting for transfers between devices: 141 us -> 130 us
  starting transfers between devices: 6.17 us -> 13 us
  blocking collectives: 73.6 us -> 76.6 us
    ppermute x0 -> x15, waiting for transfers between devices: none -> 130 us  [permute(): return lax.ppermute(x, 'row', [(i, target(i)) for i in range(devices)])]
    all_to_all x1, waiting for transfers between devices: 79.6 us -> 0.01 us  [per_device(): columns = lax.all_to_all(send, 'row', 0, 0, tiled=True)]
    all_gather x1 -> x0, waiting for transfers between devices: 61.1 us -> none  [per_device(): h_all = lax.all_gather(h_blocks, 'row', axis=0, tiled=True)]
    ppermute x0 -> x15, starting transfers between devices: none -> 7.78 us  [permute(): return lax.ppermute(x, 'row', [(i, target(i)) for i in range(devices)])]
    all_to_all x1, blocking collectives: 73.6 us -> 76.6 us  [per_device(): back = lax.all_to_all(result, 'row', 0, 0, tiled=True)]
  transfers between devices with their start and end apart: 2 -> 16, of which waited for: 2 -> 7; matrix products, arithmetic and copies ran while one was open for 1% -> 1% of each run, Pallas kernels for 1% -> 1%
where the time goes in v4:
time: 264 us; the launch traced here: 260 us
  waiting for transfers between devices  130 us (49%)
  blocking collectives  76.6 us (29%)
  Pallas kernels  32.5 us (12%)
  starting transfers between devices  13 us (5%)
  other arithmetic  3.16 us (1%)
  local copies, waits for them, and re-layouts  2.71 us (1%)
    ppermute x15, waiting for transfers between devices, permute(): return lax.ppermute(x, 'row', [(i, target(i)) for i in range(devices)])  130 us
    all_to_all x1, blocking collectives, per_device(): back = lax.all_to_all(result, 'row', 0, 0, tiled=True)  76.6 us
    pallas_call x1, Pallas kernels, per_device(): pl.pallas_call(functools.partial(column_kernel, total, window, group), ou...  25.6 us
    ppermute x15, starting transfers between devices, permute(): return lax.ppermute(x, 'row', [(i, target(i)) for i in range(devices)])  7.78 us
  transfers between devices with their start and end apart: 16, of which 7 were waited for; matrix products, arithmetic and copies ran while one was open for 1% of the time, Pallas kernels for 1%

profile of v4, /device:TPU:22, one launch (start us, length us, event | category | flops | bytes accessed | tf_op | source)
XLA Modules:
  0.0 259.9 jit_solution(6706423718282178395)
XLA Ops:
  0.6 1.6 collective-permute-start.3
  2.3 1.3 fusion.1
  4.9 0.7 pad_add_fusion.info_ref
  5.5 3.2 %pack.1 = f32[16,264,128]{2,1,0:T(8,128)} custom-call(s32[3]{0:T(128)} %pad_add_fusion.info_ref, s32[14]{0:T(128)} %bitcast.33, f32[14,128,128]{2,1,0:T(8,128)} %bitcast.30, f32[14,128,128]{2,1,0:T(8,128)} %bitcast.31), custom_call_target="tpu_custom_call" | custom-call | tf_op jit(solution)/shard_map/pack/pallas_call | solution.py:213
  8.8 0.0 copy-start
  8.8 0.0 copy-start.3
  8.8 5.3 %all-to-all-start = ((f32[16,264,128]{2,1,0:T(8,128)}), f32[16,264,128]{2,1,0:T(8,128)}, u32[]{:S(2)}, u32[]{:S(2)}) async-start(f32[16,264,128]{2,1,0:T(8,128)} %pack.1), calls=%async_computation | async-start | bytes 4325376 | tf_op jit(solution)/shard_map/all_to_all | solution.py:227
  14.1 10.2 %collective-permute-done.3.refs_4_ = f32[14,128,128]{2,1,0:T(8,128)} collective-permute-done((f32[14,128,128]{2,1,0:T(8,128)}, f32[14,128,128]{2,1,0:T(8,128)}, u32[]{:S(2)}, u32[]{:S(2)}) %collective-permute-start.3) | collective-permute-done | bytes 917536 | tf_op jit(solution)/shard_map/ppermute | solution.py:17
  24.2 1.6 collective-permute-start.7
  25.8 0.0 copy-done
  25.8 0.5 collective-permute-start.1
  26.3 0.0 collective-permute-start
  26.3 62.9 %collective-permute-done.7.refs_8_ = f32[14,128,128]{2,1,0:T(8,128)} collective-permute-done((f32[14,128,128]{2,1,0:T(8,128)}, f32[14,128,128]{2,1,0:T(8,128)}, u32[]{:S(2)}, u32[]{:S(2)}) %collective-permute-start.7) | collective-permute-done | bytes 917536 | tf_op jit(solution)/shard_map/ppermute | solution.py:17
  89.2 0.0 collective-permute-start.11
  89.2 0.5 collective-permute-start.5
  89.7 0.0 collective-permute-start.4
  89.7 0.0 collective-permute-done.1.refs_2_
  89.7 0.5 collective-permute-start.2
  90.2 0.0 collective-permute-done.refs_1_
  90.2 1.5 collective-permute-start.9
  91.8 19.0 %collective-permute-done.11.refs_12_ = f32[14,128,128]{2,1,0:T(8,128)} collective-permute-done((f32[14,128,128]{2,1,0:T(8,128)}, f32[14,128,128]{2,1,0:T(8,128)}, u32[]{:S(2)}, u32[]{:S(2)}) %collective-permute-start.11) | collective-permute-done | bytes 917536 | tf_op jit(solution)/shard_map/ppermute | solution.py:17
  110.8 0.5 collective-permute-start.13
  111.3 1.6 collective-permute-done.5.refs_6_
  112.8 0.0 collective-permute-start.8
  112.8 0.0 collective-permute-done.4.refs_5_
  112.8 0.5 collective-permute-start.6
  113.3 0.0 collective-permute-done.2.refs_3_
  113.3 0.4 copy-done.4
  113.8 0.9 copy-done.1
  114.7 0.5 collective-permute-start.12
  115.2 17.3 %collective-permute-done.9.refs_10_ = f32[14,128,128]{2,1,0:T(8,128)} collective-permute-done((f32[14,128,128]{2,1,0:T(8,128)}, f32[14,128,128]{2,1,0:T(8,128)}, u32[]{:S(2)}, u32[]{:S(2)}) %collective-permute-start.9) | collective-permute-done | bytes 917536 | tf_op jit(solution)/shard_map/ppermute | solution.py:17
  132.5 0.0 collective-permute-start.10
  132.5 17.6 %collective-permute-done.13.refs_14_ = f32[14,128,128]{2,1,0:T(8,128)} collective-permute-done((f32[14,128,128]{2,1,0:T(8,128)}, f32[14,128,128]{2,1,0:T(8,128)}, u32[]{:S(2)}, u32[]{:S(2)}) %collective-permute-start.13) | collective-permute-done | bytes 917536 | tf_op jit(solution)/shard_map/ppermute | solution.py:17
  150.1 0.0 collective-permute-start.14
  150.1 0.1 concatenate.3.rows_ref
  150.2 0.0 all-to-all-done.refs_16_
  150.2 1.2 fusion
  151.4 0.1 convert_element_type.8.drops_ref
  151.5 0.0 collective-permute-done.8.refs_9_
  151.5 0.0 collective-permute-done.6.refs_7_
  151.5 0.0 collective-permute-done.12.refs_13_
  151.5 0.0 collective-permute-done.10.refs_11_
  151.5 1.4 collective-permute-done.14.refs_15_
  152.9 0.0 copy-done.3
  152.9 1.2 copy-done.2
  154.1 25.6 %steps.1 = f32[16,3,128,128]{3,2,1,0:T(8,128)} custom-call(s32[32]{0:T(128)S(1)} %convert_element_type.8.drops_ref, s32[17]{0:T(128)S(1)} %concatenate.3.rows_ref, f32[3]{0:T(128)S(1)} %copy-done.3, f32[14,128,128]{2,1,0:T(8,128)S(1)} %bitcast.29, f32[14,128,128]{2,1,0:T(8,128)S(1)} %collective-permute-done.refs_1_, ...), custom_call_target="tpu_custom_call" | custom-call | tf_op jit(solution)/shard_map/steps/pallas_call | solution.py:230
  179.7 76.6 %all_to_all.10.recv_ref = f32[16,3,128,128]{3,2,1,0:T(8,128)} all-to-all(f32[16,3,128,128]{3,2,1,0:T(8,128)} %steps.1), channel_id=1, replica_groups=mesh['groups'=2,'row'=16] {'row'}, dimensions={0} | all-to-all | bytes 6291456 | tf_op jit(solution)/shard_map/all_to_all | solution.py:247
  256.3 3.6 %unpack.1 = (f32[14,128,128]{2,1,0:T(8,128)}, f32[14,128,128]{2,1,0:T(8,128)}, f32[14,128,128]{2,1,0:T(8,128)}) custom-call(s32[14]{0:T(128)} %bitcast.34, f32[16,3,128,128]{3,2,1,0:T(8,128)} %all_to_all.10.recv_ref, f32[14,128,128]{2,1,0:T(8,128)} %bitcast.32), custom_call_target="tpu_custom_call" | custom-call | tf_op jit(solution)/shard_map/unpack/pallas_call | solution.py:249
  (3 shorter events, 0.0 us)
Async XLA Ops:
  0.6 23.6 %collective-permute-start.3 = (f32[14,128,128]{2,1,0:T(8,128)}, f32[14,128,128]{2,1,0:T(8,128)}, u32[]{:S(2)}, u32[]{:S(2)}) collective-permute-start(f32[14,128,128]{2,1,0:T(8,128)} %bitcast.26), channel_id=1, source_target_pairs={{0,4},{1,5},{2,6},{3,7},{4,8},{5,9},{6,10},{7,11},{8,12},{9,13},{1... | collective-permute-start | bytes 2752520 | tf_op jit(solution)/shard_map/ppermute | solution.py:17
  8.8 17.0 %copy-start = (f32[1,14,128,128]{3,2,1,0:T(8,128)S(1)}, f32[1,14,128,128]{3,2,1,0:T(8,128)}, u32[]{:S(2)}) copy-start(f32[1,14,128,128]{3,2,1,0:T(8,128)} %param.7) | copy-start | bytes 2752516
  8.8 144.1 %copy-start.3 = (f32[3]{0:T(128)S(1)}, f32[3]{0:T(128)}, u32[]{:S(2)}) copy-start(f32[3]{0:T(128)} %coefs_ref.1) | copy-start | bytes 40
  8.8 141.4 %all-to-all-start = ((f32[16,264,128]{2,1,0:T(8,128)}), f32[16,264,128]{2,1,0:T(8,128)}, u32[]{:S(2)}, u32[]{:S(2)}) async-start(f32[16,264,128]{2,1,0:T(8,128)} %pack.1), calls=%async_computation | async-start | bytes 4325376 | tf_op jit(solution)/shard_map/all_to_all | solution.py:227
  24.2 65.0 %collective-permute-start.7 = (f32[14,128,128]{2,1,0:T(8,128)}, f32[14,128,128]{2,1,0:T(8,128)}, u32[]{:S(2)}, u32[]{:S(2)}) collective-permute-start(f32[14,128,128]{2,1,0:T(8,128)} %collective-permute-done.3.refs_4_), channel_id=1, source_target_pairs={{0,4},{1,5},{2,6},{3,7},{4,8},{5,9},{6,10},{7,11},{8,12},{9,13},{1... | collective-permute-start | bytes 2752520 | tf_op jit(solution)/shard_map/ppermute | solution.py:17
  25.8 63.9 %collective-permute-start.1 = (f32[14,128,128]{2,1,0:T(8,128)S(1)}, f32[14,128,128]{2,1,0:T(8,128)S(1)}, u32[]{:S(2)}, u32[]{:S(2)}) collective-permute-start(f32[14,128,128]{2,1,0:T(8,128)S(1)} %bitcast.27), channel_id=1, source_target_pairs={{0,2},{1,3},{2,0},{3,1},{4,6},{5,7},{6,4},{7,5},{8,10},{9,11},{10,... | collective-permute-start | bytes 2752520 | tf_op jit(solution)/shard_map/ppermute | solution.py:17
  26.3 63.9 %collective-permute-start = (f32[14,128,128]{2,1,0:T(8,128)S(1)}, f32[14,128,128]{2,1,0:T(8,128)S(1)}, u32[]{:S(2)}, u32[]{:S(2)}) collective-permute-start(f32[14,128,128]{2,1,0:T(8,128)S(1)} %bitcast.28), channel_id=1, source_target_pairs={{0,1},{1,0},{2,3},{3,2},{4,5},{5,4},{6,7},{7,6},{8,9},{9,8},{10,11... | collective-permute-start | bytes 2752520 | tf_op jit(solution)/shard_map/ppermute | solution.py:17
  89.2 21.5 %collective-permute-start.11 = (f32[14,128,128]{2,1,0:T(8,128)}, f32[14,128,128]{2,1,0:T(8,128)}, u32[]{:S(2)}, u32[]{:S(2)}) collective-permute-start(f32[14,128,128]{2,1,0:T(8,128)} %collective-permute-done.7.refs_8_), channel_id=1, source_target_pairs={{0,4},{1,5},{2,6},{3,7},{4,8},{5,9},{6,10},{7,11},{8,12},{9,13},{1... | collective-permute-start | bytes 2752520 | tf_op jit(solution)/shard_map/ppermute | solution.py:17
  89.2 23.6 %collective-permute-start.5 = (f32[14,128,128]{2,1,0:T(8,128)}, f32[14,128,128]{2,1,0:T(8,128)}, u32[]{:S(2)}, u32[]{:S(2)}) collective-permute-start(f32[14,128,128]{2,1,0:T(8,128)} %collective-permute-done.3.refs_4_), channel_id=1, source_target_pairs={{0,2},{1,3},{2,0},{3,1},{4,6},{5,7},{6,4},{7,5},{8,10},{9,11},{10,... | collective-permute-start | bytes 2752520 | tf_op jit(solution)/shard_map/ppermute | solution.py:17
  89.7 23.1 %collective-permute-start.4 = (f32[14,128,128]{2,1,0:T(8,128)}, f32[14,128,128]{2,1,0:T(8,128)S(1)}, u32[]{:S(2)}, u32[]{:S(2)}) collective-permute-start(f32[14,128,128]{2,1,0:T(8,128)} %collective-permute-done.3.refs_4_), channel_id=1, source_target_pairs={{0,1},{1,0},{2,3},{3,2},{4,5},{5,4},{6,7},{7,6},{8,9},{9,8},{10,11... | collective-permute-start | bytes 2752520 | tf_op jit(solution)/shard_map/ppermute | solution.py:17
  89.7 23.6 %collective-permute-start.2 = (f32[14,128,128]{2,1,0:T(8,128)S(1)}, f32[14,128,128]{2,1,0:T(8,128)S(1)}, u32[]{:S(2)}, u32[]{:S(2)}) collective-permute-start(f32[14,128,128]{2,1,0:T(8,128)S(1)} %collective-permute-done.1.refs_2_), channel_id=1, source_target_pairs={{0,1},{1,0},{2,3},{3,2},{4,5},{5,4},{6,7},{7,6},{8,9},{9,8},{10,11... | collective-permute-start | bytes 2752520 | tf_op jit(solution)/shard_map/ppermute | solution.py:17
  90.2 42.2 %collective-permute-start.9 = (f32[14,128,128]{2,1,0:T(8,128)}, f32[14,128,128]{2,1,0:T(8,128)}, u32[]{:S(2)}, u32[]{:S(2)}) collective-permute-start(f32[14,128,128]{2,1,0:T(8,128)} %collective-permute-done.7.refs_8_), channel_id=1, source_target_pairs={{0,2},{1,3},{2,0},{3,1},{4,6},{5,7},{6,4},{7,5},{8,10},{9,11},{10,... | collective-permute-start | bytes 2752520 | tf_op jit(solution)/shard_map/ppermute | solution.py:17
  110.8 39.3 %collective-permute-start.13 = (f32[14,128,128]{2,1,0:T(8,128)}, f32[14,128,128]{2,1,0:T(8,128)}, u32[]{:S(2)}, u32[]{:S(2)}) collective-permute-start(f32[14,128,128]{2,1,0:T(8,128)} %collective-permute-done.11.refs_12_), channel_id=1, source_target_pairs={{0,2},{1,3},{2,0},{3,1},{4,6},{5,7},{6,4},{7,5},{8,10},{9,11},{10,... | collective-permute-start | bytes 2752520 | tf_op jit(solution)/shard_map/ppermute | solution.py:17
  112.8 38.6 %collective-permute-start.8 = (f32[14,128,128]{2,1,0:T(8,128)}, f32[14,128,128]{2,1,0:T(8,128)}, u32[]{:S(2)}, u32[]{:S(2)}) collective-permute-start(f32[14,128,128]{2,1,0:T(8,128)} %collective-permute-done.7.refs_8_), channel_id=1, source_target_pairs={{0,1},{1,0},{2,3},{3,2},{4,5},{5,4},{6,7},{7,6},{8,9},{9,8},{10,11... | collective-permute-start | bytes 2752520 | tf_op jit(solution)/shard_map/ppermute | solution.py:17
  112.8 0.9 copy-start.4
  112.8 38.6 %collective-permute-start.6 = (f32[14,128,128]{2,1,0:T(8,128)}, f32[14,128,128]{2,1,0:T(8,128)}, u32[]{:S(2)}, u32[]{:S(2)}) collective-permute-start(f32[14,128,128]{2,1,0:T(8,128)} %collective-permute-done.5.refs_6_), channel_id=1, source_target_pairs={{0,1},{1,0},{2,3},{3,2},{4,5},{5,4},{6,7},{7,6},{8,9},{9,8},{10,11... | collective-permute-start | bytes 2752520 | tf_op jit(solution)/shard_map/ppermute | solution.py:17
  113.8 0.9 copy-start.1
  114.7 36.8 %collective-permute-start.12 = (f32[14,128,128]{2,1,0:T(8,128)}, f32[14,128,128]{2,1,0:T(8,128)}, u32[]{:S(2)}, u32[]{:S(2)}) collective-permute-start(f32[14,128,128]{2,1,0:T(8,128)} %collective-permute-done.11.refs_12_), channel_id=1, source_target_pairs={{0,1},{1,0},{2,3},{3,2},{4,5},{5,4},{6,7},{7,6},{8,9},{9,8},{10,11... | collective-permute-start | bytes 2752520 | tf_op jit(solution)/shard_map/ppermute | solution.py:17
  132.5 19.0 %collective-permute-start.10 = (f32[14,128,128]{2,1,0:T(8,128)}, f32[14,128,128]{2,1,0:T(8,128)}, u32[]{:S(2)}, u32[]{:S(2)}) collective-permute-start(f32[14,128,128]{2,1,0:T(8,128)} %collective-permute-done.9.refs_10_), channel_id=1, source_target_pairs={{0,1},{1,0},{2,3},{3,2},{4,5},{5,4},{6,7},{7,6},{8,9},{9,8},{10,11... | collective-permute-start | bytes 2752520 | tf_op jit(solution)/shard_map/ppermute | solution.py:17
  150.1 2.8 %collective-permute-start.14 = (f32[14,128,128]{2,1,0:T(8,128)}, f32[14,128,128]{2,1,0:T(8,128)}, u32[]{:S(2)}, u32[]{:S(2)}) collective-permute-start(f32[14,128,128]{2,1,0:T(8,128)} %collective-permute-done.13.refs_14_), channel_id=1, source_target_pairs={{0,1},{1,0},{2,3},{3,2},{4,5},{5,4},{6,7},{7,6},{8,9},{9,8},{10,11... | collective-permute-start | bytes 2752520 | tf_op jit(solution)/shard_map/ppermute | solution.py:17
  152.9 1.2 copy-start.2

commit v5 on v4

v5 whole, which is shorter than its diff:
```python
import functools

import jax
import jax.numpy as jnp
from jax import lax
from jax.experimental import pallas as pl
from jax.experimental.pallas import tpu as pltpu
from jax.sharding import PartitionSpec as P

REACH = 7
STEPS = 3
NOTE = 8
SMEM = pl.BlockSpec(memory_space=pltpu.SMEM)
ANY = pl.BlockSpec(memory_space=pl.ANY)
VMEM_LIMIT = 50 * 1024 * 1024


def permute(x, target):
    devices = lax.axis_size("row")
    return lax.ppermute(x, "row", [(i, target(i)) for i in range(devices)])


def nothing(*refs):
    pass


def after(x, *others):
    return pl.pallas_call(
        nothing,
        out_shape=jax.ShapeDtypeStruct(x.shape, x.dtype),
        in_specs=[ANY] * (1 + len(others)),
        out_specs=ANY,
        input_output_aliases={0: 0},
        name="after",
    )(x, *others)


def gathered_rows(x, me, total):
    if total != 16:
        rows = [x]
        for hop in range(1, REACH + 1):
            rows.insert(0, permute(x, lambda i, hop=hop: (i + hop) % total))
            rows.append(permute(x, lambda i, hop=hop: (i - hop) % total))
        return rows, jnp.mod(me + jnp.arange(-REACH, REACH + 1, dtype=jnp.int32), total), x
    rows, indices = [], []
    along, level = x, me
    for hop in range(4):
        if hop:
            along, level = permute(along, lambda i: (i + 4) % 16), jnp.mod(level - 4, 16)
        across = permute(along, lambda i: i ^ 2)
        for row, index in ((along, level), (across, level ^ 2)):
            rows += [row, permute(row, lambda i: i ^ 1)]
            indices += [index, index ^ 1]
    return rows, jnp.stack(indices), along


def place_of(offset, dropped):
    named = jnp.logical_and(offset <= 2 * REACH, offset != dropped)
    slot = offset - jnp.where(offset > dropped, 1, 0)
    return jnp.clip(slot, 0, 2 * REACH - 1), named


def dropped_offset(cols, row, total):
    offsets = jnp.mod(cols - row + REACH, total)
    return REACH * (2 * REACH + 1) - jnp.sum(offsets, axis=1)


def pack_kernel(total, info_ref, cols_ref, cur_ref, prev_ref, cur_out, prev_out, cur, prev, zeros, note, sems):
    row = info_ref[0]
    drop = info_ref[2]
    count, size = cur.shape[:2]
    loads = (
        pltpu.make_async_copy(cur_ref, cur, sems.at[0]),
        pltpu.make_async_copy(prev_ref, prev, sems.at[1]),
    )
    for load in loads:
        load.start()
    zeros[...] = jnp.zeros_like(zeros)
    line = lax.broadcasted_iota(jnp.int32, note.shape, 0)
    note[...] = jnp.where(line == 0, info_ref[1], drop).astype(jnp.float32)

    def fill(j, carry):
        offset = lax.rem(j - row + REACH + total, total)
        _, named = place_of(offset, drop)
        pltpu.make_async_copy(note, cur_out.at[j, pl.ds(size, NOTE)], sems.at[2]).start()

        @pl.when(jnp.logical_not(named))
        def _():
            pltpu.make_async_copy(zeros, cur_out.at[j, pl.ds(0, size)], sems.at[2]).start()
            pltpu.make_async_copy(zeros, prev_out.at[j], sems.at[3]).start()

        return carry

    lax.fori_loop(0, total, fill, 0)
    loads[0].wait()
    for k in range(count):
        pltpu.make_async_copy(cur.at[k], cur_out.at[cols_ref[k], pl.ds(0, size)], sems.at[2]).start()
    loads[1].wait()
    for k in range(count):
        pltpu.make_async_copy(prev.at[k], prev_out.at[cols_ref[k]], sems.at[3]).start()
    pltpu.make_async_copy(cur_out, cur_out, sems.at[2]).wait()
    pltpu.make_async_copy(prev_out, prev_out, sems.at[3]).wait()


def split(x):
    high = x.astype(jnp.bfloat16)
    low = (x - high.astype(jnp.float32)).astype(jnp.bfloat16)
    return high, low


def kept_rows(total, rows_ref, drops_ref, w):
    row = rows_ref[w]
    offset = lax.rem(rows_ref[rows_ref.shape[0] - 1] - row + REACH + total, total)
    _, named = place_of(offset, drops_ref[2 * row + 1])
    return named


def fill_pair(pair, blocks, kept):
    size = blocks.shape[-1]
    for w in range(blocks.shape[0]):
        high, low = split(jnp.where(kept(w), blocks[w], 0.0))
        pair[pl.ds(w * size, size), pl.ds(0, size)] = high
        pair[pl.ds(w * size, size), pl.ds(size, size)] = low


def products_of(rows, pair, size):
    group = rows.shape[0]
    flat = rows.reshape(group * 2 * size, rows.shape[2])
    products = jnp.dot(flat, pair, preferred_element_type=jnp.float32)
    for r in range(group):
        parts = products[2 * r * size:(2 * r + 1) * size] + products[(2 * r + 1) * size:(2 * r + 2) * size]
        yield parts[:, :size] + parts[:, size:]


def first_kernel(total, window, group, drops_ref, rows_ref, *refs):
    h_refs = refs[:window]
    t_ref, dense_ref, out_ref, stage, dense, blocks, pair, h_sem, t_sem, dense_sem, out_sem = refs[window:]
    size = t_ref.shape[-1]
    kept = functools.partial(kept_rows, total, rows_ref, drops_ref)

    for w in range(window):
        pltpu.make_async_copy(t_ref.at[rows_ref[w], pl.ds(0, size)], blocks.at[w], t_sem).start()
    for w in range(window):
        pltpu.make_async_copy(h_refs[w], stage.at[w], h_sem.at[w]).start()
    pltpu.make_async_copy(blocks, blocks, t_sem).wait()
    fill_pair(pair, blocks, kept)

    def densify(w, slot, r):
        row = rows_ref[w]
        drop = drops_ref[2 * row]
        for p in range(window):
            offset = lax.rem(rows_ref[p] - row + REACH + total, total)
            k, named = place_of(offset, drop)
            high, low = split(jnp.where(named, stage[w, k], 0.0))
            dense[slot, r, pl.ds(0, size), pl.ds(p * size, size)] = high
            dense[slot, r, pl.ds(size, size), pl.ds(p * size, size)] = low

    def store(g, slot):
        return pltpu.make_async_copy(dense.at[slot], dense_ref.at[pl.ds(g * group, group)], dense_sem.at[slot])

    def one(g, carry):
        slot = lax.rem(g, 2)

        @pl.when(g >= 2)
        def _():
            store(g - 2, slot).wait()

        for r in range(group):
            w = g * group + r
            pltpu.make_async_copy(stage.at[w], stage.at[w], h_sem.at[w]).wait()
            densify(w, slot, r)
        store(g, slot).start()
        for r, product in enumerate(products_of(dense[slot], pair[...], size)):
            w = g * group + r
            blocks[w] = 2.0 * product
            pltpu.make_async_copy(blocks.at[w], out_ref.at[rows_ref[w]], out_sem).start()
        return carry

    groups = window // group
    lax.fori_loop(0, groups, one, 0)
    for g in range(groups - 2, groups):
        store(g, g % 2).wait()
    pltpu.make_async_copy(blocks, blocks, out_sem).wait()


def step_kernel(
    total, window, group, drops_ref, rows_ref, dense_ref, cur_ref, prev_ref, out_ref,
    dense, cur, prev, pair, dense_sem, cur_sem, prev_sem, out_sem,
):
    size = cur.shape[-1]
    groups = window // group
    kept = functools.partial(kept_rows, total, rows_ref, drops_ref)
    for w in range(window):
        pltpu.make_async_copy(cur_ref.at[rows_ref[w], pl.ds(0, size)], cur.at[w], cur_sem).start()
    for g in range(groups):
        at = pl.ds(g * group, group)
        pltpu.make_async_copy(dense_ref.at[at], dense.at[at], dense_sem.at[g]).start()
    for w in range(window):
        pltpu.make_async_copy(prev_ref.at[rows_ref[w], pl.ds(0, size)], prev.at[w], prev_sem).start()
    pltpu.make_async_copy(cur, cur, cur_sem).wait()
    fill_pair(pair, cur, kept)
    pltpu.make_async_copy(prev, prev, prev_sem).wait()

    def one(g, carry):
        rows = dense.at[pl.ds(g * group, group)]
        pltpu.make_async_copy(rows, rows, dense_sem.at[g]).wait()
        for r, product in enumerate(products_of(rows[...], pair[...], size)):
            w = g * group + r
            prev[w] = jnp.where(kept(w), 2.0 * product - prev[w], 0.0)
            pltpu.make_async_copy(prev.at[w], out_ref.at[rows_ref[w]], out_sem).start()
        return carry

    lax.fori_loop(0, groups, one, 0)
    pltpu.make_async_copy(prev, prev, out_sem).wait()


def unpack_two_kernel(
    cols_ref, coefs_ref, first_ref, second_ref, density_ref, sum_ref, second_out, sums, one, two, sems
):
    load = pltpu.make_async_copy(density_ref, sums, sems.at[0])
    load.start()
    for k in range(cols_ref.shape[0]):
        pltpu.make_async_copy(first_ref.at[cols_ref[k]], one.at[k], sems.at[1]).start()
        pltpu.make_async_copy(second_ref.at[cols_ref[k]], two.at[k], sems.at[2]).start()
    pltpu.make_async_copy(two, two, sems.at[2]).wait()
    before = pltpu.make_async_copy(two, second_out, sems.at[2])
    before.start()
    load.wait()
    pltpu.make_async_copy(one, one, sems.at[1]).wait()
    sums[...] = sums[...] + coefs_ref[0] * one[...] + coefs_ref[1] * two[...]
    density = pltpu.make_async_copy(sums, sum_ref, sems.at[0])
    density.start()
    before.wait()
    density.wait()


def unpack_last_kernel(cols_ref, coefs_ref, third_ref, sum_ref, density_ref, third_out, sums, three, sems):
    load = pltpu.make_async_copy(sum_ref, sums, sems.at[0])
    load.start()
    for k in range(cols_ref.shape[0]):
        pltpu.make_async_copy(third_ref.at[cols_ref[k]], three.at[k], sems.at[1]).start()
    pltpu.make_async_copy(three, three, sems.at[1]).wait()
    last = pltpu.make_async_copy(three, third_out, sems.at[1])
    last.start()
    load.wait()
    sums[...] += coefs_ref[2] * three[...]
    density = pltpu.make_async_copy(sums, density_ref, sems.at[0])
    density.start()
    last.wait()
    density.wait()


def per_device(h_blocks, h_cols, term_prev, term_cur, t_cols, density_in, coefs):
    total = lax.axis_size("row")
    me = lax.axis_index("row")
    count, size = h_blocks.shape[1:3]
    window = total if total <= 2 * REACH + 2 else 2 * REACH + 1
    group = max(g for g in (3, 4) if window % g == 0)
    drop_h = dropped_offset(h_cols, me, total)
    drop_t = dropped_offset(t_cols, me, total)
    f32 = jnp.float32
    dma = pltpu.SemaphoreType.DMA
    column = jax.ShapeDtypeStruct((total, size, size), f32)
    row = jax.ShapeDtypeStruct((count, size, size), f32)
    row_scratch = pltpu.VMEM(row.shape, f32)
    window_scratch = pltpu.VMEM((window, size, size), f32)
    pair_scratch = pltpu.VMEM((window * size, 2 * size), jnp.bfloat16)
    dense_shape = (window, 2 * size, window * size)
    params = pltpu.CompilerParams(vmem_limit_bytes=VMEM_LIMIT)

    def exchange(x):
        return lax.all_to_all(x, "row", 0, 0, tiled=True)

    send_cur, send_prev = pl.pallas_call(
        functools.partial(pack_kernel, total),
        out_shape=(jax.ShapeDtypeStruct((total, size + NOTE, size), f32), column),
        in_specs=[SMEM, SMEM, ANY, ANY],
        out_specs=(ANY, ANY),
        scratch_shapes=[
            row_scratch,
            row_scratch,
            pltpu.VMEM((size, size), f32),
            pltpu.VMEM((NOTE, size), f32),
            dma((4,)),
        ],
        name="pack",
    )(jnp.stack([me, drop_h[0], drop_t[0]]), t_cols[0], term_cur[0], term_prev[0])

    h_rows, indices, last_hop = gathered_rows(h_blocks[0], me, total)
    rows = jnp.concatenate([indices, me[None]])
    cur = exchange(after(send_cur, last_hop))
    prev = exchange(after(send_prev, cur))
    notes = cur[:, size:size + 2, 0].astype(jnp.int32)
    drops = notes.reshape(-1)
    dense, doubled = pl.pallas_call(
        functools.partial(first_kernel, total, window, group),
        out_shape=(jax.ShapeDtypeStruct(dense_shape, jnp.bfloat16), column),
        in_specs=[SMEM, SMEM] + [ANY] * (window + 1),
        out_specs=(ANY, ANY),
        scratch_shapes=[
            pltpu.VMEM((window, count, size, size), f32),
            pltpu.VMEM((2, group) + dense_shape[1:], jnp.bfloat16),
            window_scratch,
            pair_scratch,
            dma((window,)),
            dma,
            dma((2,)),
            dma,
        ],
        compiler_params=params,
        name="first",
    )(drops, rows, *h_rows, cur)

    offsets = jnp.mod(me - jnp.arange(total, dtype=jnp.int32) + REACH, total)
    _, named = place_of(offsets, notes[:, 1])

    def step(current, previous):
        return pl.pallas_call(
            functools.partial(step_kernel, total, window, group),
            out_shape=column,
            in_specs=[SMEM, SMEM, ANY, ANY, ANY],
            out_specs=ANY,
            scratch_shapes=[
                pltpu.VMEM(dense_shape, jnp.bfloat16),
                window_scratch,
                window_scratch,
                pair_scratch,
                dma((window // group,)),
                dma,
                dma,
                dma,
            ],
            compiler_params=params,
            name="step",
        )(drops, rows, dense, current, previous)

    term1 = jnp.where(named[:, None, None], doubled - prev, 0.0)
    back1 = exchange(term1)
    term2 = step(term1, cur)
    back2 = exchange(term2)
    term3 = step(term2, term1)
    back3 = exchange(term3)
    sums, before = pl.pallas_call(
        unpack_two_kernel,
        out_shape=(row, row),
        in_specs=[SMEM, SMEM, ANY, ANY, ANY],
        out_specs=(ANY, ANY),
        scratch_shapes=[row_scratch, row_scratch, row_scratch, dma((3,))],
        name="unpack_two",
    )(t_cols[0], coefs, back1, back2, density_in[0])
    density, last = pl.pallas_call(
        unpack_last_kernel,
        out_shape=(row, row),
        in_specs=[SMEM, SMEM, ANY, ANY],
        out_specs=(ANY, ANY),
        scratch_shapes=[row_scratch, row_scratch, dma((2,))],
        name="unpack_last",
    )(t_cols[0], coefs, back3, sums)
    return density[None], last[None], before[None]


def solution(mesh):
    blocks = P(("groups", "row"), None, None, None)
    cols = P(("groups", "row"), None)
    return jax.shard_map(
        per_device,
        mesh=mesh,
        in_specs=(blocks, cols, blocks, blocks, cols, blocks, P()),
        out_specs=(blocks, blocks, blocks),
        check_vma=False,
    )
```

time: 264 us -> 306 us (1.16)
  blocking collectives: 76.6 us -> 29 us
  waiting for transfers between devices: 130 us -> 174 us
  starting transfers between devices: 13 us -> 38.7 us
  Pallas kernels: 32.5 us -> 48.2 us
  other arithmetic: 3.16 us -> 6.9 us
    all_to_all x1, blocking collectives: 76.6 us -> 29 us  [exchange(): return lax.all_to_all(x, 'row', 0, 0, tiled=True)]
    all_to_all x1 -> x4, waiting for transfers between devices: 0.01 us -> 29.5 us  [exchange(): return lax.all_to_all(x, 'row', 0, 0, tiled=True)]
    all_to_all x1 -> x4, starting transfers between devices: 5.26 us -> 28.9 us  [exchange(): return lax.all_to_all(x, 'row', 0, 0, tiled=True)]
    pallas_call x3 -> x8, Pallas kernels: 32.5 us -> 48.2 us  [the longest x2 25.9 us: step(): pl.pallas_call(functools.partial(step_kernel, total, window, group), out_...]
    ppermute x15, waiting for transfers between devices: 130 us -> 144 us  [permute(): return lax.ppermute(x, 'row', [(i, target(i)) for i in range(devices)])]
  transfers between devices with their start and end apart: 16 -> 19, of which waited for: 7 -> 10; matrix products, arithmetic and copies ran while one was open for 1% -> 1% of each run, Pallas kernels for 1% -> 11%
where the time goes in v5:
time: 306 us; the launch traced here: 303 us
  waiting for transfers between devices  174 us (57%)
  Pallas kernels  48.2 us (16%)
  starting transfers between devices  38.7 us (13%)
  blocking collectives  29 us (9%)
  other arithmetic  6.9 us (2%)
  local copies, waits for them, and re-layouts  4.16 us (1%)
    ppermute x15, waiting for transfers between devices, permute(): return lax.ppermute(x, 'row', [(i, target(i)) for i in range(devices)])  144 us
    all_to_all x4, waiting for transfers between devices, exchange(): return lax.all_to_all(x, 'row', 0, 0, tiled=True)  29.5 us
    all_to_all x1, blocking collectives, exchange(): return lax.all_to_all(x, 'row', 0, 0, tiled=True)  29 us
    all_to_all x4, starting transfers between devices, exchange(): return lax.all_to_all(x, 'row', 0, 0, tiled=True)  28.9 us
    pallas_call x2, Pallas kernels, step(): pl.pallas_call(functools.partial(step_kernel, total, window, group), out_...  25.9 us
    pallas_call x1, Pallas kernels, per_device(): pl.pallas_call(functools.partial(first_kernel, total, window, group), out...  12.1 us
    ppermute x15, starting transfers between devices, permute(): return lax.ppermute(x, 'row', [(i, target(i)) for i in range(devices)])  9.86 us
  transfers between devices with their start and end apart: 19, of which 10 were waited for; matrix products, arithmetic and copies ran while one was open for 1% of the time, Pallas kernels for 11%

profile of v5, /device:TPU:22, one launch (start us, length us, event | category | flops | bytes accessed | tf_op | source)
XLA Modules:
  0.0 302.9 jit_solution(4428555753782320681)
XLA Ops:
  0.6 1.6 collective-permute-start
  2.3 20.7 %collective-permute-done.refs_4_ = f32[14,128,128]{2,1,0:T(8,128)S(1)} collective-permute-done((f32[14,128,128]{2,1,0:T(8,128)}, f32[14,128,128]{2,1,0:T(8,128)S(1)}, u32[]{:S(2)}, u32[]{:S(2)}) %collective-permute-start) | collective-permute-done | bytes 917536 | tf_op jit(solution)/shard_map/ppermute | solution.py:20
  23.0 0.9 copy-done.7
  23.9 1.6 collective-permute-start.1
  25.5 19.6 %collective-permute-done.1.refs_8_ = f32[14,128,128]{2,1,0:T(8,128)S(1)} collective-permute-done((f32[14,128,128]{2,1,0:T(8,128)S(1)}, f32[14,128,128]{2,1,0:T(8,128)S(1)}, u32[]{:S(2)}, u32[]{:S(2)}) %collective-permute-start.1) | collective-permute-done | bytes 917536 | tf_op jit(solution)/shard_map/ppermute | solution.py:20
  45.1 1.6 collective-permute-start.2
  46.7 1.4 fusion
  49.4 0.7 pad_add_fusion.info_ref
  50.1 3.3 %pack.1 = (f32[16,136,128]{2,1,0:T(8,128)}, f32[16,128,128]{2,1,0:T(8,128)}) custom-call(s32[3]{0:T(128)} %pad_add_fusion.info_ref, s32[14]{0:T(128)} %bitcast.36, f32[14,128,128]{2,1,0:T(8,128)} %bitcast.33, f32[14,128,128]{2,1,0:T(8,128)} %bitcast.34), custom_call_target="tpu_custom_call" | custom-call | tf_op jit(solution)/shard_map/pack/pallas_call | solution.py:274
  53.4 12.2 %collective-permute-done.2.refs_1_.refs_12_ = f32[14,128,128]{2,1,0:T(8,128)} collective-permute-done((f32[14,128,128]{2,1,0:T(8,128)S(1)}, f32[14,128,128]{2,1,0:T(8,128)}, u32[]{:S(2)}, u32[]{:S(2)}) %collective-permute-start.2) | collective-permute-done | bytes 917536 | tf_op jit(solution)/shard_map/ppermute | solution.py:20
  65.5 9.6 %all-to-all-start = ((f32[16,136,128]{2,1,0:T(8,128)}), f32[16,136,128]{2,1,0:T(8,128)S(1)}, u32[]{:S(2)}, u32[]{:S(2)}) async-start(f32[16,136,128]{2,1,0:T(8,128)} %after.2), calls=%async_computation | async-start | bytes 2228224 | tf_op jit(solution)/shard_map/all_to_all | solution.py:272
  75.1 0.6 collective-permute-start.4
  75.7 32.7 %collective-permute-done.4.refs_2_ = f32[14,128,128]{2,1,0:T(8,128)S(1)} collective-permute-done((f32[14,128,128]{2,1,0:T(8,128)S(1)}, f32[14,128,128]{2,1,0:T(8,128)S(1)}, u32[]{:S(2)}, u32[]{:S(2)}) %collective-permute-start.4) | collective-permute-done | bytes 917536 | tf_op jit(solution)/shard_map/ppermute | solution.py:20
  108.5 1.5 collective-permute-start.7
  109.9 0.2 collective-permute-start.6
  110.2 0.6 collective-permute-start.10
  110.7 0.0 collective-permute-done.3.refs_1_
  110.7 0.9 copy-done.3
  111.6 1.5 collective-permute-start.13
  113.1 0.0 all-to-all-done.refs_16_.refs_1_.prev_ref
  113.1 1.0 copy-done
  114.1 6.2 %all-to-all-start.1 = ((f32[16,128,128]{2,1,0:T(8,128)}), f32[16,128,128]{2,1,0:T(8,128)}, u32[]{:S(2)}, u32[]{:S(2)}) async-start(f32[16,128,128]{2,1,0:T(8,128)} %after.3), calls=%async_computation.1 | async-start | bytes 2097152 | tf_op jit(solution)/shard_map/all_to_all | solution.py:272
  120.3 0.0 collective-permute-done.5.refs_3_
  120.3 0.2 collective-permute-start.9
  120.5 17.0 %collective-permute-done.7.refs_6_ = f32[14,128,128]{2,1,0:T(8,128)} collective-permute-done((f32[14,128,128]{2,1,0:T(8,128)}, f32[14,128,128]{2,1,0:T(8,128)}, u32[]{:S(2)}, u32[]{:S(2)}) %collective-permute-start.7) | collective-permute-done | bytes 917536 | tf_op jit(solution)/shard_map/ppermute | solution.py:20
  137.5 0.5 collective-permute-start.12
  138.1 22.0 %collective-permute-done.10.refs_10_ = f32[14,128,128]{2,1,0:T(8,128)} collective-permute-done((f32[14,128,128]{2,1,0:T(8,128)}, f32[14,128,128]{2,1,0:T(8,128)}, u32[]{:S(2)}, u32[]{:S(2)}) %collective-permute-start.10) | collective-permute-done | bytes 917536 | tf_op jit(solution)/shard_map/ppermute | solution.py:20
  160.0 19.7 %collective-permute-done.13.refs_14_ = f32[14,128,128]{2,1,0:T(8,128)} collective-permute-done((f32[14,128,128]{2,1,0:T(8,128)}, f32[14,128,128]{2,1,0:T(8,128)}, u32[]{:S(2)}, u32[]{:S(2)}) %collective-permute-start.13) | collective-permute-done | bytes 917536 | tf_op jit(solution)/shard_map/ppermute | solution.py:20
  179.7 0.1 concatenate.3.rows_ref
  179.8 1.2 fusion.5
  181.0 0.1 convert_element_type.11.drops_ref
  181.1 0.9 slice_convert_fusion
  181.9 0.1 copy.13
  182.0 0.0 collective-permute-done.8.refs_7_
  182.0 0.0 collective-permute-done.9.refs_9_
  182.0 0.5 collective-permute-done.14.refs_15_
  182.5 12.1 %first.1 = (bf16[16,256,2048]{2,1,0:T(8,128)(2,1)}, f32[16,128,128]{2,1,0:T(8,128)}) custom-call(s32[32]{0:T(128)S(1)} %convert_element_type.11.drops_ref, s32[17]{0:T(128)S(1)} %concatenate.3.rows_ref, f32[14,128,128]{2,1,0:T(8,128)S(1)} %bitcast.32, f32[14,128,128]{2,1,0:T(8,128)S(1)} %copy-done.4, f32[14,128,128]{2,1,0:T(8,128)S(1)} %collective-permute-done.4.refs_2_, ...), custom_call_target="tpu_custom_call" | custom-call | tf_op jit(solution)/shard_map/first/pallas_call | solution.py:295
  194.7 2.8 subtract_select_fusion.cur_ref.prev_ref
  197.5 12.2 %step.2.cur_ref = f32[16,128,128]{2,1,0:T(8,128)S(1)} custom-call(s32[32]{0:T(128)S(1)} %convert_element_type.11.drops_ref, s32[17]{0:T(128)S(1)} %concatenate.3.rows_ref, bf16[16,256,2048]{2,1,0:T(8,128)(2,1)} %get-tuple-element.12.dense_ref, f32[16,128,128]{2,1,0:T(8,128)} %subtract_select_fusion.cur_ref.prev_ref, f32[16,136,128]{2,1,0:T(8,128)S(1)} %copy-done.1), custom_call_target="tpu_custom_call" | custom-call | tf_op jit(solution)/shard_map/step/pallas_call | solution.py:318
  209.6 29.0 %all_to_all.25.second_ref = f32[16,128,128]{2,1,0:T(8,128)} all-to-all(f32[16,128,128]{2,1,0:T(8,128)S(1)} %step.2.cur_ref), channel_id=1, replica_groups=mesh['groups'=2,'row'=16] {'row'}, dimensions={0} | all-to-all | bytes 2097152 | tf_op jit(solution)/shard_map/all_to_all | solution.py:272
  238.7 6.7 %all-to-all-start.3 = ((f32[16,128,128]{2,1,0:T(8,128)}), f32[16,128,128]{2,1,0:T(8,128)S(1)}, u32[]{:S(2)}, u32[]{:S(2)}) async-start(f32[16,128,128]{2,1,0:T(8,128)} %subtract_select_fusion.cur_ref.prev_ref), calls=%async_computation.3 | async-start | bytes 2097152 | tf_op jit(solution)/shard_map/all_to_all | solution.py:272
  245.4 13.7 %step.3 = f32[16,128,128]{2,1,0:T(8,128)} custom-call(s32[32]{0:T(128)S(1)} %convert_element_type.11.drops_ref, s32[17]{0:T(128)S(1)} %concatenate.3.rows_ref, bf16[16,256,2048]{2,1,0:T(8,128)(2,1)} %get-tuple-element.12.dense_ref, f32[16,128,128]{2,1,0:T(8,128)S(1)} %step.2.cur_ref, f32[16,128,128]{2,1,0:T(8,128)} %subtract_select_fusion.cur_ref.prev_ref), custom_call_target="tpu_custom_call" | custom-call | tf_op jit(solution)/shard_map/step/pallas_call | solution.py:318
  259.1 9.7 %all-to-all-done.3.first_ref = f32[16,128,128]{2,1,0:T(8,128)S(1)} async-done(((f32[16,128,128]{2,1,0:T(8,128)}), f32[16,128,128]{2,1,0:T(8,128)S(1)}, u32[]{:S(2)}, u32[]{:S(2)}) %all-to-all-start.3) | async-done | bytes 1048608 | tf_op jit(solution)/shard_map/all_to_all | solution.py:272
  268.8 6.4 %all-to-all-start.2 = ((f32[16,128,128]{2,1,0:T(8,128)}), f32[16,128,128]{2,1,0:T(8,128)S(1)}, u32[]{:S(2)}, u32[]{:S(2)}) async-start(f32[16,128,128]{2,1,0:T(8,128)} %step.3), calls=%async_computation.2 | async-start | bytes 2097152 | tf_op jit(solution)/shard_map/all_to_all | solution.py:272
  275.2 3.6 %unpack_two.1 = (f32[14,128,128]{2,1,0:T(8,128)}, f32[14,128,128]{2,1,0:T(8,128)}) custom-call(s32[14]{0:T(128)} %bitcast.37, f32[3]{0:T(128)} %coefs_ref.3, f32[16,128,128]{2,1,0:T(8,128)} %copy-done.6, f32[16,128,128]{2,1,0:T(8,128)} %all_to_all.25.second_ref, f32[14,128,128]{2,1,0:T(8,128)} %bitcast.35), custom_call_target="tpu_custom_call" | custom-call | tf_op jit(solution)/shard_map/unpack_two/pallas_call | solution.py:343
  278.8 19.8 %all-to-all-done.2.third_ref = f32[16,128,128]{2,1,0:T(8,128)S(1)} async-done(((f32[16,128,128]{2,1,0:T(8,128)}), f32[16,128,128]{2,1,0:T(8,128)S(1)}, u32[]{:S(2)}, u32[]{:S(2)}) %all-to-all-start.2) | async-done | bytes 1048608 | tf_op jit(solution)/shard_map/all_to_all | solution.py:272
  298.6 1.0 copy-done.5
  299.6 3.3 %unpack_last.1 = (f32[14,128,128]{2,1,0:T(8,128)}, f32[14,128,128]{2,1,0:T(8,128)}) custom-call(s32[14]{0:T(128)} %bitcast.38, f32[3]{0:T(128)} %coefs_ref.3, f32[16,128,128]{2,1,0:T(8,128)} %copy-done.5, f32[14,128,128]{2,1,0:T(8,128)} %get-tuple-element.15.sum_ref), custom_call_target="tpu_custom_call" | custom-call | tf_op jit(solution)/shard_map/unpack_last/pallas_call | solution.py:351
  (26 shorter events, 0.1 us)
Async XLA Ops:
  0.6 22.4 %collective-permute-start = (f32[14,128,128]{2,1,0:T(8,128)}, f32[14,128,128]{2,1,0:T(8,128)S(1)}, u32[]{:S(2)}, u32[]{:S(2)}) collective-permute-start(f32[14,128,128]{2,1,0:T(8,128)} %bitcast.29), channel_id=1, source_target_pairs={{0,4},{1,5},{2,6},{3,7},{4,8},{5,9},{6,10},{7,11},{8,12},{9,13},{1... | collective-permute-start | bytes 2752520 | tf_op jit(solution)/shard_map/ppermute | solution.py:20
  23.0 0.9 copy-start.7
  23.9 21.2 %collective-permute-start.1 = (f32[14,128,128]{2,1,0:T(8,128)S(1)}, f32[14,128,128]{2,1,0:T(8,128)S(1)}, u32[]{:S(2)}, u32[]{:S(2)}) collective-permute-start(f32[14,128,128]{2,1,0:T(8,128)S(1)} %collective-permute-done.refs_4_), channel_id=1, source_target_pairs={{0,4},{1,5},{2,6},{3,7},{4,8},{5,9},{6,10},{7,11},{8,12},{9,13},{1... | collective-permute-start | bytes 2752520 | tf_op jit(solution)/shard_map/ppermute | solution.py:20
  45.1 20.4 %copy-start.8 = (f32[14,128,128]{2,1,0:T(8,128)}, f32[14,128,128]{2,1,0:T(8,128)S(1)}, u32[]{:S(2)}) copy-start(f32[14,128,128]{2,1,0:T(8,128)S(1)} %collective-permute-done.1.refs_8_) | copy-start | bytes 2752516
  45.1 20.4 %collective-permute-start.2 = (f32[14,128,128]{2,1,0:T(8,128)S(1)}, f32[14,128,128]{2,1,0:T(8,128)}, u32[]{:S(2)}, u32[]{:S(2)}) collective-permute-start(f32[14,128,128]{2,1,0:T(8,128)S(1)} %collective-permute-done.1.refs_8_), channel_id=1, source_target_pairs={{0,4},{1,5},{2,6},{3,7},{4,8},{5,9},{6,10},{7,11},{8,12},{9,13},{1... | collective-permute-start | bytes 2752520 | tf_op jit(solution)/shard_map/ppermute | solution.py:20
  65.5 9.6 %copy-start.2 = (f32[1,14,128,128]{3,2,1,0:T(8,128)S(1)}, f32[1,14,128,128]{3,2,1,0:T(8,128)}, u32[]{:S(2)}) copy-start(f32[1,14,128,128]{3,2,1,0:T(8,128)} %param.7) | copy-start | bytes 2752516
  65.5 47.6 %all-to-all-start = ((f32[16,136,128]{2,1,0:T(8,128)}), f32[16,136,128]{2,1,0:T(8,128)S(1)}, u32[]{:S(2)}, u32[]{:S(2)}) async-start(f32[16,136,128]{2,1,0:T(8,128)} %after.2), calls=%async_computation | async-start | bytes 2228224 | tf_op jit(solution)/shard_map/all_to_all | solution.py:272
  75.1 33.3 %collective-permute-start.4 = (f32[14,128,128]{2,1,0:T(8,128)S(1)}, f32[14,128,128]{2,1,0:T(8,128)S(1)}, u32[]{:S(2)}, u32[]{:S(2)}) collective-permute-start(f32[14,128,128]{2,1,0:T(8,128)S(1)} %bitcast.30), channel_id=1, source_target_pairs={{0,2},{1,3},{2,0},{3,1},{4,6},{5,7},{6,4},{7,5},{8,10},{9,11},{10,... | collective-permute-start | bytes 2752520 | tf_op jit(solution)/shard_map/ppermute | solution.py:20
  75.7 35.0 %collective-permute-start.3 = (f32[14,128,128]{2,1,0:T(8,128)S(1)}, f32[14,128,128]{2,1,0:T(8,128)S(1)}, u32[]{:S(2)}, u32[]{:S(2)}) collective-permute-start(f32[14,128,128]{2,1,0:T(8,128)S(1)} %bitcast.31), channel_id=1, source_target_pairs={{0,1},{1,0},{2,3},{3,2},{4,5},{5,4},{6,7},{7,6},{8,9},{9,8},{10,11... | collective-permute-start | bytes 2752520 | tf_op jit(solution)/shard_map/ppermute | solution.py:20
  108.5 11.9 %collective-permute-start.5 = (f32[14,128,128]{2,1,0:T(8,128)S(1)}, f32[14,128,128]{2,1,0:T(8,128)}, u32[]{:S(2)}, u32[]{:S(2)}) collective-permute-start(f32[14,128,128]{2,1,0:T(8,128)S(1)} %collective-permute-done.4.refs_2_), channel_id=1, source_target_pairs={{0,1},{1,0},{2,3},{3,2},{4,5},{5,4},{6,7},{7,6},{8,9},{9,8},{10,11... | collective-permute-start | bytes 2752520 | tf_op jit(solution)/shard_map/ppermute | solution.py:20
  108.5 29.1 %collective-permute-start.7 = (f32[14,128,128]{2,1,0:T(8,128)}, f32[14,128,128]{2,1,0:T(8,128)}, u32[]{:S(2)}, u32[]{:S(2)}) collective-permute-start(f32[14,128,128]{2,1,0:T(8,128)} %copy-done.7), channel_id=1, source_target_pairs={{0,2},{1,3},{2,0},{3,1},{4,6},{5,7},{6,4},{7,5},{8,10},{9,11},{10,... | collective-permute-start | bytes 2752520 | tf_op jit(solution)/shard_map/ppermute | solution.py:20
  109.9 27.6 %collective-permute-start.6 = (f32[14,128,128]{2,1,0:T(8,128)}, f32[14,128,128]{2,1,0:T(8,128)}, u32[]{:S(2)}, u32[]{:S(2)}) collective-permute-start(f32[14,128,128]{2,1,0:T(8,128)} %copy-done.7), channel_id=1, source_target_pairs={{0,1},{1,0},{2,3},{3,2},{4,5},{5,4},{6,7},{7,6},{8,9},{9,8},{10,11... | collective-permute-start | bytes 2752520 | tf_op jit(solution)/shard_map/ppermute | solution.py:20
  110.2 49.8 %collective-permute-start.10 = (f32[14,128,128]{2,1,0:T(8,128)}, f32[14,128,128]{2,1,0:T(8,128)}, u32[]{:S(2)}, u32[]{:S(2)}) collective-permute-start(f32[14,128,128]{2,1,0:T(8,128)} %copy-done.8), channel_id=1, source_target_pairs={{0,2},{1,3},{2,0},{3,1},{4,6},{5,7},{6,4},{7,5},{8,10},{9,11},{10,... | collective-permute-start | bytes 2752520 | tf_op jit(solution)/shard_map/ppermute | solution.py:20
  110.7 0.9 copy-start.3
  111.6 68.0 %collective-permute-start.13 = (f32[14,128,128]{2,1,0:T(8,128)}, f32[14,128,128]{2,1,0:T(8,128)}, u32[]{:S(2)}, u32[]{:S(2)}) collective-permute-start(f32[14,128,128]{2,1,0:T(8,128)} %collective-permute-done.2.refs_1_.refs_12_), channel_id=1, source_target_pairs={{0,2},{1,3},{2,0},{3,1},{4,6},{5,7},{6,4},{7,5},{8,10},{9,11},{10,... | collective-permute-start | bytes 2752520 | tf_op jit(solution)/shard_map/ppermute | solution.py:20
  113.1 1.0 copy-start
  114.1 68.4 %copy-start.4 = (f32[14,128,128]{2,1,0:T(8,128)S(1)}, f32[14,128,128]{2,1,0:T(8,128)}, u32[]{:S(2)}) copy-start(f32[14,128,128]{2,1,0:T(8,128)} %copy-done.3) | copy-start | bytes 2752516
  114.1 80.5 %all-to-all-start.1 = ((f32[16,128,128]{2,1,0:T(8,128)}), f32[16,128,128]{2,1,0:T(8,128)}, u32[]{:S(2)}, u32[]{:S(2)}) async-start(f32[16,128,128]{2,1,0:T(8,128)} %after.3), calls=%async_computation.1 | async-start | bytes 2097152 | tf_op jit(solution)/shard_map/all_to_all | solution.py:272
  120.3 61.7 %collective-permute-start.9 = (f32[14,128,128]{2,1,0:T(8,128)}, f32[14,128,128]{2,1,0:T(8,128)}, u32[]{:S(2)}, u32[]{:S(2)}) collective-permute-start(f32[14,128,128]{2,1,0:T(8,128)} %copy-done.8), channel_id=1, source_target_pairs={{0,1},{1,0},{2,3},{3,2},{4,5},{5,4},{6,7},{7,6},{8,9},{9,8},{10,11... | collective-permute-start | bytes 2752520 | tf_op jit(solution)/shard_map/ppermute | solution.py:20
  137.5 44.5 %collective-permute-start.8 = (f32[14,128,128]{2,1,0:T(8,128)}, f32[14,128,128]{2,1,0:T(8,128)}, u32[]{:S(2)}, u32[]{:S(2)}) collective-permute-start(f32[14,128,128]{2,1,0:T(8,128)} %collective-permute-done.7.refs_6_), channel_id=1, source_target_pairs={{0,1},{1,0},{2,3},{3,2},{4,5},{5,4},{6,7},{7,6},{8,9},{9,8},{10,11... | collective-permute-start | bytes 2752520 | tf_op jit(solution)/shard_map/ppermute | solution.py:20
  137.5 44.5 %collective-permute-start.12 = (f32[14,128,128]{2,1,0:T(8,128)}, f32[14,128,128]{2,1,0:T(8,128)}, u32[]{:S(2)}, u32[]{:S(2)}) collective-permute-start(f32[14,128,128]{2,1,0:T(8,128)} %collective-permute-done.2.refs_1_.refs_12_), channel_id=1, source_target_pairs={{0,1},{1,0},{2,3},{3,2},{4,5},{5,4},{6,7},{7,6},{8,9},{9,8},{10,11... | collective-permute-start | bytes 2752520 | tf_op jit(solution)/shard_map/ppermute | solution.py:20
  160.0 22.0 %collective-permute-start.11 = (f32[14,128,128]{2,1,0:T(8,128)}, f32[14,128,128]{2,1,0:T(8,128)}, u32[]{:S(2)}, u32[]{:S(2)}) collective-permute-start(f32[14,128,128]{2,1,0:T(8,128)} %collective-permute-done.10.refs_10_), channel_id=1, source_target_pairs={{0,1},{1,0},{2,3},{3,2},{4,5},{5,4},{6,7},{7,6},{8,9},{9,8},{10,11... | collective-permute-start | bytes 2752520 | tf_op jit(solution)/shard_map/ppermute | solution.py:20
  179.7 2.8 collective-permute-start.14
  194.6 2.8 copy-start.1
  238.7 30.1 %all-to-all-start.3 = ((f32[16,128,128]{2,1,0:T(8,128)}), f32[16,128,128]{2,1,0:T(8,128)S(1)}, u32[]{:S(2)}, u32[]{:S(2)}) async-start(f32[16,128,128]{2,1,0:T(8,128)} %subtract_select_fusion.cur_ref.prev_ref), calls=%async_computation.3 | async-start | bytes 2097152 | tf_op jit(solution)/shard_map/all_to_all | solution.py:272
  268.8 6.4 %copy-start.6 = (f32[16,128,128]{2,1,0:T(8,128)}, f32[16,128,128]{2,1,0:T(8,128)S(1)}, u32[]{:S(2)}) copy-start(f32[16,128,128]{2,1,0:T(8,128)S(1)} %all-to-all-done.3.first_ref) | copy-start | bytes 3145732
  268.8 29.8 %all-to-all-start.2 = ((f32[16,128,128]{2,1,0:T(8,128)}), f32[16,128,128]{2,1,0:T(8,128)S(1)}, u32[]{:S(2)}, u32[]{:S(2)}) async-start(f32[16,128,128]{2,1,0:T(8,128)} %step.3), calls=%async_computation.2 | async-start | bytes 2097152 | tf_op jit(solution)/shard_map/all_to_all | solution.py:272
  298.6 1.0 copy-start.5

commit v6 on v0

v6 whole, which is shorter than its diff:
```python
import functools

import jax
import jax.numpy as jnp
from jax import lax
from jax.experimental import pallas as pl
from jax.experimental.pallas import tpu as pltpu
from jax.sharding import PartitionSpec as P

REACH = 7
WINDOW = 2 * REACH + 1
GROUP = 5
NOTE = 8
SMEM = pl.BlockSpec(memory_space=pltpu.SMEM)
ANY = pl.BlockSpec(memory_space=pl.ANY)
VMEM_LIMIT = 50 * 1024 * 1024


def cycle_of(total):
    if total != 16:
        return list(range(total))
    chips = [0, 2, 4, 6, 7, 5, 3, 1]
    return [2 * chip + core for chip in chips for core in (0, 1)]


def shifted(x, by):
    devices = lax.axis_size("row")
    if by == 0:
        return x
    return lax.ppermute(x, "row", [(i, (i + by) % devices) for i in range(devices)])


def place_of(offset, dropped):
    named = jnp.logical_and(offset < WINDOW, offset != dropped)
    slot = offset - jnp.where(offset > dropped, 1, 0)
    return jnp.clip(slot, 0, WINDOW - 2), named


def dropped_offset(cols, row, total):
    offsets = jnp.mod(cols - row + REACH, total)
    return REACH * WINDOW - jnp.sum(offsets)


def pack_kernel(drops_ref, cur_ref, prev_ref, *refs):
    outs = refs[:WINDOW]
    cur, prev, zeros, note, sems = refs[WINDOW:]
    size = cur.shape[1]
    loads = (
        pltpu.make_async_copy(cur_ref, cur, sems.at[0]),
        pltpu.make_async_copy(prev_ref, prev, sems.at[1]),
    )
    for load in loads:
        load.start()
    drop = drops_ref[1]
    zeros[...] = jnp.zeros_like(zeros)
    line = lax.broadcasted_iota(jnp.int32, note.shape, 0)
    note[...] = jnp.where(line == 0, drops_ref[0], drop).astype(jnp.float32)
    for offset in range(WINDOW):
        pltpu.make_async_copy(note, outs[offset].at[pl.ds(2 * size, NOTE)], sems.at[2]).start()
    for which, held in enumerate((cur, prev)):
        loads[which].wait()
        for offset in range(WINDOW):
            slot, named = place_of(jnp.int32(offset), drop)
            place = outs[offset].at[pl.ds(which * size, size)]

            @pl.when(named)
            def _(slot=slot, place=place, held=held):
                pltpu.make_async_copy(held.at[slot], place, sems.at[2]).start()

            @pl.when(jnp.logical_not(named))
            def _(place=place):
                pltpu.make_async_copy(zeros, place, sems.at[2]).start()

    for out in outs:
        pltpu.make_async_copy(out, out, sems.at[2]).wait()


def split(x):
    high = x.astype(jnp.bfloat16)
    low = (x - high.astype(jnp.float32)).astype(jnp.bfloat16)
    return high, low


def kept(drops_ref, w):
    return 2 * REACH - w != drops_ref[2 * w + 1]


def fill_pair(pair, block, w):
    size = block.shape[-1]
    high, low = split(block)
    at = pl.ds(pl.multiple_of(w * size, size), size)
    pair[at, pl.ds(0, size)] = high
    pair[at, pl.ds(size, size)] = low


def products_of(rows, pair):
    group, double = rows.shape[:2]
    size = double // 2
    products = jnp.dot(rows.reshape(group * double, rows.shape[2]), pair, preferred_element_type=jnp.float32)
    for r in range(group):
        parts = products[r * double:r * double + size] + products[r * double + size:(r + 1) * double]
        yield parts[:, :size] + parts[:, size:]


def first_kernel(total, drops_ref, places_ref, h_ref, *refs):
    t_refs = refs[:WINDOW]
    dense_ref = refs[WINDOW]
    outs = refs[WINDOW + 1:2 * WINDOW + 1]
    stage, dense, blocks, pair, h_sem, t_sem, dense_sem, out_sem = refs[2 * WINDOW + 1:]
    size = h_ref.shape[-1]

    for w in range(WINDOW):
        for which in range(2):
            pltpu.make_async_copy(t_refs[w].at[pl.ds(which * size, size)], blocks.at[which, w], t_sem).start()
    for w in range(WINDOW):
        pltpu.make_async_copy(h_ref.at[places_ref[w]], stage.at[w], h_sem.at[w]).start()
    pltpu.make_async_copy(blocks, blocks, t_sem).wait()
    for w in range(WINDOW):
        fill_pair(pair, jnp.where(kept(drops_ref, w), blocks[0, w], 0.0), w)

    def densify(w, slot, r):
        drop = drops_ref[2 * w]
        for p in range(WINDOW):
            k, named = place_of(lax.rem(p - w + REACH + total, total), drop)
            high, low = split(jnp.where(named, stage[w, k], 0.0))
            dense[slot, r, pl.ds(0, size), pl.ds(p * size, size)] = high
            dense[slot, r, pl.ds(size, size), pl.ds(p * size, size)] = low

    def store(g, slot):
        return pltpu.make_async_copy(dense.at[slot], dense_ref.at[pl.ds(g * GROUP, GROUP)], dense_sem.at[slot])

    def one(g, carry):
        slot = lax.rem(g, 2)

        @pl.when(g >= 2)
        def _():
            store(g - 2, slot).wait()

        for r in range(GROUP):
            w = g * GROUP + r
            pltpu.make_async_copy(stage.at[w], stage.at[w], h_sem.at[w]).wait()
            densify(w, slot, r)
        store(g, slot).start()
        for r, product in enumerate(products_of(dense[slot], pair[...])):
            w = g * GROUP + r
            blocks[1, w] = jnp.where(kept(drops_ref, w), 2.0 * product - blocks[1, w], 0.0)
        return carry

    groups = WINDOW // GROUP
    lax.fori_loop(0, groups, one, 0)
    for w in range(WINDOW):
        pltpu.make_async_copy(blocks.at[1, w], outs[w], out_sem).start()
    for g in range(groups - 2, groups):
        store(g, g % 2).wait()
    pltpu.make_async_copy(blocks.at[1], blocks.at[1], out_sem).wait()


def later_kernel(drops_ref, dense_ref, *refs):
    t_refs = refs[:WINDOW]
    first_refs = refs[WINDOW:2 * WINDOW]
    outs = refs[2 * WINDOW:3 * WINDOW]
    dense, terms, pairs, dense_sem, t_sem, first_sem, out_sem = refs[3 * WINDOW:]
    size = terms.shape[-1]
    groups = WINDOW // GROUP
    for w in range(WINDOW):
        pltpu.make_async_copy(first_refs[w], terms.at[1, w], first_sem).start()
    for g in range(groups):
        at = pl.ds(g * GROUP, GROUP)
        pltpu.make_async_copy(dense_ref.at[at], dense.at[at], dense_sem.at[g]).start()
    for w in range(WINDOW):
        pltpu.make_async_copy(t_refs[w].at[pl.ds(0, size)], terms.at[0, w], t_sem).start()
    pltpu.make_async_copy(terms.at[1], terms.at[1], first_sem).wait()
    for w in range(WINDOW):
        fill_pair(pairs.at[0], terms[1, w], w)
    pltpu.make_async_copy(terms.at[0], terms.at[0], t_sem).wait()

    def one(g, carry, step):
        rows = dense.at[pl.ds(g * GROUP, GROUP)]
        if step == 0:
            pltpu.make_async_copy(rows, rows, dense_sem.at[g]).wait()
        for r, product in enumerate(products_of(rows[...], pairs[step])):
            w = g * GROUP + r
            newest = jnp.where(kept(drops_ref, w), 2.0 * product - terms[step, w], 0.0)
            terms[step, w] = newest
            if step == 0:
                fill_pair(pairs.at[1], newest, w)
        return carry

    for step in range(2):
        lax.fori_loop(0, groups, functools.partial(one, step=step), 0)
        for w in range(WINDOW):
            pltpu.make_async_copy(terms.at[step, w], outs[w].at[pl.ds(step * size, size)], out_sem).start()
    pltpu.make_async_copy(terms, terms, out_sem).wait()


def collect(drops_ref, held_refs, place, sem, rows=None):
    for k in range(place.shape[0]):
        for skipped in (0, 1):
            held = held_refs[2 * REACH - k - skipped]
            source = held if rows is None else held.at[rows]

            @pl.when((k >= drops_ref[1]) == bool(skipped))
            def _(source=source, k=k):
                pltpu.make_async_copy(source, place.at[k], sem).start()


def unpack_first_kernel(drops_ref, coefs_ref, density_ref, *refs):
    held = refs[:WINDOW]
    out_ref, sums, one, sems = refs[WINDOW:]
    load = pltpu.make_async_copy(density_ref, sums, sems.at[0])
    load.start()
    collect(drops_ref, held, one, sems.at[1])
    load.wait()
    pltpu.make_async_copy(one, one, sems.at[1]).wait()
    sums[...] += coefs_ref[0] * one[...]
    store = pltpu.make_async_copy(sums, out_ref, sems.at[0])
    store.start()
    store.wait()


def unpack_last_kernel(drops_ref, coefs_ref, sum_ref, *refs):
    held = refs[:WINDOW]
    density_ref, last_ref, before_ref, sums, two, three, sems = refs[WINDOW:]
    size = two.shape[-1]
    load = pltpu.make_async_copy(sum_ref, sums, sems.at[0])
    load.start()
    collect(drops_ref, held, two, sems.at[1], pl.ds(0, size))
    collect(drops_ref, held, three, sems.at[2], pl.ds(size, size))
    pltpu.make_async_copy(two, two, sems.at[1]).wait()
    before = pltpu.make_async_copy(two, before_ref, sems.at[1])
    before.start()
    pltpu.make_async_copy(three, three, sems.at[2]).wait()
    last = pltpu.make_async_copy(three, last_ref, sems.at[2])
    last.start()
    load.wait()
    sums[...] = sums[...] + coefs_ref[1] * two[...] + coefs_ref[2] * three[...]
    store = pltpu.make_async_copy(sums, density_ref, sems.at[0])
    store.start()
    before.wait()
    last.wait()
    store.wait()


def per_device(h_blocks, h_cols, term_prev, term_cur, t_cols, density_in, coefs):
    total = lax.axis_size("row")
    me = lax.axis_index("row")
    count, size = h_blocks.shape[1:3]
    own = jnp.stack([dropped_offset(h_cols, me, total), dropped_offset(t_cols, me, total)])
    f32, bf16 = jnp.float32, jnp.bfloat16
    dma = pltpu.SemaphoreType.DMA
    params = pltpu.CompilerParams(vmem_limit_bytes=VMEM_LIMIT)
    row = jax.ShapeDtypeStruct((count, size, size), f32)
    row_scratch = pltpu.VMEM(row.shape, f32)
    dense = jax.ShapeDtypeStruct((WINDOW, 2 * size, WINDOW * size), bf16)
    pair_shape = (WINDOW * size, 2 * size)
    terms_scratch = pltpu.VMEM((2, WINDOW, size, size), f32)
    groups = WINDOW // GROUP

    def call(kernel, smem, arrays, outs, scratch, name):
        return pl.pallas_call(
            kernel,
            out_shape=outs,
            in_specs=[SMEM] * len(smem) + [ANY] * len(arrays),
            out_specs=[ANY] * len(outs),
            scratch_shapes=scratch,
            compiler_params=params,
            name=name,
        )(*smem, *arrays)

    cycle = cycle_of(total)
    places = [cycle.index(place) for place in range(total)]
    h_all = lax.all_gather(h_blocks, "row", axis=0, tiled=True, axis_index_groups=[cycle])
    window = jnp.mod(me + jnp.arange(-REACH, REACH + 1, dtype=jnp.int32), total)
    window = jnp.array(places, jnp.int32)[window]

    message = jax.ShapeDtypeStruct((2 * size + NOTE, size), f32)
    sent = call(
        pack_kernel,
        [own],
        [term_cur[0], term_prev[0]],
        [message] * WINDOW,
        [row_scratch, row_scratch, pltpu.VMEM((size, size), f32), pltpu.VMEM((NOTE, size), f32), dma((3,))],
        "pack",
    )
    column = [shifted(sent[offset], offset - REACH) for offset in reversed(range(WINDOW))]
    drops = jnp.concatenate([part[2 * size:2 * size + 2, 0] for part in column]).astype(jnp.int32)
    dense_rows, *term1 = call(
        functools.partial(first_kernel, total),
        [drops, window],
        [h_all, *column],
        [dense] + [jax.ShapeDtypeStruct((size, size), f32)] * WINDOW,
        [
            pltpu.VMEM((WINDOW, count, size, size), f32),
            pltpu.VMEM((2, GROUP) + dense.shape[1:], bf16),
            terms_scratch,
            pltpu.VMEM(pair_shape, bf16),
            dma((WINDOW,)),
            dma,
            dma((2,)),
            dma,
        ],
        "first",
    )
    back1 = [shifted(term1[w], w - REACH) for w in range(WINDOW)]
    terms = call(
        later_kernel,
        [drops],
        [dense_rows, *column, *term1],
        [jax.ShapeDtypeStruct((2 * size, size), f32)] * WINDOW,
        [
            pltpu.VMEM(dense.shape, bf16),
            terms_scratch,
            pltpu.VMEM((2,) + pair_shape, bf16),
            dma((groups,)),
            dma,
            dma,
            dma,
        ],
        "later",
    )
    back = [shifted(terms[w], w - REACH) for w in range(WINDOW)]
    (sums,) = call(
        unpack_first_kernel,
        [own, coefs],
        [density_in[0], *back1],
        [row],
        [row_scratch, row_scratch, dma((2,))],
        "unpack_first",
    )
    density, last, before = call(
        unpack_last_kernel,
        [own, coefs],
        [sums, *back],
        [row] * 3,
        [row_scratch, row_scratch, row_scratch, dma((3,))],
        "unpack_last",
    )
    return density[None], last[None], before[None]


def solution(mesh):
    blocks = P(("groups", "row"), None, None, None)
    cols = P(("groups", "row"), None)
    return jax.shard_map(
        per_device,
        mesh=mesh,
        in_specs=(blocks, cols, blocks, blocks, cols, blocks, P()),
        out_specs=(blocks, blocks, blocks),
        check_vma=False,
    )
```

time: 923 us -> 258 us (0.28)
  local copies, waits for them, and re-layouts: 376 us -> 5.53 us
  waiting for transfers between devices: 397 us -> 102 us
  matrix products: 67.6 us -> 0 us
  Pallas kernels: 0 us -> 44.8 us
  starting transfers between devices: 38.8 us -> 83.5 us
  blocking collectives: 19.8 us -> 0 us
  other arithmetic: 18.6 us -> 1.42 us
  between operations: 0.81 us -> 15.6 us
    ppermute x42, waiting for transfers between devices: 397 us -> 63.3 us  [shifted(): lax.ppermute(x, 'row', [(i, (i + by) % devices) for i in range(devices)])]
    gather x44 -> x1, local copies, waits for them, and re-layouts: 245 us -> 1.32 us  [per_device(): window = jnp.array(places, jnp.int32)[window]]
    dot_general x42 -> x0, matrix products: 67.6 us -> none  [target_block(): jnp.einsum('iaxy,iayz->ixz', h_blocks, gathered, precision=lax.Precision....]
    unnamed x80 -> x22, local copies, waits for them, and re-layouts: 65.2 us -> 2.4 us
    pallas_call x0 -> x5, Pallas kernels: none -> 44.8 us  [call(): pl.pallas_call(kernel, out_shape=outs, in_specs=[SMEM] * len(smem) + [ANY...]
    ppermute x42, starting transfers between devices: 38.8 us -> 83.5 us  [shifted(): lax.ppermute(x, 'row', [(i, (i + by) % devices) for i in range(devices)])]
    concatenate x6 -> x1, local copies, waits for them, and re-layouts: 41.2 us -> 0.08 us  [per_device(): jnp.concatenate([part[2 * size:2 * size + 2, 0] for part in column])]
    all_gather x0 -> x1, waiting for transfers between devices: none -> 37.9 us  [per_device(): lax.all_gather(h_blocks, 'row', axis=0, tiled=True, axis_index_groups=[cy...]
  transfers between devices with their start and end apart: 42 -> 43, of which waited for: 37 -> 14; matrix products, arithmetic and copies ran while one was open for 8% -> 2% of each run, Pallas kernels for 0% -> 10%
where the time goes in v6:
time: 258 us; the launch traced here: 253 us
  waiting for transfers between devices  102 us (40%)
  starting transfers between devices  83.5 us (32%)
  Pallas kernels  44.8 us (17%)
  between operations  15.6 us (6%)
  local copies, waits for them, and re-layouts  5.53 us (2%)
    ppermute x42, starting transfers between devices, shifted(): lax.ppermute(x, 'row', [(i, (i + by) % devices) for i in range(devices)])  83.5 us
    ppermute x42, waiting for transfers between devices, shifted(): lax.ppermute(x, 'row', [(i, (i + by) % devices) for i in range(devices)])  63.3 us
    pallas_call x5, Pallas kernels, call(): pl.pallas_call(kernel, out_shape=outs, in_specs=[SMEM] * len(smem) + [ANY...  44.8 us
    all_gather x1, waiting for transfers between devices, per_device(): lax.all_gather(h_blocks, 'row', axis=0, tiled=True, axis_index_groups=[cy...  37.9 us
  transfers between devices with their start and end apart: 43, of which 14 were waited for; matrix products, arithmetic and copies ran while one was open for 2% of the time, Pallas kernels for 10%

profile of v6, /device:TPU:22, one launch (start us, length us, event | category | flops | bytes accessed | tf_op | source)
XLA Modules:
  0.0 252.7 jit_solution(6388725203391466985)
XLA Ops:
  7.2 0.7 all-gather.2.cloned.1.call-update
  7.9 1.3 fusion
  10.6 1.2 copy-done
  11.8 1.2 copy-done.1
  13.0 4.0 %pack.1 = (f32[264,128]{1,0:T(8,128)S(1)}, f32[264,128]{1,0:T(8,128)S(1)}, f32[264,128]{1,0:T(8,128)S(1)}, f32[264,128]{1,0:T(8,128)S(1)}, f32[264,128]{1,0:T(8,...) custom-call(s32[2]{0:T(128)S(1)} %pad_add_fusion.drops_ref, ...), custom_call_target="tpu_custom_call" | custom-call | tf_op jit(solution)/shard_map/pack/pallas_call | solution.py:260
  17.0 2.2 collective-permute-start.1
  19.2 1.6 collective-permute-start.2
  21.1 2.8 %collective-permute-start.4 = (f32[264,128]{1,0:T(8,128)S(1)}, f32[264,128]{1,0:T(8,128)S(1)}, u32[]{:S(2)}, u32[]{:S(2)}) collective-permute-start(f32[264,128]{1,0:T(8,128)S(1)} %get-tuple-element.56), channel_id=1, source_target_pairs={{0,3},{1,4},{2,5},{3,6},{4,7},{5,8},{6,9},{7,10},{8,11},{9,12},{10... | collective-permute-start | bytes 405512 | tf_op jit(solution)/shard_map/ppermute | solution.py:30
  24.0 1.3 gather_fusion
  25.4 2.2 collective-permute-done.refs_0_
  27.6 2.0 collective-permute-start.5
  29.7 9.5 %collective-permute-done.1.refs_1_ = f32[264,128]{1,0:T(8,128)S(1)} collective-permute-done((f32[264,128]{1,0:T(8,128)S(1)}, f32[264,128]{1,0:T(8,128)S(1)}, u32[]{:S(2)}, u32[]{:S(2)}) %collective-permute-start.1) | collective-permute-done | bytes 135200 | tf_op jit(solution)/shard_map/ppermute | solution.py:30
  39.7 1.4 collective-permute-start.7
  41.2 10.1 %collective-permute-done.3.refs_3_ = f32[264,128]{1,0:T(8,128)S(1)} collective-permute-done((f32[264,128]{1,0:T(8,128)S(1)}, f32[264,128]{1,0:T(8,128)S(1)}, u32[]{:S(2)}, u32[]{:S(2)}) %collective-permute-start.3) | collective-permute-done | bytes 135200 | tf_op jit(solution)/shard_map/ppermute | solution.py:30
  51.4 6.2 %collective-permute-done.4.refs_4_ = f32[264,128]{1,0:T(8,128)S(1)} collective-permute-done((f32[264,128]{1,0:T(8,128)S(1)}, f32[264,128]{1,0:T(8,128)S(1)}, u32[]{:S(2)}, u32[]{:S(2)}) %collective-permute-start.4) | collective-permute-done | bytes 135200 | tf_op jit(solution)/shard_map/ppermute | solution.py:30
  57.7 7.9 %collective-permute-start.10 = (f32[264,128]{1,0:T(8,128)S(1)}, f32[264,128]{1,0:T(8,128)S(1)}, u32[]{:S(2)}, u32[]{:S(2)}) collective-permute-start(f32[264,128]{1,0:T(8,128)S(1)} %get-tuple-element.63), channel_id=1, source_target_pairs={{0,12},{1,13},{2,14},{3,15},{4,0},{5,1},{6,2},{7,3},{8,4},{9,5},{1... | collective-permute-start | bytes 405512 | tf_op jit(solution)/shard_map/ppermute | solution.py:30
  66.2 12.0 %collective-permute-start.13 = (f32[264,128]{1,0:T(8,128)S(1)}, f32[264,128]{1,0:T(8,128)S(1)}, u32[]{:S(2)}, u32[]{:S(2)}) collective-permute-start(f32[264,128]{1,0:T(8,128)S(1)} %get-tuple-element.66), channel_id=1, source_target_pairs={{0,9},{1,10},{2,11},{3,12},{4,13},{5,14},{6,15},{7,0},{8,1},{9,2},... | collective-permute-start | bytes 405512 | tf_op jit(solution)/shard_map/ppermute | solution.py:30
  78.6 9.5 %collective-permute-done.12.refs_13_ = f32[264,128]{1,0:T(8,128)S(1)} collective-permute-done((f32[264,128]{1,0:T(8,128)S(1)}, f32[264,128]{1,0:T(8,128)S(1)}, u32[]{:S(2)}, u32[]{:S(2)}) %collective-permute-start.12) | collective-permute-done | bytes 135200 | tf_op jit(solution)/shard_map/ppermute | solution.py:30
  88.2 3.1 %collective-permute-done.13.refs_14_ = f32[264,128]{1,0:T(8,128)S(1)} collective-permute-done((f32[264,128]{1,0:T(8,128)S(1)}, f32[264,128]{1,0:T(8,128)S(1)}, u32[]{:S(2)}, u32[]{:S(2)}) %collective-permute-start.13) | collective-permute-done | bytes 135200 | tf_op jit(solution)/shard_map/ppermute | solution.py:30
  91.5 37.9 %all-gather.2.cloned.1.call-done.h_ref = f32[16,14,128,128]{3,2,1,0:T(8,128)} async-done(((f32[1,14,128,128]{3,2,1,0:T(8,128)}), f32[16,14,128,128]{3,2,1,0:T(8,128)}) %all-gather.2.cloned.1.call-update) | async-done | bytes 14680080 | tf_op jit(solution)/shard_map/all_gather | solution.py:272
  129.4 13.7 %first.1 = (bf16[15,256,1920]{2,1,0:T(8,128)(2,1)}, f32[128,128]{1,0:T(8,128)S(1)}, f32[128,128]{1,0:T(8,128)S(1)}, f32[128,128]{1,0:T(8,128)S(1)}, f32[128,128]...) custom-call(s32[30]{0:T(128)S(1)} %convert_element_type.3.drops_ref,, ...), custom_call_target="tpu_custom_call" | custom-call | tf_op jit(solution)/shard_map/first/pallas_call | solution.py:260
  143.2 1.5 collective-permute-start.15
  144.7 2.2 collective-permute-start.16
  146.9 1.6 collective-permute-start.17
  149.0 1.2 collective-permute-start.19
  150.2 0.7 collective-permute-start.20
  151.7 4.4 %collective-permute-start.22 = (f32[128,128]{1,0:T(8,128)S(1)}, f32[128,128]{1,0:T(8,128)S(1)}, u32[]{:S(2)}, u32[]{:S(2)}) collective-permute-start(f32[128,128]{1,0:T(8,128)S(1)} %get-tuple-element.76.refs_24_), channel_id=1, source_target_pairs={{0,2},{1,3},{2,4},{3,5},{4,6},{5,7},{6,8},{7,9},{8,10},{9,11},{10,... | collective-permute-start | bytes 196616 | tf_op jit(solution)/shard_map/ppermute | solution.py:30
  156.1 7.8 %collective-permute-start.23 = (f32[128,128]{1,0:T(8,128)S(1)}, f32[128,128]{1,0:T(8,128)S(1)}, u32[]{:S(2)}, u32[]{:S(2)}) collective-permute-start(f32[128,128]{1,0:T(8,128)S(1)} %get-tuple-element.77.refs_25_), channel_id=1, source_target_pairs={{0,3},{1,4},{2,5},{3,6},{4,7},{5,8},{6,9},{7,10},{8,11},{9,12},{10... | collective-permute-start | bytes 196616 | tf_op jit(solution)/shard_map/ppermute | solution.py:30
  163.9 0.8 collective-permute-start.25
  164.7 3.4 %collective-permute-start.26 = (f32[128,128]{1,0:T(8,128)S(1)}, f32[128,128]{1,0:T(8,128)S(1)}, u32[]{:S(2)}, u32[]{:S(2)}) collective-permute-start(f32[128,128]{1,0:T(8,128)S(1)} %get-tuple-element.80.refs_28_), channel_id=1, source_target_pairs={{0,6},{1,7},{2,8},{3,9},{4,10},{5,11},{6,12},{7,13},{8,14},{9,15},... | collective-permute-start | bytes 196616 | tf_op jit(solution)/shard_map/ppermute | solution.py:30
  168.1 19.4 %later.1 = (f32[256,128]{1,0:T(8,128)S(1)}, f32[256,128]{1,0:T(8,128)S(1)}, f32[256,128]{1,0:T(8,128)S(1)}, f32[256,128]{1,0:T(8,128)S(1)}, f32[256,128]{1,0:T(8...) custom-call(s32[30]{0:T(128)S(1)} %convert_element_type.3.drops_ref,, ...), custom_call_target="tpu_custom_call" | custom-call | tf_op jit(solution)/shard_map/later/pallas_call | solution.py:260
  187.6 2.4 collective-permute-start.29
  190.0 1.8 collective-permute-start.31
  191.8 3.2 %collective-permute-start.27 = (f32[128,128]{1,0:T(8,128)S(1)}, f32[128,128]{1,0:T(8,128)S(1)}, u32[]{:S(2)}, u32[]{:S(2)}) collective-permute-start(f32[128,128]{1,0:T(8,128)S(1)} %get-tuple-element.81.refs_29_), channel_id=1, source_target_pairs={{0,7},{1,8},{2,9},{3,10},{4,11},{5,12},{6,13},{7,14},{8,15},{9,0},... | collective-permute-start | bytes 196616 | tf_op jit(solution)/shard_map/ppermute | solution.py:30
  195.0 8.6 %collective-permute-done.27.refs_14_ = f32[128,128]{1,0:T(8,128)S(1)} collective-permute-done((f32[128,128]{1,0:T(8,128)S(1)}, f32[128,128]{1,0:T(8,128)S(1)}, u32[]{:S(2)}, u32[]{:S(2)}) %collective-permute-start.27) | collective-permute-done | bytes 65568 | tf_op jit(solution)/shard_map/ppermute | solution.py:30
  203.5 1.2 collective-permute-start.32
  204.7 2.8 %collective-permute-start.33 = (f32[256,128]{1,0:T(8,128)S(1)}, f32[256,128]{1,0:T(8,128)S(1)}, u32[]{:S(2)}, u32[]{:S(2)}) collective-permute-start(f32[256,128]{1,0:T(8,128)S(1)} %get-tuple-element.88), channel_id=1, source_target_pairs={{0,14},{1,15},{2,0},{3,1},{4,2},{5,3},{6,4},{7,5},{8,6},{9,7},{10,... | collective-permute-start | bytes 393224 | tf_op jit(solution)/shard_map/ppermute | solution.py:30
  207.5 3.3 %collective-permute-start.34 = (f32[256,128]{1,0:T(8,128)S(1)}, f32[256,128]{1,0:T(8,128)S(1)}, u32[]{:S(2)}, u32[]{:S(2)}) collective-permute-start(f32[256,128]{1,0:T(8,128)S(1)} %get-tuple-element.89), channel_id=1, source_target_pairs={{0,15},{1,0},{2,1},{3,2},{4,3},{5,4},{6,5},{7,6},{8,7},{9,8},{10,9... | collective-permute-start | bytes 393224 | tf_op jit(solution)/shard_map/ppermute | solution.py:30
  210.9 2.2 collective-permute-start.36
  213.1 4.6 %collective-permute-start.37 = (f32[256,128]{1,0:T(8,128)S(1)}, f32[256,128]{1,0:T(8,128)S(1)}, u32[]{:S(2)}, u32[]{:S(2)}) collective-permute-start(f32[256,128]{1,0:T(8,128)S(1)} %get-tuple-element.93), channel_id=1, source_target_pairs={{0,3},{1,4},{2,5},{3,6},{4,7},{5,8},{6,9},{7,10},{8,11},{9,12},{10... | collective-permute-start | bytes 393224 | tf_op jit(solution)/shard_map/ppermute | solution.py:30
  217.7 2.2 collective-permute-start.38
  220.2 1.5 collective-permute-start.39
  221.7 3.7 %collective-permute-start.40 = (f32[256,128]{1,0:T(8,128)S(1)}, f32[256,128]{1,0:T(8,128)S(1)}, u32[]{:S(2)}, u32[]{:S(2)}) collective-permute-start(f32[256,128]{1,0:T(8,128)S(1)} %get-tuple-element.96), channel_id=1, source_target_pairs={{0,6},{1,7},{2,8},{3,9},{4,10},{5,11},{6,12},{7,13},{8,14},{9,15},... | collective-permute-start | bytes 393224 | tf_op jit(solution)/shard_map/ppermute | solution.py:30
  225.4 2.5 %unpack_first.1.sum_ref = f32[14,128,128]{2,1,0:T(8,128)S(1)} custom-call(s32[2]{0:T(128)S(1)} %pad_add_fusion.drops_ref, f32[3]{0:T(128)S(1)} %copy-done.10, f32[14,128,128]{2,1,0:T(8,128)S(1)} %bitcast.12, f32[128,128]{1,0:T(8,128)S(1)} %collective-permute-done.14.refs_0_, f32[128,128]{1,0:T(8,128)S(1)} %collective-permute-done.15.refs_1_, ...), custom_call_target="tpu_custom_call" | custom-call | tf_op jit(solution)/shard_map/unpack_first/pallas_call | solution.py:260
  228.0 2.4 collective-permute-done.39.refs_12_
  230.3 7.5 %collective-permute-done.40.refs_13_ = f32[256,128]{1,0:T(8,128)S(1)} collective-permute-done((f32[256,128]{1,0:T(8,128)S(1)}, f32[256,128]{1,0:T(8,128)S(1)}, u32[]{:S(2)}, u32[]{:S(2)}) %collective-permute-start.40) | collective-permute-done | bytes 131104 | tf_op jit(solution)/shard_map/ppermute | solution.py:30
  237.9 2.8 %collective-permute-done.41.refs_14_ = f32[256,128]{1,0:T(8,128)S(1)} collective-permute-done((f32[256,128]{1,0:T(8,128)S(1)}, f32[256,128]{1,0:T(8,128)S(1)}, u32[]{:S(2)}, u32[]{:S(2)}) %collective-permute-start.41) | collective-permute-done | bytes 131104 | tf_op jit(solution)/shard_map/ppermute | solution.py:30
  240.7 5.2 %unpack_last.1 = (f32[14,128,128]{2,1,0:T(8,128)}, f32[14,128,128]{2,1,0:T(8,128)}, f32[14,128,128]{2,1,0:T(8,128)}) custom-call(s32[2]{0:T(128)S(1)} %pad_add_fusion.drops_ref, f32[3]{0:T(128)S(1)} %copy-done.10, f32[14,128,128]{2,1,0:T(8,128)S(1)} %unpack_first.1.sum_ref, f32[256,128]{1,0:T(8,128)S(1)} %collective-permute-done.28.refs_0_, ...), custom_call_target="tpu_custom_call" | custom-call | tf_op jit(solution)/shard_map/unpack_last/pallas_call | solution.py:260
  (88 shorter events, 4.7 us)
Async XLA Ops:
  7.2 122.3 %all-gather.2.cloned.1.call-start = ((), (), s32[]{:S(2)}) async-start(), calls=%async_computation | async-start | bytes 15597568 | tf_op jit(solution)/shard_map/all_gather | solution.py:272
  16.9 10.6 %collective-permute-start = (f32[264,128]{1,0:T(8,128)S(1)}, f32[264,128]{1,0:T(8,128)S(1)}, u32[]{:S(2)}, u32[]{:S(2)}) collective-permute-start(f32[264,128]{1,0:T(8,128)S(1)} %get-tuple-element.52), channel_id=1, source_target_pairs={{0,7},{1,8},{2,9},{3,10},{4,11},{5,12},{6,13},{7,14},{8,15},{9,0},... | collective-permute-start | bytes 405512 | tf_op jit(solution)/shard_map/ppermute | solution.py:30
  17.0 22.2 %collective-permute-start.1 = (f32[264,128]{1,0:T(8,128)S(1)}, f32[264,128]{1,0:T(8,128)S(1)}, u32[]{:S(2)}, u32[]{:S(2)}) collective-permute-start(f32[264,128]{1,0:T(8,128)S(1)} %get-tuple-element.53), channel_id=1, source_target_pairs={{0,6},{1,7},{2,8},{3,9},{4,10},{5,11},{6,12},{7,13},{8,14},{9,15},... | collective-permute-start | bytes 405512 | tf_op jit(solution)/shard_map/ppermute | solution.py:30
  19.2 20.5 %collective-permute-start.2 = (f32[264,128]{1,0:T(8,128)S(1)}, f32[264,128]{1,0:T(8,128)S(1)}, u32[]{:S(2)}, u32[]{:S(2)}) collective-permute-start(f32[264,128]{1,0:T(8,128)S(1)} %get-tuple-element.54), channel_id=1, source_target_pairs={{0,5},{1,6},{2,7},{3,8},{4,9},{5,10},{6,11},{7,12},{8,13},{9,14},{... | collective-permute-start | bytes 405512 | tf_op jit(solution)/shard_map/ppermute | solution.py:30
  20.9 30.4 %collective-permute-start.3 = (f32[264,128]{1,0:T(8,128)S(1)}, f32[264,128]{1,0:T(8,128)S(1)}, u32[]{:S(2)}, u32[]{:S(2)}) collective-permute-start(f32[264,128]{1,0:T(8,128)S(1)} %get-tuple-element.55), channel_id=1, source_target_pairs={{0,4},{1,5},{2,6},{3,7},{4,8},{5,9},{6,10},{7,11},{8,12},{9,13},{1... | collective-permute-start | bytes 405512 | tf_op jit(solution)/shard_map/ppermute | solution.py:30
  21.1 36.5 %collective-permute-start.4 = (f32[264,128]{1,0:T(8,128)S(1)}, f32[264,128]{1,0:T(8,128)S(1)}, u32[]{:S(2)}, u32[]{:S(2)}) collective-permute-start(f32[264,128]{1,0:T(8,128)S(1)} %get-tuple-element.56), channel_id=1, source_target_pairs={{0,3},{1,4},{2,5},{3,6},{4,7},{5,8},{6,9},{7,10},{8,11},{9,12},{10... | collective-permute-start | bytes 405512 | tf_op jit(solution)/shard_map/ppermute | solution.py:30
  27.6 30.2 %collective-permute-start.5 = (f32[264,128]{1,0:T(8,128)S(1)}, f32[264,128]{1,0:T(8,128)S(1)}, u32[]{:S(2)}, u32[]{:S(2)}) collective-permute-start(f32[264,128]{1,0:T(8,128)S(1)} %get-tuple-element.57), channel_id=1, source_target_pairs={{0,2},{1,3},{2,4},{3,5},{4,6},{5,7},{6,8},{7,9},{8,10},{9,11},{10,... | collective-permute-start | bytes 405512 | tf_op jit(solution)/shard_map/ppermute | solution.py:30
  39.2 26.6 %collective-permute-start.6 = (f32[264,128]{1,0:T(8,128)S(1)}, f32[264,128]{1,0:T(8,128)S(1)}, u32[]{:S(2)}, u32[]{:S(2)}) collective-permute-start(f32[264,128]{1,0:T(8,128)S(1)} %get-tuple-element.58), channel_id=1, source_target_pairs={{0,1},{1,2},{2,3},{3,4},{4,5},{5,6},{6,7},{7,8},{8,9},{9,10},{10,1... | collective-permute-start | bytes 405512 | tf_op jit(solution)/shard_map/ppermute | solution.py:30
  39.7 26.3 %collective-permute-start.7 = (f32[264,128]{1,0:T(8,128)S(1)}, f32[264,128]{1,0:T(8,128)S(1)}, u32[]{:S(2)}, u32[]{:S(2)}) collective-permute-start(f32[264,128]{1,0:T(8,128)S(1)} %get-tuple-element.60), channel_id=1, source_target_pairs={{0,15},{1,0},{2,1},{3,2},{4,3},{5,4},{6,5},{7,6},{8,7},{9,8},{10,9... | collective-permute-start | bytes 405512 | tf_op jit(solution)/shard_map/ppermute | solution.py:30
  51.3 14.9 %collective-permute-start.8 = (f32[264,128]{1,0:T(8,128)S(1)}, f32[264,128]{1,0:T(8,128)S(1)}, u32[]{:S(2)}, u32[]{:S(2)}) collective-permute-start(f32[264,128]{1,0:T(8,128)S(1)} %get-tuple-element.61), channel_id=1, source_target_pairs={{0,14},{1,15},{2,0},{3,1},{4,2},{5,3},{6,4},{7,5},{8,6},{9,7},{10,... | collective-permute-start | bytes 405512 | tf_op jit(solution)/shard_map/ppermute | solution.py:30
  57.6 20.6 %collective-permute-start.9 = (f32[264,128]{1,0:T(8,128)S(1)}, f32[264,128]{1,0:T(8,128)S(1)}, u32[]{:S(2)}, u32[]{:S(2)}) collective-permute-start(f32[264,128]{1,0:T(8,128)S(1)} %get-tuple-element.62), channel_id=1, source_target_pairs={{0,13},{1,14},{2,15},{3,0},{4,1},{5,2},{6,3},{7,4},{8,5},{9,6},{10... | collective-permute-start | bytes 405512 | tf_op jit(solution)/shard_map/ppermute | solution.py:30
  57.7 20.6 %collective-permute-start.10 = (f32[264,128]{1,0:T(8,128)S(1)}, f32[264,128]{1,0:T(8,128)S(1)}, u32[]{:S(2)}, u32[]{:S(2)}) collective-permute-start(f32[264,128]{1,0:T(8,128)S(1)} %get-tuple-element.63), channel_id=1, source_target_pairs={{0,12},{1,13},{2,14},{3,15},{4,0},{5,1},{6,2},{7,3},{8,4},{9,5},{1... | collective-permute-start | bytes 405512 | tf_op jit(solution)/shard_map/ppermute | solution.py:30
  65.8 12.7 %collective-permute-start.11 = (f32[264,128]{1,0:T(8,128)S(1)}, f32[264,128]{1,0:T(8,128)S(1)}, u32[]{:S(2)}, u32[]{:S(2)}) collective-permute-start(f32[264,128]{1,0:T(8,128)S(1)} %get-tuple-element.64), channel_id=1, source_target_pairs={{0,11},{1,12},{2,13},{3,14},{4,15},{5,0},{6,1},{7,2},{8,3},{9,4},{... | collective-permute-start | bytes 405512 | tf_op jit(solution)/shard_map/ppermute | solution.py:30
  66.0 102.1 %copy-start.3 = (f32[264,128]{1,0:T(8,128)}, f32[264,128]{1,0:T(8,128)S(1)}, u32[]{:S(2)}) copy-start(f32[264,128]{1,0:T(8,128)S(1)} %collective-permute-done.7.refs_8_) | copy-start | bytes 405508
  66.0 22.1 %collective-permute-start.12 = (f32[264,128]{1,0:T(8,128)S(1)}, f32[264,128]{1,0:T(8,128)S(1)}, u32[]{:S(2)}, u32[]{:S(2)}) collective-permute-start(f32[264,128]{1,0:T(8,128)S(1)} %get-tuple-element.65), channel_id=1, source_target_pairs={{0,10},{1,11},{2,12},{3,13},{4,14},{5,15},{6,0},{7,1},{8,2},{9,3},... | collective-permute-start | bytes 405512 | tf_op jit(solution)/shard_map/ppermute | solution.py:30
  66.2 101.9 %copy-start.4 = (f32[264,128]{1,0:T(8,128)}, f32[264,128]{1,0:T(8,128)S(1)}, u32[]{:S(2)}) copy-start(f32[264,128]{1,0:T(8,128)S(1)} %collective-permute-done.8.refs_9_) | copy-start | bytes 405508
  66.2 25.1 %collective-permute-start.13 = (f32[264,128]{1,0:T(8,128)S(1)}, f32[264,128]{1,0:T(8,128)S(1)}, u32[]{:S(2)}, u32[]{:S(2)}) collective-permute-start(f32[264,128]{1,0:T(8,128)S(1)} %get-tuple-element.66), channel_id=1, source_target_pairs={{0,9},{1,10},{2,11},{3,12},{4,13},{5,14},{6,15},{7,0},{8,1},{9,2},... | collective-permute-start | bytes 405512 | tf_op jit(solution)/shard_map/ppermute | solution.py:30
  78.2 89.8 %copy-start.5 = (f32[264,128]{1,0:T(8,128)}, f32[264,128]{1,0:T(8,128)S(1)}, u32[]{:S(2)}) copy-start(f32[264,128]{1,0:T(8,128)S(1)} %collective-permute-done.9.refs_10_) | copy-start | bytes 405508
  91.5 133.9 %copy-start.2 = (f32[1,14,128,128]{3,2,1,0:T(8,128)S(1)}, f32[1,14,128,128]{3,2,1,0:T(8,128)}, u32[]{:S(2)}) copy-start(f32[1,14,128,128]{3,2,1,0:T(8,128)} %param.13) | copy-start | bytes 2752516
  91.5 133.9 %copy-start.10 = (f32[3]{0:T(128)S(1)}, f32[3]{0:T(128)}, u32[]{:S(2)}) copy-start(f32[3]{0:T(128)} %coefs_ref.3) | copy-start | bytes 40
  143.2 5.9 %collective-permute-start.14 = (f32[128,128]{1,0:T(8,128)S(1)}, f32[128,128]{1,0:T(8,128)S(1)}, u32[]{:S(2)}, u32[]{:S(2)}) collective-permute-start(f32[128,128]{1,0:T(8,128)S(1)} %get-tuple-element.67.refs_15_), channel_id=1, source_target_pairs={{0,9},{1,10},{2,11},{3,12},{4,13},{5,14},{6,15},{7,0},{8,1},{9,2},... | collective-permute-start | bytes 196616 | tf_op jit(solution)/shard_map/ppermute | solution.py:30
  143.2 7.0 %collective-permute-start.15 = (f32[128,128]{1,0:T(8,128)S(1)}, f32[128,128]{1,0:T(8,128)S(1)}, u32[]{:S(2)}, u32[]{:S(2)}) collective-permute-start(f32[128,128]{1,0:T(8,128)S(1)} %get-tuple-element.68.refs_16_), channel_id=1, source_target_pairs={{0,10},{1,11},{2,12},{3,13},{4,14},{5,15},{6,0},{7,1},{8,2},{9,3},... | collective-permute-start | bytes 196616 | tf_op jit(solution)/shard_map/ppermute | solution.py:30
  144.7 6.2 %collective-permute-start.16 = (f32[128,128]{1,0:T(8,128)S(1)}, f32[128,128]{1,0:T(8,128)S(1)}, u32[]{:S(2)}, u32[]{:S(2)}) collective-permute-start(f32[128,128]{1,0:T(8,128)S(1)} %get-tuple-element.69.refs_17_), channel_id=1, source_target_pairs={{0,11},{1,12},{2,13},{3,14},{4,15},{5,0},{6,1},{7,2},{8,3},{9,4},{... | collective-permute-start | bytes 196616 | tf_op jit(solution)/shard_map/ppermute | solution.py:30
  146.9 4.8 %collective-permute-start.17 = (f32[128,128]{1,0:T(8,128)S(1)}, f32[128,128]{1,0:T(8,128)S(1)}, u32[]{:S(2)}, u32[]{:S(2)}) collective-permute-start(f32[128,128]{1,0:T(8,128)S(1)} %get-tuple-element.70.refs_18_), channel_id=1, source_target_pairs={{0,12},{1,13},{2,14},{3,15},{4,0},{5,1},{6,2},{7,3},{8,4},{9,5},{1... | collective-permute-start | bytes 196616 | tf_op jit(solution)/shard_map/ppermute | solution.py:30
  148.5 7.6 %collective-permute-start.18 = (f32[128,128]{1,0:T(8,128)S(1)}, f32[128,128]{1,0:T(8,128)S(1)}, u32[]{:S(2)}, u32[]{:S(2)}) collective-permute-start(f32[128,128]{1,0:T(8,128)S(1)} %get-tuple-element.71.refs_19_), channel_id=1, source_target_pairs={{0,13},{1,14},{2,15},{3,0},{4,1},{5,2},{6,3},{7,4},{8,5},{9,6},{10... | collective-permute-start | bytes 196616 | tf_op jit(solution)/shard_map/ppermute | solution.py:30
  149.0 14.9 %collective-permute-start.19 = (f32[128,128]{1,0:T(8,128)S(1)}, f32[128,128]{1,0:T(8,128)S(1)}, u32[]{:S(2)}, u32[]{:S(2)}) collective-permute-start(f32[128,128]{1,0:T(8,128)S(1)} %get-tuple-element.72.refs_20_), channel_id=1, source_target_pairs={{0,14},{1,15},{2,0},{3,1},{4,2},{5,3},{6,4},{7,5},{8,6},{9,7},{10,... | collective-permute-start | bytes 196616 | tf_op jit(solution)/shard_map/ppermute | solution.py:30
  150.2 13.7 %collective-permute-start.20 = (f32[128,128]{1,0:T(8,128)S(1)}, f32[128,128]{1,0:T(8,128)S(1)}, u32[]{:S(2)}, u32[]{:S(2)}) collective-permute-start(f32[128,128]{1,0:T(8,128)S(1)} %get-tuple-element.73.refs_21_), channel_id=1, source_target_pairs={{0,15},{1,0},{2,1},{3,2},{4,3},{5,4},{6,5},{7,6},{8,7},{9,8},{10,9... | collective-permute-start | bytes 196616 | tf_op jit(solution)/shard_map/ppermute | solution.py:30
  151.0 13.8 %collective-permute-start.21 = (f32[128,128]{1,0:T(8,128)S(1)}, f32[128,128]{1,0:T(8,128)S(1)}, u32[]{:S(2)}, u32[]{:S(2)}) collective-permute-start(f32[128,128]{1,0:T(8,128)S(1)} %get-tuple-element.75.refs_23_), channel_id=1, source_target_pairs={{0,1},{1,2},{2,3},{3,4},{4,5},{5,6},{6,7},{7,8},{8,9},{9,10},{10,1... | collective-permute-start | bytes 196616 | tf_op jit(solution)/shard_map/ppermute | solution.py:30
  151.7 35.9 %collective-permute-start.22 = (f32[128,128]{1,0:T(8,128)S(1)}, f32[128,128]{1,0:T(8,128)S(1)}, u32[]{:S(2)}, u32[]{:S(2)}) collective-permute-start(f32[128,128]{1,0:T(8,128)S(1)} %get-tuple-element.76.refs_24_), channel_id=1, source_target_pairs={{0,2},{1,3},{2,4},{3,5},{4,6},{5,7},{6,8},{7,9},{8,10},{9,11},{10,... | collective-permute-start | bytes 196616 | tf_op jit(solution)/shard_map/ppermute | solution.py:30
  156.1 31.5 %collective-permute-start.23 = (f32[128,128]{1,0:T(8,128)S(1)}, f32[128,128]{1,0:T(8,128)S(1)}, u32[]{:S(2)}, u32[]{:S(2)}) collective-permute-start(f32[128,128]{1,0:T(8,128)S(1)} %get-tuple-element.77.refs_25_), channel_id=1, source_target_pairs={{0,3},{1,4},{2,5},{3,6},{4,7},{5,8},{6,9},{7,10},{8,11},{9,12},{10... | collective-permute-start | bytes 196616 | tf_op jit(solution)/shard_map/ppermute | solution.py:30
  163.9 26.1 %collective-permute-start.24 = (f32[128,128]{1,0:T(8,128)S(1)}, f32[128,128]{1,0:T(8,128)S(1)}, u32[]{:S(2)}, u32[]{:S(2)}) collective-permute-start(f32[128,128]{1,0:T(8,128)S(1)} %get-tuple-element.78.refs_26_), channel_id=1, source_target_pairs={{0,4},{1,5},{2,6},{3,7},{4,8},{5,9},{6,10},{7,11},{8,12},{9,13},{1... | collective-permute-start | bytes 196616 | tf_op jit(solution)/shard_map/ppermute | solution.py:30
  163.9 26.1 %collective-permute-start.25 = (f32[128,128]{1,0:T(8,128)S(1)}, f32[128,128]{1,0:T(8,128)S(1)}, u32[]{:S(2)}, u32[]{:S(2)}) collective-permute-start(f32[128,128]{1,0:T(8,128)S(1)} %get-tuple-element.79.refs_27_), channel_id=1, source_target_pairs={{0,5},{1,6},{2,7},{3,8},{4,9},{5,10},{6,11},{7,12},{8,13},{9,14},{... | collective-permute-start | bytes 196616 | tf_op jit(solution)/shard_map/ppermute | solution.py:30
  164.7 27.1 %collective-permute-start.26 = (f32[128,128]{1,0:T(8,128)S(1)}, f32[128,128]{1,0:T(8,128)S(1)}, u32[]{:S(2)}, u32[]{:S(2)}) collective-permute-start(f32[128,128]{1,0:T(8,128)S(1)} %get-tuple-element.80.refs_28_), channel_id=1, source_target_pairs={{0,6},{1,7},{2,8},{3,9},{4,10},{5,11},{6,12},{7,13},{8,14},{9,15},... | collective-permute-start | bytes 196616 | tf_op jit(solution)/shard_map/ppermute | solution.py:30
  187.6 17.2 %collective-permute-start.28 = (f32[256,128]{1,0:T(8,128)S(1)}, f32[256,128]{1,0:T(8,128)S(1)}, u32[]{:S(2)}, u32[]{:S(2)}) collective-permute-start(f32[256,128]{1,0:T(8,128)S(1)} %get-tuple-element.83), channel_id=1, source_target_pairs={{0,9},{1,10},{2,11},{3,12},{4,13},{5,14},{6,15},{7,0},{8,1},{9,2},... | collective-permute-start | bytes 393224 | tf_op jit(solution)/shard_map/ppermute | solution.py:30
  187.6 19.9 %collective-permute-start.29 = (f32[256,128]{1,0:T(8,128)S(1)}, f32[256,128]{1,0:T(8,128)S(1)}, u32[]{:S(2)}, u32[]{:S(2)}) collective-permute-start(f32[256,128]{1,0:T(8,128)S(1)} %get-tuple-element.84), channel_id=1, source_target_pairs={{0,10},{1,11},{2,12},{3,13},{4,14},{5,15},{6,0},{7,1},{8,2},{9,3},... | collective-permute-start | bytes 393224 | tf_op jit(solution)/shard_map/ppermute | solution.py:30
  190.0 20.8 %collective-permute-start.30 = (f32[256,128]{1,0:T(8,128)S(1)}, f32[256,128]{1,0:T(8,128)S(1)}, u32[]{:S(2)}, u32[]{:S(2)}) collective-permute-start(f32[256,128]{1,0:T(8,128)S(1)} %get-tuple-element.85), channel_id=1, source_target_pairs={{0,11},{1,12},{2,13},{3,14},{4,15},{5,0},{6,1},{7,2},{8,3},{9,4},{... | collective-permute-start | bytes 393224 | tf_op jit(solution)/shard_map/ppermute | solution.py:30
  190.0 20.8 %collective-permute-start.31 = (f32[256,128]{1,0:T(8,128)S(1)}, f32[256,128]{1,0:T(8,128)S(1)}, u32[]{:S(2)}, u32[]{:S(2)}) collective-permute-start(f32[256,128]{1,0:T(8,128)S(1)} %get-tuple-element.86), channel_id=1, source_target_pairs={{0,12},{1,13},{2,14},{3,15},{4,0},{5,1},{6,2},{7,3},{8,4},{9,5},{1... | collective-permute-start | bytes 393224 | tf_op jit(solution)/shard_map/ppermute | solution.py:30
  191.8 11.7 %collective-permute-start.27 = (f32[128,128]{1,0:T(8,128)S(1)}, f32[128,128]{1,0:T(8,128)S(1)}, u32[]{:S(2)}, u32[]{:S(2)}) collective-permute-start(f32[128,128]{1,0:T(8,128)S(1)} %get-tuple-element.81.refs_29_), channel_id=1, source_target_pairs={{0,7},{1,8},{2,9},{3,10},{4,11},{5,12},{6,13},{7,14},{8,15},{9,0},... | collective-permute-start | bytes 196616 | tf_op jit(solution)/shard_map/ppermute | solution.py:30
  203.5 9.5 %collective-permute-start.32 = (f32[256,128]{1,0:T(8,128)S(1)}, f32[256,128]{1,0:T(8,128)S(1)}, u32[]{:S(2)}, u32[]{:S(2)}) collective-permute-start(f32[256,128]{1,0:T(8,128)S(1)} %get-tuple-element.87), channel_id=1, source_target_pairs={{0,13},{1,14},{2,15},{3,0},{4,1},{5,2},{6,3},{7,4},{8,5},{9,6},{10... | collective-permute-start | bytes 393224 | tf_op jit(solution)/shard_map/ppermute | solution.py:30
  204.7 13.0 %collective-permute-start.33 = (f32[256,128]{1,0:T(8,128)S(1)}, f32[256,128]{1,0:T(8,128)S(1)}, u32[]{:S(2)}, u32[]{:S(2)}) collective-permute-start(f32[256,128]{1,0:T(8,128)S(1)} %get-tuple-element.88), channel_id=1, source_target_pairs={{0,14},{1,15},{2,0},{3,1},{4,2},{5,3},{6,4},{7,5},{8,6},{9,7},{10,... | collective-permute-start | bytes 393224 | tf_op jit(solution)/shard_map/ppermute | solution.py:30
  207.5 12.7 %collective-permute-start.34 = (f32[256,128]{1,0:T(8,128)S(1)}, f32[256,128]{1,0:T(8,128)S(1)}, u32[]{:S(2)}, u32[]{:S(2)}) collective-permute-start(f32[256,128]{1,0:T(8,128)S(1)} %get-tuple-element.89), channel_id=1, source_target_pairs={{0,15},{1,0},{2,1},{3,2},{4,3},{5,4},{6,5},{7,6},{8,7},{9,8},{10,9... | collective-permute-start | bytes 393224 | tf_op jit(solution)/shard_map/ppermute | solution.py:30
  210.9 10.9 %collective-permute-start.35 = (f32[256,128]{1,0:T(8,128)S(1)}, f32[256,128]{1,0:T(8,128)S(1)}, u32[]{:S(2)}, u32[]{:S(2)}) collective-permute-start(f32[256,128]{1,0:T(8,128)S(1)} %get-tuple-element.91), channel_id=1, source_target_pairs={{0,1},{1,2},{2,3},{3,4},{4,5},{5,6},{6,7},{7,8},{8,9},{9,10},{10,1... | collective-permute-start | bytes 393224 | tf_op jit(solution)/shard_map/ppermute | solution.py:30
  210.9 14.5 %collective-permute-start.36 = (f32[256,128]{1,0:T(8,128)S(1)}, f32[256,128]{1,0:T(8,128)S(1)}, u32[]{:S(2)}, u32[]{:S(2)}) collective-permute-start(f32[256,128]{1,0:T(8,128)S(1)} %get-tuple-element.92), channel_id=1, source_target_pairs={{0,2},{1,3},{2,4},{3,5},{4,6},{5,7},{6,8},{7,9},{8,10},{9,11},{10,... | collective-permute-start | bytes 393224 | tf_op jit(solution)/shard_map/ppermute | solution.py:30
  213.1 14.9 %collective-permute-start.37 = (f32[256,128]{1,0:T(8,128)S(1)}, f32[256,128]{1,0:T(8,128)S(1)}, u32[]{:S(2)}, u32[]{:S(2)}) collective-permute-start(f32[256,128]{1,0:T(8,128)S(1)} %get-tuple-element.93), channel_id=1, source_target_pairs={{0,3},{1,4},{2,5},{3,6},{4,7},{5,8},{6,9},{7,10},{8,11},{9,12},{10... | collective-permute-start | bytes 393224 | tf_op jit(solution)/shard_map/ppermute | solution.py:30
  217.7 10.3 %collective-permute-start.38 = (f32[256,128]{1,0:T(8,128)S(1)}, f32[256,128]{1,0:T(8,128)S(1)}, u32[]{:S(2)}, u32[]{:S(2)}) collective-permute-start(f32[256,128]{1,0:T(8,128)S(1)} %get-tuple-element.94), channel_id=1, source_target_pairs={{0,4},{1,5},{2,6},{3,7},{4,8},{5,9},{6,10},{7,11},{8,12},{9,13},{1... | collective-permute-start | bytes 393224 | tf_op jit(solution)/shard_map/ppermute | solution.py:30
  220.2 10.1 %collective-permute-start.39 = (f32[256,128]{1,0:T(8,128)S(1)}, f32[256,128]{1,0:T(8,128)S(1)}, u32[]{:S(2)}, u32[]{:S(2)}) collective-permute-start(f32[256,128]{1,0:T(8,128)S(1)} %get-tuple-element.95), channel_id=1, source_target_pairs={{0,5},{1,6},{2,7},{3,8},{4,9},{5,10},{6,11},{7,12},{8,13},{9,14},{... | collective-permute-start | bytes 393224 | tf_op jit(solution)/shard_map/ppermute | solution.py:30
  221.7 16.2 %collective-permute-start.40 = (f32[256,128]{1,0:T(8,128)S(1)}, f32[256,128]{1,0:T(8,128)S(1)}, u32[]{:S(2)}, u32[]{:S(2)}) collective-permute-start(f32[256,128]{1,0:T(8,128)S(1)} %get-tuple-element.96), channel_id=1, source_target_pairs={{0,6},{1,7},{2,8},{3,9},{4,10},{5,11},{6,12},{7,13},{8,14},{9,15},... | collective-permute-start | bytes 393224 | tf_op jit(solution)/shard_map/ppermute | solution.py:30
  225.4 15.3 %collective-permute-start.41 = (f32[256,128]{1,0:T(8,128)S(1)}, f32[256,128]{1,0:T(8,128)S(1)}, u32[]{:S(2)}, u32[]{:S(2)}) collective-permute-start(f32[256,128]{1,0:T(8,128)S(1)} %get-tuple-element.97), channel_id=1, source_target_pairs={{0,7},{1,8},{2,9},{3,10},{4,11},{5,12},{6,13},{7,14},{8,15},{9,0},... | collective-permute-start | bytes 393224 | tf_op jit(solution)/shard_map/ppermute | solution.py:30
  (6 other events, 338.5 us)
Sparse Core Ops, SparseCore 0:
  9.6 119.8 all-gather.1

commit v7 on v6

v7 whole, which is shorter than its diff:
```python
import functools

import jax
import jax.numpy as jnp
from jax import lax
from jax.experimental import pallas as pl
from jax.experimental.pallas import tpu as pltpu
from jax.sharding import PartitionSpec as P

REACH = 7
NOTE = 8
SMEM = pl.BlockSpec(memory_space=pltpu.SMEM)
ANY = pl.BlockSpec(memory_space=pl.ANY)


def permute(x, target):
    devices = lax.axis_size("row")
    return lax.ppermute(x, "row", [(i, target(i)) for i in range(devices)])


def after(x, *others):
    return lax.optimization_barrier((x, *others))[0]


RING = (0, 2, 4, 6, 7, 5, 3, 1)


def along_ring(device, by):
    return 2 * RING[(RING.index(device // 2) + by) % len(RING)] + device % 2


def window_rows(me, total):
    if total != 16:
        steps = [0] + [by for hop in range(1, REACH + 1) for by in (-hop, hop)]
        return jnp.mod(me + jnp.array(steps, jnp.int32), total), (5, 4, 4, 2)
    order = (0, -1, 1, -2, 2, -3, 3, 4)
    table = [[along_ring(i, by) ^ core for by in order for core in (0, 1)] for i in range(total)]
    return jnp.array(table, jnp.int32)[me], (6, 4, 4, 2)


def gathered_rows(x, me, total, beside):
    if total != 16:
        rows = [x]
        for hop in range(1, REACH + 1):
            for by in (hop, -hop):
                rows.append(permute(x, lambda i, by=by: (i + by) % total))
        for start, end in ((0, 5), (5, 9), (9, 13), (13, 15)):
            yield rows[start:end]
        return

    def other_core(row):
        return permute(row, lambda i: i ^ 1)

    def round_of(ahead, behind):
        ahead = permute(ahead, lambda i: along_ring(i, 1))
        behind = permute(behind, lambda i: along_ring(i, -1))
        return ahead, behind, [ahead, other_core(ahead), behind, other_core(behind)]

    rows = [x, other_core(x)]
    ahead, behind, first = round_of(x, x)
    ahead, behind, second = round_of(ahead, behind)
    yield rows + first
    beside = (beside, rows[1], first[1], first[3])
    ahead, behind, third = round_of(after(ahead, *beside), after(behind, *beside))
    made = yield second
    ahead, behind = after(ahead, made), after(behind, made)
    far = permute(jnp.where(me % 2 == 0, ahead, behind), lambda i: along_ring(i, 1 if i % 2 == 0 else -1))
    made = yield third
    far = after(far, made)
    yield [far, other_core(far)]


def place_of(offset, dropped):
    named = jnp.logical_and(offset <= 2 * REACH, offset != dropped)
    slot = offset - jnp.where(offset > dropped, 1, 0)
    return jnp.clip(slot, 0, 2 * REACH - 1), named


def dropped_offset(cols, row, total):
    offsets = jnp.mod(cols - row + REACH, total)
    return REACH * (2 * REACH + 1) - jnp.sum(offsets, axis=1)


def pack_kernel(total, info_ref, cols_ref, cur_ref, prev_ref, send_ref, cur, prev, zeros, note, sems):
    row = info_ref[0]
    drop = info_ref[2]
    count, size = cur.shape[:2]
    loads = (
        pltpu.make_async_copy(cur_ref, cur, sems.at[0]),
        pltpu.make_async_copy(prev_ref, prev, sems.at[1]),
    )
    for load in loads:
        load.start()
    zeros[...] = jnp.zeros_like(zeros)
    line = lax.broadcasted_iota(jnp.int32, note.shape, 0)
    note[...] = jnp.where(line == 0, info_ref[1], drop).astype(jnp.float32)

    def fill(j, carry):
        offset = lax.rem(j - row + REACH + total, total)
        _, named = place_of(offset, drop)
        pltpu.make_async_copy(note, send_ref.at[j, pl.ds(2 * size, NOTE)], sems.at[2]).start()

        @pl.when(jnp.logical_not(named))
        def _():
            pltpu.make_async_copy(zeros, send_ref.at[j, pl.ds(0, 2 * size)], sems.at[2]).start()

        return carry

    lax.fori_loop(0, total, fill, 0)
    for which, held in enumerate((cur, prev)):
        loads[which].wait()
        for k in range(count):
            place = send_ref.at[cols_ref[k], pl.ds(which * size, size)]
            pltpu.make_async_copy(held.at[k], place, sems.at[2]).start()
    pltpu.make_async_copy(send_ref, send_ref, sems.at[2]).wait()


def split(x):
    high = x.astype(jnp.bfloat16)
    low = (x - high.astype(jnp.float32)).astype(jnp.bfloat16)
    return high, low


def kept_rows(total, rows_ref, drops_ref, w):
    row = rows_ref[w]
    offset = lax.rem(rows_ref[rows_ref.shape[0] - 1] - row + REACH + total, total)
    _, named = place_of(offset, drops_ref[2 * row + 1])
    return named


def fill_pair(pair, block, w):
    size = block.shape[-1]
    high, low = split(block)
    at = pl.ds(pl.multiple_of(w * size, size), size)
    pair[at, pl.ds(0, size)] = high
    pair[at, pl.ds(size, size)] = low


def products_of(rows, pair):
    group, double = rows.shape[:2]
    size = double // 2
    products = jnp.dot(rows.reshape(group * double, rows.shape[2]), pair, preferred_element_type=jnp.float32)
    for r in range(group):
        parts = products[r * double:r * double + size] + products[r * double + size:(r + 1) * double]
        yield parts[:, :size] + parts[:, size:]


def first_kernel(total, window, start, count, group, drops_ref, rows_ref, t_ref, *refs):
    h_refs = refs[:count]
    if start:
        pair_in, _ = refs[count:count + 2]
        dense_ref, out_ref = refs[count + 2:count + 4]
    else:
        dense_ref, out_ref, pair_out, blocks = refs[count:count + 4]
    stage, dense, prev, pair, h_sem, t_sem, prev_sem, pair_sem, dense_sem, out_sem = refs[-10:]
    size = t_ref.shape[-1]
    kept = functools.partial(kept_rows, total, rows_ref, drops_ref)

    if start:
        pltpu.make_async_copy(pair_in, pair, pair_sem).start()
    else:
        for w in range(window):
            pltpu.make_async_copy(t_ref.at[rows_ref[w], pl.ds(0, size)], blocks.at[w], t_sem).start()
    for r in range(count):
        pltpu.make_async_copy(h_refs[r], stage.at[r], h_sem.at[r]).start()
    for r in range(count):
        block = t_ref.at[rows_ref[start + r], pl.ds(size, size)]
        pltpu.make_async_copy(block, prev.at[r], prev_sem).start()
    if not start:
        pltpu.make_async_copy(blocks, blocks, t_sem).wait()
        for w in range(window):
            fill_pair(pair, jnp.where(kept(w), blocks[w], 0.0), w)
        pltpu.make_async_copy(pair, pair_out, pair_sem).start()

    def densify(r, slot, place):
        row = rows_ref[start + r]
        drop = drops_ref[2 * row]
        for p in range(window):
            offset = lax.rem(rows_ref[p] - row + REACH + total, total)
            k, named = place_of(offset, drop)
            high, low = split(jnp.where(named, stage[r, k], 0.0))
            dense[slot, place, pl.ds(0, size), pl.ds(p * size, size)] = high
            dense[slot, place, pl.ds(size, size), pl.ds(p * size, size)] = low

    def store(g, slot):
        return pltpu.make_async_copy(dense.at[slot], dense_ref.at[pl.ds(g * group, group)], dense_sem.at[slot])

    groups = count // group

    def one(g, carry):
        slot = lax.rem(g, 2)

        @pl.when(g >= 2)
        def _():
            store(g - 2, slot).wait()

        for place in range(group):
            r = g * group + place
            pltpu.make_async_copy(stage.at[r], stage.at[r], h_sem.at[r]).wait()
            densify(r, slot, place)
        store(g, slot).start()
        if start:

            @pl.when(g == 0)
            def _():
                pltpu.make_async_copy(pair, pair, pair_sem).wait()

        @pl.when(g == 0)
        def _():
            pltpu.make_async_copy(prev, prev, prev_sem).wait()

        for place, product in enumerate(products_of(dense[slot], pair[...])):
            r = g * group + place
            prev[r] = jnp.where(kept(start + r), 2.0 * product - prev[r], 0.0)
            pltpu.make_async_copy(prev.at[r], out_ref.at[rows_ref[start + r]], out_sem).start()
        return carry

    lax.fori_loop(0, groups, one, 0)
    for g in range(max(groups - 2, 0), groups):
        store(g, g % 2).wait()
    if not start:
        pltpu.make_async_copy(pair, pair, pair_sem).wait()
    pltpu.make_async_copy(prev, prev, out_sem).wait()


def later_kernel(total, window, group, parts, drops_ref, rows_ref, *refs):
    dense_refs = refs[:len(parts)]
    t_ref, first_ref, out_ref, dense, terms, pairs, dense_sem, t_sem, first_sem, out_sem = refs[len(parts):]
    size = terms.shape[-1]
    groups = window // group
    kept = functools.partial(kept_rows, total, rows_ref, drops_ref)
    for w in range(window):
        pltpu.make_async_copy(first_ref.at[rows_ref[w]], terms.at[w, 1], first_sem).start()
    start = 0
    for part, dense_ref in zip(parts, dense_refs):
        for w in range(start, start + part):
            pltpu.make_async_copy(dense_ref.at[w - start], dense.at[w], dense_sem.at[w // group]).start()
        start += part
    for w in range(window):
        pltpu.make_async_copy(t_ref.at[rows_ref[w], pl.ds(0, size)], terms.at[w, 0], t_sem).start()
    pltpu.make_async_copy(terms.at[:, 1], terms.at[:, 1], first_sem).wait()
    for w in range(window):
        fill_pair(pairs.at[0], terms[w, 1], w)
    pltpu.make_async_copy(terms.at[:, 0], terms.at[:, 0], t_sem).wait()

    def one(g, carry, step):
        rows = dense.at[pl.ds(g * group, group)]
        if step == 0:
            pltpu.make_async_copy(rows, rows, dense_sem.at[g]).wait()
        for r, product in enumerate(products_of(rows[...], pairs[step])):
            w = g * group + r
            newest = jnp.where(kept(w), 2.0 * product - terms[w, step], 0.0)
            terms[w, step] = newest
            if step == 0:
                fill_pair(pairs.at[1], newest, w)
            pltpu.make_async_copy(terms.at[w, step], out_ref.at[rows_ref[w], step], out_sem).start()
        return carry

    for step in range(2):
        lax.fori_loop(0, groups, functools.partial(one, step=step), 0)
    pltpu.make_async_copy(terms, terms, out_sem).wait()


def unpack_first_kernel(cols_ref, coefs_ref, first_ref, density_ref, out_ref, sums, one, sems):
    load = pltpu.make_async_copy(density_ref, sums, sems.at[0])
    load.start()
    for k in range(cols_ref.shape[0]):
        pltpu.make_async_copy(first_ref.at[cols_ref[k]], one.at[k], sems.at[1]).start()
    load.wait()
    pltpu.make_async_copy(one, one, sems.at[1]).wait()
    sums[...] += coefs_ref[0] * one[...]
    store = pltpu.make_async_copy(sums, out_ref, sems.at[0])
    store.start()
    store.wait()


def unpack_last_kernel(cols_ref, coefs_ref, held_ref, sum_ref, density_ref, last_ref, before_ref, sums, two, three, sems):
    load = pltpu.make_async_copy(sum_ref, sums, sems.at[0])
    load.start()
    for place, sem, which in ((two, 1, 0), (three, 2, 1)):
        for k in range(cols_ref.shape[0]):
            pltpu.make_async_copy(held_ref.at[cols_ref[k], which], place.at[k], sems.at[sem]).start()
    pltpu.make_async_copy(two, two, sems.at[1]).wait()
    before = pltpu.make_async_copy(two, before_ref, sems.at[1])
    before.start()
    pltpu.make_async_copy(three, three, sems.at[2]).wait()
    last = pltpu.make_async_copy(three, last_ref, sems.at[2])
    last.start()
    load.wait()
    sums[...] = sums[...] + coefs_ref[1] * two[...] + coefs_ref[2] * three[...]
    store = pltpu.make_async_copy(sums, density_ref, sems.at[0])
    store.start()
    before.wait()
    last.wait()
    store.wait()


def per_device(h_blocks, h_cols, term_prev, term_cur, t_cols, density_in, coefs):
    total = lax.axis_size("row")
    me = lax.axis_index("row")
    count, size = h_blocks.shape[1:3]
    drop_h = dropped_offset(h_cols, me, total)
    drop_t = dropped_offset(t_cols, me, total)
    f32, bf16 = jnp.float32, jnp.bfloat16
    dma = pltpu.SemaphoreType.DMA
    row = jax.ShapeDtypeStruct((count, size, size), f32)
    row_scratch = pltpu.VMEM(row.shape, f32)

    def call(kernel, smem, arrays, outs, scratch, name, megabytes, aliases={}):
        return pl.pallas_call(
            kernel,
            out_shape=outs,
            in_specs=[SMEM] * len(smem) + [ANY] * len(arrays),
            out_specs=[ANY] * len(outs),
            scratch_shapes=scratch,
            input_output_aliases=aliases,
            compiler_params=pltpu.CompilerParams(vmem_limit_bytes=megabytes * 1024 * 1024),
            name=name,
        )(*smem, *arrays)

    def exchange(x):
        return lax.all_to_all(x, "row", 0, 0, tiled=True)

    (send,) = call(
        functools.partial(pack_kernel, total),
        [jnp.stack([me, drop_h[0], drop_t[0]]), t_cols[0]],
        [term_cur[0], term_prev[0]],
        [jax.ShapeDtypeStruct((total, 2 * size + NOTE, size), f32)],
        [
            row_scratch,
            row_scratch,
            pltpu.VMEM((2 * size, size), f32),
            pltpu.VMEM((NOTE, size), f32),
            dma((3,)),
        ],
        "pack",
        12,
    )
    column = exchange(send)
    drops = column[:, 2 * size:2 * size + 2, 0].astype(jnp.int32).reshape(-1)
    indices, parts = window_rows(me, total)
    gathered = gathered_rows(h_blocks[0], me, total, column)
    rows = jnp.concatenate([indices, me[None]])
    window = sum(parts)
    dense_shape = (window, 2 * size, window * size)
    pair_shape = (window * size, 2 * size)
    dense = []
    start = 0
    for part in parts:
        h_rows = gathered.send(dense[-1] if start else None)
        group = max(g for g in (2, 3, 4, 5) if part % g == 0)
        scratch = [
            pltpu.VMEM((part, count, size, size), f32),
            pltpu.VMEM((2, group) + dense_shape[1:], bf16),
            pltpu.VMEM((part, size, size), f32),
            pltpu.VMEM(pair_shape, bf16),
            dma((part,)),
            dma,
            dma,
            dma,
            dma((2,)),
            dma,
        ]
        if not start:
            scratch = [pltpu.VMEM((window, size, size), f32)] + scratch
        result = call(
            functools.partial(first_kernel, total, window, start, part, group),
            [drops, rows],
            [column, *h_rows] + ([pair, term1] if start else []),
            [
                jax.ShapeDtypeStruct((part,) + dense_shape[1:], bf16),
                jax.ShapeDtypeStruct((total, size, size), f32),
            ] + ([] if start else [jax.ShapeDtypeStruct(pair_shape, bf16)]),
            scratch,
            "first",
            29,
            {part + 4: 1} if start else {},
        )
        dense.append(result[0])
        term1 = result[1]
        if not start:
            pair = result[2]
        start += part
    back1 = exchange(term1)
    group = max(g for g in (3, 4) if window % g == 0)
    (terms,) = call(
        functools.partial(later_kernel, total, window, group, parts),
        [drops, rows],
        [*dense, column, term1],
        [jax.ShapeDtypeStruct((total, 2, size, size), f32)],
        [
            pltpu.VMEM(dense_shape, bf16),
            pltpu.VMEM((window, 2, size, size), f32),
            pltpu.VMEM((2,) + pair_shape, bf16),
            dma((window // group,)),
            dma,
            dma,
            dma,
        ],
        "later",
        28,
    )
    back = exchange(after(terms, back1))
    (sums,) = call(
        unpack_first_kernel,
        [t_cols[0], coefs],
        [back1, density_in[0]],
        [row],
        [row_scratch, row_scratch, dma((2,))],
        "unpack_first",
        12,
    )
    density, last, before = call(
        unpack_last_kernel,
        [t_cols[0], coefs],
        [back, sums],
        [row] * 3,
        [row_scratch, row_scratch, row_scratch, dma((3,))],
        "unpack_last",
        12,
    )
    return density[None], last[None], before[None]


def solution(mesh):
    blocks = P(("groups", "row"), None, None, None)
    cols = P(("groups", "row"), None)
    return jax.shard_map(
        per_device,
        mesh=mesh,
        in_specs=(blocks, cols, blocks, blocks, cols, blocks, P()),
        out_specs=(blocks, blocks, blocks),
        check_vma=False,
    )
```

time: 258 us -> 254 us (0.984)
  starting transfers between devices: 83.5 us -> 26.2 us
  waiting for transfers between devices: 102 us -> 135 us
  local copies, waits for them, and re-layouts: 5.53 us -> 37.1 us
  between operations: 15.6 us -> 2.15 us
  Pallas kernels: 44.8 us -> 48.8 us
    ppermute x42 -> x15, starting transfers between devices: 83.5 us -> 8.64 us  [permute(): return lax.ppermute(x, 'row', [(i, target(i)) for i in range(devices)])]
    all_to_all x0 -> x3, waiting for transfers between devices: none -> 42.6 us  [exchange(): return lax.all_to_all(x, 'row', 0, 0, tiled=True)]
    all_gather x1 -> x0, waiting for transfers between devices: 37.9 us -> none  [per_device(): lax.all_gather(h_blocks, 'row', axis=0, tiled=True, axis_index_groups=[cy...]
    unnamed x22 -> x60, local copies, waits for them, and re-layouts: 2.4 us -> 36.3 us
    ppermute x42 -> x15, waiting for transfers between devices: 63.3 us -> 92 us  [permute(): return lax.ppermute(x, 'row', [(i, target(i)) for i in range(devices)])]
    all_to_all x0 -> x3, starting transfers between devices: none -> 17.5 us  [exchange(): return lax.all_to_all(x, 'row', 0, 0, tiled=True)]
    pallas_call x5 -> x8, Pallas kernels: 44.8 us -> 48.8 us  [call(): pl.pallas_call(kernel, out_shape=outs, in_specs=[SMEM] * len(smem) + [ANY...]
  transfers between devices with their start and end apart: 43 -> 18, of which waited for: 14 -> 8; matrix products, arithmetic and copies ran while one was open for 2% -> 1% of each run, Pallas kernels for 10% -> 15%
where the time goes in v7:
time: 254 us; the launch traced here: 251 us
  waiting for transfers between devices  135 us (53%)
  Pallas kernels  48.8 us (19%)
  local copies, waits for them, and re-layouts  37.1 us (15%)
  starting transfers between devices  26.2 us (10%)
    ppermute x15, waiting for transfers between devices, permute(): return lax.ppermute(x, 'row', [(i, target(i)) for i in range(devices)])  92 us
    pallas_call x8, Pallas kernels, call(): pl.pallas_call(kernel, out_shape=outs, in_specs=[SMEM] * len(smem) + [ANY...  48.8 us
    all_to_all x3, waiting for transfers between devices, exchange(): return lax.all_to_all(x, 'row', 0, 0, tiled=True)  42.6 us
    unnamed x60, local copies, waits for them, and re-layouts  36.3 us
    all_to_all x3, starting transfers between devices, exchange(): return lax.all_to_all(x, 'row', 0, 0, tiled=True)  17.5 us
    ppermute x15, starting transfers between devices, permute(): return lax.ppermute(x, 'row', [(i, target(i)) for i in range(devices)])  8.64 us
  transfers between devices with their start and end apart: 18, of which 8 were waited for; matrix products, arithmetic and copies ran while one was open for 1% of the time, Pallas kernels for 15%

profile of v7, /device:TPU:22, one launch (start us, length us, event | category | flops | bytes accessed | tf_op | source)
XLA Modules:
  0.0 250.8 jit_solution(3725770766502026543)
XLA Ops:
  0.6 1.3 fusion.1
  3.3 1.2 copy-done.12
  4.5 1.2 copy-done.13
  6.3 4.1 %pack.1 = f32[16,264,128]{2,1,0:T(8,128)S(1)} custom-call(s32[3]{0:T(128)S(1)} %pad_add_fusion.info_ref, s32[14]{0:T(128)S(1)} %bitcast.20, f32[14,128,128]{2,1,0:T(8,128)S(1)} %bitcast.13, f32[14,128,128]{2,1,0:T(8,128)S(1)} %bitcast.14), custom_call_target="tpu_custom_call" | custom-call | tf_op jit(solution)/shard_map/pack/pallas_call | solution.py:310
  10.5 1.3 copy-done
  11.8 6.3 %all-to-all-start = ((f32[16,264,128]{2,1,0:T(8,128)}), f32[16,264,128]{2,1,0:T(8,128)S(1)}, u32[]{:S(2)}, u32[]{:S(2)}) async-start(f32[16,264,128]{2,1,0:T(8,128)} %copy-done), calls=%async_computation | async-start | bytes 4325376 | tf_op jit(solution)/shard_map/all_to_all | solution.py:322
  18.7 1.5 collective-permute-start.3
  20.2 64.9 %collective-permute-done.1.refs_2_ = f32[14,128,128]{2,1,0:T(8,128)S(1)} collective-permute-done((f32[14,128,128]{2,1,0:T(8,128)S(1)}, f32[14,128,128]{2,1,0:T(8,128)S(1)}, u32[]{:S(2)}, u32[]{:S(2)}) %collective-permute-start.1) | collective-permute-done | bytes 917536 | tf_op jit(solution)/shard_map/ppermute | solution.py:18
  85.1 2.5 collective-permute-start.5
  88.1 0.9 copy-done.17
  89.1 0.9 copy-done.19
  90.0 17.1 %collective-permute-done.5.refs_0_ = f32[14,128,128]{2,1,0:T(8,128)} collective-permute-done((f32[14,128,128]{2,1,0:T(8,128)S(1)}, f32[14,128,128]{2,1,0:T(8,128)}, u32[]{:S(2)}, u32[]{:S(2)}) %collective-permute-start.5) | collective-permute-done | bytes 917536 | tf_op jit(solution)/shard_map/ppermute | solution.py:18
  107.1 2.2 collective-permute-done.7.refs_2_
  109.3 0.9 copy-done.21
  110.2 0.9 copy-done.23
  111.2 0.9 copy-done.25
  112.9 1.2 collective-permute-start.11
  115.3 1.2 copy-done.15
  116.5 1.2 copy-done.18
  117.7 1.2 copy-done.20
  118.9 1.2 copy-done.22
  120.1 1.2 copy-done.24
  121.2 1.2 copy-done.26
  122.4 8.8 %first.4 = (bf16[6,256,2048]{2,1,0:T(8,128)(2,1)S(1)}, f32[16,128,128]{2,1,0:T(8,128)}, bf16[2048,256]{1,0:T(8,128)(2,1)S(1)}) custom-call(s32[32]{0:T(128)S(1)} %convert_element_type.8.drops_ref, s32[17]{0:T(128)S(1)} %pad_add_fusion.1.rows_ref, f32[16,264,128]{2,1,0:T(8,128)S(1)} %all-to-all-done.t_ref.refs_4_, f32[14,128,128]{2,1,0:T(8,128)S(1)} %bitcast.18, ...), custom_call_target="tpu_custom_call" | custom-call | tf_op jit(solution)/shard_map/first/pallas_call | solution.py:310
  131.2 2.7 %copy-done.2 = bf16[6,256,2048]{2,1,0:T(8,128)(2,1)} copy-done((bf16[6,256,2048]{2,1,0:T(8,128)(2,1)}, bf16[6,256,2048]{2,1,0:T(8,128)(2,1)S(1)}, u32[]{:S(2)}) %copy-start.2) | copy-done | bytes 6291480
  133.9 5.2 %first.5 = (bf16[4,256,2048]{2,1,0:T(8,128)(2,1)S(1)}, f32[16,128,128]{2,1,0:T(8,128)}) custom-call(s32[32]{0:T(128)S(1)} %convert_element_type.8.drops_ref, s32[17]{0:T(128)S(1)} %pad_add_fusion.1.rows_ref, f32[16,264,128]{2,1,0:T(8,128)S(1)} %all-to-all-done.t_ref.refs_4_, ...), custom_call_target="tpu_custom_call", output_to_operand_aliasing={{1}: (8, {})} | custom-call | tf_op jit(solution)/shard_map/first/pallas_call | solution.py:310
  139.1 2.0 copy-done.4
  142.6 1.6 collective-permute-done.10.refs_1_
  144.2 0.9 collective-permute-done.12.refs_3_
  145.1 5.0 %first.6 = (bf16[4,256,2048]{2,1,0:T(8,128)(2,1)S(1)}, f32[16,128,128]{2,1,0:T(8,128)}) custom-call(s32[32]{0:T(128)S(1)} %convert_element_type.8.drops_ref, s32[17]{0:T(128)S(1)} %pad_add_fusion.1.rows_ref, f32[16,264,128]{2,1,0:T(8,128)S(1)} %all-to-all-done.t_ref.refs_4_, ...), custom_call_target="tpu_custom_call", output_to_operand_aliasing={{1}: (8, {})} | custom-call | tf_op jit(solution)/shard_map/first/pallas_call | solution.py:310
  150.2 2.1 copy-done.6
  152.2 3.0 %collective-permute-done.13.refs_0_ = f32[14,128,128]{2,1,0:T(8,128)S(1)} collective-permute-done((f32[14,128,128]{2,1,0:T(8,128)S(1)}, f32[14,128,128]{2,1,0:T(8,128)S(1)}, u32[]{:S(2)}, u32[]{:S(2)}) %collective-permute-start.13) | collective-permute-done | bytes 917536 | tf_op jit(solution)/shard_map/ppermute | solution.py:18
  155.3 2.4 collective-permute-done.14.refs_1_
  157.7 3.3 %first.7 = (bf16[2,256,2048]{2,1,0:T(8,128)(2,1)S(1)}, f32[16,128,128]{2,1,0:T(8,128)}) custom-call(s32[32]{0:T(128)S(1)} %convert_element_type.8.drops_ref, s32[17]{0:T(128)S(1)} %pad_add_fusion.1.rows_ref, f32[16,264,128]{2,1,0:T(8,128)S(1)} %all-to-all-done.t_ref.refs_4_, ...), custom_call_target="tpu_custom_call", output_to_operand_aliasing={{1}: (6, {})} | custom-call | tf_op jit(solution)/shard_map/first/pallas_call | solution.py:310
  161.0 1.3 copy-done.10
  162.3 5.1 %all-to-all-start.1 = ((f32[16,128,128]{2,1,0:T(8,128)}), f32[16,128,128]{2,1,0:T(8,128)S(1)}, u32[]{:S(2)}, u32[]{:S(2)}) async-start(f32[16,128,128]{2,1,0:T(8,128)} %get-tuple-element.34.refs_5_), calls=%async_computation.1 | async-start | bytes 2097152 | tf_op jit(solution)/shard_map/all_to_all | solution.py:322
  167.4 2.8 %copy-done.3 = bf16[6,256,2048]{2,1,0:T(8,128)(2,1)S(1)} copy-done((bf16[6,256,2048]{2,1,0:T(8,128)(2,1)S(1)}, bf16[6,256,2048]{2,1,0:T(8,128)(2,1)}, u32[]{:S(2)}) %copy-start.3) | copy-done | bytes 6291480
  170.2 2.2 copy-done.5
  172.4 2.2 copy-done.7
  174.6 1.6 copy-done.11
  176.2 16.5 %later.1 = f32[16,2,128,128]{3,2,1,0:T(8,128)S(1)} custom-call(s32[32]{0:T(128)S(1)} %convert_element_type.8.drops_ref, s32[17]{0:T(128)S(1)} %pad_add_fusion.1.rows_ref, bf16[6,256,2048]{2,1,0:T(8,128)(2,1)S(1)} %copy-done.3, bf16[4,256,2048]{2,1,0:T(8,128)(2,1)S(1)} %copy-done.5, bf16[4,256,2048]{2,1,0:T(8,128)(2,1)S(1)} %copy-done.7, ...), custom_call_target="tpu_custom_call" | custom-call | tf_op jit(solution)/shard_map/later/pallas_call | solution.py:310
  192.7 1.3 copy-done.1
  194.1 6.2 %all-to-all-start.2 = ((f32[16,2,128,128]{3,2,1,0:T(8,128)}), f32[16,2,128,128]{3,2,1,0:T(8,128)}, u32[]{:S(2)}, u32[]{:S(2)}) async-start(f32[16,2,128,128]{3,2,1,0:T(8,128)} %copy-done.1), calls=%async_computation.2 | async-start | bytes 4194304 | tf_op jit(solution)/shard_map/all_to_all | solution.py:322
  200.2 2.3 unpack_first.1.sum_ref
  202.6 0.9 copy-done.8
  203.5 42.6 %all-to-all-done.2.held_ref = f32[16,2,128,128]{3,2,1,0:T(8,128)} async-done(((f32[16,2,128,128]{3,2,1,0:T(8,128)}), f32[16,2,128,128]{3,2,1,0:T(8,128)}, u32[]{:S(2)}, u32[]{:S(2)}) %all-to-all-start.2) | async-done | bytes 2097184 | tf_op jit(solution)/shard_map/all_to_all | solution.py:322
  246.1 1.2 copy-done.9
  247.3 3.5 %unpack_last.1 = (f32[14,128,128]{2,1,0:T(8,128)}, f32[14,128,128]{2,1,0:T(8,128)}, f32[14,128,128]{2,1,0:T(8,128)}) custom-call(s32[14]{0:T(128)S(1)} %bitcast.22, f32[3]{0:T(128)S(1)} %copy-done.29, f32[16,2,128,128]{3,2,1,0:T(8,128)} %all-to-all-done.2.held_ref, f32[14,128,128]{2,1,0:T(8,128)S(1)} %copy-done.9), custom_call_target="tpu_custom_call" | custom-call | tf_op jit(solution)/shard_map/unpack_last/pallas_call | solution.py:310
  (63 shorter events, 5.6 us)
Async XLA Ops:
  3.3 1.2 copy-start.12
  4.5 1.2 copy-start.13
  5.7 0.7 copy-start.27
  10.5 1.4 copy-start
  11.8 6.3 %copy-start.14 = (f32[1,14,128,128]{3,2,1,0:T(8,128)S(1)}, f32[1,14,128,128]{3,2,1,0:T(8,128)}, u32[]{:S(2)}) copy-start(f32[1,14,128,128]{3,2,1,0:T(8,128)} %param.8) | copy-start | bytes 2752516
  11.8 100.2 %all-to-all-start = ((f32[16,264,128]{2,1,0:T(8,128)}), f32[16,264,128]{2,1,0:T(8,128)S(1)}, u32[]{:S(2)}, u32[]{:S(2)}) async-start(f32[16,264,128]{2,1,0:T(8,128)} %copy-done), calls=%async_computation | async-start | bytes 4325376 | tf_op jit(solution)/shard_map/all_to_all | solution.py:322
  18.1 67.0 %collective-permute-start.1 = (f32[14,128,128]{2,1,0:T(8,128)S(1)}, f32[14,128,128]{2,1,0:T(8,128)S(1)}, u32[]{:S(2)}, u32[]{:S(2)}) collective-permute-start(f32[14,128,128]{2,1,0:T(8,128)S(1)} %bitcast.15), channel_id=1, source_target_pairs={{0,4},{1,5},{2,0},{3,1},{4,8},{5,9},{6,2},{7,3},{8,12},{9,13},{10,... | collective-permute-start | bytes 2752520 | tf_op jit(solution)/shard_map/ppermute | solution.py:18
  18.7 68.8 %collective-permute-start.3 = (f32[14,128,128]{2,1,0:T(8,128)S(1)}, f32[14,128,128]{2,1,0:T(8,128)S(1)}, u32[]{:S(2)}, u32[]{:S(2)}) collective-permute-start(f32[14,128,128]{2,1,0:T(8,128)S(1)} %bitcast.16), channel_id=1, source_target_pairs={{0,2},{1,3},{2,6},{3,7},{4,0},{5,1},{6,10},{7,11},{8,4},{9,5},{10,... | collective-permute-start | bytes 2752520 | tf_op jit(solution)/shard_map/ppermute | solution.py:18
  85.1 22.0 %collective-permute-start.5 = (f32[14,128,128]{2,1,0:T(8,128)S(1)}, f32[14,128,128]{2,1,0:T(8,128)}, u32[]{:S(2)}, u32[]{:S(2)}) collective-permute-start(f32[14,128,128]{2,1,0:T(8,128)S(1)} %collective-permute-done.1.refs_2_), channel_id=1, source_target_pairs={{0,4},{1,5},{2,0},{3,1},{4,8},{5,9},{6,2},{7,3},{8,12},{9,13},{10,... | collective-permute-start | bytes 2752520 | tf_op jit(solution)/shard_map/ppermute | solution.py:18
  87.6 21.7 %collective-permute-start.7 = (f32[14,128,128]{2,1,0:T(8,128)S(1)}, f32[14,128,128]{2,1,0:T(8,128)}, u32[]{:S(2)}, u32[]{:S(2)}) collective-permute-start(f32[14,128,128]{2,1,0:T(8,128)S(1)} %collective-permute-done.3.refs_4_), channel_id=1, source_target_pairs={{0,2},{1,3},{2,6},{3,7},{4,0},{5,1},{6,10},{7,11},{8,4},{9,5},{10,... | collective-permute-start | bytes 2752520 | tf_op jit(solution)/shard_map/ppermute | solution.py:18
  87.6 21.7 %collective-permute-start = (f32[14,128,128]{2,1,0:T(8,128)S(1)}, f32[14,128,128]{2,1,0:T(8,128)S(1)}, u32[]{:S(2)}, u32[]{:S(2)}) collective-permute-start(f32[14,128,128]{2,1,0:T(8,128)S(1)} %bitcast.17), channel_id=1, source_target_pairs={{0,1},{1,0},{2,3},{3,2},{4,5},{5,4},{6,7},{7,6},{8,9},{9,8},{10,11... | collective-permute-start | bytes 2752520 | tf_op jit(solution)/shard_map/ppermute | solution.py:18
  87.6 22.6 %collective-permute-start.2 = (f32[14,128,128]{2,1,0:T(8,128)S(1)}, f32[14,128,128]{2,1,0:T(8,128)S(1)}, u32[]{:S(2)}, u32[]{:S(2)}) collective-permute-start(f32[14,128,128]{2,1,0:T(8,128)S(1)} %collective-permute-done.1.refs_2_), channel_id=1, source_target_pairs={{0,1},{1,0},{2,3},{3,2},{4,5},{5,4},{6,7},{7,6},{8,9},{9,8},{10,11... | collective-permute-start | bytes 2752520 | tf_op jit(solution)/shard_map/ppermute | solution.py:18
  88.1 0.9 copy-start.17
  89.0 22.1 %collective-permute-start.4 = (f32[14,128,128]{2,1,0:T(8,128)S(1)}, f32[14,128,128]{2,1,0:T(8,128)S(1)}, u32[]{:S(2)}, u32[]{:S(2)}) collective-permute-start(f32[14,128,128]{2,1,0:T(8,128)S(1)} %collective-permute-done.3.refs_4_), channel_id=1, source_target_pairs={{0,1},{1,0},{2,3},{3,2},{4,5},{5,4},{6,7},{7,6},{8,9},{9,8},{10,11... | collective-permute-start | bytes 2752520 | tf_op jit(solution)/shard_map/ppermute | solution.py:18
  89.1 0.9 copy-start.19
  107.1 26.8 %collective-permute-start.6 = (f32[14,128,128]{2,1,0:T(8,128)}, f32[14,128,128]{2,1,0:T(8,128)}, u32[]{:S(2)}, u32[]{:S(2)}) collective-permute-start(f32[14,128,128]{2,1,0:T(8,128)} %collective-permute-done.5.refs_0_), channel_id=1, source_target_pairs={{0,1},{1,0},{2,3},{3,2},{4,5},{5,4},{6,7},{7,6},{8,9},{9,8},{10,11... | collective-permute-start | bytes 2752520 | tf_op jit(solution)/shard_map/ppermute | solution.py:18
  109.3 24.6 %collective-permute-start.8 = (f32[14,128,128]{2,1,0:T(8,128)}, f32[14,128,128]{2,1,0:T(8,128)}, u32[]{:S(2)}, u32[]{:S(2)}) collective-permute-start(f32[14,128,128]{2,1,0:T(8,128)} %collective-permute-done.7.refs_2_), channel_id=1, source_target_pairs={{0,1},{1,0},{2,3},{3,2},{4,5},{5,4},{6,7},{7,6},{8,9},{9,8},{10,11... | collective-permute-start | bytes 2752520 | tf_op jit(solution)/shard_map/ppermute | solution.py:18
  109.3 0.9 copy-start.21
  110.2 0.9 copy-start.23
  111.2 0.9 copy-start.25
  112.1 29.0 %collective-permute-start.9 = (f32[14,128,128]{2,1,0:T(8,128)}, f32[14,128,128]{2,1,0:T(8,128)S(1)}, u32[]{:S(2)}, u32[]{:S(2)}) collective-permute-start(f32[14,128,128]{2,1,0:T(8,128)} %collective-permute-done.5.refs_0_), channel_id=1, source_target_pairs={{0,4},{1,5},{2,0},{3,1},{4,8},{5,9},{6,2},{7,3},{8,12},{9,13},{10,... | collective-permute-start | bytes 2752520 | tf_op jit(solution)/shard_map/ppermute | solution.py:18
  112.9 28.3 %collective-permute-start.11 = (f32[14,128,128]{2,1,0:T(8,128)}, f32[14,128,128]{2,1,0:T(8,128)}, u32[]{:S(2)}, u32[]{:S(2)}) collective-permute-start(f32[14,128,128]{2,1,0:T(8,128)} %collective-permute-done.7.refs_2_), channel_id=1, source_target_pairs={{0,2},{1,3},{2,6},{3,7},{4,0},{5,1},{6,10},{7,11},{8,4},{9,5},{10,... | collective-permute-start | bytes 2752520 | tf_op jit(solution)/shard_map/ppermute | solution.py:18
  115.3 1.2 copy-start.15
  116.5 1.2 copy-start.18
  117.7 1.2 copy-start.20
  118.9 1.2 copy-start.22
  120.1 1.2 copy-start.24
  121.2 1.2 copy-start.26
  131.2 2.7 %copy-start.2 = (bf16[6,256,2048]{2,1,0:T(8,128)(2,1)}, bf16[6,256,2048]{2,1,0:T(8,128)(2,1)S(1)}, u32[]{:S(2)}) copy-start(bf16[6,256,2048]{2,1,0:T(8,128)(2,1)S(1)} %get-tuple-element.21.refs_0_) | copy-start | bytes 18874372
  139.1 2.1 copy-start.4
  141.1 3.1 %collective-permute-start.10 = (f32[14,128,128]{2,1,0:T(8,128)S(1)}, f32[14,128,128]{2,1,0:T(8,128)S(1)}, u32[]{:S(2)}, u32[]{:S(2)}) collective-permute-start(f32[14,128,128]{2,1,0:T(8,128)S(1)} %collective-permute-done.9.refs_0_), channel_id=1, source_target_pairs={{0,1},{1,0},{2,3},{3,2},{4,5},{5,4},{6,7},{7,6},{8,9},{9,8},{10,11... | collective-permute-start | bytes 2752520 | tf_op jit(solution)/shard_map/ppermute | solution.py:18
  141.1 4.0 %collective-permute-start.12 = (f32[14,128,128]{2,1,0:T(8,128)}, f32[14,128,128]{2,1,0:T(8,128)S(1)}, u32[]{:S(2)}, u32[]{:S(2)}) collective-permute-start(f32[14,128,128]{2,1,0:T(8,128)} %collective-permute-done.11.refs_2_), channel_id=1, source_target_pairs={{0,1},{1,0},{2,3},{3,2},{4,5},{5,4},{6,7},{7,6},{8,9},{9,8},{10,11... | collective-permute-start | bytes 2752520 | tf_op jit(solution)/shard_map/ppermute | solution.py:18
  141.8 13.4 %collective-permute-start.13 = (f32[14,128,128]{2,1,0:T(8,128)S(1)}, f32[14,128,128]{2,1,0:T(8,128)S(1)}, u32[]{:S(2)}, u32[]{:S(2)}) collective-permute-start(f32[14,128,128]{2,1,0:T(8,128)S(1)} %broadcast_select_fusion), channel_id=1, source_target_pairs={{0,4},{1,3},{2,0},{3,7},{4,8},{5,1},{6,2},{7,11},{8,12},{9,5},{10,... | collective-permute-start | bytes 2752520 | tf_op jit(solution)/shard_map/ppermute | solution.py:18
  150.2 2.1 copy-start.6
  155.2 2.5 collective-permute-start.14
  161.0 1.3 copy-start.10
  162.3 31.8 %all-to-all-start.1 = ((f32[16,128,128]{2,1,0:T(8,128)}), f32[16,128,128]{2,1,0:T(8,128)S(1)}, u32[]{:S(2)}, u32[]{:S(2)}) async-start(f32[16,128,128]{2,1,0:T(8,128)} %get-tuple-element.34.refs_5_), calls=%async_computation.1 | async-start | bytes 2097152 | tf_op jit(solution)/shard_map/all_to_all | solution.py:322
  167.4 2.8 %copy-start.3 = (bf16[6,256,2048]{2,1,0:T(8,128)(2,1)S(1)}, bf16[6,256,2048]{2,1,0:T(8,128)(2,1)}, u32[]{:S(2)}) copy-start(bf16[6,256,2048]{2,1,0:T(8,128)(2,1)} %copy-done.2) | copy-start | bytes 18874372
  170.2 2.2 copy-start.5
  172.4 2.2 copy-start.7
  174.6 1.6 copy-start.11
  192.7 1.3 copy-start.1
  194.0 6.2 %copy-start.16 = (f32[1,14,128,128]{3,2,1,0:T(8,128)S(1)}, f32[1,14,128,128]{3,2,1,0:T(8,128)}, u32[]{:S(2)}) copy-start(f32[1,14,128,128]{3,2,1,0:T(8,128)} %param.13) | copy-start | bytes 2752516
  194.1 6.2 %copy-start.28 = (s32[1,14]{1,0:T(1,128)S(1)}, s32[1,14]{1,0:T(1,128)}, u32[]{:S(2)}) copy-start(s32[1,14]{1,0:T(1,128)} %param.12) | copy-start | bytes 172
  194.1 6.2 %copy-start.29 = (f32[3]{0:T(128)S(1)}, f32[3]{0:T(128)}, u32[]{:S(2)}) copy-start(f32[3]{0:T(128)} %coefs_ref.3) | copy-start | bytes 40
  194.1 52.1 %all-to-all-start.2 = ((f32[16,2,128,128]{3,2,1,0:T(8,128)}), f32[16,2,128,128]{3,2,1,0:T(8,128)}, u32[]{:S(2)}, u32[]{:S(2)}) async-start(f32[16,2,128,128]{3,2,1,0:T(8,128)} %copy-done.1), calls=%async_computation.2 | async-start | bytes 4194304 | tf_op jit(solution)/shard_map/all_to_all | solution.py:322
  202.6 0.9 copy-start.8
  246.1 1.2 copy-start.9

commit v8 on v7

--- a/solution.py
+++ b/solution.py
@@ -9,6 +9,7 @@
 
 REACH = 7
 NOTE = 8
+VMEM_LIMIT = 60 * 1024 * 1024
 SMEM = pl.BlockSpec(memory_space=pltpu.SMEM)
 ANY = pl.BlockSpec(memory_space=pl.ANY)
 
@@ -38,7 +39,7 @@
     return jnp.array(table, jnp.int32)[me], (6, 4, 4, 2)
 
 
-def gathered_rows(x, me, total, beside):
+def gathered_rows(x, me, total):
     if total != 16:
         rows = [x]
         for hop in range(1, REACH + 1):
@@ -60,8 +61,8 @@
     ahead, behind, first = round_of(x, x)
     ahead, behind, second = round_of(ahead, behind)
     yield rows + first
-    beside = (beside, rows[1], first[1], first[3])
-    ahead, behind, third = round_of(after(ahead, *beside), after(behind, *beside))
+    there = (rows[1], first[1], first[3])
+    ahead, behind, third = round_of(after(ahead, *there), after(behind, *there))
     made = yield second
     ahead, behind = after(ahead, made), after(behind, made)
     far = permute(jnp.where(me % 2 == 0, ahead, behind), lambda i: along_ring(i, 1 if i % 2 == 0 else -1))
@@ -306,7 +307,7 @@
     row = jax.ShapeDtypeStruct((count, size, size), f32)
     row_scratch = pltpu.VMEM(row.shape, f32)
 
-    def call(kernel, smem, arrays, outs, scratch, name, megabytes, aliases={}):
+    def call(kernel, smem, arrays, outs, scratch, name, aliases={}):
         return pl.pallas_call(
             kernel,
             out_shape=outs,
@@ -314,7 +315,7 @@
             out_specs=[ANY] * len(outs),
             scratch_shapes=scratch,
             input_output_aliases=aliases,
-            compiler_params=pltpu.CompilerParams(vmem_limit_bytes=megabytes * 1024 * 1024),
+            compiler_params=pltpu.CompilerParams(vmem_limit_bytes=VMEM_LIMIT),
             name=name,
         )(*smem, *arrays)
 
@@ -334,12 +335,11 @@
             dma((3,)),
         ],
         "pack",
-        12,
     )
     column = exchange(send)
     drops = column[:, 2 * size:2 * size + 2, 0].astype(jnp.int32).reshape(-1)
     indices, parts = window_rows(me, total)
-    gathered = gathered_rows(h_blocks[0], me, total, column)
+    gathered = gathered_rows(h_blocks[0], me, total)
     rows = jnp.concatenate([indices, me[None]])
     window = sum(parts)
     dense_shape = (window, 2 * size, window * size)
@@ -373,7 +373,6 @@
             ] + ([] if start else [jax.ShapeDtypeStruct(pair_shape, bf16)]),
             scratch,
             "first",
-            29,
             {part + 4: 1} if start else {},
         )
         dense.append(result[0])
@@ -398,7 +397,6 @@
             dma,
         ],
         "later",
-        28,
     )
     back = exchange(after(terms, back1))
     (sums,) = call(
@@ -408,7 +406,6 @@
         [row],
         [row_scratch, row_scratch, dma((2,))],
         "unpack_first",
-        12,
     )
     density, last, before = call(
         unpack_last_kernel,
@@ -417,7 +414,6 @@
         [row] * 3,
         [row_scratch, row_scratch, row_scratch, dma((3,))],
         "unpack_last",
-        12,
     )
     return density[None], last[None], before[None]
 

time: 254 us -> 252 us (level)
  local copies, waits for them, and re-layouts: 37.1 us -> 3.93 us
  waiting for transfers between devices: 135 us -> 164 us
    unnamed x60 -> x24, local copies, waits for them, and re-layouts: 36.3 us -> 2.27 us
    ppermute x15, waiting for transfers between devices: 92 us -> 115 us  [permute(): return lax.ppermute(x, 'row', [(i, target(i)) for i in range(devices)])]
    all_to_all x3, waiting for transfers between devices: 42.6 us -> 48.4 us  [exchange(): return lax.all_to_all(x, 'row', 0, 0, tiled=True)]
  transfers between devices with their start and end apart: 18 -> 18, of which waited for: 8 -> 10; matrix products, arithmetic and copies ran while one was open for 1% -> 1% of each run, Pallas kernels for 15% -> 16%
where the time goes in v8:
time: 252 us; the launch traced here: 250 us
  waiting for transfers between devices  164 us (65%)
  Pallas kernels  50.8 us (20%)
  starting transfers between devices  26.1 us (10%)
  local copies, waits for them, and re-layouts  3.93 us (2%)
  other arithmetic  2.99 us (1%)
    ppermute x15, waiting for transfers between devices, permute(): return lax.ppermute(x, 'row', [(i, target(i)) for i in range(devices)])  115 us
    pallas_call x8, Pallas kernels, call(): pl.pallas_call(kernel, out_shape=outs, in_specs=[SMEM] * len(smem) + [ANY...  50.8 us
    all_to_all x3, waiting for transfers between devices, exchange(): return lax.all_to_all(x, 'row', 0, 0, tiled=True)  48.4 us
    all_to_all x3, starting transfers between devices, exchange(): return lax.all_to_all(x, 'row', 0, 0, tiled=True)  18.1 us
    ppermute x15, starting transfers between devices, permute(): return lax.ppermute(x, 'row', [(i, target(i)) for i in range(devices)])  7.97 us
  transfers between devices with their start and end apart: 18, of which 10 were waited for; matrix products, arithmetic and copies ran while one was open for 1% of the time, Pallas kernels for 16%

profile of v8, /device:TPU:22, one launch (start us, length us, event | category | flops | bytes accessed | tf_op | source)
XLA Modules:
  0.0 249.5 jit_solution(3542583804921380434)
XLA Ops:
  0.6 1.3 fusion.1
  3.3 0.6 pad_add_fusion.info_ref
  3.8 3.3 %pack.1 = f32[16,264,128]{2,1,0:T(8,128)} custom-call(s32[3]{0:T(128)} %pad_add_fusion.info_ref, s32[14]{0:T(128)} %bitcast.20, f32[14,128,128]{2,1,0:T(8,128)} %bitcast.13, f32[14,128,128]{2,1,0:T(8,128)} %bitcast.14), custom_call_target="tpu_custom_call" | custom-call | tf_op jit(solution)/shard_map/pack/pallas_call | solution.py:311
  7.1 0.0 copy-start.6
  7.1 6.3 %all-to-all-start = ((f32[16,264,128]{2,1,0:T(8,128)}), f32[16,264,128]{2,1,0:T(8,128)S(1)}, u32[]{:S(2)}, u32[]{:S(2)}) async-start(f32[16,264,128]{2,1,0:T(8,128)} %pack.1), calls=%async_computation | async-start | bytes 4325376 | tf_op jit(solution)/shard_map/all_to_all | solution.py:323
  13.4 0.6 collective-permute-start.1
  14.0 1.5 collective-permute-start.3
  15.5 0.0 collective-permute-start
  15.5 64.9 %collective-permute-done.1.refs_2_ = f32[14,128,128]{2,1,0:T(8,128)S(1)} collective-permute-done((f32[14,128,128]{2,1,0:T(8,128)S(1)}, f32[14,128,128]{2,1,0:T(8,128)S(1)}, u32[]{:S(2)}, u32[]{:S(2)}) %collective-permute-start.1) | collective-permute-done | bytes 917536 | tf_op jit(solution)/shard_map/ppermute | solution.py:19
  80.4 0.0 collective-permute-start.2
  80.4 0.9 collective-permute-done.3.refs_4_
  81.3 2.1 collective-permute-start.5
  83.4 0.0 collective-permute-start.7
  83.4 0.0 collective-permute-done.refs_1_
  83.4 0.0 collective-permute-done.2.refs_3_
  83.4 0.0 copy-start.10
  83.4 0.8 collective-permute-done.4.refs_5_
  84.2 20.0 %collective-permute-done.5.refs_0_ = f32[14,128,128]{2,1,0:T(8,128)} collective-permute-done((f32[14,128,128]{2,1,0:T(8,128)S(1)}, f32[14,128,128]{2,1,0:T(8,128)}, u32[]{:S(2)}, u32[]{:S(2)}) %collective-permute-start.5) | collective-permute-done | bytes 917536 | tf_op jit(solution)/shard_map/ppermute | solution.py:19
  104.1 1.7 collective-permute-start.9
  105.8 0.3 collective-permute-start.11
  106.2 0.0 collective-permute-start.6
  106.2 0.5 collective-permute-start.8
  106.7 0.7 dynamic-slice_bitcast_fusion
  107.4 0.6 pad_add_fusion.1.rows_ref
  108.0 18.3 %collective-permute-done.9.refs_0_ = f32[14,128,128]{2,1,0:T(8,128)S(1)} collective-permute-done((f32[14,128,128]{2,1,0:T(8,128)}, f32[14,128,128]{2,1,0:T(8,128)S(1)}, u32[]{:S(2)}, u32[]{:S(2)}) %collective-permute-start.9) | collective-permute-done | bytes 917536 | tf_op jit(solution)/shard_map/ppermute | solution.py:19
  126.3 0.0 collective-permute-start.10
  126.3 1.0 collective-permute-done.11.refs_2_
  127.4 0.3 fusion
  127.7 1.0 convert_element_type.8.drops_ref
  128.7 0.0 copy-done
  128.7 7.9 %first.4 = (bf16[6,256,2048]{2,1,0:T(8,128)(2,1)}, f32[16,128,128]{2,1,0:T(8,128)}, bf16[2048,256]{1,0:T(8,128)(2,1)}) custom-call(s32[32]{0:T(128)} %convert_element_type.8.drops_ref, s32[17]{0:T(128)} %pad_add_fusion.1.rows_ref, f32[16,264,128]{2,1,0:T(8,128)} %copy-done, f32[14,128,128]{2,1,0:T(8,128)} %bitcast.15, f32[14,128,128]{2,1,0:T(8,128)} %copy-done.9, ...), custom_call_target="tpu_custom_call" | custom-call | tf_op jit(solution)/shard_map/first/pallas_call | solution.py:311
  136.7 5.6 %first.5 = (bf16[4,256,2048]{2,1,0:T(8,128)(2,1)}, f32[16,128,128]{2,1,0:T(8,128)}) custom-call(s32[32]{0:T(128)} %convert_element_type.8.drops_ref, s32[17]{0:T(128)} %pad_add_fusion.1.rows_ref, f32[16,264,128]{2,1,0:T(8,128)} %copy-done, f32[14,128,128]{2,1,0:T(8,128)} %collective-permute-done.5.refs_0_, ...), custom_call_target="tpu_custom_call", output_to_operand_aliasing={{1}: (8, {})} | custom-call | tf_op jit(solution)/shard_map/first/pallas_call | solution.py:311
  142.2 0.1 broadcast_select_fusion
  142.4 0.7 collective-permute-start.13
  143.1 5.4 %first.6 = (bf16[4,256,2048]{2,1,0:T(8,128)(2,1)}, f32[16,128,128]{2,1,0:T(8,128)}) custom-call(s32[32]{0:T(128)} %convert_element_type.8.drops_ref, s32[17]{0:T(128)} %pad_add_fusion.1.rows_ref, f32[16,264,128]{2,1,0:T(8,128)} %copy-done, f32[14,128,128]{2,1,0:T(8,128)} %copy-done.3, ...), custom_call_target="tpu_custom_call", output_to_operand_aliasing={{1}: (8, {})} | custom-call | tf_op jit(solution)/shard_map/first/pallas_call | solution.py:311
  148.5 7.3 %collective-permute-done.13.refs_0_ = f32[14,128,128]{2,1,0:T(8,128)S(1)} collective-permute-done((f32[14,128,128]{2,1,0:T(8,128)S(1)}, f32[14,128,128]{2,1,0:T(8,128)S(1)}, u32[]{:S(2)}, u32[]{:S(2)}) %collective-permute-start.13) | collective-permute-done | bytes 917536 | tf_op jit(solution)/shard_map/ppermute | solution.py:19
  155.8 0.5 collective-permute-start.14
  156.3 2.1 collective-permute-done.14.refs_1_
  158.4 0.9 copy-done.5
  159.4 4.1 %first.7 = (bf16[2,256,2048]{2,1,0:T(8,128)(2,1)}, f32[16,128,128]{2,1,0:T(8,128)}) custom-call(s32[32]{0:T(128)} %convert_element_type.8.drops_ref, s32[17]{0:T(128)} %pad_add_fusion.1.rows_ref, f32[16,264,128]{2,1,0:T(8,128)} %copy-done, f32[14,128,128]{2,1,0:T(8,128)} %copy-done.4, f32[14,128,128]{2,1,0:T(8,128)} %copy-done.5, ...), custom_call_target="tpu_custom_call", output_to_operand_aliasing={{1}: (6, {})} | custom-call | tf_op jit(solution)/shard_map/first/pallas_call | solution.py:311
  163.5 5.4 %all-to-all-start.1 = ((f32[16,128,128]{2,1,0:T(8,128)}), f32[16,128,128]{2,1,0:T(8,128)S(1)}, u32[]{:S(2)}, u32[]{:S(2)}) async-start(f32[16,128,128]{2,1,0:T(8,128)} %get-tuple-element.34.refs_5_), calls=%async_computation.1 | async-start | bytes 2097152 | tf_op jit(solution)/shard_map/all_to_all | solution.py:323
  168.9 17.8 %later.1 = f32[16,2,128,128]{3,2,1,0:T(8,128)} custom-call(s32[32]{0:T(128)} %convert_element_type.8.drops_ref, s32[17]{0:T(128)} %pad_add_fusion.1.rows_ref, bf16[6,256,2048]{2,1,0:T(8,128)(2,1)} %get-tuple-element.21.refs_0_, bf16[4,256,2048]{2,1,0:T(8,128)(2,1)} %get-tuple-element.24.refs_1_, bf16[4,256,2048]{2,1,0:T(8,128)(2,1)} %get-tuple-element.28.refs_2_, ...), custom_call_target="tpu_custom_call" | custom-call | tf_op jit(solution)/shard_map/later/pallas_call | solution.py:311
  186.7 5.6 %all-to-all-done.1.first_ref = f32[16,128,128]{2,1,0:T(8,128)S(1)} async-done(((f32[16,128,128]{2,1,0:T(8,128)}), f32[16,128,128]{2,1,0:T(8,128)S(1)}, u32[]{:S(2)}, u32[]{:S(2)}) %all-to-all-start.1) | async-done | bytes 1048608 | tf_op jit(solution)/shard_map/all_to_all | solution.py:323
  192.3 6.4 %all-to-all-start.2 = ((f32[16,2,128,128]{3,2,1,0:T(8,128)}), f32[16,2,128,128]{3,2,1,0:T(8,128)S(1)}, u32[]{:S(2)}, u32[]{:S(2)}) async-start(f32[16,2,128,128]{3,2,1,0:T(8,128)} %later.1), calls=%async_computation.2 | async-start | bytes 4194304 | tf_op jit(solution)/shard_map/all_to_all | solution.py:323
  198.7 3.1 %unpack_first.1.sum_ref = f32[14,128,128]{2,1,0:T(8,128)} custom-call(s32[14]{0:T(128)} %bitcast.21, f32[3]{0:T(128)} %coefs_ref.3, f32[16,128,128]{2,1,0:T(8,128)} %copy-done.2, f32[14,128,128]{2,1,0:T(8,128)} %bitcast.19), custom_call_target="tpu_custom_call" | custom-call | tf_op jit(solution)/shard_map/unpack_first/pallas_call | solution.py:311
  201.8 42.8 %all-to-all-done.2.held_ref = f32[16,2,128,128]{3,2,1,0:T(8,128)S(1)} async-done(((f32[16,2,128,128]{3,2,1,0:T(8,128)}), f32[16,2,128,128]{3,2,1,0:T(8,128)S(1)}, u32[]{:S(2)}, u32[]{:S(2)}) %all-to-all-start.2) | async-done | bytes 2097184 | tf_op jit(solution)/shard_map/all_to_all | solution.py:323
  244.6 1.3 copy-done.1
  245.9 3.6 %unpack_last.1 = (f32[14,128,128]{2,1,0:T(8,128)}, f32[14,128,128]{2,1,0:T(8,128)}, f32[14,128,128]{2,1,0:T(8,128)}) custom-call(s32[14]{0:T(128)} %bitcast.22, f32[3]{0:T(128)} %coefs_ref.3, f32[16,2,128,128]{3,2,1,0:T(8,128)} %copy-done.1, f32[14,128,128]{2,1,0:T(8,128)} %unpack_first.1.sum_ref), custom_call_target="tpu_custom_call" | custom-call | tf_op jit(solution)/shard_map/unpack_last/pallas_call | solution.py:311
  (27 shorter events, 0.1 us)
Async XLA Ops:
  7.1 6.3 %copy-start.6 = (f32[1,14,128,128]{3,2,1,0:T(8,128)S(1)}, f32[1,14,128,128]{3,2,1,0:T(8,128)}, u32[]{:S(2)}) copy-start(f32[1,14,128,128]{3,2,1,0:T(8,128)} %param.8) | copy-start | bytes 2752516
  7.1 120.2 %all-to-all-start = ((f32[16,264,128]{2,1,0:T(8,128)}), f32[16,264,128]{2,1,0:T(8,128)S(1)}, u32[]{:S(2)}, u32[]{:S(2)}) async-start(f32[16,264,128]{2,1,0:T(8,128)} %pack.1), calls=%async_computation | async-start | bytes 4325376 | tf_op jit(solution)/shard_map/all_to_all | solution.py:323
  13.4 67.0 %collective-permute-start.1 = (f32[14,128,128]{2,1,0:T(8,128)S(1)}, f32[14,128,128]{2,1,0:T(8,128)S(1)}, u32[]{:S(2)}, u32[]{:S(2)}) collective-permute-start(f32[14,128,128]{2,1,0:T(8,128)S(1)} %bitcast.16), channel_id=1, source_target_pairs={{0,4},{1,5},{2,0},{3,1},{4,8},{5,9},{6,2},{7,3},{8,12},{9,13},{10,... | collective-permute-start | bytes 2752520 | tf_op jit(solution)/shard_map/ppermute | solution.py:19
  14.0 67.2 %collective-permute-start.3 = (f32[14,128,128]{2,1,0:T(8,128)S(1)}, f32[14,128,128]{2,1,0:T(8,128)S(1)}, u32[]{:S(2)}, u32[]{:S(2)}) collective-permute-start(f32[14,128,128]{2,1,0:T(8,128)S(1)} %bitcast.17), channel_id=1, source_target_pairs={{0,2},{1,3},{2,6},{3,7},{4,0},{5,1},{6,10},{7,11},{8,4},{9,5},{10,... | collective-permute-start | bytes 2752520 | tf_op jit(solution)/shard_map/ppermute | solution.py:19
  15.5 67.9 %collective-permute-start = (f32[14,128,128]{2,1,0:T(8,128)S(1)}, f32[14,128,128]{2,1,0:T(8,128)S(1)}, u32[]{:S(2)}, u32[]{:S(2)}) collective-permute-start(f32[14,128,128]{2,1,0:T(8,128)S(1)} %bitcast.18), channel_id=1, source_target_pairs={{0,1},{1,0},{2,3},{3,2},{4,5},{5,4},{6,7},{7,6},{8,9},{9,8},{10,11... | collective-permute-start | bytes 2752520 | tf_op jit(solution)/shard_map/ppermute | solution.py:19
  80.4 3.8 %copy-start.7 = (f32[14,128,128]{2,1,0:T(8,128)}, f32[14,128,128]{2,1,0:T(8,128)S(1)}, u32[]{:S(2)}) copy-start(f32[14,128,128]{2,1,0:T(8,128)S(1)} %collective-permute-done.1.refs_2_) | copy-start | bytes 2752516
  80.4 3.0 %collective-permute-start.2 = (f32[14,128,128]{2,1,0:T(8,128)S(1)}, f32[14,128,128]{2,1,0:T(8,128)S(1)}, u32[]{:S(2)}, u32[]{:S(2)}) collective-permute-start(f32[14,128,128]{2,1,0:T(8,128)S(1)} %collective-permute-done.1.refs_2_), channel_id=1, source_target_pairs={{0,1},{1,0},{2,3},{3,2},{4,5},{5,4},{6,7},{7,6},{8,9},{9,8},{10,11... | collective-permute-start | bytes 2752520 | tf_op jit(solution)/shard_map/ppermute | solution.py:19
  81.3 22.9 %copy-start.8 = (f32[14,128,128]{2,1,0:T(8,128)}, f32[14,128,128]{2,1,0:T(8,128)S(1)}, u32[]{:S(2)}) copy-start(f32[14,128,128]{2,1,0:T(8,128)S(1)} %collective-permute-done.3.refs_4_) | copy-start | bytes 2752516
  81.3 2.9 %collective-permute-start.4 = (f32[14,128,128]{2,1,0:T(8,128)S(1)}, f32[14,128,128]{2,1,0:T(8,128)S(1)}, u32[]{:S(2)}, u32[]{:S(2)}) collective-permute-start(f32[14,128,128]{2,1,0:T(8,128)S(1)} %collective-permute-done.3.refs_4_), channel_id=1, source_target_pairs={{0,1},{1,0},{2,3},{3,2},{4,5},{5,4},{6,7},{7,6},{8,9},{9,8},{10,11... | collective-permute-start | bytes 2752520 | tf_op jit(solution)/shard_map/ppermute | solution.py:19
  81.3 22.9 %collective-permute-start.5 = (f32[14,128,128]{2,1,0:T(8,128)S(1)}, f32[14,128,128]{2,1,0:T(8,128)}, u32[]{:S(2)}, u32[]{:S(2)}) collective-permute-start(f32[14,128,128]{2,1,0:T(8,128)S(1)} %collective-permute-done.1.refs_2_), channel_id=1, source_target_pairs={{0,4},{1,5},{2,0},{3,1},{4,8},{5,9},{6,2},{7,3},{8,12},{9,13},{10,... | collective-permute-start | bytes 2752520 | tf_op jit(solution)/shard_map/ppermute | solution.py:19
  83.4 22.4 %collective-permute-start.7 = (f32[14,128,128]{2,1,0:T(8,128)S(1)}, f32[14,128,128]{2,1,0:T(8,128)}, u32[]{:S(2)}, u32[]{:S(2)}) collective-permute-start(f32[14,128,128]{2,1,0:T(8,128)S(1)} %collective-permute-done.3.refs_4_), channel_id=1, source_target_pairs={{0,2},{1,3},{2,6},{3,7},{4,0},{5,1},{6,10},{7,11},{8,4},{9,5},{10,... | collective-permute-start | bytes 2752520 | tf_op jit(solution)/shard_map/ppermute | solution.py:19
  83.4 22.4 %copy-start.9 = (f32[14,128,128]{2,1,0:T(8,128)}, f32[14,128,128]{2,1,0:T(8,128)S(1)}, u32[]{:S(2)}) copy-start(f32[14,128,128]{2,1,0:T(8,128)S(1)} %collective-permute-done.refs_1_) | copy-start | bytes 2752516
  83.4 22.8 %copy-start.10 = (f32[14,128,128]{2,1,0:T(8,128)}, f32[14,128,128]{2,1,0:T(8,128)S(1)}, u32[]{:S(2)}) copy-start(f32[14,128,128]{2,1,0:T(8,128)S(1)} %collective-permute-done.2.refs_3_) | copy-start | bytes 2752516
  84.2 22.0 %copy-start.11 = (f32[14,128,128]{2,1,0:T(8,128)}, f32[14,128,128]{2,1,0:T(8,128)S(1)}, u32[]{:S(2)}) copy-start(f32[14,128,128]{2,1,0:T(8,128)S(1)} %collective-permute-done.4.refs_5_) | copy-start | bytes 2752516
  104.1 22.2 %collective-permute-start.9 = (f32[14,128,128]{2,1,0:T(8,128)}, f32[14,128,128]{2,1,0:T(8,128)S(1)}, u32[]{:S(2)}, u32[]{:S(2)}) collective-permute-start(f32[14,128,128]{2,1,0:T(8,128)} %collective-permute-done.5.refs_0_), channel_id=1, source_target_pairs={{0,4},{1,5},{2,0},{3,1},{4,8},{5,9},{6,2},{7,3},{8,12},{9,13},{10,... | collective-permute-start | bytes 2752520 | tf_op jit(solution)/shard_map/ppermute | solution.py:19
  105.8 21.5 %collective-permute-start.11 = (f32[14,128,128]{2,1,0:T(8,128)}, f32[14,128,128]{2,1,0:T(8,128)}, u32[]{:S(2)}, u32[]{:S(2)}) collective-permute-start(f32[14,128,128]{2,1,0:T(8,128)} %collective-permute-done.7.refs_2_), channel_id=1, source_target_pairs={{0,2},{1,3},{2,6},{3,7},{4,0},{5,1},{6,10},{7,11},{8,4},{9,5},{10,... | collective-permute-start | bytes 2752520 | tf_op jit(solution)/shard_map/ppermute | solution.py:19
  106.2 30.5 %collective-permute-start.6 = (f32[14,128,128]{2,1,0:T(8,128)}, f32[14,128,128]{2,1,0:T(8,128)}, u32[]{:S(2)}, u32[]{:S(2)}) collective-permute-start(f32[14,128,128]{2,1,0:T(8,128)} %collective-permute-done.5.refs_0_), channel_id=1, source_target_pairs={{0,1},{1,0},{2,3},{3,2},{4,5},{5,4},{6,7},{7,6},{8,9},{9,8},{10,11... | collective-permute-start | bytes 2752520 | tf_op jit(solution)/shard_map/ppermute | solution.py:19
  106.2 30.5 %collective-permute-start.8 = (f32[14,128,128]{2,1,0:T(8,128)}, f32[14,128,128]{2,1,0:T(8,128)}, u32[]{:S(2)}, u32[]{:S(2)}) collective-permute-start(f32[14,128,128]{2,1,0:T(8,128)} %collective-permute-done.7.refs_2_), channel_id=1, source_target_pairs={{0,1},{1,0},{2,3},{3,2},{4,5},{5,4},{6,7},{7,6},{8,9},{9,8},{10,11... | collective-permute-start | bytes 2752520 | tf_op jit(solution)/shard_map/ppermute | solution.py:19
  126.3 15.9 %copy-start.3 = (f32[14,128,128]{2,1,0:T(8,128)}, f32[14,128,128]{2,1,0:T(8,128)S(1)}, u32[]{:S(2)}) copy-start(f32[14,128,128]{2,1,0:T(8,128)S(1)} %collective-permute-done.9.refs_0_) | copy-start | bytes 2752516
  126.3 16.7 %collective-permute-start.10 = (f32[14,128,128]{2,1,0:T(8,128)S(1)}, f32[14,128,128]{2,1,0:T(8,128)}, u32[]{:S(2)}, u32[]{:S(2)}) collective-permute-start(f32[14,128,128]{2,1,0:T(8,128)S(1)} %collective-permute-done.9.refs_0_), channel_id=1, source_target_pairs={{0,1},{1,0},{2,3},{3,2},{4,5},{5,4},{6,7},{7,6},{8,9},{9,8},{10,11... | collective-permute-start | bytes 2752520 | tf_op jit(solution)/shard_map/ppermute | solution.py:19
  127.4 15.7 %collective-permute-start.12 = (f32[14,128,128]{2,1,0:T(8,128)}, f32[14,128,128]{2,1,0:T(8,128)}, u32[]{:S(2)}, u32[]{:S(2)}) collective-permute-start(f32[14,128,128]{2,1,0:T(8,128)} %collective-permute-done.11.refs_2_), channel_id=1, source_target_pairs={{0,1},{1,0},{2,3},{3,2},{4,5},{5,4},{6,7},{7,6},{8,9},{9,8},{10,11... | collective-permute-start | bytes 2752520 | tf_op jit(solution)/shard_map/ppermute | solution.py:19
  127.4 1.3 copy-start
  142.4 13.4 %collective-permute-start.13 = (f32[14,128,128]{2,1,0:T(8,128)S(1)}, f32[14,128,128]{2,1,0:T(8,128)S(1)}, u32[]{:S(2)}, u32[]{:S(2)}) collective-permute-start(f32[14,128,128]{2,1,0:T(8,128)S(1)} %broadcast_select_fusion), channel_id=1, source_target_pairs={{0,4},{1,3},{2,0},{3,7},{4,8},{5,1},{6,2},{7,11},{8,12},{9,5},{10,... | collective-permute-start | bytes 2752520 | tf_op jit(solution)/shard_map/ppermute | solution.py:19
  155.8 2.6 %copy-start.4 = (f32[14,128,128]{2,1,0:T(8,128)}, f32[14,128,128]{2,1,0:T(8,128)S(1)}, u32[]{:S(2)}) copy-start(f32[14,128,128]{2,1,0:T(8,128)S(1)} %collective-permute-done.13.refs_0_) | copy-start | bytes 2752516
  155.8 2.6 %collective-permute-start.14 = (f32[14,128,128]{2,1,0:T(8,128)S(1)}, f32[14,128,128]{2,1,0:T(8,128)S(1)}, u32[]{:S(2)}, u32[]{:S(2)}) collective-permute-start(f32[14,128,128]{2,1,0:T(8,128)S(1)} %collective-permute-done.13.refs_0_), channel_id=1, source_target_pairs={{0,1},{1,0},{2,3},{3,2},{4,5},{5,4},{6,7},{7,6},{8,9},{9,8},{10,11... | collective-permute-start | bytes 2752520 | tf_op jit(solution)/shard_map/ppermute | solution.py:19
  158.4 0.9 copy-start.5
  163.5 28.8 %all-to-all-start.1 = ((f32[16,128,128]{2,1,0:T(8,128)}), f32[16,128,128]{2,1,0:T(8,128)S(1)}, u32[]{:S(2)}, u32[]{:S(2)}) async-start(f32[16,128,128]{2,1,0:T(8,128)} %get-tuple-element.34.refs_5_), calls=%async_computation.1 | async-start | bytes 2097152 | tf_op jit(solution)/shard_map/all_to_all | solution.py:323
  192.3 6.4 %copy-start.2 = (f32[16,128,128]{2,1,0:T(8,128)}, f32[16,128,128]{2,1,0:T(8,128)S(1)}, u32[]{:S(2)}) copy-start(f32[16,128,128]{2,1,0:T(8,128)S(1)} %all-to-all-done.1.first_ref) | copy-start | bytes 3145732
  192.3 52.3 %all-to-all-start.2 = ((f32[16,2,128,128]{3,2,1,0:T(8,128)}), f32[16,2,128,128]{3,2,1,0:T(8,128)S(1)}, u32[]{:S(2)}, u32[]{:S(2)}) async-start(f32[16,2,128,128]{3,2,1,0:T(8,128)} %later.1), calls=%async_computation.2 | async-start | bytes 4194304 | tf_op jit(solution)/shard_map/all_to_all | solution.py:323
  244.6 1.3 copy-start.1

commit v9 on v8

--- a/solution.py
+++ b/solution.py
@@ -39,12 +39,13 @@
     return jnp.array(table, jnp.int32)[me], (6, 4, 4, 2)
 
 
-def gathered_rows(x, me, total):
+def gathered_rows(x, me, total, exchange):
     if total != 16:
         rows = [x]
         for hop in range(1, REACH + 1):
             for by in (hop, -hop):
                 rows.append(permute(x, lambda i, by=by: (i + by) % total))
+        yield exchange()
         for start, end in ((0, 5), (5, 9), (9, 13), (13, 15)):
             yield rows[start:end]
         return
@@ -59,9 +60,11 @@
 
     rows = [x, other_core(x)]
     ahead, behind, first = round_of(x, x)
+    column = exchange(ahead, behind)
     ahead, behind, second = round_of(ahead, behind)
+    yield column
     yield rows + first
-    there = (rows[1], first[1], first[3])
+    there = (column, rows[1], first[1], first[3])
     ahead, behind, third = round_of(after(ahead, *there), after(behind, *there))
     made = yield second
     ahead, behind = after(ahead, made), after(behind, made)
@@ -336,10 +339,10 @@
         ],
         "pack",
     )
-    column = exchange(send)
+    indices, parts = window_rows(me, total)
+    gathered = gathered_rows(h_blocks[0], me, total, lambda *others: exchange(after(send, *others)))
+    column = next(gathered)
     drops = column[:, 2 * size:2 * size + 2, 0].astype(jnp.int32).reshape(-1)
-    indices, parts = window_rows(me, total)
-    gathered = gathered_rows(h_blocks[0], me, total)
     rows = jnp.concatenate([indices, me[None]])
     window = sum(parts)
     dense_shape = (window, 2 * size, window * size)

time: 252 us -> 235 us (0.933)
  waiting for transfers between devices: 164 us -> 142 us
  local copies, waits for them, and re-layouts: 3.93 us -> 8.39 us
    ppermute x15, waiting for transfers between devices: 115 us -> 93.9 us  [permute(): return lax.ppermute(x, 'row', [(i, target(i)) for i in range(devices)])]
    unnamed x24 -> x26, local copies, waits for them, and re-layouts: 2.27 us -> 7.03 us
  transfers between devices with their start and end apart: 18 -> 18, of which waited for: 10 -> 11; matrix products, arithmetic and copies ran while one was open for 1% -> 2% of each run, Pallas kernels for 16% -> 19%
where the time goes in v9:
time: 235 us; the launch traced here: 232 us
  waiting for transfers between devices  142 us (60%)
  Pallas kernels  50.8 us (22%)
  starting transfers between devices  25.5 us (11%)
  local copies, waits for them, and re-layouts  8.39 us (4%)
  other arithmetic  2.96 us (1%)
    ppermute x15, waiting for transfers between devices, permute(): return lax.ppermute(x, 'row', [(i, target(i)) for i in range(devices)])  93.9 us
    pallas_call x8, Pallas kernels, call(): pl.pallas_call(kernel, out_shape=outs, in_specs=[SMEM] * len(smem) + [ANY...  50.8 us
    all_to_all x3, waiting for transfers between devices, exchange(): return lax.all_to_all(x, 'row', 0, 0, tiled=True)  48.5 us
    all_to_all x3, starting transfers between devices, exchange(): return lax.all_to_all(x, 'row', 0, 0, tiled=True)  17.7 us
    ppermute x15, starting transfers between devices, permute(): return lax.ppermute(x, 'row', [(i, target(i)) for i in range(devices)])  7.81 us
    unnamed x26, local copies, waits for them, and re-layouts  7.03 us
  transfers between devices with their start and end apart: 18, of which 11 were waited for; matrix products, arithmetic and copies ran while one was open for 2% of the time, Pallas kernels for 19%

profile of v9, /device:TPU:22, one launch (start us, length us, event | category | flops | bytes accessed | tf_op | source)
XLA Modules:
  0.0 232.1 jit_solution(4596967068638128105)
XLA Ops:
  0.6 0.5 collective-permute-start
  1.1 1.6 collective-permute-start.1
  2.7 1.3 fusion.1
  5.3 0.6 pad_add_fusion.info_ref
  5.9 3.2 %pack.1 = f32[16,264,128]{2,1,0:T(8,128)} custom-call(s32[3]{0:T(128)} %pad_add_fusion.info_ref, s32[14]{0:T(128)} %bitcast.20, f32[14,128,128]{2,1,0:T(8,128)} %bitcast.13, f32[14,128,128]{2,1,0:T(8,128)} %bitcast.14), custom_call_target="tpu_custom_call" | custom-call | tf_op jit(solution)/shard_map/pack/pallas_call | solution.py:314
  9.2 0.0 copy-start.6
  9.2 13.8 %collective-permute-done.refs_2_ = f32[14,128,128]{2,1,0:T(8,128)S(1)} collective-permute-done((f32[14,128,128]{2,1,0:T(8,128)}, f32[14,128,128]{2,1,0:T(8,128)S(1)}, u32[]{:S(2)}, u32[]{:S(2)}) %collective-permute-start) | collective-permute-done | bytes 917536 | tf_op jit(solution)/shard_map/ppermute | solution.py:19
  23.0 0.2 collective-permute-done.1.refs_4_
  23.2 0.8 copy-done.7
  23.9 0.3 copy-done.8
  24.2 6.1 %all-to-all-start = ((f32[16,264,128]{2,1,0:T(8,128)}), f32[16,264,128]{2,1,0:T(8,128)S(1)}, u32[]{:S(2)}, u32[]{:S(2)}) async-start(f32[16,264,128]{2,1,0:T(8,128)} %pack.1), calls=%async_computation | async-start | bytes 4325376 | tf_op jit(solution)/shard_map/all_to_all | solution.py:326
  30.3 0.6 collective-permute-start.5
  30.9 1.5 collective-permute-start.7
  32.4 0.5 collective-permute-start.3
  32.9 0.0 collective-permute-start.4
  32.9 64.5 %collective-permute-done.5.refs_0_ = f32[14,128,128]{2,1,0:T(8,128)} collective-permute-done((f32[14,128,128]{2,1,0:T(8,128)}, f32[14,128,128]{2,1,0:T(8,128)}, u32[]{:S(2)}, u32[]{:S(2)}) %collective-permute-start.5) | collective-permute-done | bytes 917536 | tf_op jit(solution)/shard_map/ppermute | solution.py:19
  97.4 0.9 collective-permute-done.7.refs_2_
  98.3 0.9 copy-done.9
  99.2 0.9 copy-done.10
  100.2 2.2 collective-permute-start.9
  102.3 0.7 dynamic-slice_bitcast_fusion
  103.0 0.6 pad_add_fusion.1.rows_ref
  103.6 0.3 fusion
  104.0 0.7 convert_element_type.8.drops_ref
  104.7 7.9 %first.4 = (bf16[6,256,2048]{2,1,0:T(8,128)(2,1)}, f32[16,128,128]{2,1,0:T(8,128)}, bf16[2048,256]{1,0:T(8,128)(2,1)}) custom-call(s32[32]{0:T(128)} %convert_element_type.8.drops_ref, s32[17]{0:T(128)} %pad_add_fusion.1.rows_ref, f32[16,264,128]{2,1,0:T(8,128)} %copy-done, f32[14,128,128]{2,1,0:T(8,128)} %bitcast.17, f32[14,128,128]{2,1,0:T(8,128)} %copy-done.9, ...), custom_call_target="tpu_custom_call" | custom-call | tf_op jit(solution)/shard_map/first/pallas_call | solution.py:314
  112.6 5.6 %first.5 = (bf16[4,256,2048]{2,1,0:T(8,128)(2,1)}, f32[16,128,128]{2,1,0:T(8,128)}) custom-call(s32[32]{0:T(128)} %convert_element_type.8.drops_ref, s32[17]{0:T(128)} %pad_add_fusion.1.rows_ref, f32[16,264,128]{2,1,0:T(8,128)} %copy-done, f32[14,128,128]{2,1,0:T(8,128)} %collective-permute-done.5.refs_0_, ...), custom_call_target="tpu_custom_call", output_to_operand_aliasing={{1}: (8, {})} | custom-call | tf_op jit(solution)/shard_map/first/pallas_call | solution.py:314
  118.2 5.0 %collective-permute-done.9.refs_0_ = f32[14,128,128]{2,1,0:T(8,128)S(1)} collective-permute-done((f32[14,128,128]{2,1,0:T(8,128)}, f32[14,128,128]{2,1,0:T(8,128)S(1)}, u32[]{:S(2)}, u32[]{:S(2)}) %collective-permute-start.9) | collective-permute-done | bytes 917536 | tf_op jit(solution)/shard_map/ppermute | solution.py:19
  123.2 1.4 collective-permute-done.11.refs_2_
  124.6 0.5 collective-permute-start.12
  125.1 0.1 broadcast_select_fusion
  125.3 0.4 collective-permute-start.13
  125.7 2.7 %collective-permute-done.10.refs_1_ = f32[14,128,128]{2,1,0:T(8,128)S(1)} collective-permute-done((f32[14,128,128]{2,1,0:T(8,128)S(1)}, f32[14,128,128]{2,1,0:T(8,128)S(1)}, u32[]{:S(2)}, u32[]{:S(2)}) %collective-permute-start.10) | collective-permute-done | bytes 917536 | tf_op jit(solution)/shard_map/ppermute | solution.py:19
  128.4 0.9 copy-done.11
  129.3 0.9 copy-done.12
  130.2 5.5 %first.6 = (bf16[4,256,2048]{2,1,0:T(8,128)(2,1)}, f32[16,128,128]{2,1,0:T(8,128)}) custom-call(s32[32]{0:T(128)} %convert_element_type.8.drops_ref, s32[17]{0:T(128)} %pad_add_fusion.1.rows_ref, f32[16,264,128]{2,1,0:T(8,128)} %copy-done, f32[14,128,128]{2,1,0:T(8,128)} %copy-done.3, f32[14,128,128]{2,1,0:T(8,128)} %copy-done.11, ...), custom_call_target="tpu_custom_call", output_to_operand_aliasing={{1}: (8, {})} | custom-call | tf_op jit(solution)/shard_map/first/pallas_call | solution.py:314
  135.8 3.0 %collective-permute-done.13.refs_0_ = f32[14,128,128]{2,1,0:T(8,128)S(1)} collective-permute-done((f32[14,128,128]{2,1,0:T(8,128)S(1)}, f32[14,128,128]{2,1,0:T(8,128)S(1)}, u32[]{:S(2)}, u32[]{:S(2)}) %collective-permute-start.13) | collective-permute-done | bytes 917536 | tf_op jit(solution)/shard_map/ppermute | solution.py:19
  138.7 0.1 collective-permute-start.14
  138.8 2.4 %collective-permute-done.14.refs_1_ = f32[14,128,128]{2,1,0:T(8,128)S(1)} collective-permute-done((f32[14,128,128]{2,1,0:T(8,128)S(1)}, f32[14,128,128]{2,1,0:T(8,128)S(1)}, u32[]{:S(2)}, u32[]{:S(2)}) %collective-permute-start.14) | collective-permute-done | bytes 917536 | tf_op jit(solution)/shard_map/ppermute | solution.py:19
  141.2 0.9 copy-done.5
  142.1 4.1 %first.7 = (bf16[2,256,2048]{2,1,0:T(8,128)(2,1)}, f32[16,128,128]{2,1,0:T(8,128)}) custom-call(s32[32]{0:T(128)} %convert_element_type.8.drops_ref, s32[17]{0:T(128)} %pad_add_fusion.1.rows_ref, f32[16,264,128]{2,1,0:T(8,128)} %copy-done, f32[14,128,128]{2,1,0:T(8,128)} %copy-done.4, f32[14,128,128]{2,1,0:T(8,128)} %copy-done.5, ...), custom_call_target="tpu_custom_call", output_to_operand_aliasing={{1}: (6, {})} | custom-call | tf_op jit(solution)/shard_map/first/pallas_call | solution.py:314
  146.3 5.1 %all-to-all-start.1 = ((f32[16,128,128]{2,1,0:T(8,128)}), f32[16,128,128]{2,1,0:T(8,128)S(1)}, u32[]{:S(2)}, u32[]{:S(2)}) async-start(f32[16,128,128]{2,1,0:T(8,128)} %get-tuple-element.36.refs_5_), calls=%async_computation.1 | async-start | bytes 2097152 | tf_op jit(solution)/shard_map/all_to_all | solution.py:326
  151.4 17.8 %later.1 = f32[16,2,128,128]{3,2,1,0:T(8,128)} custom-call(s32[32]{0:T(128)} %convert_element_type.8.drops_ref, s32[17]{0:T(128)} %pad_add_fusion.1.rows_ref, bf16[6,256,2048]{2,1,0:T(8,128)(2,1)} %get-tuple-element.23.refs_0_, bf16[4,256,2048]{2,1,0:T(8,128)(2,1)} %get-tuple-element.26.refs_1_, bf16[4,256,2048]{2,1,0:T(8,128)(2,1)} %get-tuple-element.30.refs_2_, ...), custom_call_target="tpu_custom_call" | custom-call | tf_op jit(solution)/shard_map/later/pallas_call | solution.py:314
  169.2 5.6 %all-to-all-done.1.first_ref = f32[16,128,128]{2,1,0:T(8,128)S(1)} async-done(((f32[16,128,128]{2,1,0:T(8,128)}), f32[16,128,128]{2,1,0:T(8,128)S(1)}, u32[]{:S(2)}, u32[]{:S(2)}) %all-to-all-start.1) | async-done | bytes 1048608 | tf_op jit(solution)/shard_map/all_to_all | solution.py:326
  174.8 6.4 %all-to-all-start.2 = ((f32[16,2,128,128]{3,2,1,0:T(8,128)}), f32[16,2,128,128]{3,2,1,0:T(8,128)S(1)}, u32[]{:S(2)}, u32[]{:S(2)}) async-start(f32[16,2,128,128]{3,2,1,0:T(8,128)} %later.1), calls=%async_computation.2 | async-start | bytes 4194304 | tf_op jit(solution)/shard_map/all_to_all | solution.py:326
  181.2 3.1 %unpack_first.1.sum_ref = f32[14,128,128]{2,1,0:T(8,128)} custom-call(s32[14]{0:T(128)} %bitcast.21, f32[3]{0:T(128)} %coefs_ref.3, f32[16,128,128]{2,1,0:T(8,128)} %copy-done.2, f32[14,128,128]{2,1,0:T(8,128)} %bitcast.19), custom_call_target="tpu_custom_call" | custom-call | tf_op jit(solution)/shard_map/unpack_first/pallas_call | solution.py:314
  184.3 42.8 %all-to-all-done.2.held_ref = f32[16,2,128,128]{3,2,1,0:T(8,128)S(1)} async-done(((f32[16,2,128,128]{3,2,1,0:T(8,128)}), f32[16,2,128,128]{3,2,1,0:T(8,128)S(1)}, u32[]{:S(2)}, u32[]{:S(2)}) %all-to-all-start.2) | async-done | bytes 2097184 | tf_op jit(solution)/shard_map/all_to_all | solution.py:326
  227.1 1.3 copy-done.1
  228.5 3.6 %unpack_last.1 = (f32[14,128,128]{2,1,0:T(8,128)}, f32[14,128,128]{2,1,0:T(8,128)}, f32[14,128,128]{2,1,0:T(8,128)}) custom-call(s32[14]{0:T(128)} %bitcast.22, f32[3]{0:T(128)} %coefs_ref.3, f32[16,2,128,128]{3,2,1,0:T(8,128)} %copy-done.1, f32[14,128,128]{2,1,0:T(8,128)} %unpack_first.1.sum_ref), custom_call_target="tpu_custom_call" | custom-call | tf_op jit(solution)/shard_map/unpack_last/pallas_call | solution.py:314
  (29 shorter events, 0.1 us)
Async XLA Ops:
  0.6 22.4 %collective-permute-start = (f32[14,128,128]{2,1,0:T(8,128)}, f32[14,128,128]{2,1,0:T(8,128)S(1)}, u32[]{:S(2)}, u32[]{:S(2)}) collective-permute-start(f32[14,128,128]{2,1,0:T(8,128)} %bitcast.15), channel_id=1, source_target_pairs={{0,4},{1,5},{2,0},{3,1},{4,8},{5,9},{6,2},{7,3},{8,12},{9,13},{10,... | collective-permute-start | bytes 2752520 | tf_op jit(solution)/shard_map/ppermute | solution.py:19
  1.1 22.0 %collective-permute-start.1 = (f32[14,128,128]{2,1,0:T(8,128)}, f32[14,128,128]{2,1,0:T(8,128)S(1)}, u32[]{:S(2)}, u32[]{:S(2)}) collective-permute-start(f32[14,128,128]{2,1,0:T(8,128)} %bitcast.16), channel_id=1, source_target_pairs={{0,2},{1,3},{2,6},{3,7},{4,0},{5,1},{6,10},{7,11},{8,4},{9,5},{10,... | collective-permute-start | bytes 2752520 | tf_op jit(solution)/shard_map/ppermute | solution.py:19
  9.2 23.2 %copy-start.6 = (f32[1,14,128,128]{3,2,1,0:T(8,128)S(1)}, f32[1,14,128,128]{3,2,1,0:T(8,128)}, u32[]{:S(2)}) copy-start(f32[1,14,128,128]{3,2,1,0:T(8,128)} %param.8) | copy-start | bytes 2752516
  23.0 0.9 copy-start.7
  23.2 1.1 copy-start.8
  24.2 76.0 %all-to-all-start = ((f32[16,264,128]{2,1,0:T(8,128)}), f32[16,264,128]{2,1,0:T(8,128)S(1)}, u32[]{:S(2)}, u32[]{:S(2)}) async-start(f32[16,264,128]{2,1,0:T(8,128)} %pack.1), calls=%async_computation | async-start | bytes 4325376 | tf_op jit(solution)/shard_map/all_to_all | solution.py:326
  30.3 67.1 %collective-permute-start.5 = (f32[14,128,128]{2,1,0:T(8,128)}, f32[14,128,128]{2,1,0:T(8,128)}, u32[]{:S(2)}, u32[]{:S(2)}) collective-permute-start(f32[14,128,128]{2,1,0:T(8,128)} %copy-done.7), channel_id=1, source_target_pairs={{0,4},{1,5},{2,0},{3,1},{4,8},{5,9},{6,2},{7,3},{8,12},{9,13},{10,... | collective-permute-start | bytes 2752520 | tf_op jit(solution)/shard_map/ppermute | solution.py:19
  30.9 67.4 %collective-permute-start.7 = (f32[14,128,128]{2,1,0:T(8,128)}, f32[14,128,128]{2,1,0:T(8,128)}, u32[]{:S(2)}, u32[]{:S(2)}) collective-permute-start(f32[14,128,128]{2,1,0:T(8,128)} %copy-done.8), channel_id=1, source_target_pairs={{0,2},{1,3},{2,6},{3,7},{4,0},{5,1},{6,10},{7,11},{8,4},{9,5},{10,... | collective-permute-start | bytes 2752520 | tf_op jit(solution)/shard_map/ppermute | solution.py:19
  32.4 65.9 %collective-permute-start.2 = (f32[14,128,128]{2,1,0:T(8,128)S(1)}, f32[14,128,128]{2,1,0:T(8,128)S(1)}, u32[]{:S(2)}, u32[]{:S(2)}) collective-permute-start(f32[14,128,128]{2,1,0:T(8,128)S(1)} %bitcast.18), channel_id=1, source_target_pairs={{0,1},{1,0},{2,3},{3,2},{4,5},{5,4},{6,7},{7,6},{8,9},{9,8},{10,11... | collective-permute-start | bytes 2752520 | tf_op jit(solution)/shard_map/ppermute | solution.py:19
  32.4 65.9 %collective-permute-start.3 = (f32[14,128,128]{2,1,0:T(8,128)}, f32[14,128,128]{2,1,0:T(8,128)S(1)}, u32[]{:S(2)}, u32[]{:S(2)}) collective-permute-start(f32[14,128,128]{2,1,0:T(8,128)} %copy-done.7), channel_id=1, source_target_pairs={{0,1},{1,0},{2,3},{3,2},{4,5},{5,4},{6,7},{7,6},{8,9},{9,8},{10,11... | collective-permute-start | bytes 2752520 | tf_op jit(solution)/shard_map/ppermute | solution.py:19
  32.9 67.3 %collective-permute-start.4 = (f32[14,128,128]{2,1,0:T(8,128)}, f32[14,128,128]{2,1,0:T(8,128)}, u32[]{:S(2)}, u32[]{:S(2)}) collective-permute-start(f32[14,128,128]{2,1,0:T(8,128)} %copy-done.8), channel_id=1, source_target_pairs={{0,1},{1,0},{2,3},{3,2},{4,5},{5,4},{6,7},{7,6},{8,9},{9,8},{10,11... | collective-permute-start | bytes 2752520 | tf_op jit(solution)/shard_map/ppermute | solution.py:19
  97.4 15.2 %collective-permute-start.6 = (f32[14,128,128]{2,1,0:T(8,128)}, f32[14,128,128]{2,1,0:T(8,128)}, u32[]{:S(2)}, u32[]{:S(2)}) collective-permute-start(f32[14,128,128]{2,1,0:T(8,128)} %collective-permute-done.5.refs_0_), channel_id=1, source_target_pairs={{0,1},{1,0},{2,3},{3,2},{4,5},{5,4},{6,7},{7,6},{8,9},{9,8},{10,11... | collective-permute-start | bytes 2752520 | tf_op jit(solution)/shard_map/ppermute | solution.py:19
  98.3 14.3 %collective-permute-start.8 = (f32[14,128,128]{2,1,0:T(8,128)}, f32[14,128,128]{2,1,0:T(8,128)}, u32[]{:S(2)}, u32[]{:S(2)}) collective-permute-start(f32[14,128,128]{2,1,0:T(8,128)} %collective-permute-done.7.refs_2_), channel_id=1, source_target_pairs={{0,1},{1,0},{2,3},{3,2},{4,5},{5,4},{6,7},{7,6},{8,9},{9,8},{10,11... | collective-permute-start | bytes 2752520 | tf_op jit(solution)/shard_map/ppermute | solution.py:19
  98.3 0.9 copy-start.9
  99.2 0.9 copy-start.10
  100.2 4.5 %copy-start = (f32[16,264,128]{2,1,0:T(8,128)}, f32[16,264,128]{2,1,0:T(8,128)S(1)}, u32[]{:S(2)}) copy-start(f32[16,264,128]{2,1,0:T(8,128)S(1)} %all-to-all-done.t_ref.refs_4_) | copy-start | bytes 6488068
  100.2 23.0 %collective-permute-start.9 = (f32[14,128,128]{2,1,0:T(8,128)}, f32[14,128,128]{2,1,0:T(8,128)S(1)}, u32[]{:S(2)}, u32[]{:S(2)}) collective-permute-start(f32[14,128,128]{2,1,0:T(8,128)} %collective-permute-done.5.refs_0_), channel_id=1, source_target_pairs={{0,4},{1,5},{2,0},{3,1},{4,8},{5,9},{6,2},{7,3},{8,12},{9,13},{10,... | collective-permute-start | bytes 2752520 | tf_op jit(solution)/shard_map/ppermute | solution.py:19
  102.3 22.3 %collective-permute-start.11 = (f32[14,128,128]{2,1,0:T(8,128)}, f32[14,128,128]{2,1,0:T(8,128)}, u32[]{:S(2)}, u32[]{:S(2)}) collective-permute-start(f32[14,128,128]{2,1,0:T(8,128)} %collective-permute-done.7.refs_2_), channel_id=1, source_target_pairs={{0,2},{1,3},{2,6},{3,7},{4,0},{5,1},{6,10},{7,11},{8,4},{9,5},{10,... | collective-permute-start | bytes 2752520 | tf_op jit(solution)/shard_map/ppermute | solution.py:19
  123.2 7.0 %copy-start.3 = (f32[14,128,128]{2,1,0:T(8,128)}, f32[14,128,128]{2,1,0:T(8,128)S(1)}, u32[]{:S(2)}) copy-start(f32[14,128,128]{2,1,0:T(8,128)S(1)} %collective-permute-done.9.refs_0_) | copy-start | bytes 2752516
  124.6 3.7 %collective-permute-start.10 = (f32[14,128,128]{2,1,0:T(8,128)S(1)}, f32[14,128,128]{2,1,0:T(8,128)S(1)}, u32[]{:S(2)}, u32[]{:S(2)}) collective-permute-start(f32[14,128,128]{2,1,0:T(8,128)S(1)} %collective-permute-done.9.refs_0_), channel_id=1, source_target_pairs={{0,1},{1,0},{2,3},{3,2},{4,5},{5,4},{6,7},{7,6},{8,9},{9,8},{10,11... | collective-permute-start | bytes 2752520 | tf_op jit(solution)/shard_map/ppermute | solution.py:19
  124.6 4.7 %collective-permute-start.12 = (f32[14,128,128]{2,1,0:T(8,128)}, f32[14,128,128]{2,1,0:T(8,128)S(1)}, u32[]{:S(2)}, u32[]{:S(2)}) collective-permute-start(f32[14,128,128]{2,1,0:T(8,128)} %collective-permute-done.11.refs_2_), channel_id=1, source_target_pairs={{0,1},{1,0},{2,3},{3,2},{4,5},{5,4},{6,7},{7,6},{8,9},{9,8},{10,11... | collective-permute-start | bytes 2752520 | tf_op jit(solution)/shard_map/ppermute | solution.py:19
  125.3 13.4 %collective-permute-start.13 = (f32[14,128,128]{2,1,0:T(8,128)S(1)}, f32[14,128,128]{2,1,0:T(8,128)S(1)}, u32[]{:S(2)}, u32[]{:S(2)}) collective-permute-start(f32[14,128,128]{2,1,0:T(8,128)S(1)} %broadcast_select_fusion), channel_id=1, source_target_pairs={{0,4},{1,3},{2,0},{3,7},{4,8},{5,1},{6,2},{7,11},{8,12},{9,5},{10,... | collective-permute-start | bytes 2752520 | tf_op jit(solution)/shard_map/ppermute | solution.py:19
  128.4 0.9 copy-start.11
  129.3 0.9 copy-start.12
  138.7 2.5 %copy-start.4 = (f32[14,128,128]{2,1,0:T(8,128)}, f32[14,128,128]{2,1,0:T(8,128)S(1)}, u32[]{:S(2)}) copy-start(f32[14,128,128]{2,1,0:T(8,128)S(1)} %collective-permute-done.13.refs_0_) | copy-start | bytes 2752516
  138.7 2.5 %collective-permute-start.14 = (f32[14,128,128]{2,1,0:T(8,128)S(1)}, f32[14,128,128]{2,1,0:T(8,128)S(1)}, u32[]{:S(2)}, u32[]{:S(2)}) collective-permute-start(f32[14,128,128]{2,1,0:T(8,128)S(1)} %collective-permute-done.13.refs_0_), channel_id=1, source_target_pairs={{0,1},{1,0},{2,3},{3,2},{4,5},{5,4},{6,7},{7,6},{8,9},{9,8},{10,11... | collective-permute-start | bytes 2752520 | tf_op jit(solution)/shard_map/ppermute | solution.py:19
  141.2 0.9 copy-start.5
  146.3 28.5 %all-to-all-start.1 = ((f32[16,128,128]{2,1,0:T(8,128)}), f32[16,128,128]{2,1,0:T(8,128)S(1)}, u32[]{:S(2)}, u32[]{:S(2)}) async-start(f32[16,128,128]{2,1,0:T(8,128)} %get-tuple-element.36.refs_5_), calls=%async_computation.1 | async-start | bytes 2097152 | tf_op jit(solution)/shard_map/all_to_all | solution.py:326
  174.8 6.4 %copy-start.2 = (f32[16,128,128]{2,1,0:T(8,128)}, f32[16,128,128]{2,1,0:T(8,128)S(1)}, u32[]{:S(2)}) copy-start(f32[16,128,128]{2,1,0:T(8,128)S(1)} %all-to-all-done.1.first_ref) | copy-start | bytes 3145732
  174.8 52.4 %all-to-all-start.2 = ((f32[16,2,128,128]{3,2,1,0:T(8,128)}), f32[16,2,128,128]{3,2,1,0:T(8,128)S(1)}, u32[]{:S(2)}, u32[]{:S(2)}) async-start(f32[16,2,128,128]{3,2,1,0:T(8,128)} %later.1), calls=%async_computation.2 | async-start | bytes 4194304 | tf_op jit(solution)/shard_map/all_to_all | solution.py:326
  227.1 1.3 copy-start.1

commit v10 on v8

v10 whole, which is shorter than its diff:
```python
import functools

import jax
import jax.numpy as jnp
from jax import lax
from jax.experimental import pallas as pl
from jax.experimental.pallas import tpu as pltpu
from jax.sharding import PartitionSpec as P

REACH = 7
NOTE = 8
VMEM_LIMIT = 60 * 1024 * 1024
WINDOW = 2 * REACH + 1
GROUP = 5
PIECES = (96, 32)
SMEM = pl.BlockSpec(memory_space=pltpu.SMEM)
ANY = pl.BlockSpec(memory_space=pl.ANY)


def cycle_of(total):
    if total != 16:
        return list(range(total))
    chips = (0, 2, 4, 6, 7, 5, 3, 1)
    return [2 * chip + core for chip in chips for core in (0, 1)]


def after(x, *others):
    return lax.optimization_barrier((x, *others))[0]


def place_of(offset, dropped):
    named = jnp.logical_and(offset <= 2 * REACH, offset != dropped)
    slot = offset - jnp.where(offset > dropped, 1, 0)
    return jnp.clip(slot, 0, 2 * REACH - 1), named


def dropped_offset(cols, row, total):
    offsets = jnp.mod(cols - row + REACH, total)
    return REACH * (2 * REACH + 1) - jnp.sum(offsets, axis=1)


def pack_kernel(total, info_ref, cols_ref, cur_ref, prev_ref, send_ref, cur, prev, zeros, note, sems):
    row = info_ref[0]
    drop = info_ref[2]
    count, size = cur.shape[:2]
    loads = (
        pltpu.make_async_copy(cur_ref, cur, sems.at[0]),
        pltpu.make_async_copy(prev_ref, prev, sems.at[1]),
    )
    for load in loads:
        load.start()
    zeros[...] = jnp.zeros_like(zeros)
    line = lax.broadcasted_iota(jnp.int32, note.shape, 0)
    note[...] = jnp.where(line == 0, info_ref[1], drop).astype(jnp.float32)

    def fill(j, carry):
        offset = lax.rem(j - row + REACH + total, total)
        _, named = place_of(offset, drop)
        pltpu.make_async_copy(note, send_ref.at[j, pl.ds(2 * size, NOTE)], sems.at[2]).start()

        @pl.when(jnp.logical_not(named))
        def _():
            pltpu.make_async_copy(zeros, send_ref.at[j, pl.ds(0, 2 * size)], sems.at[2]).start()

        return carry

    lax.fori_loop(0, total, fill, 0)
    for which, held in enumerate((cur, prev)):
        loads[which].wait()
        for k in range(count):
            place = send_ref.at[cols_ref[k], pl.ds(which * size, size)]
            pltpu.make_async_copy(held.at[k], place, sems.at[2]).start()
    pltpu.make_async_copy(send_ref, send_ref, sems.at[2]).wait()


def split(x):
    high = x.astype(jnp.bfloat16)
    low = (x - high.astype(jnp.float32)).astype(jnp.bfloat16)
    return high, low


def kept_rows(total, rows_ref, drops_ref, w):
    row = rows_ref[w]
    offset = lax.rem(rows_ref[rows_ref.shape[0] - 1] - row + REACH + total, total)
    _, named = place_of(offset, drops_ref[2 * row + 1])
    return named


def fill_pair(pair, block, w):
    size = block.shape[-1]
    high, low = split(block)
    at = pl.ds(pl.multiple_of(w * size, size), size)
    pair[at, pl.ds(0, size)] = high
    pair[at, pl.ds(size, size)] = low


def products_of(rows, pair, pieces):
    group, double = rows.shape[:2]
    size = pair.shape[1] // 2
    products = jnp.dot(rows.reshape(group * double, rows.shape[2]), pair, preferred_element_type=jnp.float32)
    for r in range(group):
        start = r * double
        for piece in pieces:
            parts = products[start:start + piece] + products[start + piece:start + 2 * piece]
            yield r, parts[:, :size] + parts[:, size:]
            start += 2 * piece


def first_kernel(total, begin, piece, drops_ref, rows_ref, places_ref, t_ref, h_ref, *refs):
    if begin:
        pair_in, _, dense_ref, out_ref = refs[:4]
    else:
        dense_ref, out_ref, pair_out, blocks = refs[:4]
    stage, dense, prev, pair, h_sem, t_sem, prev_sem, pair_sem, dense_sem, out_sem = refs[-10:]
    size = t_ref.shape[-1]
    kept = functools.partial(kept_rows, total, rows_ref, drops_ref)

    if begin:
        pltpu.make_async_copy(pair_in, pair, pair_sem).start()
    else:
        for w in range(WINDOW):
            pltpu.make_async_copy(t_ref.at[rows_ref[w], pl.ds(0, size)], blocks.at[w], t_sem).start()
    for w in range(WINDOW):
        pltpu.make_async_copy(h_ref.at[places_ref[w]], stage.at[w], h_sem.at[w]).start()
    for w in range(WINDOW):
        lines = t_ref.at[rows_ref[w], pl.ds(size + begin, piece)]
        pltpu.make_async_copy(lines, prev.at[w], prev_sem).start()
    if not begin:
        pltpu.make_async_copy(blocks, blocks, t_sem).wait()
        for w in range(WINDOW):
            fill_pair(pair, jnp.where(kept(w), blocks[w], 0.0), w)
        pltpu.make_async_copy(pair, pair_out, pair_sem).start()

    def densify(w, slot, place):
        row = rows_ref[w]
        drop = drops_ref[2 * row]
        for p in range(WINDOW):
            offset = lax.rem(p - w + REACH + total, total)
            k, named = place_of(offset, drop)
            high, low = split(jnp.where(named, stage[w, k], 0.0))
            dense[slot, place, pl.ds(0, piece), pl.ds(p * size, size)] = high
            dense[slot, place, pl.ds(piece, piece), pl.ds(p * size, size)] = low

    def store(g, slot):
        return pltpu.make_async_copy(dense.at[slot], dense_ref.at[pl.ds(g * GROUP, GROUP)], dense_sem.at[slot])

    groups = WINDOW // GROUP

    def one(g, carry):
        slot = lax.rem(g, 2)

        @pl.when(g >= 2)
        def _():
            store(g - 2, slot).wait()

        for place in range(GROUP):
            w = g * GROUP + place
            pltpu.make_async_copy(stage.at[w], stage.at[w], h_sem.at[w]).wait()
            densify(w, slot, place)
        store(g, slot).start()

        @pl.when(g == 0)
        def _():
            if begin:
                pltpu.make_async_copy(pair, pair, pair_sem).wait()
            pltpu.make_async_copy(prev, prev, prev_sem).wait()

        for place, product in products_of(dense[slot], pair[...], (piece,)):
            w = g * GROUP + place
            prev[w] = jnp.where(kept(w), 2.0 * product - prev[w], 0.0)
            pltpu.make_async_copy(prev.at[w], out_ref.at[rows_ref[w], pl.ds(begin, piece)], out_sem).start()
        return carry

    lax.fori_loop(0, groups, one, 0)
    for g in range(groups - 2, groups):
        store(g, g % 2).wait()
    if not begin:
        pltpu.make_async_copy(pair, pair, pair_sem).wait()
    pltpu.make_async_copy(prev, prev, out_sem).wait()


def later_kernel(total, drops_ref, rows_ref, *refs):
    dense_refs = refs[:len(PIECES)]
    t_ref, first_ref, out_ref, dense, terms, pairs, dense_sem, t_sem, first_sem, out_sem = refs[len(PIECES):]
    size = terms.shape[-1]
    groups = WINDOW // GROUP
    kept = functools.partial(kept_rows, total, rows_ref, drops_ref)
    for w in range(WINDOW):
        pltpu.make_async_copy(first_ref.at[rows_ref[w]], terms.at[w, 1], first_sem).start()
    for g in range(groups):
        begin = 0
        at = pl.ds(g * GROUP, GROUP)
        for piece, dense_ref in zip(PIECES, dense_refs):
            place = dense.at[at, pl.ds(2 * begin, 2 * piece)]
            pltpu.make_async_copy(dense_ref.at[at], place, dense_sem.at[g]).start()
            begin += piece
    for w in range(WINDOW):
        pltpu.make_async_copy(t_ref.at[rows_ref[w], pl.ds(0, size)], terms.at[w, 0], t_sem).start()
    pltpu.make_async_copy(terms.at[:, 1], terms.at[:, 1], first_sem).wait()
    for w in range(WINDOW):
        fill_pair(pairs.at[0], terms[w, 1], w)
    pltpu.make_async_copy(terms.at[:, 0], terms.at[:, 0], t_sem).wait()

    def one(g, carry, step):
        rows = dense.at[pl.ds(g * GROUP, GROUP)]
        if step == 0:
            pltpu.make_async_copy(rows, rows, dense_sem.at[g]).wait()
        begin = 0
        for r, product in products_of(rows[...], pairs[step], PIECES):
            w = g * GROUP + r
            lines = pl.ds(begin, product.shape[0])
            terms[w, step, lines] = jnp.where(kept(w), 2.0 * product - terms[w, step, lines], 0.0)
            begin += product.shape[0]
            if begin == size:
                begin = 0
                if step == 0:
                    fill_pair(pairs.at[1], terms[w, step], w)
                pltpu.make_async_copy(terms.at[w, step], out_ref.at[rows_ref[w], step], out_sem).start()
        return carry

    for step in range(2):
        lax.fori_loop(0, groups, functools.partial(one, step=step), 0)
    pltpu.make_async_copy(terms, terms, out_sem).wait()


def unpack_first_kernel(cols_ref, coefs_ref, first_ref, density_ref, out_ref, sums, one, sems):
    load = pltpu.make_async_copy(density_ref, sums, sems.at[0])
    load.start()
    for k in range(cols_ref.shape[0]):
        pltpu.make_async_copy(first_ref.at[cols_ref[k]], one.at[k], sems.at[1]).start()
    load.wait()
    pltpu.make_async_copy(one, one, sems.at[1]).wait()
    sums[...] += coefs_ref[0] * one[...]
    store = pltpu.make_async_copy(sums, out_ref, sems.at[0])
    store.start()
    store.wait()


def unpack_last_kernel(cols_ref, coefs_ref, held_ref, sum_ref, density_ref, last_ref, before_ref, sums, two, three, sems):
    load = pltpu.make_async_copy(sum_ref, sums, sems.at[0])
    load.start()
    for place, sem, which in ((two, 1, 0), (three, 2, 1)):
        for k in range(cols_ref.shape[0]):
            pltpu.make_async_copy(held_ref.at[cols_ref[k], which], place.at[k], sems.at[sem]).start()
    pltpu.make_async_copy(two, two, sems.at[1]).wait()
    before = pltpu.make_async_copy(two, before_ref, sems.at[1])
    before.start()
    pltpu.make_async_copy(three, three, sems.at[2]).wait()
    last = pltpu.make_async_copy(three, last_ref, sems.at[2])
    last.start()
    load.wait()
    sums[...] = sums[...] + coefs_ref[1] * two[...] + coefs_ref[2] * three[...]
    store = pltpu.make_async_copy(sums, density_ref, sems.at[0])
    store.start()
    before.wait()
    last.wait()
    store.wait()


def per_device(h_blocks, h_cols, term_prev, term_cur, t_cols, density_in, coefs):
    total = lax.axis_size("row")
    me = lax.axis_index("row")
    count, size = h_blocks.shape[1:3]
    drop_h = dropped_offset(h_cols, me, total)
    drop_t = dropped_offset(t_cols, me, total)
    f32, bf16 = jnp.float32, jnp.bfloat16
    dma = pltpu.SemaphoreType.DMA
    row = jax.ShapeDtypeStruct((count, size, size), f32)
    row_scratch = pltpu.VMEM(row.shape, f32)

    def call(kernel, smem, arrays, outs, scratch, name, aliases={}):
        return pl.pallas_call(
            kernel,
            out_shape=outs,
            in_specs=[SMEM] * len(smem) + [ANY] * len(arrays),
            out_specs=[ANY] * len(outs),
            scratch_shapes=scratch,
            input_output_aliases=aliases,
            compiler_params=pltpu.CompilerParams(vmem_limit_bytes=VMEM_LIMIT),
            name=name,
        )(*smem, *arrays)

    def exchange(x):
        return lax.all_to_all(x, "row", 0, 0, tiled=True)

    (send,) = call(
        functools.partial(pack_kernel, total),
        [jnp.stack([me, drop_h[0], drop_t[0]]), t_cols[0]],
        [term_cur[0], term_prev[0]],
        [jax.ShapeDtypeStruct((total, 2 * size + NOTE, size), f32)],
        [
            row_scratch,
            row_scratch,
            pltpu.VMEM((2 * size, size), f32),
            pltpu.VMEM((NOTE, size), f32),
            dma((3,)),
        ],
        "pack",
    )
    cycle = cycle_of(total)
    indices = jnp.mod(me + jnp.arange(-REACH, REACH + 1, dtype=jnp.int32), total)
    places = jnp.array([cycle.index(i) for i in range(total)], jnp.int32)[indices]
    column = exchange(send)
    drops = column[:, 2 * size:2 * size + 2, 0].astype(jnp.int32).reshape(-1)
    rows = jnp.concatenate([indices, me[None]])
    pair_shape = (WINDOW * size, 2 * size)
    dense = []
    begin = 0
    for piece in PIECES:
        h_piece = h_blocks[:, :, begin:begin + piece]
        if begin:
            h_piece = after(h_piece, h_all)
        h_all = lax.all_gather(h_piece, "row", axis=0, tiled=True, axis_index_groups=[cycle])
        scratch = [
            pltpu.VMEM((WINDOW, count, piece, size), f32),
            pltpu.VMEM((2, GROUP, 2 * piece, WINDOW * size), bf16),
            pltpu.VMEM((WINDOW, piece, size), f32),
            pltpu.VMEM(pair_shape, bf16),
            dma((WINDOW,)),
            dma,
            dma,
            dma,
            dma((2,)),
            dma,
        ]
        if not begin:
            scratch = [pltpu.VMEM((WINDOW, size, size), f32)] + scratch
        result = call(
            functools.partial(first_kernel, total, begin, piece),
            [drops, rows, places],
            [column, h_all] + ([pair, term1] if begin else []),
            [
                jax.ShapeDtypeStruct((WINDOW, 2 * piece, WINDOW * size), bf16),
                jax.ShapeDtypeStruct((total, size, size), f32),
            ] + ([] if begin else [jax.ShapeDtypeStruct(pair_shape, bf16)]),
            scratch,
            "first",
            {6: 1} if begin else {},
        )
        dense.append(result[0])
        term1 = result[1]
        if not begin:
            pair = result[2]
        begin += piece
    back1 = exchange(term1)
    (terms,) = call(
        functools.partial(later_kernel, total),
        [drops, rows],
        [*dense, column, term1],
        [jax.ShapeDtypeStruct((total, 2, size, size), f32)],
        [
            pltpu.VMEM((WINDOW, 2 * size, WINDOW * size), bf16),
            pltpu.VMEM((WINDOW, 2, size, size), f32),
            pltpu.VMEM((2,) + pair_shape, bf16),
            dma((WINDOW // GROUP,)),
            dma,
            dma,
            dma,
        ],
        "later",
    )
    back = exchange(after(terms, back1))
    (sums,) = call(
        unpack_first_kernel,
        [t_cols[0], coefs],
        [back1, density_in[0]],
        [row],
        [row_scratch, row_scratch, dma((2,))],
        "unpack_first",
    )
    density, last, before = call(
        unpack_last_kernel,
        [t_cols[0], coefs],
        [back, sums],
        [row] * 3,
        [row_scratch, row_scratch, row_scratch, dma((3,))],
        "unpack_last",
    )
    return density[None], last[None], before[None]


def solution(mesh):
    blocks = P(("groups", "row"), None, None, None)
    cols = P(("groups", "row"), None)
    return jax.shard_map(
        per_device,
        mesh=mesh,
        in_specs=(blocks, cols, blocks, blocks, cols, blocks, P()),
        out_specs=(blocks, blocks, blocks),
        check_vma=False,
    )
```

time: 252 us -> 263 us (1.044)
  between operations: 2.09 us -> 15.5 us
  waiting for transfers between devices: 164 us -> 172 us
  starting transfers between devices: 26.1 us -> 18.6 us
  Pallas kernels: 50.8 us -> 44.5 us
  local copies, waits for them, and re-layouts: 3.93 us -> 7.24 us
    ppermute x15 -> x0, waiting for transfers between devices: 115 us -> none  [permute(): return lax.ppermute(x, 'row', [(i, target(i)) for i in range(devices)])]
    all_gather x0 -> x2, waiting for transfers between devices: none -> 62.1 us  [per_device(): lax.all_gather(h_piece, 'row', axis=0, tiled=True, axis_index_groups=[cyc...]
    all_to_all x3, waiting for transfers between devices: 48.4 us -> 110 us  [exchange(): return lax.all_to_all(x, 'row', 0, 0, tiled=True)]
    ppermute x15 -> x0, starting transfers between devices: 7.97 us -> none  [permute(): return lax.ppermute(x, 'row', [(i, target(i)) for i in range(devices)])]
    pallas_call x8 -> x6, Pallas kernels: 50.8 us -> 44.5 us  [call(): pl.pallas_call(kernel, out_shape=outs, in_specs=[SMEM] * len(smem) + [ANY...]
    slice x0 -> x2, local copies, waits for them, and re-layouts: none -> 3.65 us  [per_device(): h_piece = h_blocks[:, :, begin:begin + piece]]
  transfers between devices with their start and end apart: 18 -> 5, of which waited for: 10 -> 4; matrix products, arithmetic and copies ran while one was open for 1% -> 2% of each run, Pallas kernels for 16% -> 13%
where the time goes in v10:
time: 263 us; the launch traced here: 260 us
  waiting for transfers between devices  172 us (65%)
  Pallas kernels  44.5 us (17%)
  starting transfers between devices  18.6 us (7%)
  between operations  15.5 us (6%)
  local copies, waits for them, and re-layouts  7.24 us (3%)
    all_to_all x3, waiting for transfers between devices, exchange(): return lax.all_to_all(x, 'row', 0, 0, tiled=True)  110 us
    all_gather x2, waiting for transfers between devices, per_device(): lax.all_gather(h_piece, 'row', axis=0, tiled=True, axis_index_groups=[cyc...  62.1 us
    pallas_call x6, Pallas kernels, call(): pl.pallas_call(kernel, out_shape=outs, in_specs=[SMEM] * len(smem) + [ANY...  44.5 us
    all_to_all x3, starting transfers between devices, exchange(): return lax.all_to_all(x, 'row', 0, 0, tiled=True)  18.5 us
  transfers between devices with their start and end apart: 5, of which 4 were waited for; matrix products, arithmetic and copies ran while one was open for 2% of the time, Pallas kernels for 13%

profile of v10, /device:TPU:22, one launch (start us, length us, event | category | flops | bytes accessed | tf_op | source)
XLA Modules:
  0.0 260.1 jit_solution(6587831686753075166)
XLA Ops:
  7.2 0.0 copy-start.4
  7.2 0.0 copy-start.5
  7.2 0.0 all-gather.3.cloned.1.call-start
  7.2 2.0 slice.10
  9.2 0.0 all-gather.3.cloned.1.call-update
  9.3 0.0 all-gather.5.cloned.1.call-start
  9.3 1.7 slice.11
  11.0 62.1 %all-gather.3.cloned.1.call-done.h_ref = f32[16,14,96,128]{3,2,1,0:T(8,128)} async-done(((f32[1,14,96,128]{3,2,1,0:T(8,128)}), f32[16,14,96,128]{3,2,1,0:T(8,128)}) %all-gather.3.cloned.1.call-update) | async-done | bytes 11010064 | tf_op jit(solution)/shard_map/all_gather | solution.py:313
  73.0 0.0 all-gather.5.cloned.1.call-update
  73.1 0.0 copy-done.4
  73.1 0.0 copy-done.5
  73.1 0.7 fusion.1
  75.1 0.7 pad_add_fusion.info_ref
  75.7 3.2 %pack.1 = f32[16,264,128]{2,1,0:T(8,128)} custom-call(s32[3]{0:T(128)} %pad_add_fusion.info_ref, s32[14]{0:T(128)} %bitcast.15, f32[14,128,128]{2,1,0:T(8,128)} %bitcast.12, f32[14,128,128]{2,1,0:T(8,128)} %bitcast.13), custom_call_target="tpu_custom_call" | custom-call | tf_op jit(solution)/shard_map/pack/pallas_call | solution.py:272
  79.0 0.0 copy-start
  79.0 5.3 %all-to-all-start = ((f32[16,264,128]{2,1,0:T(8,128)}), f32[16,264,128]{2,1,0:T(8,128)S(1)}, u32[]{:S(2)}, u32[]{:S(2)}) async-start(f32[16,264,128]{2,1,0:T(8,128)} %pack.1), calls=%async_computation | async-start | bytes 4325376 | tf_op jit(solution)/shard_map/all_to_all | solution.py:284
  84.3 0.0 copy-done
  84.3 1.2 gather_fusion
  85.5 0.6 pad_add_fusion.1.rows_ref
  86.1 60.1 %all-to-all-done.t_ref.refs_2_ = f32[16,264,128]{2,1,0:T(8,128)S(1)} async-done(((f32[16,264,128]{2,1,0:T(8,128)}), f32[16,264,128]{2,1,0:T(8,128)S(1)}, u32[]{:S(2)}, u32[]{:S(2)}) %all-to-all-start) | async-done | bytes 2162720 | tf_op jit(solution)/shard_map/all_to_all | solution.py:284
  146.2 0.0 copy-start.1
  146.2 0.3 fusion
  146.5 0.9 convert_element_type.8.drops_ref
  147.4 0.1 copy-done.1
  147.5 11.6 %first.2 = (bf16[15,192,1920]{2,1,0:T(8,128)(2,1)}, f32[16,128,128]{2,1,0:T(8,128)}, bf16[1920,256]{1,0:T(8,128)(2,1)}) custom-call(s32[32]{0:T(128)} %convert_element_type.8.drops_ref, s32[16]{0:T(128)} %pad_add_fusion.1.rows_ref, s32[15]{0:T(128)} %gather_fusion, f32[16,264,128]{2,1,0:T(8,128)} %copy-done.1, ...), custom_call_target="tpu_custom_call" | custom-call | tf_op jit(solution)/shard_map/first/pallas_call | solution.py:272
  159.1 0.0 all-gather.5.cloned.1.call-done.h_ref
  159.2 6.6 %first.3 = (bf16[15,64,1920]{2,1,0:T(8,128)(2,1)}, f32[16,128,128]{2,1,0:T(8,128)}) custom-call(s32[32]{0:T(128)} %convert_element_type.8.drops_ref, s32[16]{0:T(128)} %pad_add_fusion.1.rows_ref, s32[15]{0:T(128)} %gather_fusion, f32[16,264,128]{2,1,0:T(8,128)} %copy-done.1, ...), custom_call_target="tpu_custom_call", output_to_operand_aliasing={{1}: (6, {})} | custom-call | tf_op jit(solution)/shard_map/first/pallas_call | solution.py:272
  165.7 6.8 %all-to-all-start.1 = ((f32[16,128,128]{2,1,0:T(8,128)}), f32[16,128,128]{2,1,0:T(8,128)S(1)}, u32[]{:S(2)}, u32[]{:S(2)}) async-start(f32[16,128,128]{2,1,0:T(8,128)} %get-tuple-element.18.refs_3_), calls=%async_computation.1 | async-start | bytes 2097152 | tf_op jit(solution)/shard_map/all_to_all | solution.py:284
  172.6 16.4 %later.1 = f32[16,2,128,128]{3,2,1,0:T(8,128)} custom-call(s32[32]{0:T(128)} %convert_element_type.8.drops_ref, s32[16]{0:T(128)} %pad_add_fusion.1.rows_ref, bf16[15,192,1920]{2,1,0:T(8,128)(2,1)} %get-tuple-element.13.refs_0_, bf16[15,64,1920]{2,1,0:T(8,128)(2,1)} %get-tuple-element.17.refs_1_, f32[16,264,128]{2,1,0:T(8,128)} %copy-done.1, ...), custom_call_target="tpu_custom_call" | custom-call | tf_op jit(solution)/shard_map/later/pallas_call | solution.py:272
  189.0 7.0 %all-to-all-done.1.first_ref = f32[16,128,128]{2,1,0:T(8,128)S(1)} async-done(((f32[16,128,128]{2,1,0:T(8,128)}), f32[16,128,128]{2,1,0:T(8,128)S(1)}, u32[]{:S(2)}, u32[]{:S(2)}) %all-to-all-start.1) | async-done | bytes 1048608 | tf_op jit(solution)/shard_map/all_to_all | solution.py:284
  196.0 0.0 copy-start.3
  196.0 6.4 %all-to-all-start.2 = ((f32[16,2,128,128]{3,2,1,0:T(8,128)}), f32[16,2,128,128]{3,2,1,0:T(8,128)S(1)}, u32[]{:S(2)}, u32[]{:S(2)}) async-start(f32[16,2,128,128]{3,2,1,0:T(8,128)} %later.1), calls=%async_computation.2 | async-start | bytes 4194304 | tf_op jit(solution)/shard_map/all_to_all | solution.py:284
  202.4 0.0 copy-done.3
  202.4 3.1 %unpack_first.1.sum_ref = f32[14,128,128]{2,1,0:T(8,128)} custom-call(s32[14]{0:T(128)} %bitcast.16, f32[3]{0:T(128)} %coefs_ref.3, f32[16,128,128]{2,1,0:T(8,128)} %copy-done.3, f32[14,128,128]{2,1,0:T(8,128)} %bitcast.14), custom_call_target="tpu_custom_call" | custom-call | tf_op jit(solution)/shard_map/unpack_first/pallas_call | solution.py:272
  205.5 42.8 %all-to-all-done.2.held_ref = f32[16,2,128,128]{3,2,1,0:T(8,128)S(1)} async-done(((f32[16,2,128,128]{3,2,1,0:T(8,128)}), f32[16,2,128,128]{3,2,1,0:T(8,128)S(1)}, u32[]{:S(2)}, u32[]{:S(2)}) %all-to-all-start.2) | async-done | bytes 2097184 | tf_op jit(solution)/shard_map/all_to_all | solution.py:284
  248.3 0.0 copy-start.2
  248.3 1.3 copy-done.2
  249.6 3.6 %unpack_last.1 = (f32[14,128,128]{2,1,0:T(8,128)}, f32[14,128,128]{2,1,0:T(8,128)}, f32[14,128,128]{2,1,0:T(8,128)}) custom-call(s32[14]{0:T(128)} %bitcast.17, f32[3]{0:T(128)} %coefs_ref.3, f32[16,2,128,128]{3,2,1,0:T(8,128)} %copy-done.2, f32[14,128,128]{2,1,0:T(8,128)} %unpack_first.1.sum_ref), custom_call_target="tpu_custom_call" | custom-call | tf_op jit(solution)/shard_map/unpack_last/pallas_call | solution.py:272
  (3 shorter events, 0.0 us)
Async XLA Ops:
  7.2 65.9 %copy-start.4 = (s32[1,14]{1,0:T(1,128)S(1)}, s32[1,14]{1,0:T(1,128)}, u32[]{:S(2)}) copy-start(s32[1,14]{1,0:T(1,128)} %param.12) | copy-start | bytes 172
  7.2 65.9 %copy-start.5 = (s32[1,14]{1,0:T(1,128)S(1)}, s32[1,14]{1,0:T(1,128)}, u32[]{:S(2)}) copy-start(s32[1,14]{1,0:T(1,128)} %param.9) | copy-start | bytes 172
  7.2 65.9 %all-gather.3.cloned.1.call-start = ((), (), s32[]{:S(2)}) async-start(), calls=%async_computation.3 | async-start | bytes 11698176 | tf_op jit(solution)/shard_map/all_gather | solution.py:313
  9.3 149.9 %all-gather.5.cloned.1.call-start = ((), (), s32[]{:S(2)}) async-start(), calls=%async_computation.4 | async-start | bytes 3899392 | tf_op jit(solution)/shard_map/all_gather | solution.py:313
  79.0 5.3 %copy-start = (s32[16]{0:T(128)S(1)}, s32[16]{0:T(128)}, u32[]{:S(2)}) copy-start(s32[16]{0:T(128)} %constant.47.clone) | copy-start | bytes 196
  79.0 67.2 %all-to-all-start = ((f32[16,264,128]{2,1,0:T(8,128)}), f32[16,264,128]{2,1,0:T(8,128)S(1)}, u32[]{:S(2)}, u32[]{:S(2)}) async-start(f32[16,264,128]{2,1,0:T(8,128)} %pack.1), calls=%async_computation | async-start | bytes 4325376 | tf_op jit(solution)/shard_map/all_to_all | solution.py:284
  146.2 1.4 copy-start.1
  165.7 30.2 %all-to-all-start.1 = ((f32[16,128,128]{2,1,0:T(8,128)}), f32[16,128,128]{2,1,0:T(8,128)S(1)}, u32[]{:S(2)}, u32[]{:S(2)}) async-start(f32[16,128,128]{2,1,0:T(8,128)} %get-tuple-element.18.refs_3_), calls=%async_computation.1 | async-start | bytes 2097152 | tf_op jit(solution)/shard_map/all_to_all | solution.py:284
  196.0 6.4 %copy-start.3 = (f32[16,128,128]{2,1,0:T(8,128)}, f32[16,128,128]{2,1,0:T(8,128)S(1)}, u32[]{:S(2)}) copy-start(f32[16,128,128]{2,1,0:T(8,128)S(1)} %all-to-all-done.1.first_ref) | copy-start | bytes 3145732
  196.0 52.4 %all-to-all-start.2 = ((f32[16,2,128,128]{3,2,1,0:T(8,128)}), f32[16,2,128,128]{3,2,1,0:T(8,128)S(1)}, u32[]{:S(2)}, u32[]{:S(2)}) async-start(f32[16,2,128,128]{3,2,1,0:T(8,128)} %later.1), calls=%async_computation.2 | async-start | bytes 4194304 | tf_op jit(solution)/shard_map/all_to_all | solution.py:284
  248.3 1.3 copy-start.2
Sparse Core Ops, SparseCore 0:
  10.2 62.8 all-gather.2
  75.2 64.8 all-gather.4

commit v11 on v9

--- a/solution.py
+++ b/solution.py
@@ -9,7 +9,6 @@
 
 REACH = 7
 NOTE = 8
-VMEM_LIMIT = 60 * 1024 * 1024
 SMEM = pl.BlockSpec(memory_space=pltpu.SMEM)
 ANY = pl.BlockSpec(memory_space=pl.ANY)
 
@@ -30,13 +29,15 @@
     return 2 * RING[(RING.index(device // 2) + by) % len(RING)] + device % 2
 
 
-def window_rows(me, total):
+LAST = 2
+
+
+def window_table(total):
     if total != 16:
         steps = [0] + [by for hop in range(1, REACH + 1) for by in (-hop, hop)]
-        return jnp.mod(me + jnp.array(steps, jnp.int32), total), (5, 4, 4, 2)
+        return [[(i + by) % total for by in steps] for i in range(total)], (5, 4, 4, LAST)
     order = (0, -1, 1, -2, 2, -3, 3, 4)
-    table = [[along_ring(i, by) ^ core for by in order for core in (0, 1)] for i in range(total)]
-    return jnp.array(table, jnp.int32)[me], (6, 4, 4, 2)
+    return [[along_ring(i, by) ^ core for by in order for core in (0, 1)] for i in range(total)], (6, 4, 4, LAST)
 
 
 def gathered_rows(x, me, total, exchange):
@@ -151,9 +152,11 @@
 
 def first_kernel(total, window, start, count, group, drops_ref, rows_ref, t_ref, *refs):
     h_refs = refs[:count]
-    if start:
-        pair_in, _ = refs[count:count + 2]
-        dense_ref, out_ref = refs[count + 2:count + 4]
+    last = start + count == window
+    if last:
+        pair_in, dense_ref, out_ref = refs[count:count + 3]
+    elif start:
+        pair_in, _, dense_ref, out_ref = refs[count:count + 4]
     else:
         dense_ref, out_ref, pair_out, blocks = refs[count:count + 4]
     stage, dense, prev, pair, h_sem, t_sem, prev_sem, pair_sem, dense_sem, out_sem = refs[-10:]
@@ -213,10 +216,11 @@
         def _():
             pltpu.make_async_copy(prev, prev, prev_sem).wait()
 
-        for place, product in enumerate(products_of(dense[slot], pair[...])):
-            r = g * group + place
+        for at, product in enumerate(products_of(dense[slot], pair[...])):
+            r = g * group + at
             prev[r] = jnp.where(kept(start + r), 2.0 * product - prev[r], 0.0)
-            pltpu.make_async_copy(prev.at[r], out_ref.at[rows_ref[start + r]], out_sem).start()
+            place = out_ref.at[r if last else rows_ref[start + r]]
+            pltpu.make_async_copy(prev.at[r], place, out_sem).start()
         return carry
 
     lax.fori_loop(0, groups, one, 0)
@@ -229,12 +233,14 @@
 
 def later_kernel(total, window, group, parts, drops_ref, rows_ref, *refs):
     dense_refs = refs[:len(parts)]
-    t_ref, first_ref, out_ref, dense, terms, pairs, dense_sem, t_sem, first_sem, out_sem = refs[len(parts):]
+    t_ref, first_ref, far_ref, out_ref, dense, terms, pairs, dense_sem, t_sem, first_sem, out_sem = refs[len(parts):]
     size = terms.shape[-1]
     groups = window // group
     kept = functools.partial(kept_rows, total, rows_ref, drops_ref)
     for w in range(window):
-        pltpu.make_async_copy(first_ref.at[rows_ref[w]], terms.at[w, 1], first_sem).start()
+        r = w - (window - LAST)
+        source = first_ref.at[rows_ref[w]] if r < 0 else far_ref.at[r]
+        pltpu.make_async_copy(source, terms.at[w, 1], first_sem).start()
     start = 0
     for part, dense_ref in zip(parts, dense_refs):
         for w in range(start, start + part):
@@ -265,11 +271,19 @@
     pltpu.make_async_copy(terms, terms, out_sem).wait()
 
 
-def unpack_first_kernel(cols_ref, coefs_ref, first_ref, density_ref, out_ref, sums, one, sems):
+def unpack_first_kernel(cols_ref, far_cols_ref, coefs_ref, first_ref, density_ref, far0_ref, far1_ref, out_ref, sums, one, sems):
     load = pltpu.make_async_copy(density_ref, sums, sems.at[0])
     load.start()
     for k in range(cols_ref.shape[0]):
-        pltpu.make_async_copy(first_ref.at[cols_ref[k]], one.at[k], sems.at[1]).start()
+        col = cols_ref[k]
+        far = [col == far_cols_ref[r] for r in range(LAST)]
+        choices = ((jnp.logical_not(jnp.logical_or(*far)), first_ref.at[col]), (far[0], far0_ref), (far[1], far1_ref))
+        for chosen, source in choices:
+
+            @pl.when(chosen)
+            def _(source=source, k=k):
+                pltpu.make_async_copy(source, one.at[k], sems.at[1]).start()
+
     load.wait()
     pltpu.make_async_copy(one, one, sems.at[1]).wait()
     sums[...] += coefs_ref[0] * one[...]
@@ -310,15 +324,15 @@
     row = jax.ShapeDtypeStruct((count, size, size), f32)
     row_scratch = pltpu.VMEM(row.shape, f32)
 
-    def call(kernel, smem, arrays, outs, scratch, name, aliases={}):
+    def call(kernel, smem, arrays, outs, scratch, name, megabytes=60, aliases={}):
         return pl.pallas_call(
             kernel,
-            out_shape=outs,
+            out_shape=[pltpu.HBM(out.shape, out.dtype) for out in outs],
             in_specs=[SMEM] * len(smem) + [ANY] * len(arrays),
             out_specs=[ANY] * len(outs),
             scratch_shapes=scratch,
             input_output_aliases=aliases,
-            compiler_params=pltpu.CompilerParams(vmem_limit_bytes=VMEM_LIMIT),
+            compiler_params=pltpu.CompilerParams(vmem_limit_bytes=megabytes * 1024 * 1024),
             name=name,
         )(*smem, *arrays)
 
@@ -339,12 +353,15 @@
         ],
         "pack",
     )
-    indices, parts = window_rows(me, total)
+    table, parts = window_table(total)
+    window = sum(parts)
+    far_targets = [[row[window - LAST + r] for row in table] for r in range(LAST)]
+    sources = [[targets.index(i) for targets in far_targets] for i in range(total)]
+    places = jnp.array([row + from_ for row, from_ in zip(table, sources)], jnp.int32)[me]
     gathered = gathered_rows(h_blocks[0], me, total, lambda *others: exchange(after(send, *others)))
     column = next(gathered)
     drops = column[:, 2 * size:2 * size + 2, 0].astype(jnp.int32).reshape(-1)
-    rows = jnp.concatenate([indices, me[None]])
-    window = sum(parts)
+    rows = jnp.concatenate([places[:window], me[None]])
     dense_shape = (window, 2 * size, window * size)
     pair_shape = (window * size, 2 * size)
     dense = []
@@ -354,7 +371,7 @@
         group = max(g for g in (2, 3, 4, 5) if part % g == 0)
         scratch = [
             pltpu.VMEM((part, count, size, size), f32),
-            pltpu.VMEM((2, group) + dense_shape[1:], bf16),
+            pltpu.VMEM((min(2, part // group), group) + dense_shape[1:], bf16),
             pltpu.VMEM((part, size, size), f32),
             pltpu.VMEM(pair_shape, bf16),
             dma((part,)),
@@ -366,29 +383,34 @@
         ]
         if not start:
             scratch = [pltpu.VMEM((window, size, size), f32)] + scratch
+        last = start + part == window
+        term = jax.ShapeDtypeStruct((LAST if last else total, size, size), f32)
         result = call(
             functools.partial(first_kernel, total, window, start, part, group),
             [drops, rows],
-            [column, *h_rows] + ([pair, term1] if start else []),
-            [
-                jax.ShapeDtypeStruct((part,) + dense_shape[1:], bf16),
-                jax.ShapeDtypeStruct((total, size, size), f32),
-            ] + ([] if start else [jax.ShapeDtypeStruct(pair_shape, bf16)]),
+            [column, *h_rows] + ([pair] if start else []) + ([term1] if start and not last else []),
+            [jax.ShapeDtypeStruct((part,) + dense_shape[1:], bf16), term]
+            + ([] if start else [jax.ShapeDtypeStruct(pair_shape, bf16)]),
             scratch,
             "first",
-            {part + 4: 1} if start else {},
+            24 if start + part + LAST >= window else 60,
+            {part + 4: 1} if start and not last else {},
         )
         dense.append(result[0])
-        term1 = result[1]
+        if last:
+            far = result[1]
+        else:
+            term1 = result[1]
         if not start:
             pair = result[2]
         start += part
     back1 = exchange(term1)
+    far_back = [permute(far[r], lambda i, r=r: far_targets[r][i]) for r in range(LAST)]
     group = max(g for g in (3, 4) if window % g == 0)
     (terms,) = call(
         functools.partial(later_kernel, total, window, group, parts),
         [drops, rows],
-        [*dense, column, term1],
+        [*dense, column, term1, far],
         [jax.ShapeDtypeStruct((total, 2, size, size), f32)],
         [
             pltpu.VMEM(dense_shape, bf16),
@@ -404,8 +426,8 @@
     back = exchange(after(terms, back1))
     (sums,) = call(
         unpack_first_kernel,
-        [t_cols[0], coefs],
-        [back1, density_in[0]],
+        [t_cols[0], places[window:], coefs],
+        [back1, density_in[0], *far_back],
         [row],
         [row_scratch, row_scratch, dma((2,))],
         "unpack_first",
@@ -417,6 +439,7 @@
         [row] * 3,
         [row_scratch, row_scratch, row_scratch, dma((3,))],
         "unpack_last",
+        14,
     )
     return density[None], last[None], before[None]
 

time: 235 us -> 277 us (1.18)
  waiting for transfers between devices: 142 us -> 181 us
  starting transfers between devices: 25.5 us -> 29 us
    ppermute x15 -> x17, waiting for transfers between devices: 93.9 us -> 181 us  [permute(): return lax.ppermute(x, 'row', [(i, target(i)) for i in range(devices)])]
    all_to_all x3, waiting for transfers between devices: 48.5 us -> 0.01 us  [exchange(): return lax.all_to_all(x, 'row', 0, 0, tiled=True)]
    ppermute x15 -> x17, starting transfers between devices: 7.81 us -> 11.8 us  [permute(): return lax.ppermute(x, 'row', [(i, target(i)) for i in range(devices)])]
    unnamed x26 -> x36, local copies, waits for them, and re-layouts: 7.03 us -> 4.74 us
  transfers between devices with their start and end apart: 18 -> 20, of which waited for: 11 -> 11; matrix products, arithmetic and copies ran while one was open for 2% -> 2% of each run, Pallas kernels for 19% -> 15%
where the time goes in v11:
time: 277 us; the launch traced here: 274 us
  waiting for transfers between devices  181 us (65%)
  Pallas kernels  50.8 us (18%)
  starting transfers between devices  29 us (10%)
  local copies, waits for them, and re-layouts  6.77 us (2%)
  other arithmetic  4.14 us (1%)
    ppermute x17, waiting for transfers between devices, permute(): return lax.ppermute(x, 'row', [(i, target(i)) for i in range(devices)])  181 us
    pallas_call x8, Pallas kernels, call(): pl.pallas_call(kernel, out_shape=[pltpu.HBM(out.shape, out.dtype) for out...  50.8 us
    all_to_all x3, starting transfers between devices, exchange(): return lax.all_to_all(x, 'row', 0, 0, tiled=True)  17.2 us
    ppermute x17, starting transfers between devices, permute(): return lax.ppermute(x, 'row', [(i, target(i)) for i in range(devices)])  11.8 us
  transfers between devices with their start and end apart: 20, of which 11 were waited for; matrix products, arithmetic and copies ran while one was open for 2% of the time, Pallas kernels for 15%

profile of v11, /device:TPU:22, one launch (start us, length us, event | category | flops | bytes accessed | tf_op | source)
XLA Modules:
  0.0 273.8 jit_solution(13367320873399620704)
XLA Ops:
  0.6 0.5 collective-permute-start
  1.1 1.6 collective-permute-start.1
  2.7 1.3 fusion.1
  5.3 0.6 pad_add_fusion.info_ref
  5.9 3.2 %pack.1 = f32[16,264,128]{2,1,0:T(8,128)} custom-call(s32[3]{0:T(128)} %pad_add_fusion.info_ref, s32[14]{0:T(128)} %bitcast.19, f32[14,128,128]{2,1,0:T(8,128)} %bitcast.22, f32[14,128,128]{2,1,0:T(8,128)} %bitcast.23), custom_call_target="tpu_custom_call" | custom-call | tf_op jit(solution)/shard_map/pack/pallas_call | solution.py:328
  9.2 13.8 %collective-permute-done.refs_2_ = f32[14,128,128]{2,1,0:T(8,128)S(1)} collective-permute-done((f32[14,128,128]{2,1,0:T(8,128)}, f32[14,128,128]{2,1,0:T(8,128)S(1)}, u32[]{:S(2)}, u32[]{:S(2)}) %collective-permute-start) | collective-permute-done | bytes 917536 | tf_op jit(solution)/shard_map/ppermute | solution.py:18
  23.2 0.8 copy-done.9
  23.9 0.3 copy-done.10
  24.2 6.1 %all-to-all-start = ((f32[16,264,128]{2,1,0:T(8,128)}), f32[16,264,128]{2,1,0:T(8,128)S(1)}, u32[]{:S(2)}, u32[]{:S(2)}) async-start(f32[16,264,128]{2,1,0:T(8,128)} %pack.1), calls=%async_computation | async-start | bytes 4325376 | tf_op jit(solution)/shard_map/all_to_all | solution.py:340
  30.3 0.2 collective-permute-start.2
  30.5 0.4 collective-permute-start.3
  31.1 0.6 collective-permute-start.5
  31.6 1.5 collective-permute-start.7
  33.1 1.3 collective-permute-done.3.refs_3_
  34.4 1.3 collective-permute-done.4.refs_5_
  35.7 0.9 copy-done.13
  36.6 60.8 %collective-permute-done.5.refs_0_ = f32[14,128,128]{2,1,0:T(8,128)} collective-permute-done((f32[14,128,128]{2,1,0:T(8,128)}, f32[14,128,128]{2,1,0:T(8,128)}, u32[]{:S(2)}, u32[]{:S(2)}) %collective-permute-start.5) | collective-permute-done | bytes 917536 | tf_op jit(solution)/shard_map/ppermute | solution.py:18
  97.4 2.5 collective-permute-start.9
  99.9 0.5 collective-permute-start.8
  100.4 19.2 %collective-permute-done.9.refs_0_ = f32[14,128,128]{2,1,0:T(8,128)} collective-permute-done((f32[14,128,128]{2,1,0:T(8,128)}, f32[14,128,128]{2,1,0:T(8,128)}, u32[]{:S(2)}, u32[]{:S(2)}) %collective-permute-start.9) | collective-permute-done | bytes 917536 | tf_op jit(solution)/shard_map/ppermute | solution.py:18
  119.6 2.2 collective-permute-done.11.refs_2_
  121.8 0.7 constant_dynamic-slice_fusion
  122.5 0.6 pad_add_fusion.1.rows_ref
  123.1 0.3 fusion
  123.5 0.7 convert_element_type.8.drops_ref
  124.2 8.0 %first.4 = (bf16[6,256,2048]{2,1,0:T(8,128)(2,1)}, f32[16,128,128]{2,1,0:T(8,128)}, bf16[2048,256]{1,0:T(8,128)(2,1)}) custom-call(s32[32]{0:T(128)} %convert_element_type.8.drops_ref, s32[17]{0:T(128)} %pad_add_fusion.1.rows_ref, f32[16,264,128]{2,1,0:T(8,128)} %copy-done, f32[14,128,128]{2,1,0:T(8,128)} %bitcast.27, f32[14,128,128]{2,1,0:T(8,128)} %copy-done.11, ...), custom_call_target="tpu_custom_call" | custom-call | tf_op jit(solution)/shard_map/first/pallas_call | solution.py:328
  132.2 0.9 copy-done.14
  133.1 5.8 %first.5 = (bf16[4,256,2048]{2,1,0:T(8,128)(2,1)}, f32[16,128,128]{2,1,0:T(8,128)}) custom-call(s32[32]{0:T(128)} %convert_element_type.8.drops_ref, s32[17]{0:T(128)} %pad_add_fusion.1.rows_ref, f32[16,264,128]{2,1,0:T(8,128)} %copy-done, f32[14,128,128]{2,1,0:T(8,128)} %collective-permute-done.5.refs_0_, ...), custom_call_target="tpu_custom_call", output_to_operand_aliasing={{1}: (8, {})} | custom-call | tf_op jit(solution)/shard_map/first/pallas_call | solution.py:328
  139.0 5.0 %first.6 = (bf16[4,256,2048]{2,1,0:T(8,128)(2,1)}, f32[16,128,128]{2,1,0:T(8,128)}) custom-call(s32[32]{0:T(128)S(1)} %copy-done.4, s32[17]{0:T(128)S(1)} %copy-done.5, f32[16,264,128]{2,1,0:T(8,128)S(1)} %copy-done.1, f32[14,128,128]{2,1,0:T(8,128)} %collective-permute-done.9.refs_0_, ...), custom_call_target="tpu_custom_call", output_to_operand_aliasing={{1}: (8, {})} | custom-call | tf_op jit(solution)/shard_map/first/pallas_call | solution.py:328
  144.0 5.3 %all-to-all-start.1 = ((f32[16,128,128]{2,1,0:T(8,128)}), f32[16,128,128]{2,1,0:T(8,128)}, u32[]{:S(2)}, u32[]{:S(2)}) async-start(f32[16,128,128]{2,1,0:T(8,128)} %get-tuple-element.35.refs_5_), calls=%async_computation.1 | async-start | bytes 2097152 | tf_op jit(solution)/shard_map/all_to_all | solution.py:340
  149.3 1.3 broadcast_select_fusion
  150.5 0.6 collective-permute-start.13
  151.2 31.3 %collective-permute-done.13.refs_0_ = f32[14,128,128]{2,1,0:T(8,128)S(1)} collective-permute-done((f32[14,128,128]{2,1,0:T(8,128)S(1)}, f32[14,128,128]{2,1,0:T(8,128)S(1)}, u32[]{:S(2)}, u32[]{:S(2)}) %collective-permute-start.13) | collective-permute-done | bytes 917536 | tf_op jit(solution)/shard_map/ppermute | solution.py:18
  182.4 0.9 collective-permute-start.14
  183.3 2.1 collective-permute-done.14.refs_1_
  185.4 3.2 %first.7 = (bf16[2,256,2048]{2,1,0:T(8,128)(2,1)}, f32[2,128,128]{2,1,0:T(8,128)}) custom-call(s32[32]{0:T(128)S(1)} %copy-done.4, s32[17]{0:T(128)S(1)} %copy-done.5, f32[16,264,128]{2,1,0:T(8,128)S(1)} %copy-done.1, f32[14,128,128]{2,1,0:T(8,128)S(1)} %collective-permute-done.13.refs_0_, f32[14,128,128]{2,1,0:T(8,128)S(1)} %collective-permute-done.14.refs_1_, ...), custom_call_target="tpu_custom_call" | custom-call | tf_op jit(solution)/shard_map/first/pallas_call | solution.py:328
  188.5 17.8 %later.1 = f32[16,2,128,128]{3,2,1,0:T(8,128)} custom-call(s32[32]{0:T(128)} %convert_element_type.8.drops_ref, s32[17]{0:T(128)} %pad_add_fusion.1.rows_ref, bf16[6,256,2048]{2,1,0:T(8,128)(2,1)} %get-tuple-element.23.refs_0_, bf16[4,256,2048]{2,1,0:T(8,128)(2,1)} %get-tuple-element.26.refs_1_, bf16[4,256,2048]{2,1,0:T(8,128)(2,1)} %get-tuple-element.30.refs_2_, ...), custom_call_target="tpu_custom_call" | custom-call | tf_op jit(solution)/shard_map/later/pallas_call | solution.py:328
  206.3 5.8 %all-to-all-start.2 = ((f32[16,2,128,128]{3,2,1,0:T(8,128)}), f32[16,2,128,128]{3,2,1,0:T(8,128)S(1)}, u32[]{:S(2)}, u32[]{:S(2)}) async-start(f32[16,2,128,128]{3,2,1,0:T(8,128)} %later.1), calls=%async_computation.2 | async-start | bytes 4194304 | tf_op jit(solution)/shard_map/all_to_all | solution.py:340
  212.2 0.6 collective-permute-start.15
  212.8 1.8 collective-permute-start.16
  214.7 0.6 slice_bitcast_fusion.2.far_cols_ref
  215.3 48.3 %collective-permute-done.15.far0_ref = f32[128,128]{1,0:T(8,128)S(1)} collective-permute-done((f32[128,128]{1,0:T(8,128)S(1)}, f32[128,128]{1,0:T(8,128)S(1)}, u32[]{:S(2)}, u32[]{:S(2)}) %collective-permute-start.15) | collective-permute-done | bytes 65568 | tf_op jit(solution)/shard_map/ppermute | solution.py:18
  263.6 0.5 collective-permute-done.16.far1_ref
  264.1 0.2 copy-done.16
  264.2 0.5 copy-done.17
  264.7 3.1 %unpack_first.1.sum_ref = f32[14,128,128]{2,1,0:T(8,128)} custom-call(s32[14]{0:T(128)} %bitcast.20, s32[2]{0:T(128)} %slice_bitcast_fusion.2.far_cols_ref, f32[3]{0:T(128)} %coefs_ref.3, f32[16,128,128]{2,1,0:T(8,128)} %all-to-all-done.1.first_ref, f32[14,128,128]{2,1,0:T(8,128)} %bitcast.24, f32[128,128]{1,0:T(8,128)} %copy-done.16, f32[128,128]{1,0:T(8,128)} %copy-done.17), custom_call_target="tpu_custom_call" | custom-call | tf_op jit(solution)/shard_map/unpack_first/pallas_call | solution.py:328
  267.8 1.2 copy-done.3
  269.0 4.8 %unpack_last.1 = (f32[14,128,128]{2,1,0:T(8,128)}, f32[14,128,128]{2,1,0:T(8,128)}, f32[14,128,128]{2,1,0:T(8,128)}) custom-call(s32[14]{0:T(128)S(1)} %bitcast.21, f32[3]{0:T(128)S(1)} %copy-done.7, f32[16,2,128,128]{3,2,1,0:T(8,128)S(1)} %all-to-all-done.2.held_ref, f32[14,128,128]{2,1,0:T(8,128)S(1)} %copy-done.3), custom_call_target="tpu_custom_call" | custom-call | tf_op jit(solution)/shard_map/unpack_last/pallas_call | solution.py:328
  (46 shorter events, 0.4 us)
Async XLA Ops:
  0.6 22.4 %collective-permute-start = (f32[14,128,128]{2,1,0:T(8,128)}, f32[14,128,128]{2,1,0:T(8,128)S(1)}, u32[]{:S(2)}, u32[]{:S(2)}) collective-permute-start(f32[14,128,128]{2,1,0:T(8,128)} %bitcast.25), channel_id=1, source_target_pairs={{0,4},{1,5},{2,0},{3,1},{4,8},{5,9},{6,2},{7,3},{8,12},{9,13},{10,... | collective-permute-start | bytes 2752520 | tf_op jit(solution)/shard_map/ppermute | solution.py:18
  1.1 22.0 %collective-permute-start.1 = (f32[14,128,128]{2,1,0:T(8,128)}, f32[14,128,128]{2,1,0:T(8,128)S(1)}, u32[]{:S(2)}, u32[]{:S(2)}) collective-permute-start(f32[14,128,128]{2,1,0:T(8,128)} %bitcast.26), channel_id=1, source_target_pairs={{0,2},{1,3},{2,6},{3,7},{4,0},{5,1},{6,10},{7,11},{8,4},{9,5},{10,... | collective-permute-start | bytes 2752520 | tf_op jit(solution)/shard_map/ppermute | solution.py:18
  9.2 21.2 %copy-start.8 = (f32[1,14,128,128]{3,2,1,0:T(8,128)S(1)}, f32[1,14,128,128]{3,2,1,0:T(8,128)}, u32[]{:S(2)}) copy-start(f32[1,14,128,128]{3,2,1,0:T(8,128)} %param.8) | copy-start | bytes 2752516
  23.0 0.9 copy-start.9
  23.2 1.0 copy-start.10
  24.2 73.2 %all-to-all-start = ((f32[16,264,128]{2,1,0:T(8,128)}), f32[16,264,128]{2,1,0:T(8,128)S(1)}, u32[]{:S(2)}, u32[]{:S(2)}) async-start(f32[16,264,128]{2,1,0:T(8,128)} %pack.1), calls=%async_computation | async-start | bytes 4325376 | tf_op jit(solution)/shard_map/all_to_all | solution.py:340
  30.3 2.8 %collective-permute-start.2 = (f32[14,128,128]{2,1,0:T(8,128)S(1)}, f32[14,128,128]{2,1,0:T(8,128)S(1)}, u32[]{:S(2)}, u32[]{:S(2)}) collective-permute-start(f32[14,128,128]{2,1,0:T(8,128)S(1)} %bitcast.28), channel_id=1, source_target_pairs={{0,1},{1,0},{2,3},{3,2},{4,5},{5,4},{6,7},{7,6},{8,9},{9,8},{10,11... | collective-permute-start | bytes 2752520 | tf_op jit(solution)/shard_map/ppermute | solution.py:18
  30.5 3.8 %collective-permute-start.3 = (f32[14,128,128]{2,1,0:T(8,128)}, f32[14,128,128]{2,1,0:T(8,128)S(1)}, u32[]{:S(2)}, u32[]{:S(2)}) collective-permute-start(f32[14,128,128]{2,1,0:T(8,128)} %copy-done.9), channel_id=1, source_target_pairs={{0,1},{1,0},{2,3},{3,2},{4,5},{5,4},{6,7},{7,6},{8,9},{9,8},{10,11... | collective-permute-start | bytes 2752520 | tf_op jit(solution)/shard_map/ppermute | solution.py:18
  30.9 4.8 %collective-permute-start.4 = (f32[14,128,128]{2,1,0:T(8,128)}, f32[14,128,128]{2,1,0:T(8,128)S(1)}, u32[]{:S(2)}, u32[]{:S(2)}) collective-permute-start(f32[14,128,128]{2,1,0:T(8,128)} %copy-done.10), channel_id=1, source_target_pairs={{0,1},{1,0},{2,3},{3,2},{4,5},{5,4},{6,7},{7,6},{8,9},{9,8},{10,11... | collective-permute-start | bytes 2752520 | tf_op jit(solution)/shard_map/ppermute | solution.py:18
  31.1 66.4 %collective-permute-start.5 = (f32[14,128,128]{2,1,0:T(8,128)}, f32[14,128,128]{2,1,0:T(8,128)}, u32[]{:S(2)}, u32[]{:S(2)}) collective-permute-start(f32[14,128,128]{2,1,0:T(8,128)} %copy-done.9), channel_id=1, source_target_pairs={{0,4},{1,5},{2,0},{3,1},{4,8},{5,9},{6,2},{7,3},{8,12},{9,13},{10,... | collective-permute-start | bytes 2752520 | tf_op jit(solution)/shard_map/ppermute | solution.py:18
  31.6 68.3 %collective-permute-start.7 = (f32[14,128,128]{2,1,0:T(8,128)}, f32[14,128,128]{2,1,0:T(8,128)}, u32[]{:S(2)}, u32[]{:S(2)}) collective-permute-start(f32[14,128,128]{2,1,0:T(8,128)} %copy-done.10), channel_id=1, source_target_pairs={{0,2},{1,3},{2,6},{3,7},{4,0},{5,1},{6,10},{7,11},{8,4},{9,5},{10,... | collective-permute-start | bytes 2752520 | tf_op jit(solution)/shard_map/ppermute | solution.py:18
  33.1 2.6 copy-start.11
  34.4 1.3 copy-start.12
  35.7 0.9 copy-start.13
  97.4 26.8 %copy-start = (f32[16,264,128]{2,1,0:T(8,128)}, f32[16,264,128]{2,1,0:T(8,128)S(1)}, u32[]{:S(2)}) copy-start(f32[16,264,128]{2,1,0:T(8,128)S(1)} %all-to-all-done.t_ref.refs_4_) | copy-start | bytes 6488068
  97.4 22.2 %collective-permute-start.9 = (f32[14,128,128]{2,1,0:T(8,128)}, f32[14,128,128]{2,1,0:T(8,128)}, u32[]{:S(2)}, u32[]{:S(2)}) collective-permute-start(f32[14,128,128]{2,1,0:T(8,128)} %collective-permute-done.5.refs_0_), channel_id=1, source_target_pairs={{0,4},{1,5},{2,0},{3,1},{4,8},{5,9},{6,2},{7,3},{8,12},{9,13},{10,... | collective-permute-start | bytes 2752520 | tf_op jit(solution)/shard_map/ppermute | solution.py:18
  99.9 21.9 %collective-permute-start.11 = (f32[14,128,128]{2,1,0:T(8,128)}, f32[14,128,128]{2,1,0:T(8,128)}, u32[]{:S(2)}, u32[]{:S(2)}) collective-permute-start(f32[14,128,128]{2,1,0:T(8,128)} %collective-permute-done.7.refs_2_), channel_id=1, source_target_pairs={{0,2},{1,3},{2,6},{3,7},{4,0},{5,1},{6,10},{7,11},{8,4},{9,5},{10,... | collective-permute-start | bytes 2752520 | tf_op jit(solution)/shard_map/ppermute | solution.py:18
  99.9 32.2 %collective-permute-start.6 = (f32[14,128,128]{2,1,0:T(8,128)}, f32[14,128,128]{2,1,0:T(8,128)S(1)}, u32[]{:S(2)}, u32[]{:S(2)}) collective-permute-start(f32[14,128,128]{2,1,0:T(8,128)} %collective-permute-done.5.refs_0_), channel_id=1, source_target_pairs={{0,1},{1,0},{2,3},{3,2},{4,5},{5,4},{6,7},{7,6},{8,9},{9,8},{10,11... | collective-permute-start | bytes 2752520 | tf_op jit(solution)/shard_map/ppermute | solution.py:18
  99.9 32.3 %collective-permute-start.8 = (f32[14,128,128]{2,1,0:T(8,128)}, f32[14,128,128]{2,1,0:T(8,128)}, u32[]{:S(2)}, u32[]{:S(2)}) collective-permute-start(f32[14,128,128]{2,1,0:T(8,128)} %collective-permute-done.7.refs_2_), channel_id=1, source_target_pairs={{0,1},{1,0},{2,3},{3,2},{4,5},{5,4},{6,7},{7,6},{8,9},{9,8},{10,11... | collective-permute-start | bytes 2752520 | tf_op jit(solution)/shard_map/ppermute | solution.py:18
  119.6 19.3 %collective-permute-start.10 = (f32[14,128,128]{2,1,0:T(8,128)}, f32[14,128,128]{2,1,0:T(8,128)}, u32[]{:S(2)}, u32[]{:S(2)}) collective-permute-start(f32[14,128,128]{2,1,0:T(8,128)} %collective-permute-done.9.refs_0_), channel_id=1, source_target_pairs={{0,1},{1,0},{2,3},{3,2},{4,5},{5,4},{6,7},{7,6},{8,9},{9,8},{10,11... | collective-permute-start | bytes 2752520 | tf_op jit(solution)/shard_map/ppermute | solution.py:18
  121.8 17.1 %collective-permute-start.12 = (f32[14,128,128]{2,1,0:T(8,128)}, f32[14,128,128]{2,1,0:T(8,128)}, u32[]{:S(2)}, u32[]{:S(2)}) collective-permute-start(f32[14,128,128]{2,1,0:T(8,128)} %collective-permute-done.11.refs_2_), channel_id=1, source_target_pairs={{0,1},{1,0},{2,3},{3,2},{4,5},{5,4},{6,7},{7,6},{8,9},{9,8},{10,11... | collective-permute-start | bytes 2752520 | tf_op jit(solution)/shard_map/ppermute | solution.py:18
  132.1 0.9 copy-start.14
  133.1 5.9 %copy-start.1 = (f32[16,264,128]{2,1,0:T(8,128)S(1)}, f32[16,264,128]{2,1,0:T(8,128)}, u32[]{:S(2)}) copy-start(f32[16,264,128]{2,1,0:T(8,128)} %copy-done) | copy-start | bytes 6488068
  133.1 5.9 %copy-start.2 = (bf16[2048,256]{1,0:T(8,128)(2,1)S(1)}, bf16[2048,256]{1,0:T(8,128)(2,1)}, u32[]{:S(2)}) copy-start(bf16[2048,256]{1,0:T(8,128)(2,1)} %get-tuple-element.24.refs_4_.refs_2_) | copy-start | bytes 3145732
  133.1 5.9 %copy-start.4 = (s32[32]{0:T(128)S(1)}, s32[32]{0:T(128)}, u32[]{:S(2)}) copy-start(s32[32]{0:T(128)} %convert_element_type.8.drops_ref) | copy-start | bytes 388
  133.1 5.9 %copy-start.5 = (s32[17]{0:T(128)S(1)}, s32[17]{0:T(128)}, u32[]{:S(2)}) copy-start(s32[17]{0:T(128)} %pad_add_fusion.1.rows_ref) | copy-start | bytes 208
  144.0 62.3 %all-to-all-start.1 = ((f32[16,128,128]{2,1,0:T(8,128)}), f32[16,128,128]{2,1,0:T(8,128)}, u32[]{:S(2)}, u32[]{:S(2)}) async-start(f32[16,128,128]{2,1,0:T(8,128)} %get-tuple-element.35.refs_5_), calls=%async_computation.1 | async-start | bytes 2097152 | tf_op jit(solution)/shard_map/all_to_all | solution.py:340
  150.5 31.9 %collective-permute-start.13 = (f32[14,128,128]{2,1,0:T(8,128)S(1)}, f32[14,128,128]{2,1,0:T(8,128)S(1)}, u32[]{:S(2)}, u32[]{:S(2)}) collective-permute-start(f32[14,128,128]{2,1,0:T(8,128)S(1)} %broadcast_select_fusion), channel_id=1, source_target_pairs={{0,4},{1,3},{2,0},{3,7},{4,8},{5,1},{6,2},{7,11},{8,12},{9,5},{10,... | collective-permute-start | bytes 2752520 | tf_op jit(solution)/shard_map/ppermute | solution.py:18
  182.4 3.0 %collective-permute-start.14 = (f32[14,128,128]{2,1,0:T(8,128)S(1)}, f32[14,128,128]{2,1,0:T(8,128)S(1)}, u32[]{:S(2)}, u32[]{:S(2)}) collective-permute-start(f32[14,128,128]{2,1,0:T(8,128)S(1)} %collective-permute-done.13.refs_0_), channel_id=1, source_target_pairs={{0,1},{1,0},{2,3},{3,2},{4,5},{5,4},{6,7},{7,6},{8,9},{9,8},{10,11... | collective-permute-start | bytes 2752520 | tf_op jit(solution)/shard_map/ppermute | solution.py:18
  206.3 5.8 %copy-start.15 = (f32[2,128,128]{2,1,0:T(8,128)S(1)}, f32[2,128,128]{2,1,0:T(8,128)}, u32[]{:S(2)}) copy-start(f32[2,128,128]{2,1,0:T(8,128)} %get-tuple-element.36.refs_6_) | copy-start | bytes 393220
  206.3 61.5 %all-to-all-start.2 = ((f32[16,2,128,128]{3,2,1,0:T(8,128)}), f32[16,2,128,128]{3,2,1,0:T(8,128)S(1)}, u32[]{:S(2)}, u32[]{:S(2)}) async-start(f32[16,2,128,128]{3,2,1,0:T(8,128)} %later.1), calls=%async_computation.2 | async-start | bytes 4194304 | tf_op jit(solution)/shard_map/all_to_all | solution.py:340
  212.1 55.7 %copy-start.6 = (s32[1,14]{1,0:T(1,128)S(1)}, s32[1,14]{1,0:T(1,128)}, u32[]{:S(2)}) copy-start(s32[1,14]{1,0:T(1,128)} %param.12) | copy-start | bytes 172
  212.2 55.7 %copy-start.7 = (f32[3]{0:T(128)S(1)}, f32[3]{0:T(128)}, u32[]{:S(2)}) copy-start(f32[3]{0:T(128)} %coefs_ref.3) | copy-start | bytes 40
  212.2 51.4 %collective-permute-start.15 = (f32[128,128]{1,0:T(8,128)S(1)}, f32[128,128]{1,0:T(8,128)S(1)}, u32[]{:S(2)}, u32[]{:S(2)}) collective-permute-start(f32[128,128]{1,0:T(8,128)S(1)} %get-tuple-element.42), channel_id=1, source_target_pairs={{0,14},{1,15},{2,12},{3,13},{4,10},{5,11},{6,8},{7,9},{8,6},{9,7},... | collective-permute-start | bytes 196616 | tf_op jit(solution)/shard_map/ppermute | solution.py:18
  212.8 51.3 %collective-permute-start.16 = (f32[128,128]{1,0:T(8,128)S(1)}, f32[128,128]{1,0:T(8,128)S(1)}, u32[]{:S(2)}, u32[]{:S(2)}) collective-permute-start(f32[128,128]{1,0:T(8,128)S(1)} %get-tuple-element.41), channel_id=1, source_target_pairs={{0,15},{1,14},{2,13},{3,12},{4,11},{5,10},{6,9},{7,8},{8,7},{9,6},... | collective-permute-start | bytes 196616 | tf_op jit(solution)/shard_map/ppermute | solution.py:18
  263.6 0.6 copy-start.16
  264.1 0.6 copy-start.17
  267.8 1.2 copy-start.3

commit v12 on v9

--- a/solution.py
+++ b/solution.py
@@ -9,7 +9,6 @@
 
 REACH = 7
 NOTE = 8
-VMEM_LIMIT = 60 * 1024 * 1024
 SMEM = pl.BlockSpec(memory_space=pltpu.SMEM)
 ANY = pl.BlockSpec(memory_space=pl.ANY)
 
@@ -27,6 +26,8 @@
 
 
 def along_ring(device, by):
+    if device % 2:
+        by = -by
     return 2 * RING[(RING.index(device // 2) + by) % len(RING)] + device % 2
 
 
@@ -34,12 +35,12 @@
     if total != 16:
         steps = [0] + [by for hop in range(1, REACH + 1) for by in (-hop, hop)]
         return jnp.mod(me + jnp.array(steps, jnp.int32), total), (5, 4, 4, 2)
-    order = (0, -1, 1, -2, 2, -3, 3, 4)
-    table = [[along_ring(i, by) ^ core for by in order for core in (0, 1)] for i in range(total)]
+    order = (0, -1, 1, -2, 2, -3, 3, -4)
+    table = [[along_ring(source, by) for by in order for source in (i, i ^ 1)] for i in range(total)]
     return jnp.array(table, jnp.int32)[me], (6, 4, 4, 2)
 
 
-def gathered_rows(x, me, total, exchange):
+def gathered_rows(x, total, exchange):
     if total != 16:
         rows = [x]
         for hop in range(1, REACH + 1):
@@ -60,17 +61,14 @@
 
     rows = [x, other_core(x)]
     ahead, behind, first = round_of(x, x)
-    column = exchange(ahead, behind)
     ahead, behind, second = round_of(ahead, behind)
+    column = exchange(ahead, behind, rows[1], first[1], first[3])
     yield column
+    ahead, behind, third = round_of(ahead, behind)
+    far = permute(after(ahead, column), lambda i: along_ring(i, 1))
     yield rows + first
-    there = (column, rows[1], first[1], first[3])
-    ahead, behind, third = round_of(after(ahead, *there), after(behind, *there))
-    made = yield second
-    ahead, behind = after(ahead, made), after(behind, made)
-    far = permute(jnp.where(me % 2 == 0, ahead, behind), lambda i: along_ring(i, 1 if i % 2 == 0 else -1))
-    made = yield third
-    far = after(far, made)
+    yield second
+    yield third
     yield [far, other_core(far)]
 
 
@@ -310,15 +308,15 @@
     row = jax.ShapeDtypeStruct((count, size, size), f32)
     row_scratch = pltpu.VMEM(row.shape, f32)
 
-    def call(kernel, smem, arrays, outs, scratch, name, aliases={}):
+    def call(kernel, smem, arrays, outs, scratch, name, megabytes, aliases={}):
         return pl.pallas_call(
             kernel,
-            out_shape=outs,
+            out_shape=[pltpu.HBM(out.shape, out.dtype) for out in outs],
             in_specs=[SMEM] * len(smem) + [ANY] * len(arrays),
             out_specs=[ANY] * len(outs),
             scratch_shapes=scratch,
             input_output_aliases=aliases,
-            compiler_params=pltpu.CompilerParams(vmem_limit_bytes=VMEM_LIMIT),
+            compiler_params=pltpu.CompilerParams(vmem_limit_bytes=megabytes * 1024 * 1024),
             name=name,
         )(*smem, *arrays)
 
@@ -338,9 +336,10 @@
             dma((3,)),
         ],
         "pack",
+        12,
     )
     indices, parts = window_rows(me, total)
-    gathered = gathered_rows(h_blocks[0], me, total, lambda *others: exchange(after(send, *others)))
+    gathered = gathered_rows(h_blocks[0], total, lambda *others: exchange(after(send, *others)))
     column = next(gathered)
     drops = column[:, 2 * size:2 * size + 2, 0].astype(jnp.int32).reshape(-1)
     rows = jnp.concatenate([indices, me[None]])
@@ -350,11 +349,11 @@
     dense = []
     start = 0
     for part in parts:
-        h_rows = gathered.send(dense[-1] if start else None)
+        h_rows = next(gathered)
         group = max(g for g in (2, 3, 4, 5) if part % g == 0)
         scratch = [
             pltpu.VMEM((part, count, size, size), f32),
-            pltpu.VMEM((2, group) + dense_shape[1:], bf16),
+            pltpu.VMEM((min(2, part // group), group) + dense_shape[1:], bf16),
             pltpu.VMEM((part, size, size), f32),
             pltpu.VMEM(pair_shape, bf16),
             dma((part,)),
@@ -376,6 +375,7 @@
             ] + ([] if start else [jax.ShapeDtypeStruct(pair_shape, bf16)]),
             scratch,
             "first",
+            24,
             {part + 4: 1} if start else {},
         )
         dense.append(result[0])
@@ -400,6 +400,7 @@
             dma,
         ],
         "later",
+        60,
     )
     back = exchange(after(terms, back1))
     (sums,) = call(
@@ -409,6 +410,7 @@
         [row],
         [row_scratch, row_scratch, dma((2,))],
         "unpack_first",
+        60,
     )
     density, last, before = call(
         unpack_last_kernel,
@@ -417,6 +419,7 @@
         [row] * 3,
         [row_scratch, row_scratch, row_scratch, dma((3,))],
         "unpack_last",
+        60,
     )
     return density[None], last[None], before[None]
 

time: 235 us -> 250 us (1.064)
  waiting for transfers between devices: 142 us -> 156 us
  starting transfers between devices: 25.5 us -> 28 us
    ppermute x15, waiting for transfers between devices: 93.9 us -> 108 us  [permute(): return lax.ppermute(x, 'row', [(i, target(i)) for i in range(devices)])]
    unnamed x26 -> x32, local copies, waits for them, and re-layouts: 7.03 us -> 9.14 us
  transfers between devices with their start and end apart: 18 -> 18, of which waited for: 11 -> 6; matrix products, arithmetic and copies ran while one was open for 2% -> 1% of each run, Pallas kernels for 19% -> 17%
where the time goes in v12:
time: 250 us; the launch traced here: 247 us
  waiting for transfers between devices  156 us (62%)
  Pallas kernels  48.5 us (19%)
  starting transfers between devices  28 us (11%)
  local copies, waits for them, and re-layouts  9.93 us (4%)
    ppermute x15, waiting for transfers between devices, permute(): return lax.ppermute(x, 'row', [(i, target(i)) for i in range(devices)])  108 us
    pallas_call x8, Pallas kernels, call(): pl.pallas_call(kernel, out_shape=[pltpu.HBM(out.shape, out.dtype) for out...  48.5 us
    all_to_all x3, waiting for transfers between devices, exchange(): return lax.all_to_all(x, 'row', 0, 0, tiled=True)  48.4 us
    all_to_all x3, starting transfers between devices, exchange(): return lax.all_to_all(x, 'row', 0, 0, tiled=True)  17.7 us
    ppermute x15, starting transfers between devices, permute(): return lax.ppermute(x, 'row', [(i, target(i)) for i in range(devices)])  10.3 us
    unnamed x32, local copies, waits for them, and re-layouts  9.14 us
  transfers between devices with their start and end apart: 18, of which 6 were waited for; matrix products, arithmetic and copies ran while one was open for 1% of the time, Pallas kernels for 17%

profile of v12, /device:TPU:22, one launch (start us, length us, event | category | flops | bytes accessed | tf_op | source)
XLA Modules:
  0.0 246.8 jit_solution(2779145930796076087)
XLA Ops:
  0.6 0.5 collective-permute-start
  1.1 1.6 collective-permute-start.2
  2.7 0.0 collective-permute-start.4
  2.7 21.2 %collective-permute-done.refs_2_ = f32[14,128,128]{2,1,0:T(8,128)S(1)} collective-permute-done((f32[14,128,128]{2,1,0:T(8,128)}, f32[14,128,128]{2,1,0:T(8,128)S(1)}, u32[]{:S(2)}, u32[]{:S(2)}) %collective-permute-start) | collective-permute-done | bytes 917536 | tf_op jit(solution)/shard_map/ppermute | solution.py:18
  24.0 0.4 collective-permute-start.1
  24.4 1.6 collective-permute-start.3
  26.0 0.5 collective-permute-start.6
  26.5 1.4 fusion.1
  29.1 0.1 pad_add_fusion.info_ref
  29.2 1.2 copy-done.2
  30.4 1.2 copy-done.3
  31.6 0.7 copy-done.13
  32.2 2.4 pack.1
  34.7 11.6 %collective-permute-done.1.refs_0_ = f32[14,128,128]{2,1,0:T(8,128)S(1)} collective-permute-done((f32[14,128,128]{2,1,0:T(8,128)S(1)}, f32[14,128,128]{2,1,0:T(8,128)S(1)}, u32[]{:S(2)}, u32[]{:S(2)}) %collective-permute-start.1) | collective-permute-done | bytes 917536 | tf_op jit(solution)/shard_map/ppermute | solution.py:18
  46.3 0.0 collective-permute-done.3.refs_2_
  46.3 0.0 collective-permute-done.5.refs_3_
  46.3 0.0 collective-permute-done.6.refs_5_
  46.4 5.1 %all-to-all-start = ((f32[16,264,128]{2,1,0:T(8,128)}), f32[16,264,128]{2,1,0:T(8,128)S(1)}, u32[]{:S(2)}, u32[]{:S(2)}) async-start(f32[16,264,128]{2,1,0:T(8,128)} %pack.1), calls=%async_computation | async-start | bytes 4325376 | tf_op jit(solution)/shard_map/all_to_all | solution.py:324
  51.5 0.6 collective-permute-start.9
  52.1 1.5 collective-permute-start.11
  53.6 64.9 %collective-permute-done.9.refs_0_ = f32[14,128,128]{2,1,0:T(8,128)} collective-permute-done((f32[14,128,128]{2,1,0:T(8,128)S(1)}, f32[14,128,128]{2,1,0:T(8,128)}, u32[]{:S(2)}, u32[]{:S(2)}) %collective-permute-start.9) | collective-permute-done | bytes 917536 | tf_op jit(solution)/shard_map/ppermute | solution.py:18
  118.5 2.6 %collective-permute-start.13 = (f32[14,128,128]{2,1,0:T(8,128)}, f32[14,128,128]{2,1,0:T(8,128)S(1)}, u32[]{:S(2)}, u32[]{:S(2)}) collective-permute-start(f32[14,128,128]{2,1,0:T(8,128)} %collective-permute-done.9.refs_0_), channel_id=1, source_target_pairs={{0,4},{1,3},{2,0},{3,7},{4,8},{5,1},{6,2},{7,11},{8,12},{9,5},{10,... | collective-permute-start | bytes 2752520 | tf_op jit(solution)/shard_map/ppermute | solution.py:18
  121.1 0.5 collective-permute-start.8
  121.6 0.0 collective-permute-start.10
  121.6 0.0 collective-permute-done.11.refs_2_
  121.6 0.5 collective-permute-start.12
  122.1 10.2 %collective-permute-done.13.refs_0_ = f32[14,128,128]{2,1,0:T(8,128)S(1)} collective-permute-done((f32[14,128,128]{2,1,0:T(8,128)}, f32[14,128,128]{2,1,0:T(8,128)S(1)}, u32[]{:S(2)}, u32[]{:S(2)}) %collective-permute-start.13) | collective-permute-done | bytes 917536 | tf_op jit(solution)/shard_map/ppermute | solution.py:18
  132.3 0.7 dynamic-slice_bitcast_fusion
  133.0 0.1 pad_add_fusion.1.rows_ref
  133.1 0.3 fusion
  133.4 0.1 convert_element_type.8.drops_ref
  133.5 0.0 copy-start.4
  133.5 1.2 copy-done.4
  134.7 1.2 copy-done.6
  135.9 1.2 copy-done.10
  137.1 7.7 %first.4 = (bf16[6,256,2048]{2,1,0:T(8,128)(2,1)}, f32[16,128,128]{2,1,0:T(8,128)}, bf16[2048,256]{1,0:T(8,128)(2,1)}) custom-call(s32[32]{0:T(128)S(1)} %convert_element_type.8.drops_ref, s32[17]{0:T(128)S(1)} %pad_add_fusion.1.rows_ref, f32[16,264,128]{2,1,0:T(8,128)S(1)} %all-to-all-done.t_ref.refs_4_, f32[14,128,128]{2,1,0:T(8,128)S(1)} %bitcast.18, ...), custom_call_target="tpu_custom_call" | custom-call | tf_op jit(solution)/shard_map/first/pallas_call | solution.py:312
  144.9 1.2 copy-done.1
  146.1 5.1 %first.5 = (bf16[4,256,2048]{2,1,0:T(8,128)(2,1)}, f32[16,128,128]{2,1,0:T(8,128)}) custom-call(s32[32]{0:T(128)S(1)} %convert_element_type.8.drops_ref, s32[17]{0:T(128)S(1)} %pad_add_fusion.1.rows_ref, f32[16,264,128]{2,1,0:T(8,128)S(1)} %all-to-all-done.t_ref.refs_4_, f32[14,128,128]{2,1,0:T(8,128)S(1)} %copy-done.8, ...), custom_call_target="tpu_custom_call", output_to_operand_aliasing={{1}: (8, {})} | custom-call | tf_op jit(solution)/shard_map/first/pallas_call | solution.py:312
  151.2 5.0 %first.6 = (bf16[4,256,2048]{2,1,0:T(8,128)(2,1)}, f32[16,128,128]{2,1,0:T(8,128)}) custom-call(s32[32]{0:T(128)S(1)} %convert_element_type.8.drops_ref, s32[17]{0:T(128)S(1)} %pad_add_fusion.1.rows_ref, f32[16,264,128]{2,1,0:T(8,128)S(1)} %all-to-all-done.t_ref.refs_4_, ...), custom_call_target="tpu_custom_call", output_to_operand_aliasing={{1}: (8, {})} | custom-call | tf_op jit(solution)/shard_map/first/pallas_call | solution.py:312
  156.3 3.7 %first.7 = (bf16[2,256,2048]{2,1,0:T(8,128)(2,1)}, f32[16,128,128]{2,1,0:T(8,128)}) custom-call(s32[32]{0:T(128)S(1)} %convert_element_type.8.drops_ref, s32[17]{0:T(128)S(1)} %pad_add_fusion.1.rows_ref, f32[16,264,128]{2,1,0:T(8,128)S(1)} %all-to-all-done.t_ref.refs_4_, ...), custom_call_target="tpu_custom_call", output_to_operand_aliasing={{1}: (6, {})} | custom-call | tf_op jit(solution)/shard_map/first/pallas_call | solution.py:312
  160.0 6.1 %all-to-all-start.1 = ((f32[16,128,128]{2,1,0:T(8,128)}), f32[16,128,128]{2,1,0:T(8,128)S(1)}, u32[]{:S(2)}, u32[]{:S(2)}) async-start(f32[16,128,128]{2,1,0:T(8,128)} %get-tuple-element.28.refs_5_), calls=%async_computation.1 | async-start | bytes 2097152 | tf_op jit(solution)/shard_map/all_to_all | solution.py:324
  166.1 17.8 %later.1 = f32[16,2,128,128]{3,2,1,0:T(8,128)} custom-call(s32[32]{0:T(128)} %copy-done.11, s32[17]{0:T(128)} %copy-done.12, bf16[6,256,2048]{2,1,0:T(8,128)(2,1)} %get-tuple-element.19.refs_0_, bf16[4,256,2048]{2,1,0:T(8,128)(2,1)} %get-tuple-element.22.refs_1_, bf16[4,256,2048]{2,1,0:T(8,128)(2,1)} %get-tuple-element.24.refs_2_, ...), custom_call_target="tpu_custom_call" | custom-call | tf_op jit(solution)/shard_map/later/pallas_call | solution.py:312
  183.9 5.6 %all-to-all-done.1.first_ref = f32[16,128,128]{2,1,0:T(8,128)S(1)} async-done(((f32[16,128,128]{2,1,0:T(8,128)}), f32[16,128,128]{2,1,0:T(8,128)S(1)}, u32[]{:S(2)}, u32[]{:S(2)}) %all-to-all-start.1) | async-done | bytes 1048608 | tf_op jit(solution)/shard_map/all_to_all | solution.py:324
  189.5 6.4 %all-to-all-start.2 = ((f32[16,2,128,128]{3,2,1,0:T(8,128)}), f32[16,2,128,128]{3,2,1,0:T(8,128)S(1)}, u32[]{:S(2)}, u32[]{:S(2)}) async-start(f32[16,2,128,128]{3,2,1,0:T(8,128)} %later.1), calls=%async_computation.2 | async-start | bytes 4194304 | tf_op jit(solution)/shard_map/all_to_all | solution.py:324
  196.0 3.1 %unpack_first.1.sum_ref = f32[14,128,128]{2,1,0:T(8,128)} custom-call(s32[14]{0:T(128)} %bitcast.19, f32[3]{0:T(128)} %coefs_ref.3, f32[16,128,128]{2,1,0:T(8,128)} %copy-done.15, f32[14,128,128]{2,1,0:T(8,128)} %bitcast.22), custom_call_target="tpu_custom_call" | custom-call | tf_op jit(solution)/shard_map/unpack_first/pallas_call | solution.py:312
  199.1 42.8 %all-to-all-done.2.held_ref = f32[16,2,128,128]{3,2,1,0:T(8,128)S(1)} async-done(((f32[16,2,128,128]{3,2,1,0:T(8,128)}), f32[16,2,128,128]{3,2,1,0:T(8,128)S(1)}, u32[]{:S(2)}, u32[]{:S(2)}) %all-to-all-start.2) | async-done | bytes 2097184 | tf_op jit(solution)/shard_map/all_to_all | solution.py:324
  241.9 1.3 copy-done.14
  243.2 3.6 %unpack_last.1 = (f32[14,128,128]{2,1,0:T(8,128)}, f32[14,128,128]{2,1,0:T(8,128)}, f32[14,128,128]{2,1,0:T(8,128)}) custom-call(s32[14]{0:T(128)} %bitcast.20, f32[3]{0:T(128)} %coefs_ref.3, f32[16,2,128,128]{3,2,1,0:T(8,128)} %copy-done.14, f32[14,128,128]{2,1,0:T(8,128)} %unpack_first.1.sum_ref), custom_call_target="tpu_custom_call" | custom-call | tf_op jit(solution)/shard_map/unpack_last/pallas_call | solution.py:312
  (34 shorter events, 0.1 us)
Async XLA Ops:
  0.6 23.3 %collective-permute-start = (f32[14,128,128]{2,1,0:T(8,128)}, f32[14,128,128]{2,1,0:T(8,128)S(1)}, u32[]{:S(2)}, u32[]{:S(2)}) collective-permute-start(f32[14,128,128]{2,1,0:T(8,128)} %bitcast.15), channel_id=1, source_target_pairs={{0,4},{1,3},{2,0},{3,7},{4,8},{5,1},{6,2},{7,11},{8,12},{9,5},{10,... | collective-permute-start | bytes 2752520 | tf_op jit(solution)/shard_map/ppermute | solution.py:18
  1.1 23.3 %collective-permute-start.2 = (f32[14,128,128]{2,1,0:T(8,128)}, f32[14,128,128]{2,1,0:T(8,128)S(1)}, u32[]{:S(2)}, u32[]{:S(2)}) collective-permute-start(f32[14,128,128]{2,1,0:T(8,128)} %bitcast.16), channel_id=1, source_target_pairs={{0,2},{1,5},{2,6},{3,1},{4,0},{5,9},{6,10},{7,3},{8,4},{9,13},{10,... | collective-permute-start | bytes 2752520 | tf_op jit(solution)/shard_map/ppermute | solution.py:18
  2.7 32.0 %collective-permute-start.4 = (f32[14,128,128]{2,1,0:T(8,128)}, f32[14,128,128]{2,1,0:T(8,128)}, u32[]{:S(2)}, u32[]{:S(2)}) collective-permute-start(f32[14,128,128]{2,1,0:T(8,128)} %bitcast.17), channel_id=1, source_target_pairs={{0,1},{1,0},{2,3},{3,2},{4,5},{5,4},{6,7},{7,6},{8,9},{9,8},{10,11... | collective-permute-start | bytes 2752520 | tf_op jit(solution)/shard_map/ppermute | solution.py:18
  24.0 22.4 %copy-start.5 = (f32[14,128,128]{2,1,0:T(8,128)}, f32[14,128,128]{2,1,0:T(8,128)S(1)}, u32[]{:S(2)}) copy-start(f32[14,128,128]{2,1,0:T(8,128)S(1)} %collective-permute-done.refs_2_) | copy-start | bytes 2752516
  24.0 22.4 %collective-permute-start.1 = (f32[14,128,128]{2,1,0:T(8,128)S(1)}, f32[14,128,128]{2,1,0:T(8,128)S(1)}, u32[]{:S(2)}, u32[]{:S(2)}) collective-permute-start(f32[14,128,128]{2,1,0:T(8,128)S(1)} %collective-permute-done.refs_2_), channel_id=1, source_target_pairs={{0,4},{1,3},{2,0},{3,7},{4,8},{5,1},{6,2},{7,11},{8,12},{9,5},{10,... | collective-permute-start | bytes 2752520 | tf_op jit(solution)/shard_map/ppermute | solution.py:18
  24.4 22.0 %copy-start.9 = (f32[14,128,128]{2,1,0:T(8,128)}, f32[14,128,128]{2,1,0:T(8,128)S(1)}, u32[]{:S(2)}) copy-start(f32[14,128,128]{2,1,0:T(8,128)S(1)} %collective-permute-done.2.refs_4_) | copy-start | bytes 2752516
  24.4 21.9 %collective-permute-start.3 = (f32[14,128,128]{2,1,0:T(8,128)S(1)}, f32[14,128,128]{2,1,0:T(8,128)}, u32[]{:S(2)}, u32[]{:S(2)}) collective-permute-start(f32[14,128,128]{2,1,0:T(8,128)S(1)} %collective-permute-done.2.refs_4_), channel_id=1, source_target_pairs={{0,2},{1,5},{2,6},{3,1},{4,0},{5,9},{6,10},{7,3},{8,4},{9,13},{10,... | collective-permute-start | bytes 2752520 | tf_op jit(solution)/shard_map/ppermute | solution.py:18
  26.0 20.3 %collective-permute-start.5 = (f32[14,128,128]{2,1,0:T(8,128)S(1)}, f32[14,128,128]{2,1,0:T(8,128)}, u32[]{:S(2)}, u32[]{:S(2)}) collective-permute-start(f32[14,128,128]{2,1,0:T(8,128)S(1)} %collective-permute-done.refs_2_), channel_id=1, source_target_pairs={{0,1},{1,0},{2,3},{3,2},{4,5},{5,4},{6,7},{7,6},{8,9},{9,8},{10,11... | collective-permute-start | bytes 2752520 | tf_op jit(solution)/shard_map/ppermute | solution.py:18
  26.0 20.3 %collective-permute-start.6 = (f32[14,128,128]{2,1,0:T(8,128)S(1)}, f32[14,128,128]{2,1,0:T(8,128)}, u32[]{:S(2)}, u32[]{:S(2)}) collective-permute-start(f32[14,128,128]{2,1,0:T(8,128)S(1)} %collective-permute-done.2.refs_4_), channel_id=1, source_target_pairs={{0,1},{1,0},{2,3},{3,2},{4,5},{5,4},{6,7},{7,6},{8,9},{9,8},{10,11... | collective-permute-start | bytes 2752520 | tf_op jit(solution)/shard_map/ppermute | solution.py:18
  29.2 1.2 copy-start.2
  30.4 1.2 copy-start.3
  31.6 0.7 copy-start.13
  46.3 5.2 %copy-start.7 = (f32[14,128,128]{2,1,0:T(8,128)}, f32[14,128,128]{2,1,0:T(8,128)S(1)}, u32[]{:S(2)}) copy-start(f32[14,128,128]{2,1,0:T(8,128)S(1)} %collective-permute-done.1.refs_0_) | copy-start | bytes 2752516
  46.4 72.1 %all-to-all-start = ((f32[16,264,128]{2,1,0:T(8,128)}), f32[16,264,128]{2,1,0:T(8,128)S(1)}, u32[]{:S(2)}, u32[]{:S(2)}) async-start(f32[16,264,128]{2,1,0:T(8,128)} %pack.1), calls=%async_computation | async-start | bytes 4325376 | tf_op jit(solution)/shard_map/all_to_all | solution.py:324
  51.5 67.0 %collective-permute-start.9 = (f32[14,128,128]{2,1,0:T(8,128)S(1)}, f32[14,128,128]{2,1,0:T(8,128)}, u32[]{:S(2)}, u32[]{:S(2)}) collective-permute-start(f32[14,128,128]{2,1,0:T(8,128)S(1)} %collective-permute-done.1.refs_0_), channel_id=1, source_target_pairs={{0,4},{1,3},{2,0},{3,7},{4,8},{5,1},{6,2},{7,11},{8,12},{9,5},{10,... | collective-permute-start | bytes 2752520 | tf_op jit(solution)/shard_map/ppermute | solution.py:18
  52.1 69.5 %collective-permute-start.11 = (f32[14,128,128]{2,1,0:T(8,128)}, f32[14,128,128]{2,1,0:T(8,128)}, u32[]{:S(2)}, u32[]{:S(2)}) collective-permute-start(f32[14,128,128]{2,1,0:T(8,128)} %collective-permute-done.3.refs_2_), channel_id=1, source_target_pairs={{0,2},{1,5},{2,6},{3,1},{4,0},{5,9},{6,10},{7,3},{8,4},{9,13},{10,... | collective-permute-start | bytes 2752520 | tf_op jit(solution)/shard_map/ppermute | solution.py:18
  118.5 37.8 %copy-start = (f32[16,264,128]{2,1,0:T(8,128)}, f32[16,264,128]{2,1,0:T(8,128)S(1)}, u32[]{:S(2)}) copy-start(f32[16,264,128]{2,1,0:T(8,128)S(1)} %all-to-all-done.t_ref.refs_4_) | copy-start | bytes 6488068
  118.5 13.8 %collective-permute-start.13 = (f32[14,128,128]{2,1,0:T(8,128)}, f32[14,128,128]{2,1,0:T(8,128)S(1)}, u32[]{:S(2)}, u32[]{:S(2)}) collective-permute-start(f32[14,128,128]{2,1,0:T(8,128)} %collective-permute-done.9.refs_0_), channel_id=1, source_target_pairs={{0,4},{1,3},{2,0},{3,7},{4,8},{5,1},{6,2},{7,11},{8,12},{9,5},{10,... | collective-permute-start | bytes 2752520 | tf_op jit(solution)/shard_map/ppermute | solution.py:18
  121.1 23.8 %collective-permute-start.7 = (f32[14,128,128]{2,1,0:T(8,128)}, f32[14,128,128]{2,1,0:T(8,128)}, u32[]{:S(2)}, u32[]{:S(2)}) collective-permute-start(f32[14,128,128]{2,1,0:T(8,128)} %copy-done.7), channel_id=1, source_target_pairs={{0,1},{1,0},{2,3},{3,2},{4,5},{5,4},{6,7},{7,6},{8,9},{9,8},{10,11... | collective-permute-start | bytes 2752520 | tf_op jit(solution)/shard_map/ppermute | solution.py:18
  121.1 23.8 %collective-permute-start.8 = (f32[14,128,128]{2,1,0:T(8,128)}, f32[14,128,128]{2,1,0:T(8,128)}, u32[]{:S(2)}, u32[]{:S(2)}) collective-permute-start(f32[14,128,128]{2,1,0:T(8,128)} %collective-permute-done.3.refs_2_), channel_id=1, source_target_pairs={{0,1},{1,0},{2,3},{3,2},{4,5},{5,4},{6,7},{7,6},{8,9},{9,8},{10,11... | collective-permute-start | bytes 2752520 | tf_op jit(solution)/shard_map/ppermute | solution.py:18
  121.6 29.6 %collective-permute-start.10 = (f32[14,128,128]{2,1,0:T(8,128)}, f32[14,128,128]{2,1,0:T(8,128)}, u32[]{:S(2)}, u32[]{:S(2)}) collective-permute-start(f32[14,128,128]{2,1,0:T(8,128)} %collective-permute-done.9.refs_0_), channel_id=1, source_target_pairs={{0,1},{1,0},{2,3},{3,2},{4,5},{5,4},{6,7},{7,6},{8,9},{9,8},{10,11... | collective-permute-start | bytes 2752520 | tf_op jit(solution)/shard_map/ppermute | solution.py:18
  121.6 29.6 %collective-permute-start.12 = (f32[14,128,128]{2,1,0:T(8,128)}, f32[14,128,128]{2,1,0:T(8,128)}, u32[]{:S(2)}, u32[]{:S(2)}) collective-permute-start(f32[14,128,128]{2,1,0:T(8,128)} %collective-permute-done.11.refs_2_), channel_id=1, source_target_pairs={{0,1},{1,0},{2,3},{3,2},{4,5},{5,4},{6,7},{7,6},{8,9},{9,8},{10,11... | collective-permute-start | bytes 2752520 | tf_op jit(solution)/shard_map/ppermute | solution.py:18
  132.3 23.9 %collective-permute-start.14 = (f32[14,128,128]{2,1,0:T(8,128)S(1)}, f32[14,128,128]{2,1,0:T(8,128)}, u32[]{:S(2)}, u32[]{:S(2)}) collective-permute-start(f32[14,128,128]{2,1,0:T(8,128)S(1)} %collective-permute-done.13.refs_0_), channel_id=1, source_target_pairs={{0,1},{1,0},{2,3},{3,2},{4,5},{5,4},{6,7},{7,6},{8,9},{9,8},{10,11... | collective-permute-start | bytes 2752520 | tf_op jit(solution)/shard_map/ppermute | solution.py:18
  133.1 23.2 %copy-start.12 = (s32[17]{0:T(128)}, s32[17]{0:T(128)S(1)}, u32[]{:S(2)}) copy-start(s32[17]{0:T(128)S(1)} %pad_add_fusion.1.rows_ref) | copy-start | bytes 208
  133.5 1.2 copy-start.4
  134.7 1.2 copy-start.6
  135.9 1.2 copy-start.10
  137.1 19.2 %copy-start.11 = (s32[32]{0:T(128)}, s32[32]{0:T(128)S(1)}, u32[]{:S(2)}) copy-start(s32[32]{0:T(128)S(1)} %convert_element_type.8.drops_ref) | copy-start | bytes 388
  137.1 7.8 %copy-start.8 = (f32[14,128,128]{2,1,0:T(8,128)S(1)}, f32[14,128,128]{2,1,0:T(8,128)}, u32[]{:S(2)}) copy-start(f32[14,128,128]{2,1,0:T(8,128)} %copy-done.7) | copy-start | bytes 2752516
  144.9 1.2 copy-start.1
  160.0 29.5 %all-to-all-start.1 = ((f32[16,128,128]{2,1,0:T(8,128)}), f32[16,128,128]{2,1,0:T(8,128)S(1)}, u32[]{:S(2)}, u32[]{:S(2)}) async-start(f32[16,128,128]{2,1,0:T(8,128)} %get-tuple-element.28.refs_5_), calls=%async_computation.1 | async-start | bytes 2097152 | tf_op jit(solution)/shard_map/all_to_all | solution.py:324
  189.5 6.4 %copy-start.15 = (f32[16,128,128]{2,1,0:T(8,128)}, f32[16,128,128]{2,1,0:T(8,128)S(1)}, u32[]{:S(2)}) copy-start(f32[16,128,128]{2,1,0:T(8,128)S(1)} %all-to-all-done.1.first_ref) | copy-start | bytes 3145732
  189.5 52.4 %all-to-all-start.2 = ((f32[16,2,128,128]{3,2,1,0:T(8,128)}), f32[16,2,128,128]{3,2,1,0:T(8,128)S(1)}, u32[]{:S(2)}, u32[]{:S(2)}) async-start(f32[16,2,128,128]{3,2,1,0:T(8,128)} %later.1), calls=%async_computation.2 | async-start | bytes 4194304 | tf_op jit(solution)/shard_map/all_to_all | solution.py:324
  241.9 1.4 copy-start.14

commit v13 on v12

--- a/solution.py
+++ b/solution.py
@@ -67,8 +67,9 @@
     ahead, behind, third = round_of(ahead, behind)
     far = permute(after(ahead, column), lambda i: along_ring(i, 1))
     yield rows + first
-    yield second
+    made = yield second
     yield third
+    far = after(far, made)
     yield [far, other_core(far)]
 
 
@@ -336,7 +337,7 @@
             dma((3,)),
         ],
         "pack",
-        12,
+        60,
     )
     indices, parts = window_rows(me, total)
     gathered = gathered_rows(h_blocks[0], total, lambda *others: exchange(after(send, *others)))
@@ -349,7 +350,7 @@
     dense = []
     start = 0
     for part in parts:
-        h_rows = next(gathered)
+        h_rows = gathered.send(dense[-1] if start else None)
         group = max(g for g in (2, 3, 4, 5) if part % g == 0)
         scratch = [
             pltpu.VMEM((part, count, size, size), f32),
@@ -375,7 +376,7 @@
             ] + ([] if start else [jax.ShapeDtypeStruct(pair_shape, bf16)]),
             scratch,
             "first",
-            24,
+            60 if start < 10 else 24,
             {part + 4: 1} if start else {},
         )
         dense.append(result[0])

time: 250 us -> 237 us (0.948)
  waiting for transfers between devices: 156 us -> 148 us
  local copies, waits for them, and re-layouts: 9.93 us -> 4.54 us
    ppermute x15, waiting for transfers between devices: 108 us -> 99.1 us  [permute(): return lax.ppermute(x, 'row', [(i, target(i)) for i in range(devices)])]
    unnamed x32 -> x22, local copies, waits for them, and re-layouts: 9.14 us -> 3.17 us
  transfers between devices with their start and end apart: 18 -> 18, of which waited for: 6 -> 5; matrix products, arithmetic and copies ran while one was open for 1% -> 2% of each run, Pallas kernels for 17% -> 18%
where the time goes in v13:
time: 237 us; the launch traced here: 234 us
  waiting for transfers between devices  148 us (62%)
  Pallas kernels  50.3 us (21%)
  starting transfers between devices  27 us (11%)
  local copies, waits for them, and re-layouts  4.54 us (2%)
  other arithmetic  2.95 us (1%)
    ppermute x15, waiting for transfers between devices, permute(): return lax.ppermute(x, 'row', [(i, target(i)) for i in range(devices)])  99.1 us
    pallas_call x8, Pallas kernels, call(): pl.pallas_call(kernel, out_shape=[pltpu.HBM(out.shape, out.dtype) for out...  50.3 us
    all_to_all x3, waiting for transfers between devices, exchange(): return lax.all_to_all(x, 'row', 0, 0, tiled=True)  48.5 us
    all_to_all x3, starting transfers between devices, exchange(): return lax.all_to_all(x, 'row', 0, 0, tiled=True)  16.8 us
    ppermute x15, starting transfers between devices, permute(): return lax.ppermute(x, 'row', [(i, target(i)) for i in range(devices)])  10.2 us
  transfers between devices with their start and end apart: 18, of which 5 were waited for; matrix products, arithmetic and copies ran while one was open for 2% of the time, Pallas kernels for 18%

profile of v13, /device:TPU:22, one launch (start us, length us, event | category | flops | bytes accessed | tf_op | source)
XLA Modules:
  0.0 234.4 jit_solution(6567564614792697562)
XLA Ops:
  0.6 0.5 collective-permute-start
  1.1 1.6 collective-permute-start.2
  2.7 0.0 collective-permute-start.4
  2.7 21.2 %collective-permute-done.refs_2_ = f32[14,128,128]{2,1,0:T(8,128)S(1)} collective-permute-done((f32[14,128,128]{2,1,0:T(8,128)}, f32[14,128,128]{2,1,0:T(8,128)S(1)}, u32[]{:S(2)}, u32[]{:S(2)}) %collective-permute-start) | collective-permute-done | bytes 917536 | tf_op jit(solution)/shard_map/ppermute | solution.py:18
  24.0 0.4 collective-permute-start.1
  24.4 0.0 collective-permute-done.2.refs_4_
  24.4 1.6 collective-permute-start.3
  26.0 0.0 collective-permute-start.5
  26.0 0.5 collective-permute-start.6
  26.5 1.3 fusion.1
  29.1 0.6 pad_add_fusion.info_ref
  29.7 3.3 %pack.1 = f32[16,264,128]{2,1,0:T(8,128)} custom-call(s32[3]{0:T(128)} %pad_add_fusion.info_ref, s32[14]{0:T(128)} %bitcast.20, f32[14,128,128]{2,1,0:T(8,128)} %bitcast.13, f32[14,128,128]{2,1,0:T(8,128)} %bitcast.14), custom_call_target="tpu_custom_call" | custom-call | tf_op jit(solution)/shard_map/pack/pallas_call | solution.py:313
  33.0 0.0 collective-permute-done.4.refs_1_
  33.0 13.3 %collective-permute-done.1.refs_0_ = f32[14,128,128]{2,1,0:T(8,128)S(1)} collective-permute-done((f32[14,128,128]{2,1,0:T(8,128)S(1)}, f32[14,128,128]{2,1,0:T(8,128)S(1)}, u32[]{:S(2)}, u32[]{:S(2)}) %collective-permute-start.1) | collective-permute-done | bytes 917536 | tf_op jit(solution)/shard_map/ppermute | solution.py:18
  46.3 0.0 collective-permute-done.3.refs_2_
  46.3 0.0 collective-permute-done.5.refs_3_
  46.3 0.0 collective-permute-done.6.refs_5_
  46.4 0.9 copy-done.8
  47.3 5.1 %all-to-all-start = ((f32[16,264,128]{2,1,0:T(8,128)}), f32[16,264,128]{2,1,0:T(8,128)S(1)}, u32[]{:S(2)}, u32[]{:S(2)}) async-start(f32[16,264,128]{2,1,0:T(8,128)} %pack.1), calls=%async_computation | async-start | bytes 4325376 | tf_op jit(solution)/shard_map/all_to_all | solution.py:325
  52.4 0.6 collective-permute-start.9
  52.9 1.5 collective-permute-start.11
  54.4 0.5 collective-permute-start.8
  54.9 64.5 %collective-permute-done.9.refs_0_ = f32[14,128,128]{2,1,0:T(8,128)} collective-permute-done((f32[14,128,128]{2,1,0:T(8,128)}, f32[14,128,128]{2,1,0:T(8,128)}, u32[]{:S(2)}, u32[]{:S(2)}) %collective-permute-start.9) | collective-permute-done | bytes 917536 | tf_op jit(solution)/shard_map/ppermute | solution.py:18
  119.5 2.5 %collective-permute-start.13 = (f32[14,128,128]{2,1,0:T(8,128)}, f32[14,128,128]{2,1,0:T(8,128)}, u32[]{:S(2)}, u32[]{:S(2)}) collective-permute-start(f32[14,128,128]{2,1,0:T(8,128)} %collective-permute-done.9.refs_0_), channel_id=1, source_target_pairs={{0,4},{1,3},{2,0},{3,7},{4,8},{5,1},{6,2},{7,11},{8,12},{9,5},{10,... | collective-permute-start | bytes 2752520 | tf_op jit(solution)/shard_map/ppermute | solution.py:18
  121.9 0.7 dynamic-slice_bitcast_fusion
  122.6 0.6 pad_add_fusion.1.rows_ref
  123.3 0.0 collective-permute-done.11.refs_2_
  123.3 0.5 collective-permute-start.12
  123.8 0.3 fusion
  124.1 0.7 convert_element_type.8.drops_ref
  124.8 7.9 %first.4 = (bf16[6,256,2048]{2,1,0:T(8,128)(2,1)}, f32[16,128,128]{2,1,0:T(8,128)}, bf16[2048,256]{1,0:T(8,128)(2,1)}) custom-call(s32[32]{0:T(128)} %convert_element_type.8.drops_ref, s32[17]{0:T(128)} %pad_add_fusion.1.rows_ref, f32[16,264,128]{2,1,0:T(8,128)} %copy-done, f32[14,128,128]{2,1,0:T(8,128)} %bitcast.18, ...), custom_call_target="tpu_custom_call" | custom-call | tf_op jit(solution)/shard_map/first/pallas_call | solution.py:313
  132.8 0.0 collective-permute-done.7.refs_1_
  132.8 0.0 copy-start.10
  132.8 0.9 copy-done.10
  133.7 5.8 %first.5 = (bf16[4,256,2048]{2,1,0:T(8,128)(2,1)}, f32[16,128,128]{2,1,0:T(8,128)}) custom-call(s32[32]{0:T(128)} %convert_element_type.8.drops_ref, s32[17]{0:T(128)} %pad_add_fusion.1.rows_ref, f32[16,264,128]{2,1,0:T(8,128)} %copy-done, f32[14,128,128]{2,1,0:T(8,128)} %copy-done.8, f32[14,128,128]{2,1,0:T(8,128)} %copy-done.10, ...), custom_call_target="tpu_custom_call", output_to_operand_aliasing={{1}: (8, {})} | custom-call | tf_op jit(solution)/shard_map/first/pallas_call | solution.py:313
  139.5 0.0 collective-permute-done.13.refs_0_
  139.5 0.1 collective-permute-start.14
  139.7 5.1 %first.6 = (bf16[4,256,2048]{2,1,0:T(8,128)(2,1)}, f32[16,128,128]{2,1,0:T(8,128)}) custom-call(s32[32]{0:T(128)S(1)} %copy-done.3, s32[17]{0:T(128)S(1)} %copy-done.4, f32[16,264,128]{2,1,0:T(8,128)S(1)} %copy-done.1, f32[14,128,128]{2,1,0:T(8,128)} %collective-permute-done.9.refs_0_, ...), custom_call_target="tpu_custom_call", output_to_operand_aliasing={{1}: (8, {})} | custom-call | tf_op jit(solution)/shard_map/first/pallas_call | solution.py:313
  144.8 0.0 collective-permute-done.14.refs_1_
  144.8 3.8 %first.7 = (bf16[2,256,2048]{2,1,0:T(8,128)(2,1)}, f32[16,128,128]{2,1,0:T(8,128)}) custom-call(s32[32]{0:T(128)S(1)} %copy-done.3, s32[17]{0:T(128)S(1)} %copy-done.4, f32[16,264,128]{2,1,0:T(8,128)S(1)} %copy-done.1, f32[14,128,128]{2,1,0:T(8,128)} %collective-permute-done.13.refs_0_, ...), custom_call_target="tpu_custom_call", output_to_operand_aliasing={{1}: (6, {})} | custom-call | tf_op jit(solution)/shard_map/first/pallas_call | solution.py:313
  148.5 5.2 %all-to-all-start.1 = ((f32[16,128,128]{2,1,0:T(8,128)}), f32[16,128,128]{2,1,0:T(8,128)S(1)}, u32[]{:S(2)}, u32[]{:S(2)}) async-start(f32[16,128,128]{2,1,0:T(8,128)} %get-tuple-element.30.refs_5_), calls=%async_computation.1 | async-start | bytes 2097152 | tf_op jit(solution)/shard_map/all_to_all | solution.py:325
  153.8 17.8 %later.1 = f32[16,2,128,128]{3,2,1,0:T(8,128)} custom-call(s32[32]{0:T(128)} %convert_element_type.8.drops_ref, s32[17]{0:T(128)} %pad_add_fusion.1.rows_ref, bf16[6,256,2048]{2,1,0:T(8,128)(2,1)} %get-tuple-element.20.refs_0_, bf16[4,256,2048]{2,1,0:T(8,128)(2,1)} %get-tuple-element.23.refs_1_, bf16[4,256,2048]{2,1,0:T(8,128)(2,1)} %get-tuple-element.25.refs_2_, ...), custom_call_target="tpu_custom_call" | custom-call | tf_op jit(solution)/shard_map/later/pallas_call | solution.py:313
  171.5 5.6 %all-to-all-done.1.first_ref = f32[16,128,128]{2,1,0:T(8,128)S(1)} async-done(((f32[16,128,128]{2,1,0:T(8,128)}), f32[16,128,128]{2,1,0:T(8,128)S(1)}, u32[]{:S(2)}, u32[]{:S(2)}) %all-to-all-start.1) | async-done | bytes 1048608 | tf_op jit(solution)/shard_map/all_to_all | solution.py:325
  177.2 6.4 %all-to-all-start.2 = ((f32[16,2,128,128]{3,2,1,0:T(8,128)}), f32[16,2,128,128]{3,2,1,0:T(8,128)S(1)}, u32[]{:S(2)}, u32[]{:S(2)}) async-start(f32[16,2,128,128]{3,2,1,0:T(8,128)} %later.1), calls=%async_computation.2 | async-start | bytes 4194304 | tf_op jit(solution)/shard_map/all_to_all | solution.py:325
  183.6 3.1 %unpack_first.1.sum_ref = f32[14,128,128]{2,1,0:T(8,128)} custom-call(s32[14]{0:T(128)} %bitcast.21, f32[3]{0:T(128)} %coefs_ref.3, f32[16,128,128]{2,1,0:T(8,128)} %copy-done.6, f32[14,128,128]{2,1,0:T(8,128)} %bitcast.19), custom_call_target="tpu_custom_call" | custom-call | tf_op jit(solution)/shard_map/unpack_first/pallas_call | solution.py:313
  186.7 42.8 %all-to-all-done.2.held_ref = f32[16,2,128,128]{3,2,1,0:T(8,128)S(1)} async-done(((f32[16,2,128,128]{3,2,1,0:T(8,128)}), f32[16,2,128,128]{3,2,1,0:T(8,128)S(1)}, u32[]{:S(2)}, u32[]{:S(2)}) %all-to-all-start.2) | async-done | bytes 2097184 | tf_op jit(solution)/shard_map/all_to_all | solution.py:325
  229.5 1.3 copy-done.5
  230.8 3.6 %unpack_last.1 = (f32[14,128,128]{2,1,0:T(8,128)}, f32[14,128,128]{2,1,0:T(8,128)}, f32[14,128,128]{2,1,0:T(8,128)}) custom-call(s32[14]{0:T(128)} %bitcast.22, f32[3]{0:T(128)} %coefs_ref.3, f32[16,2,128,128]{3,2,1,0:T(8,128)} %copy-done.5, f32[14,128,128]{2,1,0:T(8,128)} %unpack_first.1.sum_ref), custom_call_target="tpu_custom_call" | custom-call | tf_op jit(solution)/shard_map/unpack_last/pallas_call | solution.py:313
  (24 shorter events, 0.0 us)
Async XLA Ops:
  0.6 23.3 %collective-permute-start = (f32[14,128,128]{2,1,0:T(8,128)}, f32[14,128,128]{2,1,0:T(8,128)S(1)}, u32[]{:S(2)}, u32[]{:S(2)}) collective-permute-start(f32[14,128,128]{2,1,0:T(8,128)} %bitcast.15), channel_id=1, source_target_pairs={{0,4},{1,3},{2,0},{3,7},{4,8},{5,1},{6,2},{7,11},{8,12},{9,5},{10,... | collective-permute-start | bytes 2752520 | tf_op jit(solution)/shard_map/ppermute | solution.py:18
  1.1 23.3 %collective-permute-start.2 = (f32[14,128,128]{2,1,0:T(8,128)}, f32[14,128,128]{2,1,0:T(8,128)S(1)}, u32[]{:S(2)}, u32[]{:S(2)}) collective-permute-start(f32[14,128,128]{2,1,0:T(8,128)} %bitcast.16), channel_id=1, source_target_pairs={{0,2},{1,5},{2,6},{3,1},{4,0},{5,9},{6,10},{7,3},{8,4},{9,13},{10,... | collective-permute-start | bytes 2752520 | tf_op jit(solution)/shard_map/ppermute | solution.py:18
  2.7 30.3 %collective-permute-start.4 = (f32[14,128,128]{2,1,0:T(8,128)}, f32[14,128,128]{2,1,0:T(8,128)}, u32[]{:S(2)}, u32[]{:S(2)}) collective-permute-start(f32[14,128,128]{2,1,0:T(8,128)} %bitcast.17), channel_id=1, source_target_pairs={{0,1},{1,0},{2,3},{3,2},{4,5},{5,4},{6,7},{7,6},{8,9},{9,8},{10,11... | collective-permute-start | bytes 2752520 | tf_op jit(solution)/shard_map/ppermute | solution.py:18
  24.0 23.3 %copy-start.7 = (f32[14,128,128]{2,1,0:T(8,128)}, f32[14,128,128]{2,1,0:T(8,128)S(1)}, u32[]{:S(2)}) copy-start(f32[14,128,128]{2,1,0:T(8,128)S(1)} %collective-permute-done.refs_2_) | copy-start | bytes 2752516
  24.0 22.4 %collective-permute-start.1 = (f32[14,128,128]{2,1,0:T(8,128)S(1)}, f32[14,128,128]{2,1,0:T(8,128)S(1)}, u32[]{:S(2)}, u32[]{:S(2)}) collective-permute-start(f32[14,128,128]{2,1,0:T(8,128)S(1)} %collective-permute-done.refs_2_), channel_id=1, source_target_pairs={{0,4},{1,3},{2,0},{3,7},{4,8},{5,1},{6,2},{7,11},{8,12},{9,5},{10,... | collective-permute-start | bytes 2752520 | tf_op jit(solution)/shard_map/ppermute | solution.py:18
  24.4 21.9 %copy-start.9 = (f32[14,128,128]{2,1,0:T(8,128)}, f32[14,128,128]{2,1,0:T(8,128)S(1)}, u32[]{:S(2)}) copy-start(f32[14,128,128]{2,1,0:T(8,128)S(1)} %collective-permute-done.2.refs_4_) | copy-start | bytes 2752516
  24.4 21.9 %collective-permute-start.3 = (f32[14,128,128]{2,1,0:T(8,128)S(1)}, f32[14,128,128]{2,1,0:T(8,128)}, u32[]{:S(2)}, u32[]{:S(2)}) collective-permute-start(f32[14,128,128]{2,1,0:T(8,128)S(1)} %collective-permute-done.2.refs_4_), channel_id=1, source_target_pairs={{0,2},{1,5},{2,6},{3,1},{4,0},{5,9},{6,10},{7,3},{8,4},{9,13},{10,... | collective-permute-start | bytes 2752520 | tf_op jit(solution)/shard_map/ppermute | solution.py:18
  26.0 20.3 %collective-permute-start.5 = (f32[14,128,128]{2,1,0:T(8,128)S(1)}, f32[14,128,128]{2,1,0:T(8,128)}, u32[]{:S(2)}, u32[]{:S(2)}) collective-permute-start(f32[14,128,128]{2,1,0:T(8,128)S(1)} %collective-permute-done.refs_2_), channel_id=1, source_target_pairs={{0,1},{1,0},{2,3},{3,2},{4,5},{5,4},{6,7},{7,6},{8,9},{9,8},{10,11... | collective-permute-start | bytes 2752520 | tf_op jit(solution)/shard_map/ppermute | solution.py:18
  26.0 20.3 %collective-permute-start.6 = (f32[14,128,128]{2,1,0:T(8,128)S(1)}, f32[14,128,128]{2,1,0:T(8,128)}, u32[]{:S(2)}, u32[]{:S(2)}) collective-permute-start(f32[14,128,128]{2,1,0:T(8,128)S(1)} %collective-permute-done.2.refs_4_), channel_id=1, source_target_pairs={{0,1},{1,0},{2,3},{3,2},{4,5},{5,4},{6,7},{7,6},{8,9},{9,8},{10,11... | collective-permute-start | bytes 2752520 | tf_op jit(solution)/shard_map/ppermute | solution.py:18
  46.3 0.9 copy-start.8
  47.3 72.2 %all-to-all-start = ((f32[16,264,128]{2,1,0:T(8,128)}), f32[16,264,128]{2,1,0:T(8,128)S(1)}, u32[]{:S(2)}, u32[]{:S(2)}) async-start(f32[16,264,128]{2,1,0:T(8,128)} %pack.1), calls=%async_computation | async-start | bytes 4325376 | tf_op jit(solution)/shard_map/all_to_all | solution.py:325
  52.4 67.1 %collective-permute-start.9 = (f32[14,128,128]{2,1,0:T(8,128)}, f32[14,128,128]{2,1,0:T(8,128)}, u32[]{:S(2)}, u32[]{:S(2)}) collective-permute-start(f32[14,128,128]{2,1,0:T(8,128)} %copy-done.8), channel_id=1, source_target_pairs={{0,4},{1,3},{2,0},{3,7},{4,8},{5,1},{6,2},{7,11},{8,12},{9,5},{10,... | collective-permute-start | bytes 2752520 | tf_op jit(solution)/shard_map/ppermute | solution.py:18
  52.9 70.4 %collective-permute-start.11 = (f32[14,128,128]{2,1,0:T(8,128)}, f32[14,128,128]{2,1,0:T(8,128)}, u32[]{:S(2)}, u32[]{:S(2)}) collective-permute-start(f32[14,128,128]{2,1,0:T(8,128)} %collective-permute-done.3.refs_2_), channel_id=1, source_target_pairs={{0,2},{1,5},{2,6},{3,1},{4,0},{5,9},{6,10},{7,3},{8,4},{9,13},{10,... | collective-permute-start | bytes 2752520 | tf_op jit(solution)/shard_map/ppermute | solution.py:18
  54.4 78.4 %collective-permute-start.7 = (f32[14,128,128]{2,1,0:T(8,128)}, f32[14,128,128]{2,1,0:T(8,128)S(1)}, u32[]{:S(2)}, u32[]{:S(2)}) collective-permute-start(f32[14,128,128]{2,1,0:T(8,128)} %copy-done.8), channel_id=1, source_target_pairs={{0,1},{1,0},{2,3},{3,2},{4,5},{5,4},{6,7},{7,6},{8,9},{9,8},{10,11... | collective-permute-start | bytes 2752520 | tf_op jit(solution)/shard_map/ppermute | solution.py:18
  54.4 78.4 %collective-permute-start.8 = (f32[14,128,128]{2,1,0:T(8,128)}, f32[14,128,128]{2,1,0:T(8,128)}, u32[]{:S(2)}, u32[]{:S(2)}) collective-permute-start(f32[14,128,128]{2,1,0:T(8,128)} %collective-permute-done.3.refs_2_), channel_id=1, source_target_pairs={{0,1},{1,0},{2,3},{3,2},{4,5},{5,4},{6,7},{7,6},{8,9},{9,8},{10,11... | collective-permute-start | bytes 2752520 | tf_op jit(solution)/shard_map/ppermute | solution.py:18
  119.5 5.4 %copy-start = (f32[16,264,128]{2,1,0:T(8,128)}, f32[16,264,128]{2,1,0:T(8,128)S(1)}, u32[]{:S(2)}) copy-start(f32[16,264,128]{2,1,0:T(8,128)S(1)} %all-to-all-done.t_ref.refs_4_) | copy-start | bytes 6488068
  119.5 20.1 %collective-permute-start.13 = (f32[14,128,128]{2,1,0:T(8,128)}, f32[14,128,128]{2,1,0:T(8,128)}, u32[]{:S(2)}, u32[]{:S(2)}) collective-permute-start(f32[14,128,128]{2,1,0:T(8,128)} %collective-permute-done.9.refs_0_), channel_id=1, source_target_pairs={{0,4},{1,3},{2,0},{3,7},{4,8},{5,1},{6,2},{7,11},{8,12},{9,5},{10,... | collective-permute-start | bytes 2752520 | tf_op jit(solution)/shard_map/ppermute | solution.py:18
  123.3 16.4 %collective-permute-start.10 = (f32[14,128,128]{2,1,0:T(8,128)}, f32[14,128,128]{2,1,0:T(8,128)}, u32[]{:S(2)}, u32[]{:S(2)}) collective-permute-start(f32[14,128,128]{2,1,0:T(8,128)} %collective-permute-done.9.refs_0_), channel_id=1, source_target_pairs={{0,1},{1,0},{2,3},{3,2},{4,5},{5,4},{6,7},{7,6},{8,9},{9,8},{10,11... | collective-permute-start | bytes 2752520 | tf_op jit(solution)/shard_map/ppermute | solution.py:18
  123.3 16.4 %collective-permute-start.12 = (f32[14,128,128]{2,1,0:T(8,128)}, f32[14,128,128]{2,1,0:T(8,128)}, u32[]{:S(2)}, u32[]{:S(2)}) collective-permute-start(f32[14,128,128]{2,1,0:T(8,128)} %collective-permute-done.11.refs_2_), channel_id=1, source_target_pairs={{0,1},{1,0},{2,3},{3,2},{4,5},{5,4},{6,7},{7,6},{8,9},{9,8},{10,11... | collective-permute-start | bytes 2752520 | tf_op jit(solution)/shard_map/ppermute | solution.py:18
  132.8 0.9 copy-start.10
  133.7 5.9 %copy-start.1 = (f32[16,264,128]{2,1,0:T(8,128)S(1)}, f32[16,264,128]{2,1,0:T(8,128)}, u32[]{:S(2)}) copy-start(f32[16,264,128]{2,1,0:T(8,128)} %copy-done) | copy-start | bytes 6488068
  133.7 6.0 %copy-start.2 = (bf16[2048,256]{1,0:T(8,128)(2,1)S(1)}, bf16[2048,256]{1,0:T(8,128)(2,1)}, u32[]{:S(2)}) copy-start(bf16[2048,256]{1,0:T(8,128)(2,1)} %get-tuple-element.21.refs_4_.refs_2_) | copy-start | bytes 3145732
  133.7 6.0 %copy-start.3 = (s32[32]{0:T(128)S(1)}, s32[32]{0:T(128)}, u32[]{:S(2)}) copy-start(s32[32]{0:T(128)} %convert_element_type.8.drops_ref) | copy-start | bytes 388
  133.7 6.0 %copy-start.4 = (s32[17]{0:T(128)S(1)}, s32[17]{0:T(128)}, u32[]{:S(2)}) copy-start(s32[17]{0:T(128)} %pad_add_fusion.1.rows_ref) | copy-start | bytes 208
  139.5 5.2 %collective-permute-start.14 = (f32[14,128,128]{2,1,0:T(8,128)}, f32[14,128,128]{2,1,0:T(8,128)S(1)}, u32[]{:S(2)}, u32[]{:S(2)}) collective-permute-start(f32[14,128,128]{2,1,0:T(8,128)} %collective-permute-done.13.refs_0_), channel_id=1, source_target_pairs={{0,1},{1,0},{2,3},{3,2},{4,5},{5,4},{6,7},{7,6},{8,9},{9,8},{10,11... | collective-permute-start | bytes 2752520 | tf_op jit(solution)/shard_map/ppermute | solution.py:18
  148.5 28.6 %all-to-all-start.1 = ((f32[16,128,128]{2,1,0:T(8,128)}), f32[16,128,128]{2,1,0:T(8,128)S(1)}, u32[]{:S(2)}, u32[]{:S(2)}) async-start(f32[16,128,128]{2,1,0:T(8,128)} %get-tuple-element.30.refs_5_), calls=%async_computation.1 | async-start | bytes 2097152 | tf_op jit(solution)/shard_map/all_to_all | solution.py:325
  177.1 6.4 %copy-start.6 = (f32[16,128,128]{2,1,0:T(8,128)}, f32[16,128,128]{2,1,0:T(8,128)S(1)}, u32[]{:S(2)}) copy-start(f32[16,128,128]{2,1,0:T(8,128)S(1)} %all-to-all-done.1.first_ref) | copy-start | bytes 3145732
  177.2 52.4 %all-to-all-start.2 = ((f32[16,2,128,128]{3,2,1,0:T(8,128)}), f32[16,2,128,128]{3,2,1,0:T(8,128)S(1)}, u32[]{:S(2)}, u32[]{:S(2)}) async-start(f32[16,2,128,128]{3,2,1,0:T(8,128)} %later.1), calls=%async_computation.2 | async-start | bytes 4194304 | tf_op jit(solution)/shard_map/all_to_all | solution.py:325
  229.5 1.3 copy-start.5

commit v14 on v13

--- a/solution.py
+++ b/solution.py
@@ -31,13 +31,13 @@
     return 2 * RING[(RING.index(device // 2) + by) % len(RING)] + device % 2
 
 
-def window_rows(me, total):
+def window_table(total):
     if total != 16:
         steps = [0] + [by for hop in range(1, REACH + 1) for by in (-hop, hop)]
-        return jnp.mod(me + jnp.array(steps, jnp.int32), total), (5, 4, 4, 2)
+        return [[(i + by) % total for by in steps] for i in range(total)], (13, 2)
     order = (0, -1, 1, -2, 2, -3, 3, -4)
     table = [[along_ring(source, by) for by in order for source in (i, i ^ 1)] for i in range(total)]
-    return jnp.array(table, jnp.int32)[me], (6, 4, 4, 2)
+    return table, (14, 2)
 
 
 def gathered_rows(x, total, exchange):
@@ -47,8 +47,8 @@
             for by in (hop, -hop):
                 rows.append(permute(x, lambda i, by=by: (i + by) % total))
         yield exchange()
-        for start, end in ((0, 5), (5, 9), (9, 13), (13, 15)):
-            yield rows[start:end]
+        yield rows[:13]
+        yield rows[13:]
         return
 
     def other_core(row):
@@ -66,9 +66,7 @@
     yield column
     ahead, behind, third = round_of(ahead, behind)
     far = permute(after(ahead, column), lambda i: along_ring(i, 1))
-    yield rows + first
-    made = yield second
-    yield third
+    made = yield rows + first + second + third
     far = after(far, made)
     yield [far, other_core(far)]
 
@@ -124,9 +122,19 @@
     return high, low
 
 
-def kept_rows(total, rows_ref, drops_ref, w):
-    row = rows_ref[w]
-    offset = lax.rem(rows_ref[rows_ref.shape[0] - 1] - row + REACH + total, total)
+class Rows:
+    def __init__(self, total, me_ref, table_ref):
+        self.me = me_ref[0]
+        self.table_ref = table_ref
+        self.window = table_ref.shape[0] // total
+
+    def __getitem__(self, w):
+        return self.table_ref[self.me * self.window + w]
+
+
+def kept_rows(total, rows, drops_ref, w):
+    row = rows[w]
+    offset = lax.rem(rows.me - row + REACH + total, total)
     _, named = place_of(offset, drops_ref[2 * row + 1])
     return named
 
@@ -148,7 +156,8 @@
         yield parts[:, :size] + parts[:, size:]
 
 
-def first_kernel(total, window, start, count, group, drops_ref, rows_ref, t_ref, *refs):
+def first_kernel(total, window, start, count, group, drops_ref, me_ref, table_ref, t_ref, *refs):
+    rows = Rows(total, me_ref, table_ref)
     h_refs = refs[:count]
     if start:
         pair_in, _ = refs[count:count + 2]
@@ -157,17 +166,17 @@
         dense_ref, out_ref, pair_out, blocks = refs[count:count + 4]
     stage, dense, prev, pair, h_sem, t_sem, prev_sem, pair_sem, dense_sem, out_sem = refs[-10:]
     size = t_ref.shape[-1]
-    kept = functools.partial(kept_rows, total, rows_ref, drops_ref)
+    kept = functools.partial(kept_rows, total, rows, drops_ref)
 
     if start:
         pltpu.make_async_copy(pair_in, pair, pair_sem).start()
     else:
         for w in range(window):
-            pltpu.make_async_copy(t_ref.at[rows_ref[w], pl.ds(0, size)], blocks.at[w], t_sem).start()
+            pltpu.make_async_copy(t_ref.at[rows[w], pl.ds(0, size)], blocks.at[w], t_sem).start()
     for r in range(count):
         pltpu.make_async_copy(h_refs[r], stage.at[r], h_sem.at[r]).start()
     for r in range(count):
-        block = t_ref.at[rows_ref[start + r], pl.ds(size, size)]
+        block = t_ref.at[rows[start + r], pl.ds(size, size)]
         pltpu.make_async_copy(block, prev.at[r], prev_sem).start()
     if not start:
         pltpu.make_async_copy(blocks, blocks, t_sem).wait()
@@ -176,10 +185,10 @@
         pltpu.make_async_copy(pair, pair_out, pair_sem).start()
 
     def densify(r, slot, place):
-        row = rows_ref[start + r]
+        row = rows[start + r]
         drop = drops_ref[2 * row]
         for p in range(window):
-            offset = lax.rem(rows_ref[p] - row + REACH + total, total)
+            offset = lax.rem(rows[p] - row + REACH + total, total)
             k, named = place_of(offset, drop)
             high, low = split(jnp.where(named, stage[r, k], 0.0))
             dense[slot, place, pl.ds(0, size), pl.ds(p * size, size)] = high
@@ -215,7 +224,7 @@
         for place, product in enumerate(products_of(dense[slot], pair[...])):
             r = g * group + place
             prev[r] = jnp.where(kept(start + r), 2.0 * product - prev[r], 0.0)
-            pltpu.make_async_copy(prev.at[r], out_ref.at[rows_ref[start + r]], out_sem).start()
+            pltpu.make_async_copy(prev.at[r], out_ref.at[rows[start + r]], out_sem).start()
         return carry
 
     lax.fori_loop(0, groups, one, 0)
@@ -226,37 +235,38 @@
     pltpu.make_async_copy(prev, prev, out_sem).wait()
 
 
-def later_kernel(total, window, group, parts, drops_ref, rows_ref, *refs):
+def later_kernel(total, window, group, parts, drops_ref, me_ref, table_ref, *refs):
+    rows = Rows(total, me_ref, table_ref)
     dense_refs = refs[:len(parts)]
     t_ref, first_ref, out_ref, dense, terms, pairs, dense_sem, t_sem, first_sem, out_sem = refs[len(parts):]
     size = terms.shape[-1]
     groups = window // group
-    kept = functools.partial(kept_rows, total, rows_ref, drops_ref)
+    kept = functools.partial(kept_rows, total, rows, drops_ref)
     for w in range(window):
-        pltpu.make_async_copy(first_ref.at[rows_ref[w]], terms.at[w, 1], first_sem).start()
+        pltpu.make_async_copy(first_ref.at[rows[w]], terms.at[w, 1], first_sem).start()
     start = 0
     for part, dense_ref in zip(parts, dense_refs):
         for w in range(start, start + part):
             pltpu.make_async_copy(dense_ref.at[w - start], dense.at[w], dense_sem.at[w // group]).start()
         start += part
     for w in range(window):
-        pltpu.make_async_copy(t_ref.at[rows_ref[w], pl.ds(0, size)], terms.at[w, 0], t_sem).start()
+        pltpu.make_async_copy(t_ref.at[rows[w], pl.ds(0, size)], terms.at[w, 0], t_sem).start()
     pltpu.make_async_copy(terms.at[:, 1], terms.at[:, 1], first_sem).wait()
     for w in range(window):
         fill_pair(pairs.at[0], terms[w, 1], w)
     pltpu.make_async_copy(terms.at[:, 0], terms.at[:, 0], t_sem).wait()
 
     def one(g, carry, step):
-        rows = dense.at[pl.ds(g * group, group)]
+        held = dense.at[pl.ds(g * group, group)]
         if step == 0:
-            pltpu.make_async_copy(rows, rows, dense_sem.at[g]).wait()
-        for r, product in enumerate(products_of(rows[...], pairs[step])):
+            pltpu.make_async_copy(held, held, dense_sem.at[g]).wait()
+        for r, product in enumerate(products_of(held[...], pairs[step])):
             w = g * group + r
             newest = jnp.where(kept(w), 2.0 * product - terms[w, step], 0.0)
             terms[w, step] = newest
             if step == 0:
                 fill_pair(pairs.at[1], newest, w)
-            pltpu.make_async_copy(terms.at[w, step], out_ref.at[rows_ref[w], step], out_sem).start()
+            pltpu.make_async_copy(terms.at[w, step], out_ref.at[rows[w], step], out_sem).start()
         return carry
 
     for step in range(2):
@@ -339,11 +349,11 @@
         "pack",
         60,
     )
-    indices, parts = window_rows(me, total)
+    table, parts = window_table(total)
     gathered = gathered_rows(h_blocks[0], total, lambda *others: exchange(after(send, *others)))
     column = next(gathered)
     drops = column[:, 2 * size:2 * size + 2, 0].astype(jnp.int32).reshape(-1)
-    rows = jnp.concatenate([indices, me[None]])
+    rows = jnp.array(table, jnp.int32).reshape(-1)
     window = sum(parts)
     dense_shape = (window, 2 * size, window * size)
     pair_shape = (window * size, 2 * size)
@@ -351,7 +361,7 @@
     start = 0
     for part in parts:
         h_rows = gathered.send(dense[-1] if start else None)
-        group = max(g for g in (2, 3, 4, 5) if part % g == 0)
+        group = max(g for g in (2, 7, 13) if part % g == 0)
         scratch = [
             pltpu.VMEM((part, count, size, size), f32),
             pltpu.VMEM((min(2, part // group), group) + dense_shape[1:], bf16),
@@ -368,7 +378,7 @@
             scratch = [pltpu.VMEM((window, size, size), f32)] + scratch
         result = call(
             functools.partial(first_kernel, total, window, start, part, group),
-            [drops, rows],
+            [drops, me[None], rows],
             [column, *h_rows] + ([pair, term1] if start else []),
             [
                 jax.ShapeDtypeStruct((part,) + dense_shape[1:], bf16),
@@ -376,8 +386,8 @@
             ] + ([] if start else [jax.ShapeDtypeStruct(pair_shape, bf16)]),
             scratch,
             "first",
-            60 if start < 10 else 24,
-            {part + 4: 1} if start else {},
+            60,
+            {part + 5: 1} if start else {},
         )
         dense.append(result[0])
         term1 = result[1]
@@ -388,7 +398,7 @@
     group = max(g for g in (3, 4) if window % g == 0)
     (terms,) = call(
         functools.partial(later_kernel, total, window, group, parts),
-        [drops, rows],
+        [drops, me[None], rows],
         [*dense, column, term1],
         [jax.ShapeDtypeStruct((total, 2, size, size), f32)],
         [

time: 237 us -> 235 us (level)
  Pallas kernels: 50.3 us -> 46.6 us
  waiting for transfers between devices: 148 us -> 151 us
    pallas_call x8 -> x6, Pallas kernels: 50.3 us -> 46.6 us  [call(): pl.pallas_call(kernel, out_shape=[pltpu.HBM(out.shape, out.dtype) for out...]
    ppermute x15, waiting for transfers between devices: 99.1 us -> 102 us  [permute(): return lax.ppermute(x, 'row', [(i, target(i)) for i in range(devices)])]
  transfers between devices with their start and end apart: 18 -> 18, of which waited for: 5 -> 8; matrix products, arithmetic and copies ran while one was open for 2% -> 1% of each run, Pallas kernels for 18% -> 17%
where the time goes in v14:
time: 235 us; the launch traced here: 232 us
  waiting for transfers between devices  151 us (64%)
  Pallas kernels  46.6 us (20%)
  starting transfers between devices  27.6 us (12%)
  local copies, waits for them, and re-layouts  2.88 us (1%)
    ppermute x15, waiting for transfers between devices, permute(): return lax.ppermute(x, 'row', [(i, target(i)) for i in range(devices)])  102 us
    all_to_all x3, waiting for transfers between devices, exchange(): return lax.all_to_all(x, 'row', 0, 0, tiled=True)  48.4 us
    pallas_call x6, Pallas kernels, call(): pl.pallas_call(kernel, out_shape=[pltpu.HBM(out.shape, out.dtype) for out...  46.6 us
    all_to_all x3, starting transfers between devices, exchange(): return lax.all_to_all(x, 'row', 0, 0, tiled=True)  17.5 us
    ppermute x15, starting transfers between devices, permute(): return lax.ppermute(x, 'row', [(i, target(i)) for i in range(devices)])  10.1 us
  transfers between devices with their start and end apart: 18, of which 8 were waited for; matrix products, arithmetic and copies ran while one was open for 1% of the time, Pallas kernels for 17%

profile of v14, /device:TPU:22, one launch (start us, length us, event | category | flops | bytes accessed | tf_op | source)
XLA Modules:
  0.0 232.2 jit_solution(16231728764394673775)
XLA Ops:
  0.6 0.5 collective-permute-start
  1.1 1.6 collective-permute-start.2
  2.7 0.0 collective-permute-start.4
  2.7 21.2 %collective-permute-done.refs_2_ = f32[14,128,128]{2,1,0:T(8,128)S(1)} collective-permute-done((f32[14,128,128]{2,1,0:T(8,128)}, f32[14,128,128]{2,1,0:T(8,128)S(1)}, u32[]{:S(2)}, u32[]{:S(2)}) %collective-permute-start) | collective-permute-done | bytes 917536 | tf_op jit(solution)/shard_map/ppermute | solution.py:18
  24.0 0.4 collective-permute-start.1
  24.4 0.0 collective-permute-done.2.refs_4_
  24.4 1.6 collective-permute-start.3
  26.0 0.0 collective-permute-start.5
  26.0 0.5 collective-permute-start.6
  26.5 1.4 fusion.1
  29.2 0.6 pad_add_fusion.info_ref
  29.8 3.2 %pack.1 = f32[16,264,128]{2,1,0:T(8,128)} custom-call(s32[3]{0:T(128)} %pad_add_fusion.info_ref, s32[14]{0:T(128)} %bitcast.18, f32[14,128,128]{2,1,0:T(8,128)} %bitcast.11, f32[14,128,128]{2,1,0:T(8,128)} %bitcast.12), custom_call_target="tpu_custom_call" | custom-call | tf_op jit(solution)/shard_map/pack/pallas_call | solution.py:323
  33.1 0.0 collective-permute-done.4.refs_1_
  33.1 0.0 copy-start.5
  33.1 13.3 %collective-permute-done.1.refs_6_ = f32[14,128,128]{2,1,0:T(8,128)} collective-permute-done((f32[14,128,128]{2,1,0:T(8,128)S(1)}, f32[14,128,128]{2,1,0:T(8,128)}, u32[]{:S(2)}, u32[]{:S(2)}) %collective-permute-start.1) | collective-permute-done | bytes 917536 | tf_op jit(solution)/shard_map/ppermute | solution.py:18
  46.4 0.0 collective-permute-done.3.refs_8_
  46.4 0.0 collective-permute-done.5.refs_3_
  46.4 0.0 collective-permute-done.6.refs_5_
  46.5 5.1 %all-to-all-start = ((f32[16,264,128]{2,1,0:T(8,128)}), f32[16,264,128]{2,1,0:T(8,128)S(1)}, u32[]{:S(2)}, u32[]{:S(2)}) async-start(f32[16,264,128]{2,1,0:T(8,128)} %pack.1), calls=%async_computation | async-start | bytes 4325376 | tf_op jit(solution)/shard_map/all_to_all | solution.py:335
  51.6 0.6 collective-permute-start.9
  52.2 1.5 collective-permute-start.11
  53.6 0.0 collective-permute-start.7
  53.6 0.5 collective-permute-start.8
  54.1 64.5 %collective-permute-done.9.refs_10_ = f32[14,128,128]{2,1,0:T(8,128)S(1)} collective-permute-done((f32[14,128,128]{2,1,0:T(8,128)}, f32[14,128,128]{2,1,0:T(8,128)S(1)}, u32[]{:S(2)}, u32[]{:S(2)}) %collective-permute-start.9) | collective-permute-done | bytes 917536 | tf_op jit(solution)/shard_map/ppermute | solution.py:18
  118.7 0.5 collective-permute-start.10
  119.2 0.4 collective-permute-done.11.refs_12_
  119.6 0.0 collective-permute-start.12
  119.6 0.0 all-to-all-done.t_ref.refs_2_
  119.6 2.0 collective-permute-start.13
  121.6 0.3 fusion
  121.9 0.6 convert_element_type.8.drops_ref
  122.6 0.0 collective-permute-done.7.refs_7_
  122.6 0.0 collective-permute-done.8.refs_9_
  122.6 0.0 collective-permute-done.10.refs_11_
  122.6 0.4 collective-permute-done.12.refs_13_
  123.0 14.7 %first.2 = (bf16[14,256,2048]{2,1,0:T(8,128)(2,1)}, f32[16,128,128]{2,1,0:T(8,128)}, bf16[2048,256]{1,0:T(8,128)(2,1)}) custom-call(s32[32]{0:T(128)} %convert_element_type.8.drops_ref, s32[1]{0:T(128)} %bitcast.1.me_ref, s32[256]{0:T(256)} %constant.40.table_ref, f32[16,264,128]{2,1,0:T(8,128)} %copy-done, f32[14,128,128]{2,1,0:T(8,128)} %bitcast.16, ...), custom_call_target="tpu_custom_call" | custom-call | tf_op jit(solution)/shard_map/first/pallas_call | solution.py:323
  137.7 0.4 collective-permute-start.14
  138.1 2.3 %collective-permute-done.14.refs_1_ = f32[14,128,128]{2,1,0:T(8,128)S(1)} collective-permute-done((f32[14,128,128]{2,1,0:T(8,128)}, f32[14,128,128]{2,1,0:T(8,128)S(1)}, u32[]{:S(2)}, u32[]{:S(2)}) %collective-permute-start.14) | collective-permute-done | bytes 917536 | tf_op jit(solution)/shard_map/ppermute | solution.py:18
  140.5 0.9 copy-done.7
  141.4 4.2 %first.3 = (bf16[2,256,2048]{2,1,0:T(8,128)(2,1)}, f32[16,128,128]{2,1,0:T(8,128)}) custom-call(s32[32]{0:T(128)} %convert_element_type.8.drops_ref, s32[1]{0:T(128)} %bitcast.1.me_ref, s32[256]{0:T(256)} %constant.40.table_ref, f32[16,264,128]{2,1,0:T(8,128)} %copy-done, ...), custom_call_target="tpu_custom_call", output_to_operand_aliasing={{1}: (7, {})} | custom-call | tf_op jit(solution)/shard_map/first/pallas_call | solution.py:323
  145.6 5.9 %all-to-all-start.1 = ((f32[16,128,128]{2,1,0:T(8,128)}), f32[16,128,128]{2,1,0:T(8,128)S(1)}, u32[]{:S(2)}, u32[]{:S(2)}) async-start(f32[16,128,128]{2,1,0:T(8,128)} %get-tuple-element.22.refs_3_), calls=%async_computation.1 | async-start | bytes 2097152 | tf_op jit(solution)/shard_map/all_to_all | solution.py:335
  151.5 17.8 %later.1 = f32[16,2,128,128]{3,2,1,0:T(8,128)} custom-call(s32[32]{0:T(128)} %convert_element_type.8.drops_ref, s32[1]{0:T(128)} %bitcast.1.me_ref, s32[256]{0:T(256)} %constant.40.table_ref, bf16[14,256,2048]{2,1,0:T(8,128)(2,1)} %get-tuple-element.16.refs_0_, bf16[2,256,2048]{2,1,0:T(8,128)(2,1)} %get-tuple-element.21.refs_1_, f32[16,264,128]{2,1,0:T(8,128)} %copy-done, ...), custom_call_target="tpu_custom_call" | custom-call | tf_op jit(solution)/shard_map/later/pallas_call | solution.py:323
  169.3 5.6 %all-to-all-done.1.first_ref = f32[16,128,128]{2,1,0:T(8,128)S(1)} async-done(((f32[16,128,128]{2,1,0:T(8,128)}), f32[16,128,128]{2,1,0:T(8,128)S(1)}, u32[]{:S(2)}, u32[]{:S(2)}) %all-to-all-start.1) | async-done | bytes 1048608 | tf_op jit(solution)/shard_map/all_to_all | solution.py:335
  174.9 6.4 %all-to-all-start.2 = ((f32[16,2,128,128]{3,2,1,0:T(8,128)}), f32[16,2,128,128]{3,2,1,0:T(8,128)S(1)}, u32[]{:S(2)}, u32[]{:S(2)}) async-start(f32[16,2,128,128]{3,2,1,0:T(8,128)} %later.1), calls=%async_computation.2 | async-start | bytes 4194304 | tf_op jit(solution)/shard_map/all_to_all | solution.py:335
  181.3 3.1 %unpack_first.1.sum_ref = f32[14,128,128]{2,1,0:T(8,128)} custom-call(s32[14]{0:T(128)} %bitcast.19, f32[3]{0:T(128)} %coefs_ref.3, f32[16,128,128]{2,1,0:T(8,128)} %copy-done.2, f32[14,128,128]{2,1,0:T(8,128)} %bitcast.17), custom_call_target="tpu_custom_call" | custom-call | tf_op jit(solution)/shard_map/unpack_first/pallas_call | solution.py:323
  184.4 42.8 %all-to-all-done.2.held_ref = f32[16,2,128,128]{3,2,1,0:T(8,128)S(1)} async-done(((f32[16,2,128,128]{3,2,1,0:T(8,128)}), f32[16,2,128,128]{3,2,1,0:T(8,128)S(1)}, u32[]{:S(2)}, u32[]{:S(2)}) %all-to-all-start.2) | async-done | bytes 2097184 | tf_op jit(solution)/shard_map/all_to_all | solution.py:335
  227.2 1.3 copy-done.1
  228.6 3.6 %unpack_last.1 = (f32[14,128,128]{2,1,0:T(8,128)}, f32[14,128,128]{2,1,0:T(8,128)}, f32[14,128,128]{2,1,0:T(8,128)}) custom-call(s32[14]{0:T(128)} %bitcast.20, f32[3]{0:T(128)} %coefs_ref.3, f32[16,2,128,128]{3,2,1,0:T(8,128)} %copy-done.1, f32[14,128,128]{2,1,0:T(8,128)} %unpack_first.1.sum_ref), custom_call_target="tpu_custom_call" | custom-call | tf_op jit(solution)/shard_map/unpack_last/pallas_call | solution.py:323
  (14 shorter events, 0.0 us)
Async XLA Ops:
  0.6 23.3 %collective-permute-start = (f32[14,128,128]{2,1,0:T(8,128)}, f32[14,128,128]{2,1,0:T(8,128)S(1)}, u32[]{:S(2)}, u32[]{:S(2)}) collective-permute-start(f32[14,128,128]{2,1,0:T(8,128)} %bitcast.13), channel_id=1, source_target_pairs={{0,4},{1,3},{2,0},{3,7},{4,8},{5,1},{6,2},{7,11},{8,12},{9,5},{10,... | collective-permute-start | bytes 2752520 | tf_op jit(solution)/shard_map/ppermute | solution.py:18
  1.1 23.3 %collective-permute-start.2 = (f32[14,128,128]{2,1,0:T(8,128)}, f32[14,128,128]{2,1,0:T(8,128)S(1)}, u32[]{:S(2)}, u32[]{:S(2)}) collective-permute-start(f32[14,128,128]{2,1,0:T(8,128)} %bitcast.14), channel_id=1, source_target_pairs={{0,2},{1,5},{2,6},{3,1},{4,0},{5,9},{6,10},{7,3},{8,4},{9,13},{10,... | collective-permute-start | bytes 2752520 | tf_op jit(solution)/shard_map/ppermute | solution.py:18
  2.7 30.4 %collective-permute-start.4 = (f32[14,128,128]{2,1,0:T(8,128)}, f32[14,128,128]{2,1,0:T(8,128)S(1)}, u32[]{:S(2)}, u32[]{:S(2)}) collective-permute-start(f32[14,128,128]{2,1,0:T(8,128)} %bitcast.15), channel_id=1, source_target_pairs={{0,1},{1,0},{2,3},{3,2},{4,5},{5,4},{6,7},{7,6},{8,9},{9,8},{10,11... | collective-permute-start | bytes 2752520 | tf_op jit(solution)/shard_map/ppermute | solution.py:18
  24.0 22.5 %copy-start.3 = (f32[14,128,128]{2,1,0:T(8,128)}, f32[14,128,128]{2,1,0:T(8,128)S(1)}, u32[]{:S(2)}) copy-start(f32[14,128,128]{2,1,0:T(8,128)S(1)} %collective-permute-done.refs_2_) | copy-start | bytes 2752516
  24.0 22.5 %collective-permute-start.1 = (f32[14,128,128]{2,1,0:T(8,128)S(1)}, f32[14,128,128]{2,1,0:T(8,128)}, u32[]{:S(2)}, u32[]{:S(2)}) collective-permute-start(f32[14,128,128]{2,1,0:T(8,128)S(1)} %collective-permute-done.refs_2_), channel_id=1, source_target_pairs={{0,4},{1,3},{2,0},{3,7},{4,8},{5,1},{6,2},{7,11},{8,12},{9,5},{10,... | collective-permute-start | bytes 2752520 | tf_op jit(solution)/shard_map/ppermute | solution.py:18
  24.4 22.0 %copy-start.4 = (f32[14,128,128]{2,1,0:T(8,128)}, f32[14,128,128]{2,1,0:T(8,128)S(1)}, u32[]{:S(2)}) copy-start(f32[14,128,128]{2,1,0:T(8,128)S(1)} %collective-permute-done.2.refs_4_) | copy-start | bytes 2752516
  24.4 22.0 %collective-permute-start.3 = (f32[14,128,128]{2,1,0:T(8,128)S(1)}, f32[14,128,128]{2,1,0:T(8,128)}, u32[]{:S(2)}, u32[]{:S(2)}) collective-permute-start(f32[14,128,128]{2,1,0:T(8,128)S(1)} %collective-permute-done.2.refs_4_), channel_id=1, source_target_pairs={{0,2},{1,5},{2,6},{3,1},{4,0},{5,9},{6,10},{7,3},{8,4},{9,13},{10,... | collective-permute-start | bytes 2752520 | tf_op jit(solution)/shard_map/ppermute | solution.py:18
  26.0 20.4 %collective-permute-start.5 = (f32[14,128,128]{2,1,0:T(8,128)S(1)}, f32[14,128,128]{2,1,0:T(8,128)}, u32[]{:S(2)}, u32[]{:S(2)}) collective-permute-start(f32[14,128,128]{2,1,0:T(8,128)S(1)} %collective-permute-done.refs_2_), channel_id=1, source_target_pairs={{0,1},{1,0},{2,3},{3,2},{4,5},{5,4},{6,7},{7,6},{8,9},{9,8},{10,11... | collective-permute-start | bytes 2752520 | tf_op jit(solution)/shard_map/ppermute | solution.py:18
  26.0 20.4 %collective-permute-start.6 = (f32[14,128,128]{2,1,0:T(8,128)S(1)}, f32[14,128,128]{2,1,0:T(8,128)}, u32[]{:S(2)}, u32[]{:S(2)}) collective-permute-start(f32[14,128,128]{2,1,0:T(8,128)S(1)} %collective-permute-done.2.refs_4_), channel_id=1, source_target_pairs={{0,1},{1,0},{2,3},{3,2},{4,5},{5,4},{6,7},{7,6},{8,9},{9,8},{10,11... | collective-permute-start | bytes 2752520 | tf_op jit(solution)/shard_map/ppermute | solution.py:18
  33.1 13.4 %copy-start.5 = (f32[14,128,128]{2,1,0:T(8,128)}, f32[14,128,128]{2,1,0:T(8,128)S(1)}, u32[]{:S(2)}) copy-start(f32[14,128,128]{2,1,0:T(8,128)S(1)} %collective-permute-done.4.refs_1_) | copy-start | bytes 2752516
  46.5 73.1 %all-to-all-start = ((f32[16,264,128]{2,1,0:T(8,128)}), f32[16,264,128]{2,1,0:T(8,128)S(1)}, u32[]{:S(2)}, u32[]{:S(2)}) async-start(f32[16,264,128]{2,1,0:T(8,128)} %pack.1), calls=%async_computation | async-start | bytes 4325376 | tf_op jit(solution)/shard_map/all_to_all | solution.py:335
  51.6 67.1 %collective-permute-start.9 = (f32[14,128,128]{2,1,0:T(8,128)}, f32[14,128,128]{2,1,0:T(8,128)S(1)}, u32[]{:S(2)}, u32[]{:S(2)}) collective-permute-start(f32[14,128,128]{2,1,0:T(8,128)} %collective-permute-done.1.refs_6_), channel_id=1, source_target_pairs={{0,4},{1,3},{2,0},{3,7},{4,8},{5,1},{6,2},{7,11},{8,12},{9,5},{10,... | collective-permute-start | bytes 2752520 | tf_op jit(solution)/shard_map/ppermute | solution.py:18
  52.2 67.4 %collective-permute-start.11 = (f32[14,128,128]{2,1,0:T(8,128)}, f32[14,128,128]{2,1,0:T(8,128)}, u32[]{:S(2)}, u32[]{:S(2)}) collective-permute-start(f32[14,128,128]{2,1,0:T(8,128)} %collective-permute-done.3.refs_8_), channel_id=1, source_target_pairs={{0,2},{1,5},{2,6},{3,1},{4,0},{5,9},{6,10},{7,3},{8,4},{9,13},{10,... | collective-permute-start | bytes 2752520 | tf_op jit(solution)/shard_map/ppermute | solution.py:18
  53.6 68.9 %collective-permute-start.7 = (f32[14,128,128]{2,1,0:T(8,128)}, f32[14,128,128]{2,1,0:T(8,128)}, u32[]{:S(2)}, u32[]{:S(2)}) collective-permute-start(f32[14,128,128]{2,1,0:T(8,128)} %collective-permute-done.1.refs_6_), channel_id=1, source_target_pairs={{0,1},{1,0},{2,3},{3,2},{4,5},{5,4},{6,7},{7,6},{8,9},{9,8},{10,11... | collective-permute-start | bytes 2752520 | tf_op jit(solution)/shard_map/ppermute | solution.py:18
  53.6 68.9 %collective-permute-start.8 = (f32[14,128,128]{2,1,0:T(8,128)}, f32[14,128,128]{2,1,0:T(8,128)}, u32[]{:S(2)}, u32[]{:S(2)}) collective-permute-start(f32[14,128,128]{2,1,0:T(8,128)} %collective-permute-done.3.refs_8_), channel_id=1, source_target_pairs={{0,1},{1,0},{2,3},{3,2},{4,5},{5,4},{6,7},{7,6},{8,9},{9,8},{10,11... | collective-permute-start | bytes 2752520 | tf_op jit(solution)/shard_map/ppermute | solution.py:18
  118.7 4.3 %copy-start.6 = (f32[14,128,128]{2,1,0:T(8,128)}, f32[14,128,128]{2,1,0:T(8,128)S(1)}, u32[]{:S(2)}) copy-start(f32[14,128,128]{2,1,0:T(8,128)S(1)} %collective-permute-done.9.refs_10_) | copy-start | bytes 2752516
  118.7 3.9 %collective-permute-start.10 = (f32[14,128,128]{2,1,0:T(8,128)S(1)}, f32[14,128,128]{2,1,0:T(8,128)}, u32[]{:S(2)}, u32[]{:S(2)}) collective-permute-start(f32[14,128,128]{2,1,0:T(8,128)S(1)} %collective-permute-done.9.refs_10_), channel_id=1, source_target_pairs={{0,1},{1,0},{2,3},{3,2},{4,5},{5,4},{6,7},{7,6},{8,9},{9,8},{10,11... | collective-permute-start | bytes 2752520 | tf_op jit(solution)/shard_map/ppermute | solution.py:18
  119.6 3.4 %collective-permute-start.12 = (f32[14,128,128]{2,1,0:T(8,128)}, f32[14,128,128]{2,1,0:T(8,128)}, u32[]{:S(2)}, u32[]{:S(2)}) collective-permute-start(f32[14,128,128]{2,1,0:T(8,128)} %collective-permute-done.11.refs_12_), channel_id=1, source_target_pairs={{0,1},{1,0},{2,3},{3,2},{4,5},{5,4},{6,7},{7,6},{8,9},{9,8},{10,11... | collective-permute-start | bytes 2752520 | tf_op jit(solution)/shard_map/ppermute | solution.py:18
  119.6 3.4 %copy-start = (f32[16,264,128]{2,1,0:T(8,128)}, f32[16,264,128]{2,1,0:T(8,128)S(1)}, u32[]{:S(2)}) copy-start(f32[16,264,128]{2,1,0:T(8,128)S(1)} %all-to-all-done.t_ref.refs_2_) | copy-start | bytes 6488068
  119.6 18.1 %collective-permute-start.13 = (f32[14,128,128]{2,1,0:T(8,128)S(1)}, f32[14,128,128]{2,1,0:T(8,128)}, u32[]{:S(2)}, u32[]{:S(2)}) collective-permute-start(f32[14,128,128]{2,1,0:T(8,128)S(1)} %collective-permute-done.9.refs_10_), channel_id=1, source_target_pairs={{0,4},{1,3},{2,0},{3,7},{4,8},{5,1},{6,2},{7,11},{8,12},{9,5},{10,... | collective-permute-start | bytes 2752520 | tf_op jit(solution)/shard_map/ppermute | solution.py:18
  137.7 2.7 %collective-permute-start.14 = (f32[14,128,128]{2,1,0:T(8,128)}, f32[14,128,128]{2,1,0:T(8,128)S(1)}, u32[]{:S(2)}, u32[]{:S(2)}) collective-permute-start(f32[14,128,128]{2,1,0:T(8,128)} %collective-permute-done.13.refs_0_), channel_id=1, source_target_pairs={{0,1},{1,0},{2,3},{3,2},{4,5},{5,4},{6,7},{7,6},{8,9},{9,8},{10,11... | collective-permute-start | bytes 2752520 | tf_op jit(solution)/shard_map/ppermute | solution.py:18
  140.5 0.9 copy-start.7
  145.6 29.3 %all-to-all-start.1 = ((f32[16,128,128]{2,1,0:T(8,128)}), f32[16,128,128]{2,1,0:T(8,128)S(1)}, u32[]{:S(2)}, u32[]{:S(2)}) async-start(f32[16,128,128]{2,1,0:T(8,128)} %get-tuple-element.22.refs_3_), calls=%async_computation.1 | async-start | bytes 2097152 | tf_op jit(solution)/shard_map/all_to_all | solution.py:335
  174.9 6.4 %copy-start.2 = (f32[16,128,128]{2,1,0:T(8,128)}, f32[16,128,128]{2,1,0:T(8,128)S(1)}, u32[]{:S(2)}) copy-start(f32[16,128,128]{2,1,0:T(8,128)S(1)} %all-to-all-done.1.first_ref) | copy-start | bytes 3145732
  174.9 52.4 %all-to-all-start.2 = ((f32[16,2,128,128]{3,2,1,0:T(8,128)}), f32[16,2,128,128]{3,2,1,0:T(8,128)S(1)}, u32[]{:S(2)}, u32[]{:S(2)}) async-start(f32[16,2,128,128]{3,2,1,0:T(8,128)} %later.1), calls=%async_computation.2 | async-start | bytes 4194304 | tf_op jit(solution)/shard_map/all_to_all | solution.py:335
  227.2 1.3 copy-start.1

commit v15 on v14

--- a/solution.py
+++ b/solution.py
@@ -9,6 +9,7 @@
 
 REACH = 7
 NOTE = 8
+LAST = 2
 SMEM = pl.BlockSpec(memory_space=pltpu.SMEM)
 ANY = pl.BlockSpec(memory_space=pl.ANY)
 
@@ -34,10 +35,10 @@
 def window_table(total):
     if total != 16:
         steps = [0] + [by for hop in range(1, REACH + 1) for by in (-hop, hop)]
-        return [[(i + by) % total for by in steps] for i in range(total)], (13, 2)
+        return [[(i + by) % total for by in steps] for i in range(total)], (13, LAST)
     order = (0, -1, 1, -2, 2, -3, 3, -4)
     table = [[along_ring(source, by) for by in order for source in (i, i ^ 1)] for i in range(total)]
-    return table, (14, 2)
+    return table, (14, LAST)
 
 
 def gathered_rows(x, total, exchange):
@@ -160,8 +161,7 @@
     rows = Rows(total, me_ref, table_ref)
     h_refs = refs[:count]
     if start:
-        pair_in, _ = refs[count:count + 2]
-        dense_ref, out_ref = refs[count + 2:count + 4]
+        pair_in, dense_ref, out_ref = refs[count:count + 3]
     else:
         dense_ref, out_ref, pair_out, blocks = refs[count:count + 4]
     stage, dense, prev, pair, h_sem, t_sem, prev_sem, pair_sem, dense_sem, out_sem = refs[-10:]
@@ -224,7 +224,8 @@
         for place, product in enumerate(products_of(dense[slot], pair[...])):
             r = g * group + place
             prev[r] = jnp.where(kept(start + r), 2.0 * product - prev[r], 0.0)
-            pltpu.make_async_copy(prev.at[r], out_ref.at[rows[start + r]], out_sem).start()
+            block = out_ref.at[r if start else rows[start + r]]
+            pltpu.make_async_copy(prev.at[r], block, out_sem).start()
         return carry
 
     lax.fori_loop(0, groups, one, 0)
@@ -238,12 +239,14 @@
 def later_kernel(total, window, group, parts, drops_ref, me_ref, table_ref, *refs):
     rows = Rows(total, me_ref, table_ref)
     dense_refs = refs[:len(parts)]
-    t_ref, first_ref, out_ref, dense, terms, pairs, dense_sem, t_sem, first_sem, out_sem = refs[len(parts):]
+    t_ref, first_ref, last_ref, out_ref, dense, terms, pairs, dense_sem, t_sem, first_sem, out_sem = refs[len(parts):]
     size = terms.shape[-1]
     groups = window // group
     kept = functools.partial(kept_rows, total, rows, drops_ref)
     for w in range(window):
-        pltpu.make_async_copy(first_ref.at[rows[w]], terms.at[w, 1], first_sem).start()
+        late = w - (window - LAST)
+        source = first_ref.at[rows[w]] if late < 0 else last_ref.at[late]
+        pltpu.make_async_copy(source, terms.at[w, 1], first_sem).start()
     start = 0
     for part, dense_ref in zip(parts, dense_refs):
         for w in range(start, start + part):
@@ -274,11 +277,24 @@
     pltpu.make_async_copy(terms, terms, out_sem).wait()
 
 
-def unpack_first_kernel(cols_ref, coefs_ref, first_ref, density_ref, out_ref, sums, one, sems):
+def unpack_first_kernel(
+    cols_ref, me_ref, sources_ref, coefs_ref, first_ref, density_ref, *refs
+):
+    late_refs = refs[:LAST]
+    out_ref, sums, one, sems = refs[LAST:]
     load = pltpu.make_async_copy(density_ref, sums, sems.at[0])
     load.start()
+    late = [sources_ref[me_ref[0] * LAST + r] for r in range(LAST)]
     for k in range(cols_ref.shape[0]):
-        pltpu.make_async_copy(first_ref.at[cols_ref[k]], one.at[k], sems.at[1]).start()
+        col = cols_ref[k]
+        early = jnp.logical_and(col != late[0], col != late[1])
+        choices = [(early, first_ref.at[col])] + [(col == late[r], late_refs[r]) for r in range(LAST)]
+        for chosen, source in choices:
+
+            @pl.when(chosen)
+            def _(source=source, k=k):
+                pltpu.make_async_copy(source, one.at[k], sems.at[1]).start()
+
     load.wait()
     pltpu.make_async_copy(one, one, sems.at[1]).wait()
     sums[...] += coefs_ref[0] * one[...]
@@ -379,27 +395,31 @@
         result = call(
             functools.partial(first_kernel, total, window, start, part, group),
             [drops, me[None], rows],
-            [column, *h_rows] + ([pair, term1] if start else []),
+            [column, *h_rows] + ([pair] if start else []),
             [
                 jax.ShapeDtypeStruct((part,) + dense_shape[1:], bf16),
-                jax.ShapeDtypeStruct((total, size, size), f32),
-            ] + ([] if start else [jax.ShapeDtypeStruct(pair_shape, bf16)]),
+                jax.ShapeDtypeStruct((LAST if start else total, size, size), f32),
+            ]
+            + ([] if start else [jax.ShapeDtypeStruct(pair_shape, bf16)]),
             scratch,
             "first",
             60,
-            {part + 5: 1} if start else {},
         )
         dense.append(result[0])
-        term1 = result[1]
-        if not start:
-            pair = result[2]
+        if start:
+            late1 = result[1]
+        else:
+            term1, pair = result[1:]
         start += part
     back1 = exchange(term1)
+    targets = [[row[window - LAST + r] for row in table] for r in range(LAST)]
+    late_back = [permute(late1[r], lambda i, r=r: targets[r][i]) for r in range(LAST)]
+    sources = jnp.array([[to.index(i) for to in targets] for i in range(total)], jnp.int32).reshape(-1)
     group = max(g for g in (3, 4) if window % g == 0)
     (terms,) = call(
         functools.partial(later_kernel, total, window, group, parts),
         [drops, me[None], rows],
-        [*dense, column, term1],
+        [*dense, column, term1, late1],
         [jax.ShapeDtypeStruct((total, 2, size, size), f32)],
         [
             pltpu.VMEM(dense_shape, bf16),
@@ -413,11 +433,11 @@
         "later",
         60,
     )
-    back = exchange(after(terms, back1))
+    back = exchange(after(terms, back1, *late_back))
     (sums,) = call(
         unpack_first_kernel,
-        [t_cols[0], coefs],
-        [back1, density_in[0]],
+        [t_cols[0], me[None], sources, coefs],
+        [back1, density_in[0], *late_back],
         [row],
         [row_scratch, row_scratch, dma((2,))],
         "unpack_first",

time: 235 us -> 234 us (level)
  waiting for transfers between devices: 151 us -> 145 us
  starting transfers between devices: 27.6 us -> 31.3 us
    all_to_all x3, waiting for transfers between devices: 48.4 us -> 42.8 us  [exchange(): return lax.all_to_all(x, 'row', 0, 0, tiled=True)]
    ppermute x15 -> x17, starting transfers between devices: 10.1 us -> 12.5 us  [permute(): return lax.ppermute(x, 'row', [(i, target(i)) for i in range(devices)])]
    ppermute x15 -> x17, waiting for transfers between devices: 102 us -> 103 us  [permute(): return lax.ppermute(x, 'row', [(i, target(i)) for i in range(devices)])]
  transfers between devices with their start and end apart: 18 -> 20, of which waited for: 8 -> 7; matrix products, arithmetic and copies ran while one was open for 1% -> 2% of each run, Pallas kernels for 17% -> 19%
where the time goes in v15:
time: 234 us; the launch traced here: 231 us
  waiting for transfers between devices  145 us (62%)
  Pallas kernels  46.6 us (20%)
  starting transfers between devices  31.3 us (13%)
  local copies, waits for them, and re-layouts  3.81 us (2%)
    ppermute x17, waiting for transfers between devices, permute(): return lax.ppermute(x, 'row', [(i, target(i)) for i in range(devices)])  103 us
    pallas_call x6, Pallas kernels, call(): pl.pallas_call(kernel, out_shape=[pltpu.HBM(out.shape, out.dtype) for out...  46.6 us
    all_to_all x3, waiting for transfers between devices, exchange(): return lax.all_to_all(x, 'row', 0, 0, tiled=True)  42.8 us
    all_to_all x3, starting transfers between devices, exchange(): return lax.all_to_all(x, 'row', 0, 0, tiled=True)  18.8 us
    ppermute x17, starting transfers between devices, permute(): return lax.ppermute(x, 'row', [(i, target(i)) for i in range(devices)])  12.5 us
  transfers between devices with their start and end apart: 20, of which 7 were waited for; matrix products, arithmetic and copies ran while one was open for 2% of the time, Pallas kernels for 19%

profile of v15, /device:TPU:22, one launch (start us, length us, event | category | flops | bytes accessed | tf_op | source)
XLA Modules:
  0.0 231.4 jit_solution(16721666166577981553)
XLA Ops:
  0.6 0.5 collective-permute-start
  1.1 1.6 collective-permute-start.2
  2.7 0.0 collective-permute-start.4
  2.7 21.2 %collective-permute-done.refs_2_ = f32[14,128,128]{2,1,0:T(8,128)S(1)} collective-permute-done((f32[14,128,128]{2,1,0:T(8,128)}, f32[14,128,128]{2,1,0:T(8,128)S(1)}, u32[]{:S(2)}, u32[]{:S(2)}) %collective-permute-start) | collective-permute-done | bytes 917536 | tf_op jit(solution)/shard_map/ppermute | solution.py:19
  24.0 0.4 collective-permute-start.1
  24.4 0.0 collective-permute-done.2.refs_4_
  24.4 1.6 collective-permute-start.3
  26.0 0.5 collective-permute-start.6
  26.5 1.3 fusion.1
  29.1 0.6 pad_add_fusion.info_ref
  29.7 3.3 %pack.1 = f32[16,264,128]{2,1,0:T(8,128)} custom-call(s32[3]{0:T(128)} %pad_add_fusion.info_ref, s32[14]{0:T(128)} %bitcast.22, f32[14,128,128]{2,1,0:T(8,128)} %bitcast.15, f32[14,128,128]{2,1,0:T(8,128)} %bitcast.16), custom_call_target="tpu_custom_call" | custom-call | tf_op jit(solution)/shard_map/pack/pallas_call | solution.py:339
  33.0 0.0 collective-permute-done.4.refs_1_
  33.0 0.0 copy-start.5
  33.0 13.4 %collective-permute-done.1.refs_6_ = f32[14,128,128]{2,1,0:T(8,128)} collective-permute-done((f32[14,128,128]{2,1,0:T(8,128)S(1)}, f32[14,128,128]{2,1,0:T(8,128)}, u32[]{:S(2)}, u32[]{:S(2)}) %collective-permute-start.1) | collective-permute-done | bytes 917536 | tf_op jit(solution)/shard_map/ppermute | solution.py:19
  46.4 0.0 collective-permute-done.3.refs_8_
  46.5 5.1 %all-to-all-start = ((f32[16,264,128]{2,1,0:T(8,128)}), f32[16,264,128]{2,1,0:T(8,128)S(1)}, u32[]{:S(2)}, u32[]{:S(2)}) async-start(f32[16,264,128]{2,1,0:T(8,128)} %pack.1), calls=%async_computation | async-start | bytes 4325376 | tf_op jit(solution)/shard_map/all_to_all | solution.py:351
  51.6 0.6 collective-permute-start.9
  52.2 1.5 collective-permute-start.11
  53.6 0.0 collective-permute-start.7
  53.6 0.5 collective-permute-start.8
  54.1 64.5 %collective-permute-done.9.refs_10_ = f32[14,128,128]{2,1,0:T(8,128)} collective-permute-done((f32[14,128,128]{2,1,0:T(8,128)}, f32[14,128,128]{2,1,0:T(8,128)}, u32[]{:S(2)}, u32[]{:S(2)}) %collective-permute-start.9) | collective-permute-done | bytes 917536 | tf_op jit(solution)/shard_map/ppermute | solution.py:19
  118.7 0.4 collective-permute-start.10
  119.1 0.4 collective-permute-done.11.refs_12_
  119.5 0.0 collective-permute-start.12
  119.5 0.0 all-to-all-done.t_ref.refs_2_
  119.5 2.2 collective-permute-start.13
  121.7 0.3 fusion
  122.0 0.6 convert_element_type.8.drops_ref
  122.7 0.0 collective-permute-done.7.refs_7_
  122.7 0.0 collective-permute-done.8.refs_9_
  122.7 0.0 collective-permute-done.10.refs_11_
  122.7 14.7 %first.2 = (bf16[14,256,2048]{2,1,0:T(8,128)(2,1)}, f32[16,128,128]{2,1,0:T(8,128)}, bf16[2048,256]{1,0:T(8,128)(2,1)}) custom-call(s32[32]{0:T(128)} %convert_element_type.8.drops_ref, s32[1]{0:T(128)} %bitcast.1.me_ref, s32[256]{0:T(256)} %constant.43.table_ref, f32[16,264,128]{2,1,0:T(8,128)} %copy-done, f32[14,128,128]{2,1,0:T(8,128)} %bitcast.21, ...), custom_call_target="tpu_custom_call" | custom-call | tf_op jit(solution)/shard_map/first/pallas_call | solution.py:339
  137.4 6.0 %all-to-all-start.1 = ((f32[16,128,128]{2,1,0:T(8,128)}), f32[16,128,128]{2,1,0:T(8,128)S(1)}, u32[]{:S(2)}, u32[]{:S(2)}) async-start(f32[16,128,128]{2,1,0:T(8,128)} %get-tuple-element.21.refs_3_), calls=%async_computation.1 | async-start | bytes 2097152 | tf_op jit(solution)/shard_map/all_to_all | solution.py:351
  143.4 0.2 collective-permute-start.14
  143.7 2.5 %collective-permute-done.14.refs_1_ = f32[14,128,128]{2,1,0:T(8,128)S(1)} collective-permute-done((f32[14,128,128]{2,1,0:T(8,128)}, f32[14,128,128]{2,1,0:T(8,128)S(1)}, u32[]{:S(2)}, u32[]{:S(2)}) %collective-permute-start.14) | collective-permute-done | bytes 917536 | tf_op jit(solution)/shard_map/ppermute | solution.py:19
  146.2 0.9 copy-done.7
  147.1 4.1 %first.3 = (bf16[2,256,2048]{2,1,0:T(8,128)(2,1)}, f32[2,128,128]{2,1,0:T(8,128)}) custom-call(s32[32]{0:T(128)} %convert_element_type.8.drops_ref, s32[1]{0:T(128)} %bitcast.1.me_ref, s32[256]{0:T(256)} %constant.43.table_ref, f32[16,264,128]{2,1,0:T(8,128)} %copy-done, f32[14,128,128]{2,1,0:T(8,128)} %collective-permute-done.13.refs_0_, ...), custom_call_target="tpu_custom_call" | custom-call | tf_op jit(solution)/shard_map/first/pallas_call | solution.py:339
  151.3 0.9 slice_bitcast_fusion
  152.2 0.6 collective-permute-start.15
  152.8 1.8 collective-permute-start.16
  154.6 17.8 %later.1 = f32[16,2,128,128]{3,2,1,0:T(8,128)} custom-call(s32[32]{0:T(128)} %convert_element_type.8.drops_ref, s32[1]{0:T(128)} %bitcast.1.me_ref, s32[256]{0:T(256)} %constant.43.table_ref, bf16[14,256,2048]{2,1,0:T(8,128)(2,1)} %get-tuple-element.16.refs_0_, bf16[2,256,2048]{2,1,0:T(8,128)(2,1)} %get-tuple-element.20.refs_1_, f32[16,264,128]{2,1,0:T(8,128)} %copy-done, ...), custom_call_target="tpu_custom_call" | custom-call | tf_op jit(solution)/shard_map/later/pallas_call | solution.py:339
  172.4 0.0 copy-start.8
  172.5 0.4 collective-permute-done.16.refs_1_
  172.9 7.7 %all-to-all-start.2 = ((f32[16,2,128,128]{3,2,1,0:T(8,128)}), f32[16,2,128,128]{3,2,1,0:T(8,128)S(1)}, u32[]{:S(2)}, u32[]{:S(2)}) async-start(f32[16,2,128,128]{3,2,1,0:T(8,128)} %later.1), calls=%async_computation.2 | async-start | bytes 4194304 | tf_op jit(solution)/shard_map/all_to_all | solution.py:351
  180.6 3.1 %unpack_first.1.sum_ref = f32[14,128,128]{2,1,0:T(8,128)} custom-call(s32[14]{0:T(128)} %bitcast.23, s32[1]{0:T(128)} %bitcast.1.me_ref, s32[32]{0:T(128)} %constant.44.sources_ref, f32[3]{0:T(128)} %coefs_ref.3, f32[16,128,128]{2,1,0:T(8,128)} %copy-done.2, f32[14,128,128]{2,1,0:T(8,128)} %bitcast.17, f32[128,128]{1,0:T(8,128)} %copy-done.8, ...), custom_call_target="tpu_custom_call" | custom-call | tf_op jit(solution)/shard_map/unpack_first/pallas_call | solution.py:339
  183.7 42.8 %all-to-all-done.2.held_ref = f32[16,2,128,128]{3,2,1,0:T(8,128)S(1)} async-done(((f32[16,2,128,128]{3,2,1,0:T(8,128)}), f32[16,2,128,128]{3,2,1,0:T(8,128)S(1)}, u32[]{:S(2)}, u32[]{:S(2)}) %all-to-all-start.2) | async-done | bytes 2097184 | tf_op jit(solution)/shard_map/all_to_all | solution.py:351
  226.5 1.3 copy-done.1
  227.8 3.6 %unpack_last.1 = (f32[14,128,128]{2,1,0:T(8,128)}, f32[14,128,128]{2,1,0:T(8,128)}, f32[14,128,128]{2,1,0:T(8,128)}) custom-call(s32[14]{0:T(128)} %bitcast.24, f32[3]{0:T(128)} %coefs_ref.3, f32[16,2,128,128]{3,2,1,0:T(8,128)} %copy-done.1, f32[14,128,128]{2,1,0:T(8,128)} %unpack_first.1.sum_ref), custom_call_target="tpu_custom_call" | custom-call | tf_op jit(solution)/shard_map/unpack_last/pallas_call | solution.py:339
  (23 shorter events, 0.0 us)
Async XLA Ops:
  0.6 23.3 %collective-permute-start = (f32[14,128,128]{2,1,0:T(8,128)}, f32[14,128,128]{2,1,0:T(8,128)S(1)}, u32[]{:S(2)}, u32[]{:S(2)}) collective-permute-start(f32[14,128,128]{2,1,0:T(8,128)} %bitcast.18), channel_id=1, source_target_pairs={{0,4},{1,3},{2,0},{3,7},{4,8},{5,1},{6,2},{7,11},{8,12},{9,5},{10,... | collective-permute-start | bytes 2752520 | tf_op jit(solution)/shard_map/ppermute | solution.py:19
  1.1 23.3 %collective-permute-start.2 = (f32[14,128,128]{2,1,0:T(8,128)}, f32[14,128,128]{2,1,0:T(8,128)S(1)}, u32[]{:S(2)}, u32[]{:S(2)}) collective-permute-start(f32[14,128,128]{2,1,0:T(8,128)} %bitcast.19), channel_id=1, source_target_pairs={{0,2},{1,5},{2,6},{3,1},{4,0},{5,9},{6,10},{7,3},{8,4},{9,13},{10,... | collective-permute-start | bytes 2752520 | tf_op jit(solution)/shard_map/ppermute | solution.py:19
  2.7 30.3 %collective-permute-start.4 = (f32[14,128,128]{2,1,0:T(8,128)}, f32[14,128,128]{2,1,0:T(8,128)S(1)}, u32[]{:S(2)}, u32[]{:S(2)}) collective-permute-start(f32[14,128,128]{2,1,0:T(8,128)} %bitcast.20), channel_id=1, source_target_pairs={{0,1},{1,0},{2,3},{3,2},{4,5},{5,4},{6,7},{7,6},{8,9},{9,8},{10,11... | collective-permute-start | bytes 2752520 | tf_op jit(solution)/shard_map/ppermute | solution.py:19
  24.0 22.5 %copy-start.3 = (f32[14,128,128]{2,1,0:T(8,128)}, f32[14,128,128]{2,1,0:T(8,128)S(1)}, u32[]{:S(2)}) copy-start(f32[14,128,128]{2,1,0:T(8,128)S(1)} %collective-permute-done.refs_2_) | copy-start | bytes 2752516
  24.0 22.5 %collective-permute-start.1 = (f32[14,128,128]{2,1,0:T(8,128)S(1)}, f32[14,128,128]{2,1,0:T(8,128)}, u32[]{:S(2)}, u32[]{:S(2)}) collective-permute-start(f32[14,128,128]{2,1,0:T(8,128)S(1)} %collective-permute-done.refs_2_), channel_id=1, source_target_pairs={{0,4},{1,3},{2,0},{3,7},{4,8},{5,1},{6,2},{7,11},{8,12},{9,5},{10,... | collective-permute-start | bytes 2752520 | tf_op jit(solution)/shard_map/ppermute | solution.py:19
  24.4 22.0 %copy-start.4 = (f32[14,128,128]{2,1,0:T(8,128)}, f32[14,128,128]{2,1,0:T(8,128)S(1)}, u32[]{:S(2)}) copy-start(f32[14,128,128]{2,1,0:T(8,128)S(1)} %collective-permute-done.2.refs_4_) | copy-start | bytes 2752516
  24.4 22.0 %collective-permute-start.3 = (f32[14,128,128]{2,1,0:T(8,128)S(1)}, f32[14,128,128]{2,1,0:T(8,128)}, u32[]{:S(2)}, u32[]{:S(2)}) collective-permute-start(f32[14,128,128]{2,1,0:T(8,128)S(1)} %collective-permute-done.2.refs_4_), channel_id=1, source_target_pairs={{0,2},{1,5},{2,6},{3,1},{4,0},{5,9},{6,10},{7,3},{8,4},{9,13},{10,... | collective-permute-start | bytes 2752520 | tf_op jit(solution)/shard_map/ppermute | solution.py:19
  26.0 20.4 %collective-permute-start.5 = (f32[14,128,128]{2,1,0:T(8,128)S(1)}, f32[14,128,128]{2,1,0:T(8,128)}, u32[]{:S(2)}, u32[]{:S(2)}) collective-permute-start(f32[14,128,128]{2,1,0:T(8,128)S(1)} %collective-permute-done.refs_2_), channel_id=1, source_target_pairs={{0,1},{1,0},{2,3},{3,2},{4,5},{5,4},{6,7},{7,6},{8,9},{9,8},{10,11... | collective-permute-start | bytes 2752520 | tf_op jit(solution)/shard_map/ppermute | solution.py:19
  26.0 20.4 %collective-permute-start.6 = (f32[14,128,128]{2,1,0:T(8,128)S(1)}, f32[14,128,128]{2,1,0:T(8,128)}, u32[]{:S(2)}, u32[]{:S(2)}) collective-permute-start(f32[14,128,128]{2,1,0:T(8,128)S(1)} %collective-permute-done.2.refs_4_), channel_id=1, source_target_pairs={{0,1},{1,0},{2,3},{3,2},{4,5},{5,4},{6,7},{7,6},{8,9},{9,8},{10,11... | collective-permute-start | bytes 2752520 | tf_op jit(solution)/shard_map/ppermute | solution.py:19
  33.0 13.5 %copy-start.5 = (f32[14,128,128]{2,1,0:T(8,128)}, f32[14,128,128]{2,1,0:T(8,128)S(1)}, u32[]{:S(2)}) copy-start(f32[14,128,128]{2,1,0:T(8,128)S(1)} %collective-permute-done.4.refs_1_) | copy-start | bytes 2752516
  46.5 73.0 %all-to-all-start = ((f32[16,264,128]{2,1,0:T(8,128)}), f32[16,264,128]{2,1,0:T(8,128)S(1)}, u32[]{:S(2)}, u32[]{:S(2)}) async-start(f32[16,264,128]{2,1,0:T(8,128)} %pack.1), calls=%async_computation | async-start | bytes 4325376 | tf_op jit(solution)/shard_map/all_to_all | solution.py:351
  51.6 67.1 %collective-permute-start.9 = (f32[14,128,128]{2,1,0:T(8,128)}, f32[14,128,128]{2,1,0:T(8,128)}, u32[]{:S(2)}, u32[]{:S(2)}) collective-permute-start(f32[14,128,128]{2,1,0:T(8,128)} %collective-permute-done.1.refs_6_), channel_id=1, source_target_pairs={{0,4},{1,3},{2,0},{3,7},{4,8},{5,1},{6,2},{7,11},{8,12},{9,5},{10,... | collective-permute-start | bytes 2752520 | tf_op jit(solution)/shard_map/ppermute | solution.py:19
  52.2 67.3 %collective-permute-start.11 = (f32[14,128,128]{2,1,0:T(8,128)}, f32[14,128,128]{2,1,0:T(8,128)S(1)}, u32[]{:S(2)}, u32[]{:S(2)}) collective-permute-start(f32[14,128,128]{2,1,0:T(8,128)} %collective-permute-done.3.refs_8_), channel_id=1, source_target_pairs={{0,2},{1,5},{2,6},{3,1},{4,0},{5,9},{6,10},{7,3},{8,4},{9,13},{10,... | collective-permute-start | bytes 2752520 | tf_op jit(solution)/shard_map/ppermute | solution.py:19
  53.6 69.0 %collective-permute-start.7 = (f32[14,128,128]{2,1,0:T(8,128)}, f32[14,128,128]{2,1,0:T(8,128)}, u32[]{:S(2)}, u32[]{:S(2)}) collective-permute-start(f32[14,128,128]{2,1,0:T(8,128)} %collective-permute-done.1.refs_6_), channel_id=1, source_target_pairs={{0,1},{1,0},{2,3},{3,2},{4,5},{5,4},{6,7},{7,6},{8,9},{9,8},{10,11... | collective-permute-start | bytes 2752520 | tf_op jit(solution)/shard_map/ppermute | solution.py:19
  53.6 69.0 %collective-permute-start.8 = (f32[14,128,128]{2,1,0:T(8,128)}, f32[14,128,128]{2,1,0:T(8,128)}, u32[]{:S(2)}, u32[]{:S(2)}) collective-permute-start(f32[14,128,128]{2,1,0:T(8,128)} %collective-permute-done.3.refs_8_), channel_id=1, source_target_pairs={{0,1},{1,0},{2,3},{3,2},{4,5},{5,4},{6,7},{7,6},{8,9},{9,8},{10,11... | collective-permute-start | bytes 2752520 | tf_op jit(solution)/shard_map/ppermute | solution.py:19
  118.7 4.0 %collective-permute-start.10 = (f32[14,128,128]{2,1,0:T(8,128)}, f32[14,128,128]{2,1,0:T(8,128)}, u32[]{:S(2)}, u32[]{:S(2)}) collective-permute-start(f32[14,128,128]{2,1,0:T(8,128)} %collective-permute-done.9.refs_10_), channel_id=1, source_target_pairs={{0,1},{1,0},{2,3},{3,2},{4,5},{5,4},{6,7},{7,6},{8,9},{9,8},{10,11... | collective-permute-start | bytes 2752520 | tf_op jit(solution)/shard_map/ppermute | solution.py:19
  119.5 3.2 %copy-start.6 = (f32[14,128,128]{2,1,0:T(8,128)}, f32[14,128,128]{2,1,0:T(8,128)S(1)}, u32[]{:S(2)}) copy-start(f32[14,128,128]{2,1,0:T(8,128)S(1)} %collective-permute-done.11.refs_12_) | copy-start | bytes 2752516
  119.5 3.2 %collective-permute-start.12 = (f32[14,128,128]{2,1,0:T(8,128)S(1)}, f32[14,128,128]{2,1,0:T(8,128)}, u32[]{:S(2)}, u32[]{:S(2)}) collective-permute-start(f32[14,128,128]{2,1,0:T(8,128)S(1)} %collective-permute-done.11.refs_12_), channel_id=1, source_target_pairs={{0,1},{1,0},{2,3},{3,2},{4,5},{5,4},{6,7},{7,6},{8,9},{9,8},{10,11... | collective-permute-start | bytes 2752520 | tf_op jit(solution)/shard_map/ppermute | solution.py:19
  119.5 3.2 %copy-start = (f32[16,264,128]{2,1,0:T(8,128)}, f32[16,264,128]{2,1,0:T(8,128)S(1)}, u32[]{:S(2)}) copy-start(f32[16,264,128]{2,1,0:T(8,128)S(1)} %all-to-all-done.t_ref.refs_2_) | copy-start | bytes 6488068
  119.5 24.0 %collective-permute-start.13 = (f32[14,128,128]{2,1,0:T(8,128)}, f32[14,128,128]{2,1,0:T(8,128)}, u32[]{:S(2)}, u32[]{:S(2)}) collective-permute-start(f32[14,128,128]{2,1,0:T(8,128)} %collective-permute-done.9.refs_10_), channel_id=1, source_target_pairs={{0,4},{1,3},{2,0},{3,7},{4,8},{5,1},{6,2},{7,11},{8,12},{9,5},{10,... | collective-permute-start | bytes 2752520 | tf_op jit(solution)/shard_map/ppermute | solution.py:19
  137.4 35.4 %all-to-all-start.1 = ((f32[16,128,128]{2,1,0:T(8,128)}), f32[16,128,128]{2,1,0:T(8,128)S(1)}, u32[]{:S(2)}, u32[]{:S(2)}) async-start(f32[16,128,128]{2,1,0:T(8,128)} %get-tuple-element.21.refs_3_), calls=%async_computation.1 | async-start | bytes 2097152 | tf_op jit(solution)/shard_map/all_to_all | solution.py:351
  143.4 2.7 %collective-permute-start.14 = (f32[14,128,128]{2,1,0:T(8,128)}, f32[14,128,128]{2,1,0:T(8,128)S(1)}, u32[]{:S(2)}, u32[]{:S(2)}) collective-permute-start(f32[14,128,128]{2,1,0:T(8,128)} %collective-permute-done.13.refs_0_), channel_id=1, source_target_pairs={{0,1},{1,0},{2,3},{3,2},{4,5},{5,4},{6,7},{7,6},{8,9},{9,8},{10,11... | collective-permute-start | bytes 2752520 | tf_op jit(solution)/shard_map/ppermute | solution.py:19
  146.2 0.9 copy-start.7
  152.2 20.3 %collective-permute-start.15 = (f32[128,128]{1,0:T(8,128)S(1)}, f32[128,128]{1,0:T(8,128)S(1)}, u32[]{:S(2)}, u32[]{:S(2)}) collective-permute-start(f32[128,128]{1,0:T(8,128)S(1)} %get-tuple-element.28), channel_id=1, source_target_pairs={{0,14},{1,15},{2,12},{3,13},{4,10},{5,11},{6,8},{7,9},{8,6},{9,7},... | collective-permute-start | bytes 196616 | tf_op jit(solution)/shard_map/ppermute | solution.py:19
  152.8 20.1 %collective-permute-start.16 = (f32[128,128]{1,0:T(8,128)S(1)}, f32[128,128]{1,0:T(8,128)S(1)}, u32[]{:S(2)}, u32[]{:S(2)}) collective-permute-start(f32[128,128]{1,0:T(8,128)S(1)} %get-tuple-element.27), channel_id=1, source_target_pairs={{0,15},{1,14},{2,13},{3,12},{4,11},{5,10},{6,9},{7,8},{8,7},{9,6},... | collective-permute-start | bytes 196616 | tf_op jit(solution)/shard_map/ppermute | solution.py:19
  172.4 8.1 %copy-start.8 = (f32[128,128]{1,0:T(8,128)}, f32[128,128]{1,0:T(8,128)S(1)}, u32[]{:S(2)}) copy-start(f32[128,128]{1,0:T(8,128)S(1)} %collective-permute-done.15.refs_0_) | copy-start | bytes 196612
  172.9 7.7 %copy-start.9 = (f32[128,128]{1,0:T(8,128)}, f32[128,128]{1,0:T(8,128)S(1)}, u32[]{:S(2)}) copy-start(f32[128,128]{1,0:T(8,128)S(1)} %collective-permute-done.16.refs_1_) | copy-start | bytes 196612
  172.9 7.7 %copy-start.2 = (f32[16,128,128]{2,1,0:T(8,128)}, f32[16,128,128]{2,1,0:T(8,128)S(1)}, u32[]{:S(2)}) copy-start(f32[16,128,128]{2,1,0:T(8,128)S(1)} %all-to-all-done.1.first_ref) | copy-start | bytes 3145732
  172.9 53.6 %all-to-all-start.2 = ((f32[16,2,128,128]{3,2,1,0:T(8,128)}), f32[16,2,128,128]{3,2,1,0:T(8,128)S(1)}, u32[]{:S(2)}, u32[]{:S(2)}) async-start(f32[16,2,128,128]{3,2,1,0:T(8,128)} %later.1), calls=%async_computation.2 | async-start | bytes 4194304 | tf_op jit(solution)/shard_map/all_to_all | solution.py:351
  226.5 1.3 copy-start.1

commit v16 on v15

--- a/solution.py
+++ b/solution.py
@@ -161,7 +161,7 @@
     rows = Rows(total, me_ref, table_ref)
     h_refs = refs[:count]
     if start:
-        pair_in, dense_ref, out_ref = refs[count:count + 3]
+        pair_in, dense_ref, *outs = refs[count:count + 2 + LAST]
     else:
         dense_ref, out_ref, pair_out, blocks = refs[count:count + 4]
     stage, dense, prev, pair, h_sem, t_sem, prev_sem, pair_sem, dense_sem, out_sem = refs[-10:]
@@ -224,7 +224,7 @@
         for place, product in enumerate(products_of(dense[slot], pair[...])):
             r = g * group + place
             prev[r] = jnp.where(kept(start + r), 2.0 * product - prev[r], 0.0)
-            block = out_ref.at[r if start else rows[start + r]]
+            block = outs[place] if start else out_ref.at[rows[start + r]]
             pltpu.make_async_copy(prev.at[r], block, out_sem).start()
         return carry
 
@@ -239,13 +239,13 @@
 def later_kernel(total, window, group, parts, drops_ref, me_ref, table_ref, *refs):
     rows = Rows(total, me_ref, table_ref)
     dense_refs = refs[:len(parts)]
-    t_ref, first_ref, last_ref, out_ref, dense, terms, pairs, dense_sem, t_sem, first_sem, out_sem = refs[len(parts):]
+    t_ref, first_ref, *late_refs, out_ref, dense, terms, pairs, dense_sem, t_sem, first_sem, out_sem = refs[len(parts):]
     size = terms.shape[-1]
     groups = window // group
     kept = functools.partial(kept_rows, total, rows, drops_ref)
     for w in range(window):
         late = w - (window - LAST)
-        source = first_ref.at[rows[w]] if late < 0 else last_ref.at[late]
+        source = first_ref.at[rows[w]] if late < 0 else late_refs[late]
         pltpu.make_async_copy(source, terms.at[w, 1], first_sem).start()
     start = 0
     for part, dense_ref in zip(parts, dense_refs):
@@ -277,38 +277,39 @@
     pltpu.make_async_copy(terms, terms, out_sem).wait()
 
 
+def late_sources(me_ref, sources_ref):
+    return [sources_ref[me_ref[0] * LAST + r] for r in range(LAST)]
+
+
 def unpack_first_kernel(
-    cols_ref, me_ref, sources_ref, coefs_ref, first_ref, density_ref, *refs
+    cols_ref, me_ref, sources_ref, coefs_ref, first_ref, density_ref, out_ref, sums, one, sems
 ):
-    late_refs = refs[:LAST]
-    out_ref, sums, one, sems = refs[LAST:]
     load = pltpu.make_async_copy(density_ref, sums, sems.at[0])
     load.start()
-    late = [sources_ref[me_ref[0] * LAST + r] for r in range(LAST)]
+    late = late_sources(me_ref, sources_ref)
+    for k in range(cols_ref.shape[0]):
+        pltpu.make_async_copy(first_ref.at[cols_ref[k]], one.at[k], sems.at[1]).start()
+    load.wait()
+    pltpu.make_async_copy(one, one, sems.at[1]).wait()
     for k in range(cols_ref.shape[0]):
         col = cols_ref[k]
         early = jnp.logical_and(col != late[0], col != late[1])
-        choices = [(early, first_ref.at[col])] + [(col == late[r], late_refs[r]) for r in range(LAST)]
-        for chosen, source in choices:
-
-            @pl.when(chosen)
-            def _(source=source, k=k):
-                pltpu.make_async_copy(source, one.at[k], sems.at[1]).start()
-
-    load.wait()
-    pltpu.make_async_copy(one, one, sems.at[1]).wait()
-    sums[...] += coefs_ref[0] * one[...]
+        sums[k] = sums[k] + jnp.where(early, coefs_ref[0] * one[k], 0.0)
     store = pltpu.make_async_copy(sums, out_ref, sems.at[0])
     store.start()
     store.wait()
 
 
-def unpack_last_kernel(cols_ref, coefs_ref, held_ref, sum_ref, density_ref, last_ref, before_ref, sums, two, three, sems):
+def unpack_last_kernel(cols_ref, me_ref, sources_ref, coefs_ref, held_ref, sum_ref, *refs):
+    late_refs = refs[:LAST]
+    density_ref, last_ref, before_ref, sums, two, three, ones, sems = refs[LAST:]
     load = pltpu.make_async_copy(sum_ref, sums, sems.at[0])
     load.start()
     for place, sem, which in ((two, 1, 0), (three, 2, 1)):
         for k in range(cols_ref.shape[0]):
             pltpu.make_async_copy(held_ref.at[cols_ref[k], which], place.at[k], sems.at[sem]).start()
+    for r in range(LAST):
+        pltpu.make_async_copy(late_refs[r], ones.at[r], sems.at[3]).start()
     pltpu.make_async_copy(two, two, sems.at[1]).wait()
     before = pltpu.make_async_copy(two, before_ref, sems.at[1])
     before.start()
@@ -317,6 +318,14 @@
     last.start()
     load.wait()
     sums[...] = sums[...] + coefs_ref[1] * two[...] + coefs_ref[2] * three[...]
+    pltpu.make_async_copy(ones, ones, sems.at[3]).wait()
+    for r, source in enumerate(late_sources(me_ref, sources_ref)):
+        for k in range(cols_ref.shape[0]):
+
+            @pl.when(cols_ref[k] == source)
+            def _(k=k, r=r):
+                sums[k] = sums[k] + coefs_ref[0] * ones[r]
+
     store = pltpu.make_async_copy(sums, density_ref, sems.at[0])
     store.start()
     before.wait()
@@ -346,6 +355,9 @@
             compiler_params=pltpu.CompilerParams(vmem_limit_bytes=megabytes * 1024 * 1024),
             name=name,
         )(*smem, *arrays)
+
+    def in_hbm(x):
+        return pltpu.with_memory_space_constraint(x, pltpu.HBM)
 
     def exchange(x):
         return lax.all_to_all(x, "row", 0, 0, tiled=True)
@@ -395,31 +407,33 @@
         result = call(
             functools.partial(first_kernel, total, window, start, part, group),
             [drops, me[None], rows],
-            [column, *h_rows] + ([pair] if start else []),
+            [in_hbm(column), *h_rows, in_hbm(pair)] if start else [column, *h_rows],
             [
                 jax.ShapeDtypeStruct((part,) + dense_shape[1:], bf16),
-                jax.ShapeDtypeStruct((LAST if start else total, size, size), f32),
             ]
-            + ([] if start else [jax.ShapeDtypeStruct(pair_shape, bf16)]),
+            + (
+                [jax.ShapeDtypeStruct((size, size), f32)] * LAST
+                if start
+                else [jax.ShapeDtypeStruct((total, size, size), f32), jax.ShapeDtypeStruct(pair_shape, bf16)]
+            ),
             scratch,
             "first",
-            60,
+            24 if start else 60,
         )
         dense.append(result[0])
         if start:
-            late1 = result[1]
+            late1 = result[1:]
         else:
             term1, pair = result[1:]
         start += part
     back1 = exchange(term1)
     targets = [[row[window - LAST + r] for row in table] for r in range(LAST)]
-    late_back = [permute(late1[r], lambda i, r=r: targets[r][i]) for r in range(LAST)]
     sources = jnp.array([[to.index(i) for to in targets] for i in range(total)], jnp.int32).reshape(-1)
     group = max(g for g in (3, 4) if window % g == 0)
     (terms,) = call(
         functools.partial(later_kernel, total, window, group, parts),
         [drops, me[None], rows],
-        [*dense, column, term1, late1],
+        [*dense, column, term1, *late1],
         [jax.ShapeDtypeStruct((total, 2, size, size), f32)],
         [
             pltpu.VMEM(dense_shape, bf16),
@@ -433,11 +447,13 @@
         "later",
         60,
     )
-    back = exchange(after(terms, back1, *late_back))
+    back = exchange(after(terms, back1))
+    late_back = [permute(after(late1[r], terms), lambda i, r=r: targets[r][i]) for r in range(LAST)]
+    own = [t_cols[0], me[None], sources, coefs]
     (sums,) = call(
         unpack_first_kernel,
-        [t_cols[0], me[None], sources, coefs],
-        [back1, density_in[0], *late_back],
+        own,
+        [back1, density_in[0]],
         [row],
         [row_scratch, row_scratch, dma((2,))],
         "unpack_first",
@@ -445,10 +461,10 @@
     )
     density, last, before = call(
         unpack_last_kernel,
-        [t_cols[0], coefs],
-        [back, sums],
+        own,
+        [back, sums, *late_back],
         [row] * 3,
-        [row_scratch, row_scratch, row_scratch, dma((3,))],
+        [row_scratch, row_scratch, row_scratch, pltpu.VMEM((LAST, size, size), f32), dma((4,))],
         "unpack_last",
         60,
     )

time: 234 us -> 267 us (1.14)
  waiting for transfers between devices: 145 us -> 183 us
  starting transfers between devices: 31.3 us -> 28.4 us
    ppermute x17, waiting for transfers between devices: 103 us -> 183 us  [permute(): return lax.ppermute(x, 'row', [(i, target(i)) for i in range(devices)])]
    all_to_all x3, waiting for transfers between devices: 42.8 us -> 0.01 us  [exchange(): return lax.all_to_all(x, 'row', 0, 0, tiled=True)]
  transfers between devices with their start and end apart: 20 -> 20, of which waited for: 7 -> 10; matrix products, arithmetic and copies ran while one was open for 2% -> 1% of each run, Pallas kernels for 19% -> 10%
where the time goes in v16:
time: 267 us; the launch traced here: 265 us
  waiting for transfers between devices  183 us (69%)
  Pallas kernels  46 us (17%)
  starting transfers between devices  28.4 us (11%)
  local copies, waits for them, and re-layouts  2.98 us (1%)
    ppermute x17, waiting for transfers between devices, permute(): return lax.ppermute(x, 'row', [(i, target(i)) for i in range(devices)])  183 us
    pallas_call x6, Pallas kernels, call(): pl.pallas_call(kernel, out_shape=[pltpu.HBM(out.shape, out.dtype) for out...  46 us
    all_to_all x3, starting transfers between devices, exchange(): return lax.all_to_all(x, 'row', 0, 0, tiled=True)  16.7 us
    ppermute x17, starting transfers between devices, permute(): return lax.ppermute(x, 'row', [(i, target(i)) for i in range(devices)])  11.7 us
  transfers between devices with their start and end apart: 20, of which 10 were waited for; matrix products, arithmetic and copies ran while one was open for 1% of the time, Pallas kernels for 10%

profile of v16, /device:TPU:22, one launch (start us, length us, event | category | flops | bytes accessed | tf_op | source)
XLA Modules:
  0.0 264.8 jit_solution(6260300265389625313)
XLA Ops:
  0.6 0.5 collective-permute-start
  1.1 1.6 collective-permute-start.2
  2.7 0.0 collective-permute-start.4
  2.7 21.2 %collective-permute-done.refs_2_ = f32[14,128,128]{2,1,0:T(8,128)S(1)} collective-permute-done((f32[14,128,128]{2,1,0:T(8,128)}, f32[14,128,128]{2,1,0:T(8,128)S(1)}, u32[]{:S(2)}, u32[]{:S(2)}) %collective-permute-start) | collective-permute-done | bytes 917536 | tf_op jit(solution)/shard_map/ppermute | solution.py:19
  24.0 0.4 collective-permute-start.1
  24.4 1.6 collective-permute-start.3
  26.0 0.5 collective-permute-start.6
  26.5 1.4 fusion.1
  29.2 0.7 pad_add_fusion.info_ref
  29.9 3.2 %pack.1 = f32[16,264,128]{2,1,0:T(8,128)} custom-call(s32[3]{0:T(128)} %pad_add_fusion.info_ref, s32[14]{0:T(128)} %bitcast.18, f32[14,128,128]{2,1,0:T(8,128)} %bitcast.11, f32[14,128,128]{2,1,0:T(8,128)} %bitcast.12), custom_call_target="tpu_custom_call" | custom-call | tf_op jit(solution)/shard_map/pack/pallas_call | solution.py:348
  33.1 0.0 collective-permute-done.4.refs_1_
  33.2 0.0 copy-start.7
  33.2 13.3 %collective-permute-done.1.refs_6_ = f32[14,128,128]{2,1,0:T(8,128)} collective-permute-done((f32[14,128,128]{2,1,0:T(8,128)S(1)}, f32[14,128,128]{2,1,0:T(8,128)}, u32[]{:S(2)}, u32[]{:S(2)}) %collective-permute-start.1) | collective-permute-done | bytes 917536 | tf_op jit(solution)/shard_map/ppermute | solution.py:19
  46.4 0.0 collective-permute-done.3.refs_8_
  46.5 5.1 %all-to-all-start = ((f32[16,264,128]{2,1,0:T(8,128)}), f32[16,264,128]{2,1,0:T(8,128)S(1)}, u32[]{:S(2)}, u32[]{:S(2)}) async-start(f32[16,264,128]{2,1,0:T(8,128)} %pack.1), calls=%async_computation | async-start | bytes 4325376 | tf_op jit(solution)/shard_map/all_to_all | solution.py:363
  51.6 0.6 collective-permute-start.9
  52.2 1.5 collective-permute-start.11
  53.6 0.0 collective-permute-start.7
  53.6 0.5 collective-permute-start.8
  54.1 64.5 %collective-permute-done.9.refs_10_ = f32[14,128,128]{2,1,0:T(8,128)S(1)} collective-permute-done((f32[14,128,128]{2,1,0:T(8,128)}, f32[14,128,128]{2,1,0:T(8,128)S(1)}, u32[]{:S(2)}, u32[]{:S(2)}) %collective-permute-start.9) | collective-permute-done | bytes 917536 | tf_op jit(solution)/shard_map/ppermute | solution.py:19
  118.7 0.5 collective-permute-start.10
  119.2 0.4 collective-permute-done.11.refs_12_
  119.6 0.0 collective-permute-start.12
  119.6 0.0 all-to-all-done.t_ref.refs_2_
  119.6 0.3 fusion
  119.9 0.9 convert_element_type.8.drops_ref
  120.9 0.0 collective-permute-done.7.refs_7_
  120.9 0.6 collective-permute-done.10.refs_11_
  121.4 1.5 collective-permute-done.12.refs_13_
  123.0 14.9 %first.2 = (bf16[14,256,2048]{2,1,0:T(8,128)(2,1)}, f32[16,128,128]{2,1,0:T(8,128)}, bf16[2048,256]{1,0:T(8,128)(2,1)}) custom-call(s32[32]{0:T(128)} %convert_element_type.8.drops_ref, s32[1]{0:T(128)} %bitcast.1.me_ref, s32[256]{0:T(256)} %constant.44.table_ref, f32[16,264,128]{2,1,0:T(8,128)} %copy-done.2, f32[14,128,128]{2,1,0:T(8,128)} %bitcast.17, ...), custom_call_target="tpu_custom_call" | custom-call | tf_op jit(solution)/shard_map/first/pallas_call | solution.py:348
  137.8 5.8 %all-to-all-start.1 = ((f32[16,128,128]{2,1,0:T(8,128)}), f32[16,128,128]{2,1,0:T(8,128)S(1)}, u32[]{:S(2)}, u32[]{:S(2)}) async-start(f32[16,128,128]{2,1,0:T(8,128)} %get-tuple-element.24.refs_3_), calls=%async_computation.1 | async-start | bytes 2097152 | tf_op jit(solution)/shard_map/all_to_all | solution.py:363
  143.6 0.6 collective-permute-start.13
  144.2 32.7 %collective-permute-done.13.refs_0_ = f32[14,128,128]{2,1,0:T(8,128)S(1)} collective-permute-done((f32[14,128,128]{2,1,0:T(8,128)}, f32[14,128,128]{2,1,0:T(8,128)S(1)}, u32[]{:S(2)}, u32[]{:S(2)}) %collective-permute-start.13) | collective-permute-done | bytes 917536 | tf_op jit(solution)/shard_map/ppermute | solution.py:19
  176.9 0.7 collective-permute-start.14
  177.6 2.1 collective-permute-done.14.refs_1_
  179.7 3.4 %first.3 = (bf16[2,256,2048]{2,1,0:T(8,128)(2,1)}, f32[128,128]{1,0:T(8,128)}, f32[128,128]{1,0:T(8,128)}) custom-call(s32[32]{0:T(128)S(1)} %copy-done.1, s32[1]{0:T(128)} %bitcast.1.me_ref, s32[256]{0:T(256)S(1)} %copy-done, f32[16,264,128]{2,1,0:T(8,128)} %copy-done.2, f32[14,128,128]{2,1,0:T(8,128)S(1)} %collective-permute-done.13.refs_0_, ...), custom_call_target="tpu_custom_call" | custom-call | tf_op jit(solution)/shard_map/first/pallas_call | solution.py:348
  183.1 17.8 %later.1 = f32[16,2,128,128]{3,2,1,0:T(8,128)} custom-call(s32[32]{0:T(128)} %convert_element_type.8.drops_ref, s32[1]{0:T(128)} %bitcast.1.me_ref, s32[256]{0:T(256)} %constant.44.table_ref, bf16[14,256,2048]{2,1,0:T(8,128)(2,1)} %get-tuple-element.19.refs_0_, bf16[2,256,2048]{2,1,0:T(8,128)(2,1)} %get-tuple-element.23.refs_1_, f32[16,264,128]{2,1,0:T(8,128)} %copy-done.2, ...), custom_call_target="tpu_custom_call" | custom-call | tf_op jit(solution)/shard_map/later/pallas_call | solution.py:348
  200.9 0.0 copy-start.10
  200.9 0.0 copy-start.9
  200.9 5.8 %all-to-all-start.2 = ((f32[16,2,128,128]{3,2,1,0:T(8,128)}), f32[16,2,128,128]{3,2,1,0:T(8,128)S(1)}, u32[]{:S(2)}, u32[]{:S(2)}) async-start(f32[16,2,128,128]{3,2,1,0:T(8,128)} %later.1), calls=%async_computation.2 | async-start | bytes 4194304 | tf_op jit(solution)/shard_map/all_to_all | solution.py:363
  206.7 0.4 collective-permute-start.16
  207.1 2.4 collective-permute-start.15
  209.5 3.1 %unpack_first.1.sum_ref = f32[14,128,128]{2,1,0:T(8,128)} custom-call(s32[14]{0:T(128)} %bitcast.19, s32[1]{0:T(128)} %bitcast.1.me_ref, s32[32]{0:T(128)} %constant.43.sources_ref, f32[3]{0:T(128)} %coefs_ref.3, f32[16,128,128]{2,1,0:T(8,128)} %copy-done.4, f32[14,128,128]{2,1,0:T(8,128)} %bitcast.13), custom_call_target="tpu_custom_call" | custom-call | tf_op jit(solution)/shard_map/unpack_first/pallas_call | solution.py:348
  212.6 44.6 %collective-permute-done.16.refs_1_ = f32[128,128]{1,0:T(8,128)S(1)} collective-permute-done((f32[128,128]{1,0:T(8,128)S(1)}, f32[128,128]{1,0:T(8,128)S(1)}, u32[]{:S(2)}, u32[]{:S(2)}) %collective-permute-start.16) | collective-permute-done | bytes 65568 | tf_op jit(solution)/shard_map/ppermute | solution.py:19
  257.2 1.9 collective-permute-done.15.refs_0_
  259.1 0.6 copy-done.12
  259.8 1.4 copy-done.3
  261.1 3.7 %unpack_last.1 = (f32[14,128,128]{2,1,0:T(8,128)}, f32[14,128,128]{2,1,0:T(8,128)}, f32[14,128,128]{2,1,0:T(8,128)}) custom-call(s32[14]{0:T(128)} %bitcast.20, s32[1]{0:T(128)} %bitcast.1.me_ref, s32[32]{0:T(128)} %constant.43.sources_ref, f32[3]{0:T(128)} %coefs_ref.3, f32[16,2,128,128]{3,2,1,0:T(8,128)} %copy-done.3, ...), custom_call_target="tpu_custom_call" | custom-call | tf_op jit(solution)/shard_map/unpack_last/pallas_call | solution.py:348
  (28 shorter events, 0.1 us)
Async XLA Ops:
  0.6 23.3 %collective-permute-start = (f32[14,128,128]{2,1,0:T(8,128)}, f32[14,128,128]{2,1,0:T(8,128)S(1)}, u32[]{:S(2)}, u32[]{:S(2)}) collective-permute-start(f32[14,128,128]{2,1,0:T(8,128)} %bitcast.14), channel_id=1, source_target_pairs={{0,4},{1,3},{2,0},{3,7},{4,8},{5,1},{6,2},{7,11},{8,12},{9,5},{10,... | collective-permute-start | bytes 2752520 | tf_op jit(solution)/shard_map/ppermute | solution.py:19
  1.1 23.3 %collective-permute-start.2 = (f32[14,128,128]{2,1,0:T(8,128)}, f32[14,128,128]{2,1,0:T(8,128)S(1)}, u32[]{:S(2)}, u32[]{:S(2)}) collective-permute-start(f32[14,128,128]{2,1,0:T(8,128)} %bitcast.15), channel_id=1, source_target_pairs={{0,2},{1,5},{2,6},{3,1},{4,0},{5,9},{6,10},{7,3},{8,4},{9,13},{10,... | collective-permute-start | bytes 2752520 | tf_op jit(solution)/shard_map/ppermute | solution.py:19
  2.7 30.4 %collective-permute-start.4 = (f32[14,128,128]{2,1,0:T(8,128)}, f32[14,128,128]{2,1,0:T(8,128)S(1)}, u32[]{:S(2)}, u32[]{:S(2)}) collective-permute-start(f32[14,128,128]{2,1,0:T(8,128)} %bitcast.16), channel_id=1, source_target_pairs={{0,1},{1,0},{2,3},{3,2},{4,5},{5,4},{6,7},{7,6},{8,9},{9,8},{10,11... | collective-permute-start | bytes 2752520 | tf_op jit(solution)/shard_map/ppermute | solution.py:19
  24.0 22.5 %copy-start.5 = (f32[14,128,128]{2,1,0:T(8,128)}, f32[14,128,128]{2,1,0:T(8,128)S(1)}, u32[]{:S(2)}) copy-start(f32[14,128,128]{2,1,0:T(8,128)S(1)} %collective-permute-done.refs_2_) | copy-start | bytes 2752516
  24.0 22.5 %collective-permute-start.1 = (f32[14,128,128]{2,1,0:T(8,128)S(1)}, f32[14,128,128]{2,1,0:T(8,128)}, u32[]{:S(2)}, u32[]{:S(2)}) collective-permute-start(f32[14,128,128]{2,1,0:T(8,128)S(1)} %collective-permute-done.refs_2_), channel_id=1, source_target_pairs={{0,4},{1,3},{2,0},{3,7},{4,8},{5,1},{6,2},{7,11},{8,12},{9,5},{10,... | collective-permute-start | bytes 2752520 | tf_op jit(solution)/shard_map/ppermute | solution.py:19
  24.4 22.0 %copy-start.6 = (f32[14,128,128]{2,1,0:T(8,128)}, f32[14,128,128]{2,1,0:T(8,128)S(1)}, u32[]{:S(2)}) copy-start(f32[14,128,128]{2,1,0:T(8,128)S(1)} %collective-permute-done.2.refs_4_) | copy-start | bytes 2752516
  24.4 22.0 %collective-permute-start.3 = (f32[14,128,128]{2,1,0:T(8,128)S(1)}, f32[14,128,128]{2,1,0:T(8,128)}, u32[]{:S(2)}, u32[]{:S(2)}) collective-permute-start(f32[14,128,128]{2,1,0:T(8,128)S(1)} %collective-permute-done.2.refs_4_), channel_id=1, source_target_pairs={{0,2},{1,5},{2,6},{3,1},{4,0},{5,9},{6,10},{7,3},{8,4},{9,13},{10,... | collective-permute-start | bytes 2752520 | tf_op jit(solution)/shard_map/ppermute | solution.py:19
  26.0 20.4 %collective-permute-start.5 = (f32[14,128,128]{2,1,0:T(8,128)S(1)}, f32[14,128,128]{2,1,0:T(8,128)}, u32[]{:S(2)}, u32[]{:S(2)}) collective-permute-start(f32[14,128,128]{2,1,0:T(8,128)S(1)} %collective-permute-done.refs_2_), channel_id=1, source_target_pairs={{0,1},{1,0},{2,3},{3,2},{4,5},{5,4},{6,7},{7,6},{8,9},{9,8},{10,11... | collective-permute-start | bytes 2752520 | tf_op jit(solution)/shard_map/ppermute | solution.py:19
  26.0 20.4 %collective-permute-start.6 = (f32[14,128,128]{2,1,0:T(8,128)S(1)}, f32[14,128,128]{2,1,0:T(8,128)}, u32[]{:S(2)}, u32[]{:S(2)}) collective-permute-start(f32[14,128,128]{2,1,0:T(8,128)S(1)} %collective-permute-done.2.refs_4_), channel_id=1, source_target_pairs={{0,1},{1,0},{2,3},{3,2},{4,5},{5,4},{6,7},{7,6},{8,9},{9,8},{10,11... | collective-permute-start | bytes 2752520 | tf_op jit(solution)/shard_map/ppermute | solution.py:19
  33.2 13.3 %copy-start.7 = (f32[14,128,128]{2,1,0:T(8,128)}, f32[14,128,128]{2,1,0:T(8,128)S(1)}, u32[]{:S(2)}) copy-start(f32[14,128,128]{2,1,0:T(8,128)S(1)} %collective-permute-done.4.refs_1_) | copy-start | bytes 2752516
  46.5 73.1 %all-to-all-start = ((f32[16,264,128]{2,1,0:T(8,128)}), f32[16,264,128]{2,1,0:T(8,128)S(1)}, u32[]{:S(2)}, u32[]{:S(2)}) async-start(f32[16,264,128]{2,1,0:T(8,128)} %pack.1), calls=%async_computation | async-start | bytes 4325376 | tf_op jit(solution)/shard_map/all_to_all | solution.py:363
  51.6 67.1 %collective-permute-start.9 = (f32[14,128,128]{2,1,0:T(8,128)}, f32[14,128,128]{2,1,0:T(8,128)S(1)}, u32[]{:S(2)}, u32[]{:S(2)}) collective-permute-start(f32[14,128,128]{2,1,0:T(8,128)} %collective-permute-done.1.refs_6_), channel_id=1, source_target_pairs={{0,4},{1,3},{2,0},{3,7},{4,8},{5,1},{6,2},{7,11},{8,12},{9,5},{10,... | collective-permute-start | bytes 2752520 | tf_op jit(solution)/shard_map/ppermute | solution.py:19
  52.2 67.4 %collective-permute-start.11 = (f32[14,128,128]{2,1,0:T(8,128)}, f32[14,128,128]{2,1,0:T(8,128)}, u32[]{:S(2)}, u32[]{:S(2)}) collective-permute-start(f32[14,128,128]{2,1,0:T(8,128)} %collective-permute-done.3.refs_8_), channel_id=1, source_target_pairs={{0,2},{1,5},{2,6},{3,1},{4,0},{5,9},{6,10},{7,3},{8,4},{9,13},{10,... | collective-permute-start | bytes 2752520 | tf_op jit(solution)/shard_map/ppermute | solution.py:19
  53.6 67.3 %collective-permute-start.7 = (f32[14,128,128]{2,1,0:T(8,128)}, f32[14,128,128]{2,1,0:T(8,128)}, u32[]{:S(2)}, u32[]{:S(2)}) collective-permute-start(f32[14,128,128]{2,1,0:T(8,128)} %collective-permute-done.1.refs_6_), channel_id=1, source_target_pairs={{0,1},{1,0},{2,3},{3,2},{4,5},{5,4},{6,7},{7,6},{8,9},{9,8},{10,11... | collective-permute-start | bytes 2752520 | tf_op jit(solution)/shard_map/ppermute | solution.py:19
  53.6 67.3 %collective-permute-start.8 = (f32[14,128,128]{2,1,0:T(8,128)}, f32[14,128,128]{2,1,0:T(8,128)}, u32[]{:S(2)}, u32[]{:S(2)}) collective-permute-start(f32[14,128,128]{2,1,0:T(8,128)} %collective-permute-done.3.refs_8_), channel_id=1, source_target_pairs={{0,1},{1,0},{2,3},{3,2},{4,5},{5,4},{6,7},{7,6},{8,9},{9,8},{10,11... | collective-permute-start | bytes 2752520 | tf_op jit(solution)/shard_map/ppermute | solution.py:19
  118.7 4.3 %copy-start.8 = (f32[14,128,128]{2,1,0:T(8,128)}, f32[14,128,128]{2,1,0:T(8,128)S(1)}, u32[]{:S(2)}) copy-start(f32[14,128,128]{2,1,0:T(8,128)S(1)} %collective-permute-done.9.refs_10_) | copy-start | bytes 2752516
  118.7 2.8 %collective-permute-start.10 = (f32[14,128,128]{2,1,0:T(8,128)S(1)}, f32[14,128,128]{2,1,0:T(8,128)}, u32[]{:S(2)}, u32[]{:S(2)}) collective-permute-start(f32[14,128,128]{2,1,0:T(8,128)S(1)} %collective-permute-done.9.refs_10_), channel_id=1, source_target_pairs={{0,1},{1,0},{2,3},{3,2},{4,5},{5,4},{6,7},{7,6},{8,9},{9,8},{10,11... | collective-permute-start | bytes 2752520 | tf_op jit(solution)/shard_map/ppermute | solution.py:19
  119.6 3.4 %collective-permute-start.12 = (f32[14,128,128]{2,1,0:T(8,128)}, f32[14,128,128]{2,1,0:T(8,128)}, u32[]{:S(2)}, u32[]{:S(2)}) collective-permute-start(f32[14,128,128]{2,1,0:T(8,128)} %collective-permute-done.11.refs_12_), channel_id=1, source_target_pairs={{0,1},{1,0},{2,3},{3,2},{4,5},{5,4},{6,7},{7,6},{8,9},{9,8},{10,11... | collective-permute-start | bytes 2752520 | tf_op jit(solution)/shard_map/ppermute | solution.py:19
  119.6 3.4 %copy-start.2 = (f32[16,264,128]{2,1,0:T(8,128)}, f32[16,264,128]{2,1,0:T(8,128)S(1)}, u32[]{:S(2)}) copy-start(f32[16,264,128]{2,1,0:T(8,128)S(1)} %all-to-all-done.t_ref.refs_2_) | copy-start | bytes 6488068
  120.9 58.8 %copy-start = (s32[256]{0:T(256)S(1)}, s32[256]{0:T(256)}, u32[]{:S(2)}) copy-start(s32[256]{0:T(256)} %constant.44.table_ref) | copy-start | bytes 3076
  120.9 58.8 %copy-start.1 = (s32[32]{0:T(128)S(1)}, s32[32]{0:T(128)}, u32[]{:S(2)}) copy-start(s32[32]{0:T(128)} %convert_element_type.8.drops_ref) | copy-start | bytes 388
  137.8 63.1 %all-to-all-start.1 = ((f32[16,128,128]{2,1,0:T(8,128)}), f32[16,128,128]{2,1,0:T(8,128)S(1)}, u32[]{:S(2)}, u32[]{:S(2)}) async-start(f32[16,128,128]{2,1,0:T(8,128)} %get-tuple-element.24.refs_3_), calls=%async_computation.1 | async-start | bytes 2097152 | tf_op jit(solution)/shard_map/all_to_all | solution.py:363
  143.6 33.3 %collective-permute-start.13 = (f32[14,128,128]{2,1,0:T(8,128)}, f32[14,128,128]{2,1,0:T(8,128)S(1)}, u32[]{:S(2)}, u32[]{:S(2)}) collective-permute-start(f32[14,128,128]{2,1,0:T(8,128)} %copy-done.8), channel_id=1, source_target_pairs={{0,4},{1,3},{2,0},{3,7},{4,8},{5,1},{6,2},{7,11},{8,12},{9,5},{10,... | collective-permute-start | bytes 2752520 | tf_op jit(solution)/shard_map/ppermute | solution.py:19
  176.9 2.8 %collective-permute-start.14 = (f32[14,128,128]{2,1,0:T(8,128)S(1)}, f32[14,128,128]{2,1,0:T(8,128)S(1)}, u32[]{:S(2)}, u32[]{:S(2)}) collective-permute-start(f32[14,128,128]{2,1,0:T(8,128)S(1)} %collective-permute-done.13.refs_0_), channel_id=1, source_target_pairs={{0,1},{1,0},{2,3},{3,2},{4,5},{5,4},{6,7},{7,6},{8,9},{9,8},{10,11... | collective-permute-start | bytes 2752520 | tf_op jit(solution)/shard_map/ppermute | solution.py:19
  200.9 5.8 %copy-start.10 = (f32[128,128]{1,0:T(8,128)S(1)}, f32[128,128]{1,0:T(8,128)}, u32[]{:S(2)}) copy-start(f32[128,128]{1,0:T(8,128)} %get-tuple-element.29.refs_5_) | copy-start | bytes 196612
  200.9 6.2 %copy-start.9 = (f32[128,128]{1,0:T(8,128)S(1)}, f32[128,128]{1,0:T(8,128)}, u32[]{:S(2)}) copy-start(f32[128,128]{1,0:T(8,128)} %get-tuple-element.28.refs_4_) | copy-start | bytes 196612
  200.9 8.6 %copy-start.4 = (f32[16,128,128]{2,1,0:T(8,128)}, f32[16,128,128]{2,1,0:T(8,128)S(1)}, u32[]{:S(2)}) copy-start(f32[16,128,128]{2,1,0:T(8,128)S(1)} %all-to-all-done.1.first_ref) | copy-start | bytes 3145732
  200.9 58.2 %all-to-all-start.2 = ((f32[16,2,128,128]{3,2,1,0:T(8,128)}), f32[16,2,128,128]{3,2,1,0:T(8,128)S(1)}, u32[]{:S(2)}, u32[]{:S(2)}) async-start(f32[16,2,128,128]{3,2,1,0:T(8,128)} %later.1), calls=%async_computation.2 | async-start | bytes 4194304 | tf_op jit(solution)/shard_map/all_to_all | solution.py:363
  206.7 50.5 %collective-permute-start.16 = (f32[128,128]{1,0:T(8,128)S(1)}, f32[128,128]{1,0:T(8,128)S(1)}, u32[]{:S(2)}, u32[]{:S(2)}) collective-permute-start(f32[128,128]{1,0:T(8,128)S(1)} %copy-done.10), channel_id=1, source_target_pairs={{0,15},{1,14},{2,13},{3,12},{4,11},{5,10},{6,9},{7,8},{8,7},{9,6},... | collective-permute-start | bytes 196616 | tf_op jit(solution)/shard_map/ppermute | solution.py:19
  207.1 52.0 %collective-permute-start.15 = (f32[128,128]{1,0:T(8,128)S(1)}, f32[128,128]{1,0:T(8,128)S(1)}, u32[]{:S(2)}, u32[]{:S(2)}) collective-permute-start(f32[128,128]{1,0:T(8,128)S(1)} %copy-done.9), channel_id=1, source_target_pairs={{0,14},{1,15},{2,12},{3,13},{4,10},{5,11},{6,8},{7,9},{8,6},{9,7},... | collective-permute-start | bytes 196616 | tf_op jit(solution)/shard_map/ppermute | solution.py:19
  257.2 1.9 copy-start.11
  259.1 0.6 copy-start.12
  259.8 1.4 copy-start.3

commit v17 on v16

--- a/solution.py
+++ b/solution.py
@@ -426,7 +426,7 @@
         else:
             term1, pair = result[1:]
         start += part
-    back1 = exchange(term1)
+    back1 = exchange(after(term1, h_rows[0]))
     targets = [[row[window - LAST + r] for row in table] for r in range(LAST)]
     sources = jnp.array([[to.index(i) for to in targets] for i in range(total)], jnp.int32).reshape(-1)
     group = max(g for g in (3, 4) if window % g == 0)

time: 267 us -> 235 us (0.88)
  waiting for transfers between devices: 183 us -> 149 us
    ppermute x17, waiting for transfers between devices: 183 us -> 149 us  [permute(): return lax.ppermute(x, 'row', [(i, target(i)) for i in range(devices)])]
  transfers between devices with their start and end apart: 20 -> 20, of which waited for: 10 -> 8; matrix products, arithmetic and copies ran while one was open for 1% -> 1% of each run, Pallas kernels for 10% -> 18%
where the time goes in v17:
time: 235 us; the launch traced here: 233 us
  waiting for transfers between devices  149 us (63%)
  Pallas kernels  46 us (20%)
  starting transfers between devices  29.9 us (13%)
  local copies, waits for them, and re-layouts  3.56 us (2%)
    ppermute x17, waiting for transfers between devices, permute(): return lax.ppermute(x, 'row', [(i, target(i)) for i in range(devices)])  149 us
    pallas_call x6, Pallas kernels, call(): pl.pallas_call(kernel, out_shape=[pltpu.HBM(out.shape, out.dtype) for out...  46 us
    all_to_all x3, starting transfers between devices, exchange(): return lax.all_to_all(x, 'row', 0, 0, tiled=True)  17.2 us
    ppermute x17, starting transfers between devices, permute(): return lax.ppermute(x, 'row', [(i, target(i)) for i in range(devices)])  12.7 us
  transfers between devices with their start and end apart: 20, of which 8 were waited for; matrix products, arithmetic and copies ran while one was open for 1% of the time, Pallas kernels for 18%

profile of v17, /device:TPU:22, one launch (start us, length us, event | category | flops | bytes accessed | tf_op | source)
XLA Modules:
  0.0 232.6 jit_solution(885494084758381483)
XLA Ops:
  0.6 0.5 collective-permute-start
  1.1 1.6 collective-permute-start.2
  2.7 0.0 collective-permute-start.4
  2.7 21.2 %collective-permute-done.refs_2_ = f32[14,128,128]{2,1,0:T(8,128)S(1)} collective-permute-done((f32[14,128,128]{2,1,0:T(8,128)}, f32[14,128,128]{2,1,0:T(8,128)S(1)}, u32[]{:S(2)}, u32[]{:S(2)}) %collective-permute-start) | collective-permute-done | bytes 917536 | tf_op jit(solution)/shard_map/ppermute | solution.py:19
  24.0 0.4 collective-permute-start.1
  24.4 1.6 collective-permute-start.3
  26.0 0.5 collective-permute-start.6
  26.5 1.4 fusion.1
  29.1 0.6 pad_add_fusion.info_ref
  29.7 3.3 %pack.1 = f32[16,264,128]{2,1,0:T(8,128)} custom-call(s32[3]{0:T(128)} %pad_add_fusion.info_ref, s32[14]{0:T(128)} %bitcast.18, f32[14,128,128]{2,1,0:T(8,128)} %bitcast.11, f32[14,128,128]{2,1,0:T(8,128)} %bitcast.12), custom_call_target="tpu_custom_call" | custom-call | tf_op jit(solution)/shard_map/pack/pallas_call | solution.py:348
  33.0 0.0 collective-permute-done.4.refs_1_
  33.0 0.0 copy-start.7
  33.0 13.4 %collective-permute-done.1.refs_6_ = f32[14,128,128]{2,1,0:T(8,128)} collective-permute-done((f32[14,128,128]{2,1,0:T(8,128)S(1)}, f32[14,128,128]{2,1,0:T(8,128)}, u32[]{:S(2)}, u32[]{:S(2)}) %collective-permute-start.1) | collective-permute-done | bytes 917536 | tf_op jit(solution)/shard_map/ppermute | solution.py:19
  46.4 0.0 collective-permute-done.3.refs_8_
  46.5 5.1 %all-to-all-start = ((f32[16,264,128]{2,1,0:T(8,128)}), f32[16,264,128]{2,1,0:T(8,128)S(1)}, u32[]{:S(2)}, u32[]{:S(2)}) async-start(f32[16,264,128]{2,1,0:T(8,128)} %pack.1), calls=%async_computation | async-start | bytes 4325376 | tf_op jit(solution)/shard_map/all_to_all | solution.py:363
  51.6 0.6 collective-permute-start.9
  52.2 1.5 collective-permute-start.11
  53.6 0.0 collective-permute-start.7
  53.6 0.5 collective-permute-start.8
  54.1 64.5 %collective-permute-done.9.refs_10_ = f32[14,128,128]{2,1,0:T(8,128)} collective-permute-done((f32[14,128,128]{2,1,0:T(8,128)}, f32[14,128,128]{2,1,0:T(8,128)}, u32[]{:S(2)}, u32[]{:S(2)}) %collective-permute-start.9) | collective-permute-done | bytes 917536 | tf_op jit(solution)/shard_map/ppermute | solution.py:19
  118.7 0.5 collective-permute-start.10
  119.2 0.4 collective-permute-done.11.refs_12_
  119.6 0.0 collective-permute-start.12
  119.6 0.0 all-to-all-done.t_ref.refs_2_
  119.6 2.1 collective-permute-start.13
  121.7 0.3 fusion
  122.0 0.6 convert_element_type.8.drops_ref
  122.7 0.0 collective-permute-done.7.refs_7_
  122.7 0.0 collective-permute-done.8.refs_9_
  122.7 0.3 collective-permute-done.12.refs_13_
  123.0 14.8 %first.2 = (bf16[14,256,2048]{2,1,0:T(8,128)(2,1)}, f32[16,128,128]{2,1,0:T(8,128)}, bf16[2048,256]{1,0:T(8,128)(2,1)}) custom-call(s32[32]{0:T(128)} %convert_element_type.8.drops_ref, s32[1]{0:T(128)} %bitcast.1.me_ref, s32[256]{0:T(256)} %constant.44.table_ref, f32[16,264,128]{2,1,0:T(8,128)} %copy-done.2, f32[14,128,128]{2,1,0:T(8,128)} %bitcast.17, ...), custom_call_target="tpu_custom_call" | custom-call | tf_op jit(solution)/shard_map/first/pallas_call | solution.py:348
  137.8 6.0 %all-to-all-start.1 = ((f32[16,128,128]{2,1,0:T(8,128)}), f32[16,128,128]{2,1,0:T(8,128)S(1)}, u32[]{:S(2)}, u32[]{:S(2)}) async-start(f32[16,128,128]{2,1,0:T(8,128)} %get-tuple-element.28.refs_3_), calls=%async_computation.1 | async-start | bytes 2097152 | tf_op jit(solution)/shard_map/all_to_all | solution.py:363
  143.8 0.1 collective-permute-start.14
  143.9 2.3 collective-permute-done.14.refs_1_
  146.2 3.4 %first.3 = (bf16[2,256,2048]{2,1,0:T(8,128)(2,1)}, f32[128,128]{1,0:T(8,128)}, f32[128,128]{1,0:T(8,128)}) custom-call(s32[32]{0:T(128)S(1)} %copy-done.1, s32[1]{0:T(128)} %bitcast.1.me_ref, s32[256]{0:T(256)S(1)} %copy-done, f32[16,264,128]{2,1,0:T(8,128)} %copy-done.2, f32[14,128,128]{2,1,0:T(8,128)S(1)} %collective-permute-done.13.refs_0_, ...), custom_call_target="tpu_custom_call" | custom-call | tf_op jit(solution)/shard_map/first/pallas_call | solution.py:348
  149.6 17.8 %later.1 = f32[16,2,128,128]{3,2,1,0:T(8,128)} custom-call(s32[32]{0:T(128)} %convert_element_type.8.drops_ref, s32[1]{0:T(128)} %bitcast.1.me_ref, s32[256]{0:T(256)} %constant.44.table_ref, bf16[14,256,2048]{2,1,0:T(8,128)(2,1)} %get-tuple-element.20.refs_0_, bf16[2,256,2048]{2,1,0:T(8,128)(2,1)} %get-tuple-element.24.refs_1_, f32[16,264,128]{2,1,0:T(8,128)} %copy-done.2, ...), custom_call_target="tpu_custom_call" | custom-call | tf_op jit(solution)/shard_map/later/pallas_call | solution.py:348
  167.4 0.0 copy-start.9
  167.4 0.0 copy-start.8
  167.4 1.0 copy-done.4
  168.4 6.1 %all-to-all-start.2 = ((f32[16,2,128,128]{3,2,1,0:T(8,128)}), f32[16,2,128,128]{3,2,1,0:T(8,128)S(1)}, u32[]{:S(2)}, u32[]{:S(2)}) async-start(f32[16,2,128,128]{3,2,1,0:T(8,128)} %later.1), calls=%async_computation.2 | async-start | bytes 4194304 | tf_op jit(solution)/shard_map/all_to_all | solution.py:363
  174.5 0.4 collective-permute-start.16
  174.9 2.4 %collective-permute-start.15 = (f32[128,128]{1,0:T(8,128)S(1)}, f32[128,128]{1,0:T(8,128)S(1)}, u32[]{:S(2)}, u32[]{:S(2)}) collective-permute-start(f32[128,128]{1,0:T(8,128)S(1)} %copy-done.8), channel_id=1, source_target_pairs={{0,14},{1,15},{2,12},{3,13},{4,10},{5,11},{6,8},{7,9},{8,6},{9,7},... | collective-permute-start | bytes 196616 | tf_op jit(solution)/shard_map/ppermute | solution.py:19
  177.3 3.1 %unpack_first.1.sum_ref = f32[14,128,128]{2,1,0:T(8,128)} custom-call(s32[14]{0:T(128)} %bitcast.19, s32[1]{0:T(128)} %bitcast.1.me_ref, s32[32]{0:T(128)} %constant.43.sources_ref, f32[3]{0:T(128)} %coefs_ref.3, f32[16,128,128]{2,1,0:T(8,128)} %copy-done.4, f32[14,128,128]{2,1,0:T(8,128)} %bitcast.13), custom_call_target="tpu_custom_call" | custom-call | tf_op jit(solution)/shard_map/unpack_first/pallas_call | solution.py:348
  180.4 44.6 %collective-permute-done.16.refs_1_ = f32[128,128]{1,0:T(8,128)S(1)} collective-permute-done((f32[128,128]{1,0:T(8,128)S(1)}, f32[128,128]{1,0:T(8,128)S(1)}, u32[]{:S(2)}, u32[]{:S(2)}) %collective-permute-start.16) | collective-permute-done | bytes 65568 | tf_op jit(solution)/shard_map/ppermute | solution.py:19
  225.1 1.9 collective-permute-done.15.refs_0_
  227.0 0.6 copy-done.11
  227.6 1.3 copy-done.3
  228.9 3.7 %unpack_last.1 = (f32[14,128,128]{2,1,0:T(8,128)}, f32[14,128,128]{2,1,0:T(8,128)}, f32[14,128,128]{2,1,0:T(8,128)}) custom-call(s32[14]{0:T(128)} %bitcast.20, s32[1]{0:T(128)} %bitcast.1.me_ref, s32[32]{0:T(128)} %constant.43.sources_ref, f32[3]{0:T(128)} %coefs_ref.3, f32[16,2,128,128]{3,2,1,0:T(8,128)} %copy-done.3, ...), custom_call_target="tpu_custom_call" | custom-call | tf_op jit(solution)/shard_map/unpack_last/pallas_call | solution.py:348
  (26 shorter events, 0.1 us)
Async XLA Ops:
  0.6 23.3 %collective-permute-start = (f32[14,128,128]{2,1,0:T(8,128)}, f32[14,128,128]{2,1,0:T(8,128)S(1)}, u32[]{:S(2)}, u32[]{:S(2)}) collective-permute-start(f32[14,128,128]{2,1,0:T(8,128)} %bitcast.14), channel_id=1, source_target_pairs={{0,4},{1,3},{2,0},{3,7},{4,8},{5,1},{6,2},{7,11},{8,12},{9,5},{10,... | collective-permute-start | bytes 2752520 | tf_op jit(solution)/shard_map/ppermute | solution.py:19
  1.1 23.3 %collective-permute-start.2 = (f32[14,128,128]{2,1,0:T(8,128)}, f32[14,128,128]{2,1,0:T(8,128)S(1)}, u32[]{:S(2)}, u32[]{:S(2)}) collective-permute-start(f32[14,128,128]{2,1,0:T(8,128)} %bitcast.15), channel_id=1, source_target_pairs={{0,2},{1,5},{2,6},{3,1},{4,0},{5,9},{6,10},{7,3},{8,4},{9,13},{10,... | collective-permute-start | bytes 2752520 | tf_op jit(solution)/shard_map/ppermute | solution.py:19
  2.7 30.3 %collective-permute-start.4 = (f32[14,128,128]{2,1,0:T(8,128)}, f32[14,128,128]{2,1,0:T(8,128)S(1)}, u32[]{:S(2)}, u32[]{:S(2)}) collective-permute-start(f32[14,128,128]{2,1,0:T(8,128)} %bitcast.16), channel_id=1, source_target_pairs={{0,1},{1,0},{2,3},{3,2},{4,5},{5,4},{6,7},{7,6},{8,9},{9,8},{10,11... | collective-permute-start | bytes 2752520 | tf_op jit(solution)/shard_map/ppermute | solution.py:19
  24.0 22.5 %copy-start.5 = (f32[14,128,128]{2,1,0:T(8,128)}, f32[14,128,128]{2,1,0:T(8,128)S(1)}, u32[]{:S(2)}) copy-start(f32[14,128,128]{2,1,0:T(8,128)S(1)} %collective-permute-done.refs_2_) | copy-start | bytes 2752516
  24.0 22.5 %collective-permute-start.1 = (f32[14,128,128]{2,1,0:T(8,128)S(1)}, f32[14,128,128]{2,1,0:T(8,128)}, u32[]{:S(2)}, u32[]{:S(2)}) collective-permute-start(f32[14,128,128]{2,1,0:T(8,128)S(1)} %collective-permute-done.refs_2_), channel_id=1, source_target_pairs={{0,4},{1,3},{2,0},{3,7},{4,8},{5,1},{6,2},{7,11},{8,12},{9,5},{10,... | collective-permute-start | bytes 2752520 | tf_op jit(solution)/shard_map/ppermute | solution.py:19
  24.4 22.0 %copy-start.6 = (f32[14,128,128]{2,1,0:T(8,128)}, f32[14,128,128]{2,1,0:T(8,128)S(1)}, u32[]{:S(2)}) copy-start(f32[14,128,128]{2,1,0:T(8,128)S(1)} %collective-permute-done.2.refs_4_) | copy-start | bytes 2752516
  24.4 22.0 %collective-permute-start.3 = (f32[14,128,128]{2,1,0:T(8,128)S(1)}, f32[14,128,128]{2,1,0:T(8,128)}, u32[]{:S(2)}, u32[]{:S(2)}) collective-permute-start(f32[14,128,128]{2,1,0:T(8,128)S(1)} %collective-permute-done.2.refs_4_), channel_id=1, source_target_pairs={{0,2},{1,5},{2,6},{3,1},{4,0},{5,9},{6,10},{7,3},{8,4},{9,13},{10,... | collective-permute-start | bytes 2752520 | tf_op jit(solution)/shard_map/ppermute | solution.py:19
  26.0 20.4 %collective-permute-start.5 = (f32[14,128,128]{2,1,0:T(8,128)S(1)}, f32[14,128,128]{2,1,0:T(8,128)}, u32[]{:S(2)}, u32[]{:S(2)}) collective-permute-start(f32[14,128,128]{2,1,0:T(8,128)S(1)} %collective-permute-done.refs_2_), channel_id=1, source_target_pairs={{0,1},{1,0},{2,3},{3,2},{4,5},{5,4},{6,7},{7,6},{8,9},{9,8},{10,11... | collective-permute-start | bytes 2752520 | tf_op jit(solution)/shard_map/ppermute | solution.py:19
  26.0 20.4 %collective-permute-start.6 = (f32[14,128,128]{2,1,0:T(8,128)S(1)}, f32[14,128,128]{2,1,0:T(8,128)}, u32[]{:S(2)}, u32[]{:S(2)}) collective-permute-start(f32[14,128,128]{2,1,0:T(8,128)S(1)} %collective-permute-done.2.refs_4_), channel_id=1, source_target_pairs={{0,1},{1,0},{2,3},{3,2},{4,5},{5,4},{6,7},{7,6},{8,9},{9,8},{10,11... | collective-permute-start | bytes 2752520 | tf_op jit(solution)/shard_map/ppermute | solution.py:19
  33.0 13.4 %copy-start.7 = (f32[14,128,128]{2,1,0:T(8,128)}, f32[14,128,128]{2,1,0:T(8,128)S(1)}, u32[]{:S(2)}) copy-start(f32[14,128,128]{2,1,0:T(8,128)S(1)} %collective-permute-done.4.refs_1_) | copy-start | bytes 2752516
  46.5 73.1 %all-to-all-start = ((f32[16,264,128]{2,1,0:T(8,128)}), f32[16,264,128]{2,1,0:T(8,128)S(1)}, u32[]{:S(2)}, u32[]{:S(2)}) async-start(f32[16,264,128]{2,1,0:T(8,128)} %pack.1), calls=%async_computation | async-start | bytes 4325376 | tf_op jit(solution)/shard_map/all_to_all | solution.py:363
  51.6 67.1 %collective-permute-start.9 = (f32[14,128,128]{2,1,0:T(8,128)}, f32[14,128,128]{2,1,0:T(8,128)}, u32[]{:S(2)}, u32[]{:S(2)}) collective-permute-start(f32[14,128,128]{2,1,0:T(8,128)} %collective-permute-done.1.refs_6_), channel_id=1, source_target_pairs={{0,4},{1,3},{2,0},{3,7},{4,8},{5,1},{6,2},{7,11},{8,12},{9,5},{10,... | collective-permute-start | bytes 2752520 | tf_op jit(solution)/shard_map/ppermute | solution.py:19
  52.2 67.4 %collective-permute-start.11 = (f32[14,128,128]{2,1,0:T(8,128)}, f32[14,128,128]{2,1,0:T(8,128)}, u32[]{:S(2)}, u32[]{:S(2)}) collective-permute-start(f32[14,128,128]{2,1,0:T(8,128)} %collective-permute-done.3.refs_8_), channel_id=1, source_target_pairs={{0,2},{1,5},{2,6},{3,1},{4,0},{5,9},{6,10},{7,3},{8,4},{9,13},{10,... | collective-permute-start | bytes 2752520 | tf_op jit(solution)/shard_map/ppermute | solution.py:19
  53.6 69.0 %collective-permute-start.7 = (f32[14,128,128]{2,1,0:T(8,128)}, f32[14,128,128]{2,1,0:T(8,128)}, u32[]{:S(2)}, u32[]{:S(2)}) collective-permute-start(f32[14,128,128]{2,1,0:T(8,128)} %collective-permute-done.1.refs_6_), channel_id=1, source_target_pairs={{0,1},{1,0},{2,3},{3,2},{4,5},{5,4},{6,7},{7,6},{8,9},{9,8},{10,11... | collective-permute-start | bytes 2752520 | tf_op jit(solution)/shard_map/ppermute | solution.py:19
  53.6 69.0 %collective-permute-start.8 = (f32[14,128,128]{2,1,0:T(8,128)}, f32[14,128,128]{2,1,0:T(8,128)}, u32[]{:S(2)}, u32[]{:S(2)}) collective-permute-start(f32[14,128,128]{2,1,0:T(8,128)} %collective-permute-done.3.refs_8_), channel_id=1, source_target_pairs={{0,1},{1,0},{2,3},{3,2},{4,5},{5,4},{6,7},{7,6},{8,9},{9,8},{10,11... | collective-permute-start | bytes 2752520 | tf_op jit(solution)/shard_map/ppermute | solution.py:19
  118.7 4.0 %collective-permute-start.10 = (f32[14,128,128]{2,1,0:T(8,128)}, f32[14,128,128]{2,1,0:T(8,128)}, u32[]{:S(2)}, u32[]{:S(2)}) collective-permute-start(f32[14,128,128]{2,1,0:T(8,128)} %collective-permute-done.9.refs_10_), channel_id=1, source_target_pairs={{0,1},{1,0},{2,3},{3,2},{4,5},{5,4},{6,7},{7,6},{8,9},{9,8},{10,11... | collective-permute-start | bytes 2752520 | tf_op jit(solution)/shard_map/ppermute | solution.py:19
  119.6 3.4 %collective-permute-start.12 = (f32[14,128,128]{2,1,0:T(8,128)}, f32[14,128,128]{2,1,0:T(8,128)}, u32[]{:S(2)}, u32[]{:S(2)}) collective-permute-start(f32[14,128,128]{2,1,0:T(8,128)} %collective-permute-done.11.refs_12_), channel_id=1, source_target_pairs={{0,1},{1,0},{2,3},{3,2},{4,5},{5,4},{6,7},{7,6},{8,9},{9,8},{10,11... | collective-permute-start | bytes 2752520 | tf_op jit(solution)/shard_map/ppermute | solution.py:19
  119.6 3.4 %copy-start.2 = (f32[16,264,128]{2,1,0:T(8,128)}, f32[16,264,128]{2,1,0:T(8,128)S(1)}, u32[]{:S(2)}) copy-start(f32[16,264,128]{2,1,0:T(8,128)S(1)} %all-to-all-done.t_ref.refs_2_) | copy-start | bytes 6488068
  119.6 18.2 %collective-permute-start.13 = (f32[14,128,128]{2,1,0:T(8,128)}, f32[14,128,128]{2,1,0:T(8,128)S(1)}, u32[]{:S(2)}, u32[]{:S(2)}) collective-permute-start(f32[14,128,128]{2,1,0:T(8,128)} %collective-permute-done.9.refs_10_), channel_id=1, source_target_pairs={{0,4},{1,3},{2,0},{3,7},{4,8},{5,1},{6,2},{7,11},{8,12},{9,5},{10,... | collective-permute-start | bytes 2752520 | tf_op jit(solution)/shard_map/ppermute | solution.py:19
  122.7 23.6 %copy-start = (s32[256]{0:T(256)S(1)}, s32[256]{0:T(256)}, u32[]{:S(2)}) copy-start(s32[256]{0:T(256)} %constant.44.table_ref) | copy-start | bytes 3076
  122.7 23.6 %copy-start.1 = (s32[32]{0:T(128)S(1)}, s32[32]{0:T(128)}, u32[]{:S(2)}) copy-start(s32[32]{0:T(128)} %convert_element_type.8.drops_ref) | copy-start | bytes 388
  137.8 29.6 %all-to-all-start.1 = ((f32[16,128,128]{2,1,0:T(8,128)}), f32[16,128,128]{2,1,0:T(8,128)S(1)}, u32[]{:S(2)}, u32[]{:S(2)}) async-start(f32[16,128,128]{2,1,0:T(8,128)} %get-tuple-element.28.refs_3_), calls=%async_computation.1 | async-start | bytes 2097152 | tf_op jit(solution)/shard_map/all_to_all | solution.py:363
  143.8 2.5 %collective-permute-start.14 = (f32[14,128,128]{2,1,0:T(8,128)S(1)}, f32[14,128,128]{2,1,0:T(8,128)S(1)}, u32[]{:S(2)}, u32[]{:S(2)}) collective-permute-start(f32[14,128,128]{2,1,0:T(8,128)S(1)} %collective-permute-done.13.refs_0_), channel_id=1, source_target_pairs={{0,1},{1,0},{2,3},{3,2},{4,5},{5,4},{6,7},{7,6},{8,9},{9,8},{10,11... | collective-permute-start | bytes 2752520 | tf_op jit(solution)/shard_map/ppermute | solution.py:19
  167.4 7.1 %copy-start.9 = (f32[128,128]{1,0:T(8,128)S(1)}, f32[128,128]{1,0:T(8,128)}, u32[]{:S(2)}) copy-start(f32[128,128]{1,0:T(8,128)} %get-tuple-element.31.refs_5_) | copy-start | bytes 196612
  167.4 7.5 %copy-start.8 = (f32[128,128]{1,0:T(8,128)S(1)}, f32[128,128]{1,0:T(8,128)}, u32[]{:S(2)}) copy-start(f32[128,128]{1,0:T(8,128)} %get-tuple-element.30.refs_4_) | copy-start | bytes 196612
  167.4 1.0 copy-start.4
  168.4 58.6 %all-to-all-start.2 = ((f32[16,2,128,128]{3,2,1,0:T(8,128)}), f32[16,2,128,128]{3,2,1,0:T(8,128)S(1)}, u32[]{:S(2)}, u32[]{:S(2)}) async-start(f32[16,2,128,128]{3,2,1,0:T(8,128)} %later.1), calls=%async_computation.2 | async-start | bytes 4194304 | tf_op jit(solution)/shard_map/all_to_all | solution.py:363
  174.5 50.5 %collective-permute-start.16 = (f32[128,128]{1,0:T(8,128)S(1)}, f32[128,128]{1,0:T(8,128)S(1)}, u32[]{:S(2)}, u32[]{:S(2)}) collective-permute-start(f32[128,128]{1,0:T(8,128)S(1)} %copy-done.9), channel_id=1, source_target_pairs={{0,15},{1,14},{2,13},{3,12},{4,11},{5,10},{6,9},{7,8},{8,7},{9,6},... | collective-permute-start | bytes 196616 | tf_op jit(solution)/shard_map/ppermute | solution.py:19
  174.9 52.0 %collective-permute-start.15 = (f32[128,128]{1,0:T(8,128)S(1)}, f32[128,128]{1,0:T(8,128)S(1)}, u32[]{:S(2)}, u32[]{:S(2)}) collective-permute-start(f32[128,128]{1,0:T(8,128)S(1)} %copy-done.8), channel_id=1, source_target_pairs={{0,14},{1,15},{2,12},{3,13},{4,10},{5,11},{6,8},{7,9},{8,6},{9,7},... | collective-permute-start | bytes 196616 | tf_op jit(solution)/shard_map/ppermute | solution.py:19
  225.1 1.9 copy-start.10
  227.0 0.6 copy-start.11
  227.6 1.3 copy-start.3

commit v18 on v14

--- a/solution.py
+++ b/solution.py
@@ -206,10 +206,13 @@
         def _():
             store(g - 2, slot).wait()
 
-        for place in range(group):
+        def ready(place, carry):
             r = g * group + place
             pltpu.make_async_copy(stage.at[r], stage.at[r], h_sem.at[r]).wait()
             densify(r, slot, place)
+            return carry
+
+        lax.fori_loop(0, group, ready, 0)
         store(g, slot).start()
         if start:
 
@@ -331,6 +334,9 @@
             name=name,
         )(*smem, *arrays)
 
+    def in_hbm(x):
+        return pltpu.with_memory_space_constraint(x, pltpu.HBM)
+
     def exchange(x):
         return lax.all_to_all(x, "row", 0, 0, tiled=True)
 
@@ -379,14 +385,14 @@
         result = call(
             functools.partial(first_kernel, total, window, start, part, group),
             [drops, me[None], rows],
-            [column, *h_rows] + ([pair, term1] if start else []),
+            [in_hbm(column), *h_rows, in_hbm(pair), term1] if start else [column, *h_rows],
             [
                 jax.ShapeDtypeStruct((part,) + dense_shape[1:], bf16),
                 jax.ShapeDtypeStruct((total, size, size), f32),
             ] + ([] if start else [jax.ShapeDtypeStruct(pair_shape, bf16)]),
             scratch,
             "first",
-            60,
+            24 if start else 60,
             {part + 5: 1} if start else {},
         )
         dense.append(result[0])

time: 235 us -> 233 us (level)
  no operation moved by 1% of the time
where the time goes in v18:
time: 233 us; the launch traced here: 230 us
  waiting for transfers between devices  150 us (64%)
  Pallas kernels  45.9 us (20%)
  starting transfers between devices  27.7 us (12%)
  other arithmetic  2.34 us (1%)
    ppermute x15, waiting for transfers between devices, permute(): return lax.ppermute(x, 'row', [(i, target(i)) for i in range(devices)])  102 us
    all_to_all x3, waiting for transfers between devices, exchange(): return lax.all_to_all(x, 'row', 0, 0, tiled=True)  48.4 us
    pallas_call x6, Pallas kernels, call(): pl.pallas_call(kernel, out_shape=[pltpu.HBM(out.shape, out.dtype) for out...  45.9 us
    all_to_all x3, starting transfers between devices, exchange(): return lax.all_to_all(x, 'row', 0, 0, tiled=True)  17.6 us
    ppermute x15, starting transfers between devices, permute(): return lax.ppermute(x, 'row', [(i, target(i)) for i in range(devices)])  10.2 us
  transfers between devices with their start and end apart: 18, of which 8 were waited for; matrix products, arithmetic and copies ran while one was open for 1% of the time, Pallas kernels for 17%

profile of v18, /device:TPU:22, one launch (start us, length us, event | category | flops | bytes accessed | tf_op | source)
XLA Modules:
  0.0 230.4 jit_solution(15204738564725834335)
XLA Ops:
  0.6 0.5 collective-permute-start
  1.1 1.6 collective-permute-start.2
  2.7 0.0 collective-permute-start.4
  2.7 21.2 %collective-permute-done.refs_2_ = f32[14,128,128]{2,1,0:T(8,128)S(1)} collective-permute-done((f32[14,128,128]{2,1,0:T(8,128)}, f32[14,128,128]{2,1,0:T(8,128)S(1)}, u32[]{:S(2)}, u32[]{:S(2)}) %collective-permute-start) | collective-permute-done | bytes 917536 | tf_op jit(solution)/shard_map/ppermute | solution.py:18
  24.0 0.4 collective-permute-start.1
  24.4 0.0 collective-permute-done.2.refs_4_
  24.4 1.6 collective-permute-start.3
  26.0 0.0 collective-permute-start.5
  26.0 0.5 collective-permute-start.6
  26.5 1.4 fusion.1
  29.2 0.6 pad_add_fusion.info_ref
  29.8 3.2 %pack.1 = f32[16,264,128]{2,1,0:T(8,128)} custom-call(s32[3]{0:T(128)} %pad_add_fusion.info_ref, s32[14]{0:T(128)} %bitcast.18, f32[14,128,128]{2,1,0:T(8,128)} %bitcast.11, f32[14,128,128]{2,1,0:T(8,128)} %bitcast.12), custom_call_target="tpu_custom_call" | custom-call | tf_op jit(solution)/shard_map/pack/pallas_call | solution.py:326
  33.1 0.0 collective-permute-done.4.refs_1_
  33.1 0.0 copy-start.7
  33.1 13.3 %collective-permute-done.1.refs_6_ = f32[14,128,128]{2,1,0:T(8,128)} collective-permute-done((f32[14,128,128]{2,1,0:T(8,128)S(1)}, f32[14,128,128]{2,1,0:T(8,128)}, u32[]{:S(2)}, u32[]{:S(2)}) %collective-permute-start.1) | collective-permute-done | bytes 917536 | tf_op jit(solution)/shard_map/ppermute | solution.py:18
  46.4 0.0 collective-permute-done.3.refs_8_
  46.4 0.0 collective-permute-done.5.refs_3_
  46.4 0.0 collective-permute-done.6.refs_5_
  46.5 5.1 %all-to-all-start = ((f32[16,264,128]{2,1,0:T(8,128)}), f32[16,264,128]{2,1,0:T(8,128)S(1)}, u32[]{:S(2)}, u32[]{:S(2)}) async-start(f32[16,264,128]{2,1,0:T(8,128)} %pack.1), calls=%async_computation | async-start | bytes 4325376 | tf_op jit(solution)/shard_map/all_to_all | solution.py:341
  51.6 0.6 collective-permute-start.9
  52.2 1.5 collective-permute-start.11
  53.6 0.0 collective-permute-start.7
  53.6 0.5 collective-permute-start.8
  54.1 64.5 %collective-permute-done.9.refs_10_ = f32[14,128,128]{2,1,0:T(8,128)} collective-permute-done((f32[14,128,128]{2,1,0:T(8,128)}, f32[14,128,128]{2,1,0:T(8,128)}, u32[]{:S(2)}, u32[]{:S(2)}) %collective-permute-start.9) | collective-permute-done | bytes 917536 | tf_op jit(solution)/shard_map/ppermute | solution.py:18
  118.7 0.5 collective-permute-start.10
  119.2 0.4 collective-permute-done.11.refs_12_
  119.6 0.0 collective-permute-start.12
  119.6 0.0 all-to-all-done.t_ref.refs_2_
  119.6 2.1 collective-permute-start.13
  121.7 0.3 fusion
  122.0 0.6 convert_element_type.8.drops_ref
  122.7 0.0 collective-permute-done.7.refs_7_
  122.7 0.0 collective-permute-done.8.refs_9_
  122.7 0.0 collective-permute-done.10.refs_11_
  122.7 0.3 collective-permute-done.12.refs_13_
  123.0 14.8 %first.2 = (bf16[14,256,2048]{2,1,0:T(8,128)(2,1)}, f32[16,128,128]{2,1,0:T(8,128)}, bf16[2048,256]{1,0:T(8,128)(2,1)}) custom-call(s32[32]{0:T(128)} %convert_element_type.8.drops_ref, s32[1]{0:T(128)} %bitcast.1.me_ref, s32[256]{0:T(256)} %constant.40.table_ref, f32[16,264,128]{2,1,0:T(8,128)} %copy-done.2, f32[14,128,128]{2,1,0:T(8,128)} %bitcast.16, ...), custom_call_target="tpu_custom_call" | custom-call | tf_op jit(solution)/shard_map/first/pallas_call | solution.py:326
  137.8 0.0 collective-permute-done.13.refs_0_
  137.8 0.4 collective-permute-start.14
  138.2 2.2 collective-permute-done.14.refs_1_
  140.4 3.3 %first.3 = (bf16[2,256,2048]{2,1,0:T(8,128)(2,1)}, f32[16,128,128]{2,1,0:T(8,128)}) custom-call(s32[32]{0:T(128)S(1)} %copy-done.1, s32[1]{0:T(128)} %bitcast.1.me_ref, s32[256]{0:T(256)S(1)} %copy-done, f32[16,264,128]{2,1,0:T(8,128)} %copy-done.2, f32[14,128,128]{2,1,0:T(8,128)S(1)} %collective-permute-done.13.refs_0_, ...), custom_call_target="tpu_custom_call", output_to_operand_aliasing={{1}: (7, {})} | custom-call | tf_op jit(solution)/shard_map/first/pallas_call | solution.py:326
  143.7 6.0 %all-to-all-start.1 = ((f32[16,128,128]{2,1,0:T(8,128)}), f32[16,128,128]{2,1,0:T(8,128)S(1)}, u32[]{:S(2)}, u32[]{:S(2)}) async-start(f32[16,128,128]{2,1,0:T(8,128)} %get-tuple-element.22.refs_3_), calls=%async_computation.1 | async-start | bytes 2097152 | tf_op jit(solution)/shard_map/all_to_all | solution.py:341
  149.7 17.8 %later.1 = f32[16,2,128,128]{3,2,1,0:T(8,128)} custom-call(s32[32]{0:T(128)} %convert_element_type.8.drops_ref, s32[1]{0:T(128)} %bitcast.1.me_ref, s32[256]{0:T(256)} %constant.40.table_ref, bf16[14,256,2048]{2,1,0:T(8,128)(2,1)} %get-tuple-element.16.refs_0_, bf16[2,256,2048]{2,1,0:T(8,128)(2,1)} %get-tuple-element.21.refs_1_, f32[16,264,128]{2,1,0:T(8,128)} %copy-done.2, ...), custom_call_target="tpu_custom_call" | custom-call | tf_op jit(solution)/shard_map/later/pallas_call | solution.py:326
  167.5 5.6 %all-to-all-done.1.first_ref = f32[16,128,128]{2,1,0:T(8,128)S(1)} async-done(((f32[16,128,128]{2,1,0:T(8,128)}), f32[16,128,128]{2,1,0:T(8,128)S(1)}, u32[]{:S(2)}, u32[]{:S(2)}) %all-to-all-start.1) | async-done | bytes 1048608 | tf_op jit(solution)/shard_map/all_to_all | solution.py:341
  173.1 6.4 %all-to-all-start.2 = ((f32[16,2,128,128]{3,2,1,0:T(8,128)}), f32[16,2,128,128]{3,2,1,0:T(8,128)S(1)}, u32[]{:S(2)}, u32[]{:S(2)}) async-start(f32[16,2,128,128]{3,2,1,0:T(8,128)} %later.1), calls=%async_computation.2 | async-start | bytes 4194304 | tf_op jit(solution)/shard_map/all_to_all | solution.py:341
  179.5 3.1 %unpack_first.1.sum_ref = f32[14,128,128]{2,1,0:T(8,128)} custom-call(s32[14]{0:T(128)} %bitcast.19, f32[3]{0:T(128)} %coefs_ref.3, f32[16,128,128]{2,1,0:T(8,128)} %copy-done.4, f32[14,128,128]{2,1,0:T(8,128)} %bitcast.17), custom_call_target="tpu_custom_call" | custom-call | tf_op jit(solution)/shard_map/unpack_first/pallas_call | solution.py:326
  182.6 42.8 %all-to-all-done.2.held_ref = f32[16,2,128,128]{3,2,1,0:T(8,128)S(1)} async-done(((f32[16,2,128,128]{3,2,1,0:T(8,128)}), f32[16,2,128,128]{3,2,1,0:T(8,128)S(1)}, u32[]{:S(2)}, u32[]{:S(2)}) %all-to-all-start.2) | async-done | bytes 2097184 | tf_op jit(solution)/shard_map/all_to_all | solution.py:341
  225.5 1.3 copy-done.3
  226.8 3.6 %unpack_last.1 = (f32[14,128,128]{2,1,0:T(8,128)}, f32[14,128,128]{2,1,0:T(8,128)}, f32[14,128,128]{2,1,0:T(8,128)}) custom-call(s32[14]{0:T(128)} %bitcast.20, f32[3]{0:T(128)} %coefs_ref.3, f32[16,2,128,128]{3,2,1,0:T(8,128)} %copy-done.3, f32[14,128,128]{2,1,0:T(8,128)} %unpack_first.1.sum_ref), custom_call_target="tpu_custom_call" | custom-call | tf_op jit(solution)/shard_map/unpack_last/pallas_call | solution.py:326
  (14 shorter events, 0.0 us)
Async XLA Ops:
  0.6 23.3 %collective-permute-start = (f32[14,128,128]{2,1,0:T(8,128)}, f32[14,128,128]{2,1,0:T(8,128)S(1)}, u32[]{:S(2)}, u32[]{:S(2)}) collective-permute-start(f32[14,128,128]{2,1,0:T(8,128)} %bitcast.13), channel_id=1, source_target_pairs={{0,4},{1,3},{2,0},{3,7},{4,8},{5,1},{6,2},{7,11},{8,12},{9,5},{10,... | collective-permute-start | bytes 2752520 | tf_op jit(solution)/shard_map/ppermute | solution.py:18
  1.1 23.3 %collective-permute-start.2 = (f32[14,128,128]{2,1,0:T(8,128)}, f32[14,128,128]{2,1,0:T(8,128)S(1)}, u32[]{:S(2)}, u32[]{:S(2)}) collective-permute-start(f32[14,128,128]{2,1,0:T(8,128)} %bitcast.14), channel_id=1, source_target_pairs={{0,2},{1,5},{2,6},{3,1},{4,0},{5,9},{6,10},{7,3},{8,4},{9,13},{10,... | collective-permute-start | bytes 2752520 | tf_op jit(solution)/shard_map/ppermute | solution.py:18
  2.7 30.4 %collective-permute-start.4 = (f32[14,128,128]{2,1,0:T(8,128)}, f32[14,128,128]{2,1,0:T(8,128)S(1)}, u32[]{:S(2)}, u32[]{:S(2)}) collective-permute-start(f32[14,128,128]{2,1,0:T(8,128)} %bitcast.15), channel_id=1, source_target_pairs={{0,1},{1,0},{2,3},{3,2},{4,5},{5,4},{6,7},{7,6},{8,9},{9,8},{10,11... | collective-permute-start | bytes 2752520 | tf_op jit(solution)/shard_map/ppermute | solution.py:18
  24.0 22.5 %copy-start.5 = (f32[14,128,128]{2,1,0:T(8,128)}, f32[14,128,128]{2,1,0:T(8,128)S(1)}, u32[]{:S(2)}) copy-start(f32[14,128,128]{2,1,0:T(8,128)S(1)} %collective-permute-done.refs_2_) | copy-start | bytes 2752516
  24.0 22.5 %collective-permute-start.1 = (f32[14,128,128]{2,1,0:T(8,128)S(1)}, f32[14,128,128]{2,1,0:T(8,128)}, u32[]{:S(2)}, u32[]{:S(2)}) collective-permute-start(f32[14,128,128]{2,1,0:T(8,128)S(1)} %collective-permute-done.refs_2_), channel_id=1, source_target_pairs={{0,4},{1,3},{2,0},{3,7},{4,8},{5,1},{6,2},{7,11},{8,12},{9,5},{10,... | collective-permute-start | bytes 2752520 | tf_op jit(solution)/shard_map/ppermute | solution.py:18
  24.4 22.0 %copy-start.6 = (f32[14,128,128]{2,1,0:T(8,128)}, f32[14,128,128]{2,1,0:T(8,128)S(1)}, u32[]{:S(2)}) copy-start(f32[14,128,128]{2,1,0:T(8,128)S(1)} %collective-permute-done.2.refs_4_) | copy-start | bytes 2752516
  24.4 22.0 %collective-permute-start.3 = (f32[14,128,128]{2,1,0:T(8,128)S(1)}, f32[14,128,128]{2,1,0:T(8,128)}, u32[]{:S(2)}, u32[]{:S(2)}) collective-permute-start(f32[14,128,128]{2,1,0:T(8,128)S(1)} %collective-permute-done.2.refs_4_), channel_id=1, source_target_pairs={{0,2},{1,5},{2,6},{3,1},{4,0},{5,9},{6,10},{7,3},{8,4},{9,13},{10,... | collective-permute-start | bytes 2752520 | tf_op jit(solution)/shard_map/ppermute | solution.py:18
  26.0 20.4 %collective-permute-start.5 = (f32[14,128,128]{2,1,0:T(8,128)S(1)}, f32[14,128,128]{2,1,0:T(8,128)}, u32[]{:S(2)}, u32[]{:S(2)}) collective-permute-start(f32[14,128,128]{2,1,0:T(8,128)S(1)} %collective-permute-done.refs_2_), channel_id=1, source_target_pairs={{0,1},{1,0},{2,3},{3,2},{4,5},{5,4},{6,7},{7,6},{8,9},{9,8},{10,11... | collective-permute-start | bytes 2752520 | tf_op jit(solution)/shard_map/ppermute | solution.py:18
  26.0 20.4 %collective-permute-start.6 = (f32[14,128,128]{2,1,0:T(8,128)S(1)}, f32[14,128,128]{2,1,0:T(8,128)}, u32[]{:S(2)}, u32[]{:S(2)}) collective-permute-start(f32[14,128,128]{2,1,0:T(8,128)S(1)} %collective-permute-done.2.refs_4_), channel_id=1, source_target_pairs={{0,1},{1,0},{2,3},{3,2},{4,5},{5,4},{6,7},{7,6},{8,9},{9,8},{10,11... | collective-permute-start | bytes 2752520 | tf_op jit(solution)/shard_map/ppermute | solution.py:18
  33.1 13.4 %copy-start.7 = (f32[14,128,128]{2,1,0:T(8,128)}, f32[14,128,128]{2,1,0:T(8,128)S(1)}, u32[]{:S(2)}) copy-start(f32[14,128,128]{2,1,0:T(8,128)S(1)} %collective-permute-done.4.refs_1_) | copy-start | bytes 2752516
  46.5 73.1 %all-to-all-start = ((f32[16,264,128]{2,1,0:T(8,128)}), f32[16,264,128]{2,1,0:T(8,128)S(1)}, u32[]{:S(2)}, u32[]{:S(2)}) async-start(f32[16,264,128]{2,1,0:T(8,128)} %pack.1), calls=%async_computation | async-start | bytes 4325376 | tf_op jit(solution)/shard_map/all_to_all | solution.py:341
  51.6 67.1 %collective-permute-start.9 = (f32[14,128,128]{2,1,0:T(8,128)}, f32[14,128,128]{2,1,0:T(8,128)}, u32[]{:S(2)}, u32[]{:S(2)}) collective-permute-start(f32[14,128,128]{2,1,0:T(8,128)} %collective-permute-done.1.refs_6_), channel_id=1, source_target_pairs={{0,4},{1,3},{2,0},{3,7},{4,8},{5,1},{6,2},{7,11},{8,12},{9,5},{10,... | collective-permute-start | bytes 2752520 | tf_op jit(solution)/shard_map/ppermute | solution.py:18
  52.2 67.4 %collective-permute-start.11 = (f32[14,128,128]{2,1,0:T(8,128)}, f32[14,128,128]{2,1,0:T(8,128)}, u32[]{:S(2)}, u32[]{:S(2)}) collective-permute-start(f32[14,128,128]{2,1,0:T(8,128)} %collective-permute-done.3.refs_8_), channel_id=1, source_target_pairs={{0,2},{1,5},{2,6},{3,1},{4,0},{5,9},{6,10},{7,3},{8,4},{9,13},{10,... | collective-permute-start | bytes 2752520 | tf_op jit(solution)/shard_map/ppermute | solution.py:18
  53.6 69.0 %collective-permute-start.7 = (f32[14,128,128]{2,1,0:T(8,128)}, f32[14,128,128]{2,1,0:T(8,128)}, u32[]{:S(2)}, u32[]{:S(2)}) collective-permute-start(f32[14,128,128]{2,1,0:T(8,128)} %collective-permute-done.1.refs_6_), channel_id=1, source_target_pairs={{0,1},{1,0},{2,3},{3,2},{4,5},{5,4},{6,7},{7,6},{8,9},{9,8},{10,11... | collective-permute-start | bytes 2752520 | tf_op jit(solution)/shard_map/ppermute | solution.py:18
  53.6 69.0 %collective-permute-start.8 = (f32[14,128,128]{2,1,0:T(8,128)}, f32[14,128,128]{2,1,0:T(8,128)}, u32[]{:S(2)}, u32[]{:S(2)}) collective-permute-start(f32[14,128,128]{2,1,0:T(8,128)} %collective-permute-done.3.refs_8_), channel_id=1, source_target_pairs={{0,1},{1,0},{2,3},{3,2},{4,5},{5,4},{6,7},{7,6},{8,9},{9,8},{10,11... | collective-permute-start | bytes 2752520 | tf_op jit(solution)/shard_map/ppermute | solution.py:18
  118.7 4.0 %collective-permute-start.10 = (f32[14,128,128]{2,1,0:T(8,128)}, f32[14,128,128]{2,1,0:T(8,128)}, u32[]{:S(2)}, u32[]{:S(2)}) collective-permute-start(f32[14,128,128]{2,1,0:T(8,128)} %collective-permute-done.9.refs_10_), channel_id=1, source_target_pairs={{0,1},{1,0},{2,3},{3,2},{4,5},{5,4},{6,7},{7,6},{8,9},{9,8},{10,11... | collective-permute-start | bytes 2752520 | tf_op jit(solution)/shard_map/ppermute | solution.py:18
  119.6 3.4 %collective-permute-start.12 = (f32[14,128,128]{2,1,0:T(8,128)}, f32[14,128,128]{2,1,0:T(8,128)}, u32[]{:S(2)}, u32[]{:S(2)}) collective-permute-start(f32[14,128,128]{2,1,0:T(8,128)} %collective-permute-done.11.refs_12_), channel_id=1, source_target_pairs={{0,1},{1,0},{2,3},{3,2},{4,5},{5,4},{6,7},{7,6},{8,9},{9,8},{10,11... | collective-permute-start | bytes 2752520 | tf_op jit(solution)/shard_map/ppermute | solution.py:18
  119.6 3.4 %copy-start.2 = (f32[16,264,128]{2,1,0:T(8,128)}, f32[16,264,128]{2,1,0:T(8,128)S(1)}, u32[]{:S(2)}) copy-start(f32[16,264,128]{2,1,0:T(8,128)S(1)} %all-to-all-done.t_ref.refs_2_) | copy-start | bytes 6488068
  119.6 18.2 %collective-permute-start.13 = (f32[14,128,128]{2,1,0:T(8,128)}, f32[14,128,128]{2,1,0:T(8,128)S(1)}, u32[]{:S(2)}, u32[]{:S(2)}) collective-permute-start(f32[14,128,128]{2,1,0:T(8,128)} %collective-permute-done.9.refs_10_), channel_id=1, source_target_pairs={{0,4},{1,3},{2,0},{3,7},{4,8},{5,1},{6,2},{7,11},{8,12},{9,5},{10,... | collective-permute-start | bytes 2752520 | tf_op jit(solution)/shard_map/ppermute | solution.py:18
  122.7 17.7 %copy-start = (s32[256]{0:T(256)S(1)}, s32[256]{0:T(256)}, u32[]{:S(2)}) copy-start(s32[256]{0:T(256)} %constant.40.table_ref) | copy-start | bytes 3076
  122.7 17.7 %copy-start.1 = (s32[32]{0:T(128)S(1)}, s32[32]{0:T(128)}, u32[]{:S(2)}) copy-start(s32[32]{0:T(128)} %convert_element_type.8.drops_ref) | copy-start | bytes 388
  137.8 2.5 %collective-permute-start.14 = (f32[14,128,128]{2,1,0:T(8,128)S(1)}, f32[14,128,128]{2,1,0:T(8,128)S(1)}, u32[]{:S(2)}, u32[]{:S(2)}) collective-permute-start(f32[14,128,128]{2,1,0:T(8,128)S(1)} %collective-permute-done.13.refs_0_), channel_id=1, source_target_pairs={{0,1},{1,0},{2,3},{3,2},{4,5},{5,4},{6,7},{7,6},{8,9},{9,8},{10,11... | collective-permute-start | bytes 2752520 | tf_op jit(solution)/shard_map/ppermute | solution.py:18
  143.7 29.4 %all-to-all-start.1 = ((f32[16,128,128]{2,1,0:T(8,128)}), f32[16,128,128]{2,1,0:T(8,128)S(1)}, u32[]{:S(2)}, u32[]{:S(2)}) async-start(f32[16,128,128]{2,1,0:T(8,128)} %get-tuple-element.22.refs_3_), calls=%async_computation.1 | async-start | bytes 2097152 | tf_op jit(solution)/shard_map/all_to_all | solution.py:341
  173.1 6.4 %copy-start.4 = (f32[16,128,128]{2,1,0:T(8,128)}, f32[16,128,128]{2,1,0:T(8,128)S(1)}, u32[]{:S(2)}) copy-start(f32[16,128,128]{2,1,0:T(8,128)S(1)} %all-to-all-done.1.first_ref) | copy-start | bytes 3145732
  173.1 52.4 %all-to-all-start.2 = ((f32[16,2,128,128]{3,2,1,0:T(8,128)}), f32[16,2,128,128]{3,2,1,0:T(8,128)S(1)}, u32[]{:S(2)}, u32[]{:S(2)}) async-start(f32[16,2,128,128]{3,2,1,0:T(8,128)} %later.1), calls=%async_computation.2 | async-start | bytes 4194304 | tf_op jit(solution)/shard_map/all_to_all | solution.py:341
  225.5 1.3 copy-start.3

commit v19 on v18

--- a/solution.py
+++ b/solution.py
@@ -194,45 +194,38 @@
             dense[slot, place, pl.ds(0, size), pl.ds(p * size, size)] = high
             dense[slot, place, pl.ds(size, size), pl.ds(p * size, size)] = low
 
-    def store(g, slot):
-        return pltpu.make_async_copy(dense.at[slot], dense_ref.at[pl.ds(g * group, group)], dense_sem.at[slot])
+    def store(g):
+        return pltpu.make_async_copy(dense.at[g % 2], dense_ref.at[pl.ds(g * group, group)], dense_sem.at[g % 2])
+
+    def arrive(g):
+        if g >= 2:
+            store(g - 2).wait()
+        for r in range(g * group, (g + 1) * group):
+            pltpu.make_async_copy(stage.at[r], stage.at[r], h_sem.at[r]).wait()
+
+    def prepare(g):
+        for place in range(group):
+            densify(g * group + place, g % 2, place)
+        store(g).start()
 
     groups = count // group
-
-    def one(g, carry):
-        slot = lax.rem(g, 2)
-
-        @pl.when(g >= 2)
-        def _():
-            store(g - 2, slot).wait()
-
-        def ready(place, carry):
-            r = g * group + place
-            pltpu.make_async_copy(stage.at[r], stage.at[r], h_sem.at[r]).wait()
-            densify(r, slot, place)
-            return carry
-
-        lax.fori_loop(0, group, ready, 0)
-        store(g, slot).start()
-        if start:
-
-            @pl.when(g == 0)
-            def _():
-                pltpu.make_async_copy(pair, pair, pair_sem).wait()
-
-        @pl.when(g == 0)
-        def _():
-            pltpu.make_async_copy(prev, prev, prev_sem).wait()
-
-        for place, product in enumerate(products_of(dense[slot], pair[...])):
+    arrive(0)
+    prepare(0)
+    if start:
+        pltpu.make_async_copy(pair, pair, pair_sem).wait()
+    pltpu.make_async_copy(prev, prev, prev_sem).wait()
+    for g in range(groups):
+        if g + 1 < groups:
+            arrive(g + 1)
+        products = list(products_of(dense[g % 2], pair[...]))
+        if g + 1 < groups:
+            prepare(g + 1)
+        for place, product in enumerate(products):
             r = g * group + place
             prev[r] = jnp.where(kept(start + r), 2.0 * product - prev[r], 0.0)
             pltpu.make_async_copy(prev.at[r], out_ref.at[rows[start + r]], out_sem).start()
-        return carry
-
-    lax.fori_loop(0, groups, one, 0)
     for g in range(max(groups - 2, 0), groups):
-        store(g, g % 2).wait()
+        store(g).wait()
     if not start:
         pltpu.make_async_copy(pair, pair, pair_sem).wait()
     pltpu.make_async_copy(prev, prev, out_sem).wait()
@@ -367,7 +360,7 @@
     start = 0
     for part in parts:
         h_rows = gathered.send(dense[-1] if start else None)
-        group = max(g for g in (2, 7, 13) if part % g == 0)
+        group = min(g for g in (2, 13) if part % g == 0)
         scratch = [
             pltpu.VMEM((part, count, size, size), f32),
             pltpu.VMEM((min(2, part // group), group) + dense_shape[1:], bf16),

time: 233 us -> 235 us (level)
  transfers between devices with their start and end apart: 18 -> 18, of which waited for: 8 -> 8; matrix products, arithmetic and copies ran while one was open for 1% -> 1% of each run, Pallas kernels for 17% -> 18%
where the time goes in v19:
time: 235 us; the launch traced here: 233 us
  waiting for transfers between devices  150 us (64%)
  Pallas kernels  48.2 us (21%)
  starting transfers between devices  27.8 us (12%)
    ppermute x15, waiting for transfers between devices, permute(): return lax.ppermute(x, 'row', [(i, target(i)) for i in range(devices)])  102 us
    all_to_all x3, waiting for transfers between devices, exchange(): return lax.all_to_all(x, 'row', 0, 0, tiled=True)  48.4 us
    pallas_call x6, Pallas kernels, call(): pl.pallas_call(kernel, out_shape=[pltpu.HBM(out.shape, out.dtype) for out...  48.2 us
    all_to_all x3, starting transfers between devices, exchange(): return lax.all_to_all(x, 'row', 0, 0, tiled=True)  17.6 us
    ppermute x15, starting transfers between devices, permute(): return lax.ppermute(x, 'row', [(i, target(i)) for i in range(devices)])  10.2 us
  transfers between devices with their start and end apart: 18, of which 8 were waited for; matrix products, arithmetic and copies ran while one was open for 1% of the time, Pallas kernels for 18%

profile of v19, /device:TPU:22, one launch (start us, length us, event | category | flops | bytes accessed | tf_op | source)
XLA Modules:
  0.0 232.8 jit_solution(17006360517001216177)
XLA Ops:
  0.6 0.5 collective-permute-start
  1.1 1.6 collective-permute-start.2
  2.7 0.0 collective-permute-start.4
  2.7 21.2 %collective-permute-done.refs_2_ = f32[14,128,128]{2,1,0:T(8,128)S(1)} collective-permute-done((f32[14,128,128]{2,1,0:T(8,128)}, f32[14,128,128]{2,1,0:T(8,128)S(1)}, u32[]{:S(2)}, u32[]{:S(2)}) %collective-permute-start) | collective-permute-done | bytes 917536 | tf_op jit(solution)/shard_map/ppermute | solution.py:18
  24.0 0.4 collective-permute-start.1
  24.4 0.0 collective-permute-done.2.refs_4_
  24.4 1.6 collective-permute-start.3
  26.0 0.0 collective-permute-start.5
  26.0 0.5 collective-permute-start.6
  26.5 1.4 fusion.1
  29.2 0.6 pad_add_fusion.info_ref
  29.8 3.2 %pack.1 = f32[16,264,128]{2,1,0:T(8,128)} custom-call(s32[3]{0:T(128)} %pad_add_fusion.info_ref, s32[14]{0:T(128)} %bitcast.18, f32[14,128,128]{2,1,0:T(8,128)} %bitcast.11, f32[14,128,128]{2,1,0:T(8,128)} %bitcast.12), custom_call_target="tpu_custom_call" | custom-call | tf_op jit(solution)/shard_map/pack/pallas_call | solution.py:319
  33.1 0.0 collective-permute-done.4.refs_1_
  33.1 0.0 copy-start.7
  33.1 13.3 %collective-permute-done.1.refs_6_ = f32[14,128,128]{2,1,0:T(8,128)} collective-permute-done((f32[14,128,128]{2,1,0:T(8,128)S(1)}, f32[14,128,128]{2,1,0:T(8,128)}, u32[]{:S(2)}, u32[]{:S(2)}) %collective-permute-start.1) | collective-permute-done | bytes 917536 | tf_op jit(solution)/shard_map/ppermute | solution.py:18
  46.4 0.0 collective-permute-done.3.refs_8_
  46.4 0.0 collective-permute-done.5.refs_3_
  46.4 0.0 collective-permute-done.6.refs_5_
  46.5 5.1 %all-to-all-start = ((f32[16,264,128]{2,1,0:T(8,128)}), f32[16,264,128]{2,1,0:T(8,128)S(1)}, u32[]{:S(2)}, u32[]{:S(2)}) async-start(f32[16,264,128]{2,1,0:T(8,128)} %pack.1), calls=%async_computation | async-start | bytes 4325376 | tf_op jit(solution)/shard_map/all_to_all | solution.py:334
  51.6 0.6 collective-permute-start.9
  52.2 1.5 collective-permute-start.11
  53.6 0.0 collective-permute-start.7
  53.6 0.5 collective-permute-start.8
  54.1 64.5 %collective-permute-done.9.refs_10_ = f32[14,128,128]{2,1,0:T(8,128)} collective-permute-done((f32[14,128,128]{2,1,0:T(8,128)}, f32[14,128,128]{2,1,0:T(8,128)}, u32[]{:S(2)}, u32[]{:S(2)}) %collective-permute-start.9) | collective-permute-done | bytes 917536 | tf_op jit(solution)/shard_map/ppermute | solution.py:18
  118.7 0.5 collective-permute-start.10
  119.2 0.4 collective-permute-done.11.refs_12_
  119.6 0.0 collective-permute-start.12
  119.6 0.0 all-to-all-done.t_ref.refs_2_
  119.6 2.1 collective-permute-start.13
  121.7 0.3 fusion
  122.0 0.6 convert_element_type.8.drops_ref
  122.7 0.0 collective-permute-done.7.refs_7_
  122.7 0.0 collective-permute-done.8.refs_9_
  122.7 0.0 collective-permute-done.10.refs_11_
  122.7 0.3 collective-permute-done.12.refs_13_
  123.0 17.2 %first.2 = (bf16[14,256,2048]{2,1,0:T(8,128)(2,1)}, f32[16,128,128]{2,1,0:T(8,128)}, bf16[2048,256]{1,0:T(8,128)(2,1)}) custom-call(s32[32]{0:T(128)} %convert_element_type.8.drops_ref, s32[1]{0:T(128)} %bitcast.1.me_ref, s32[256]{0:T(256)} %constant.40.table_ref, f32[16,264,128]{2,1,0:T(8,128)} %copy-done.2, f32[14,128,128]{2,1,0:T(8,128)} %bitcast.16, ...), custom_call_target="tpu_custom_call" | custom-call | tf_op jit(solution)/shard_map/first/pallas_call | solution.py:319
  140.1 0.0 collective-permute-done.13.refs_0_
  140.1 0.4 collective-permute-start.14
  140.5 2.1 collective-permute-done.14.refs_1_
  142.7 3.3 %first.3 = (bf16[2,256,2048]{2,1,0:T(8,128)(2,1)}, f32[16,128,128]{2,1,0:T(8,128)}) custom-call(s32[32]{0:T(128)S(1)} %copy-done.1, s32[1]{0:T(128)} %bitcast.1.me_ref, s32[256]{0:T(256)S(1)} %copy-done, f32[16,264,128]{2,1,0:T(8,128)} %copy-done.2, f32[14,128,128]{2,1,0:T(8,128)S(1)} %collective-permute-done.13.refs_0_, ...), custom_call_target="tpu_custom_call", output_to_operand_aliasing={{1}: (7, {})} | custom-call | tf_op jit(solution)/shard_map/first/pallas_call | solution.py:319
  146.0 6.0 %all-to-all-start.1 = ((f32[16,128,128]{2,1,0:T(8,128)}), f32[16,128,128]{2,1,0:T(8,128)S(1)}, u32[]{:S(2)}, u32[]{:S(2)}) async-start(f32[16,128,128]{2,1,0:T(8,128)} %get-tuple-element.22.refs_3_), calls=%async_computation.1 | async-start | bytes 2097152 | tf_op jit(solution)/shard_map/all_to_all | solution.py:334
  152.1 17.8 %later.1 = f32[16,2,128,128]{3,2,1,0:T(8,128)} custom-call(s32[32]{0:T(128)} %convert_element_type.8.drops_ref, s32[1]{0:T(128)} %bitcast.1.me_ref, s32[256]{0:T(256)} %constant.40.table_ref, bf16[14,256,2048]{2,1,0:T(8,128)(2,1)} %get-tuple-element.16.refs_0_, bf16[2,256,2048]{2,1,0:T(8,128)(2,1)} %get-tuple-element.21.refs_1_, f32[16,264,128]{2,1,0:T(8,128)} %copy-done.2, ...), custom_call_target="tpu_custom_call" | custom-call | tf_op jit(solution)/shard_map/later/pallas_call | solution.py:319
  169.9 5.6 %all-to-all-done.1.first_ref = f32[16,128,128]{2,1,0:T(8,128)S(1)} async-done(((f32[16,128,128]{2,1,0:T(8,128)}), f32[16,128,128]{2,1,0:T(8,128)S(1)}, u32[]{:S(2)}, u32[]{:S(2)}) %all-to-all-start.1) | async-done | bytes 1048608 | tf_op jit(solution)/shard_map/all_to_all | solution.py:334
  175.5 6.4 %all-to-all-start.2 = ((f32[16,2,128,128]{3,2,1,0:T(8,128)}), f32[16,2,128,128]{3,2,1,0:T(8,128)S(1)}, u32[]{:S(2)}, u32[]{:S(2)}) async-start(f32[16,2,128,128]{3,2,1,0:T(8,128)} %later.1), calls=%async_computation.2 | async-start | bytes 4194304 | tf_op jit(solution)/shard_map/all_to_all | solution.py:334
  181.9 3.1 %unpack_first.1.sum_ref = f32[14,128,128]{2,1,0:T(8,128)} custom-call(s32[14]{0:T(128)} %bitcast.19, f32[3]{0:T(128)} %coefs_ref.3, f32[16,128,128]{2,1,0:T(8,128)} %copy-done.4, f32[14,128,128]{2,1,0:T(8,128)} %bitcast.17), custom_call_target="tpu_custom_call" | custom-call | tf_op jit(solution)/shard_map/unpack_first/pallas_call | solution.py:319
  185.0 42.8 %all-to-all-done.2.held_ref = f32[16,2,128,128]{3,2,1,0:T(8,128)S(1)} async-done(((f32[16,2,128,128]{3,2,1,0:T(8,128)}), f32[16,2,128,128]{3,2,1,0:T(8,128)S(1)}, u32[]{:S(2)}, u32[]{:S(2)}) %all-to-all-start.2) | async-done | bytes 2097184 | tf_op jit(solution)/shard_map/all_to_all | solution.py:334
  227.8 1.3 copy-done.3
  229.2 3.6 %unpack_last.1 = (f32[14,128,128]{2,1,0:T(8,128)}, f32[14,128,128]{2,1,0:T(8,128)}, f32[14,128,128]{2,1,0:T(8,128)}) custom-call(s32[14]{0:T(128)} %bitcast.20, f32[3]{0:T(128)} %coefs_ref.3, f32[16,2,128,128]{3,2,1,0:T(8,128)} %copy-done.3, f32[14,128,128]{2,1,0:T(8,128)} %unpack_first.1.sum_ref), custom_call_target="tpu_custom_call" | custom-call | tf_op jit(solution)/shard_map/unpack_last/pallas_call | solution.py:319
  (14 shorter events, 0.0 us)
Async XLA Ops:
  0.6 23.3 %collective-permute-start = (f32[14,128,128]{2,1,0:T(8,128)}, f32[14,128,128]{2,1,0:T(8,128)S(1)}, u32[]{:S(2)}, u32[]{:S(2)}) collective-permute-start(f32[14,128,128]{2,1,0:T(8,128)} %bitcast.13), channel_id=1, source_target_pairs={{0,4},{1,3},{2,0},{3,7},{4,8},{5,1},{6,2},{7,11},{8,12},{9,5},{10,... | collective-permute-start | bytes 2752520 | tf_op jit(solution)/shard_map/ppermute | solution.py:18
  1.1 23.3 %collective-permute-start.2 = (f32[14,128,128]{2,1,0:T(8,128)}, f32[14,128,128]{2,1,0:T(8,128)S(1)}, u32[]{:S(2)}, u32[]{:S(2)}) collective-permute-start(f32[14,128,128]{2,1,0:T(8,128)} %bitcast.14), channel_id=1, source_target_pairs={{0,2},{1,5},{2,6},{3,1},{4,0},{5,9},{6,10},{7,3},{8,4},{9,13},{10,... | collective-permute-start | bytes 2752520 | tf_op jit(solution)/shard_map/ppermute | solution.py:18
  2.7 30.4 %collective-permute-start.4 = (f32[14,128,128]{2,1,0:T(8,128)}, f32[14,128,128]{2,1,0:T(8,128)S(1)}, u32[]{:S(2)}, u32[]{:S(2)}) collective-permute-start(f32[14,128,128]{2,1,0:T(8,128)} %bitcast.15), channel_id=1, source_target_pairs={{0,1},{1,0},{2,3},{3,2},{4,5},{5,4},{6,7},{7,6},{8,9},{9,8},{10,11... | collective-permute-start | bytes 2752520 | tf_op jit(solution)/shard_map/ppermute | solution.py:18
  24.0 22.5 %copy-start.5 = (f32[14,128,128]{2,1,0:T(8,128)}, f32[14,128,128]{2,1,0:T(8,128)S(1)}, u32[]{:S(2)}) copy-start(f32[14,128,128]{2,1,0:T(8,128)S(1)} %collective-permute-done.refs_2_) | copy-start | bytes 2752516
  24.0 22.5 %collective-permute-start.1 = (f32[14,128,128]{2,1,0:T(8,128)S(1)}, f32[14,128,128]{2,1,0:T(8,128)}, u32[]{:S(2)}, u32[]{:S(2)}) collective-permute-start(f32[14,128,128]{2,1,0:T(8,128)S(1)} %collective-permute-done.refs_2_), channel_id=1, source_target_pairs={{0,4},{1,3},{2,0},{3,7},{4,8},{5,1},{6,2},{7,11},{8,12},{9,5},{10,... | collective-permute-start | bytes 2752520 | tf_op jit(solution)/shard_map/ppermute | solution.py:18
  24.4 22.0 %copy-start.6 = (f32[14,128,128]{2,1,0:T(8,128)}, f32[14,128,128]{2,1,0:T(8,128)S(1)}, u32[]{:S(2)}) copy-start(f32[14,128,128]{2,1,0:T(8,128)S(1)} %collective-permute-done.2.refs_4_) | copy-start | bytes 2752516
  24.4 22.0 %collective-permute-start.3 = (f32[14,128,128]{2,1,0:T(8,128)S(1)}, f32[14,128,128]{2,1,0:T(8,128)}, u32[]{:S(2)}, u32[]{:S(2)}) collective-permute-start(f32[14,128,128]{2,1,0:T(8,128)S(1)} %collective-permute-done.2.refs_4_), channel_id=1, source_target_pairs={{0,2},{1,5},{2,6},{3,1},{4,0},{5,9},{6,10},{7,3},{8,4},{9,13},{10,... | collective-permute-start | bytes 2752520 | tf_op jit(solution)/shard_map/ppermute | solution.py:18
  26.0 20.4 %collective-permute-start.5 = (f32[14,128,128]{2,1,0:T(8,128)S(1)}, f32[14,128,128]{2,1,0:T(8,128)}, u32[]{:S(2)}, u32[]{:S(2)}) collective-permute-start(f32[14,128,128]{2,1,0:T(8,128)S(1)} %collective-permute-done.refs_2_), channel_id=1, source_target_pairs={{0,1},{1,0},{2,3},{3,2},{4,5},{5,4},{6,7},{7,6},{8,9},{9,8},{10,11... | collective-permute-start | bytes 2752520 | tf_op jit(solution)/shard_map/ppermute | solution.py:18
  26.0 20.4 %collective-permute-start.6 = (f32[14,128,128]{2,1,0:T(8,128)S(1)}, f32[14,128,128]{2,1,0:T(8,128)}, u32[]{:S(2)}, u32[]{:S(2)}) collective-permute-start(f32[14,128,128]{2,1,0:T(8,128)S(1)} %collective-permute-done.2.refs_4_), channel_id=1, source_target_pairs={{0,1},{1,0},{2,3},{3,2},{4,5},{5,4},{6,7},{7,6},{8,9},{9,8},{10,11... | collective-permute-start | bytes 2752520 | tf_op jit(solution)/shard_map/ppermute | solution.py:18
  33.1 13.4 %copy-start.7 = (f32[14,128,128]{2,1,0:T(8,128)}, f32[14,128,128]{2,1,0:T(8,128)S(1)}, u32[]{:S(2)}) copy-start(f32[14,128,128]{2,1,0:T(8,128)S(1)} %collective-permute-done.4.refs_1_) | copy-start | bytes 2752516
  46.5 73.1 %all-to-all-start = ((f32[16,264,128]{2,1,0:T(8,128)}), f32[16,264,128]{2,1,0:T(8,128)S(1)}, u32[]{:S(2)}, u32[]{:S(2)}) async-start(f32[16,264,128]{2,1,0:T(8,128)} %pack.1), calls=%async_computation | async-start | bytes 4325376 | tf_op jit(solution)/shard_map/all_to_all | solution.py:334
  51.6 67.1 %collective-permute-start.9 = (f32[14,128,128]{2,1,0:T(8,128)}, f32[14,128,128]{2,1,0:T(8,128)}, u32[]{:S(2)}, u32[]{:S(2)}) collective-permute-start(f32[14,128,128]{2,1,0:T(8,128)} %collective-permute-done.1.refs_6_), channel_id=1, source_target_pairs={{0,4},{1,3},{2,0},{3,7},{4,8},{5,1},{6,2},{7,11},{8,12},{9,5},{10,... | collective-permute-start | bytes 2752520 | tf_op jit(solution)/shard_map/ppermute | solution.py:18
  52.2 67.4 %collective-permute-start.11 = (f32[14,128,128]{2,1,0:T(8,128)}, f32[14,128,128]{2,1,0:T(8,128)}, u32[]{:S(2)}, u32[]{:S(2)}) collective-permute-start(f32[14,128,128]{2,1,0:T(8,128)} %collective-permute-done.3.refs_8_), channel_id=1, source_target_pairs={{0,2},{1,5},{2,6},{3,1},{4,0},{5,9},{6,10},{7,3},{8,4},{9,13},{10,... | collective-permute-start | bytes 2752520 | tf_op jit(solution)/shard_map/ppermute | solution.py:18
  53.6 69.0 %collective-permute-start.7 = (f32[14,128,128]{2,1,0:T(8,128)}, f32[14,128,128]{2,1,0:T(8,128)}, u32[]{:S(2)}, u32[]{:S(2)}) collective-permute-start(f32[14,128,128]{2,1,0:T(8,128)} %collective-permute-done.1.refs_6_), channel_id=1, source_target_pairs={{0,1},{1,0},{2,3},{3,2},{4,5},{5,4},{6,7},{7,6},{8,9},{9,8},{10,11... | collective-permute-start | bytes 2752520 | tf_op jit(solution)/shard_map/ppermute | solution.py:18
  53.6 69.0 %collective-permute-start.8 = (f32[14,128,128]{2,1,0:T(8,128)}, f32[14,128,128]{2,1,0:T(8,128)}, u32[]{:S(2)}, u32[]{:S(2)}) collective-permute-start(f32[14,128,128]{2,1,0:T(8,128)} %collective-permute-done.3.refs_8_), channel_id=1, source_target_pairs={{0,1},{1,0},{2,3},{3,2},{4,5},{5,4},{6,7},{7,6},{8,9},{9,8},{10,11... | collective-permute-start | bytes 2752520 | tf_op jit(solution)/shard_map/ppermute | solution.py:18
  118.7 4.0 %collective-permute-start.10 = (f32[14,128,128]{2,1,0:T(8,128)}, f32[14,128,128]{2,1,0:T(8,128)}, u32[]{:S(2)}, u32[]{:S(2)}) collective-permute-start(f32[14,128,128]{2,1,0:T(8,128)} %collective-permute-done.9.refs_10_), channel_id=1, source_target_pairs={{0,1},{1,0},{2,3},{3,2},{4,5},{5,4},{6,7},{7,6},{8,9},{9,8},{10,11... | collective-permute-start | bytes 2752520 | tf_op jit(solution)/shard_map/ppermute | solution.py:18
  119.6 3.4 %collective-permute-start.12 = (f32[14,128,128]{2,1,0:T(8,128)}, f32[14,128,128]{2,1,0:T(8,128)}, u32[]{:S(2)}, u32[]{:S(2)}) collective-permute-start(f32[14,128,128]{2,1,0:T(8,128)} %collective-permute-done.11.refs_12_), channel_id=1, source_target_pairs={{0,1},{1,0},{2,3},{3,2},{4,5},{5,4},{6,7},{7,6},{8,9},{9,8},{10,11... | collective-permute-start | bytes 2752520 | tf_op jit(solution)/shard_map/ppermute | solution.py:18
  119.6 3.4 %copy-start.2 = (f32[16,264,128]{2,1,0:T(8,128)}, f32[16,264,128]{2,1,0:T(8,128)S(1)}, u32[]{:S(2)}) copy-start(f32[16,264,128]{2,1,0:T(8,128)S(1)} %all-to-all-done.t_ref.refs_2_) | copy-start | bytes 6488068
  119.6 20.5 %collective-permute-start.13 = (f32[14,128,128]{2,1,0:T(8,128)}, f32[14,128,128]{2,1,0:T(8,128)S(1)}, u32[]{:S(2)}, u32[]{:S(2)}) collective-permute-start(f32[14,128,128]{2,1,0:T(8,128)} %collective-permute-done.9.refs_10_), channel_id=1, source_target_pairs={{0,4},{1,3},{2,0},{3,7},{4,8},{5,1},{6,2},{7,11},{8,12},{9,5},{10,... | collective-permute-start | bytes 2752520 | tf_op jit(solution)/shard_map/ppermute | solution.py:18
  122.7 20.0 %copy-start = (s32[256]{0:T(256)S(1)}, s32[256]{0:T(256)}, u32[]{:S(2)}) copy-start(s32[256]{0:T(256)} %constant.40.table_ref) | copy-start | bytes 3076
  122.7 20.0 %copy-start.1 = (s32[32]{0:T(128)S(1)}, s32[32]{0:T(128)}, u32[]{:S(2)}) copy-start(s32[32]{0:T(128)} %convert_element_type.8.drops_ref) | copy-start | bytes 388
  140.1 2.5 %collective-permute-start.14 = (f32[14,128,128]{2,1,0:T(8,128)S(1)}, f32[14,128,128]{2,1,0:T(8,128)S(1)}, u32[]{:S(2)}, u32[]{:S(2)}) collective-permute-start(f32[14,128,128]{2,1,0:T(8,128)S(1)} %collective-permute-done.13.refs_0_), channel_id=1, source_target_pairs={{0,1},{1,0},{2,3},{3,2},{4,5},{5,4},{6,7},{7,6},{8,9},{9,8},{10,11... | collective-permute-start | bytes 2752520 | tf_op jit(solution)/shard_map/ppermute | solution.py:18
  146.0 29.4 %all-to-all-start.1 = ((f32[16,128,128]{2,1,0:T(8,128)}), f32[16,128,128]{2,1,0:T(8,128)S(1)}, u32[]{:S(2)}, u32[]{:S(2)}) async-start(f32[16,128,128]{2,1,0:T(8,128)} %get-tuple-element.22.refs_3_), calls=%async_computation.1 | async-start | bytes 2097152 | tf_op jit(solution)/shard_map/all_to_all | solution.py:334
  175.5 6.4 %copy-start.4 = (f32[16,128,128]{2,1,0:T(8,128)}, f32[16,128,128]{2,1,0:T(8,128)S(1)}, u32[]{:S(2)}) copy-start(f32[16,128,128]{2,1,0:T(8,128)S(1)} %all-to-all-done.1.first_ref) | copy-start | bytes 3145732
  175.5 52.4 %all-to-all-start.2 = ((f32[16,2,128,128]{3,2,1,0:T(8,128)}), f32[16,2,128,128]{3,2,1,0:T(8,128)S(1)}, u32[]{:S(2)}, u32[]{:S(2)}) async-start(f32[16,2,128,128]{3,2,1,0:T(8,128)} %later.1), calls=%async_computation.2 | async-start | bytes 4194304 | tf_op jit(solution)/shard_map/all_to_all | solution.py:334
  227.8 1.3 copy-start.3

commit v20 on v19

--- a/solution.py
+++ b/solution.py
@@ -360,7 +360,7 @@
     start = 0
     for part in parts:
         h_rows = gathered.send(dense[-1] if start else None)
-        group = min(g for g in (2, 13) if part % g == 0)
+        group = max(g for g in (2, 7, 13) if part % g == 0)
         scratch = [
             pltpu.VMEM((part, count, size, size), f32),
             pltpu.VMEM((min(2, part // group), group) + dense_shape[1:], bf16),

time: 235 us -> 233 us (level)
  transfers between devices with their start and end apart: 18 -> 18, of which waited for: 8 -> 8; matrix products, arithmetic and copies ran while one was open for 1% -> 1% of each run, Pallas kernels for 18% -> 17%
where the time goes in v20:
time: 233 us; the launch traced here: 231 us
  waiting for transfers between devices  150 us (64%)
  Pallas kernels  46 us (20%)
  starting transfers between devices  27.7 us (12%)
  other arithmetic  2.34 us (1%)
    ppermute x15, waiting for transfers between devices, permute(): return lax.ppermute(x, 'row', [(i, target(i)) for i in range(devices)])  102 us
    all_to_all x3, waiting for transfers between devices, exchange(): return lax.all_to_all(x, 'row', 0, 0, tiled=True)  48.4 us
    pallas_call x6, Pallas kernels, call(): pl.pallas_call(kernel, out_shape=[pltpu.HBM(out.shape, out.dtype) for out...  46 us
    all_to_all x3, starting transfers between devices, exchange(): return lax.all_to_all(x, 'row', 0, 0, tiled=True)  17.6 us
    ppermute x15, starting transfers between devices, permute(): return lax.ppermute(x, 'row', [(i, target(i)) for i in range(devices)])  10.2 us
  transfers between devices with their start and end apart: 18, of which 8 were waited for; matrix products, arithmetic and copies ran while one was open for 1% of the time, Pallas kernels for 17%

profile of v20, /device:TPU:22, one launch (start us, length us, event | category | flops | bytes accessed | tf_op | source)
XLA Modules:
  0.0 230.5 jit_solution(5695801539870009807)
XLA Ops:
  0.6 0.5 collective-permute-start
  1.1 1.6 collective-permute-start.2
  2.7 0.0 collective-permute-start.4
  2.7 21.2 %collective-permute-done.refs_2_ = f32[14,128,128]{2,1,0:T(8,128)S(1)} collective-permute-done((f32[14,128,128]{2,1,0:T(8,128)}, f32[14,128,128]{2,1,0:T(8,128)S(1)}, u32[]{:S(2)}, u32[]{:S(2)}) %collective-permute-start) | collective-permute-done | bytes 917536 | tf_op jit(solution)/shard_map/ppermute | solution.py:18
  24.0 0.4 collective-permute-start.1
  24.4 0.0 collective-permute-done.2.refs_4_
  24.4 1.6 collective-permute-start.3
  26.0 0.0 collective-permute-start.5
  26.0 0.5 collective-permute-start.6
  26.5 1.4 fusion.1
  29.2 0.6 pad_add_fusion.info_ref
  29.8 3.2 %pack.1 = f32[16,264,128]{2,1,0:T(8,128)} custom-call(s32[3]{0:T(128)} %pad_add_fusion.info_ref, s32[14]{0:T(128)} %bitcast.18, f32[14,128,128]{2,1,0:T(8,128)} %bitcast.11, f32[14,128,128]{2,1,0:T(8,128)} %bitcast.12), custom_call_target="tpu_custom_call" | custom-call | tf_op jit(solution)/shard_map/pack/pallas_call | solution.py:319
  33.1 0.0 collective-permute-done.4.refs_1_
  33.1 0.0 copy-start.7
  33.1 13.3 %collective-permute-done.1.refs_6_ = f32[14,128,128]{2,1,0:T(8,128)} collective-permute-done((f32[14,128,128]{2,1,0:T(8,128)S(1)}, f32[14,128,128]{2,1,0:T(8,128)}, u32[]{:S(2)}, u32[]{:S(2)}) %collective-permute-start.1) | collective-permute-done | bytes 917536 | tf_op jit(solution)/shard_map/ppermute | solution.py:18
  46.4 0.0 collective-permute-done.3.refs_8_
  46.4 0.0 collective-permute-done.5.refs_3_
  46.4 0.0 collective-permute-done.6.refs_5_
  46.5 5.1 %all-to-all-start = ((f32[16,264,128]{2,1,0:T(8,128)}), f32[16,264,128]{2,1,0:T(8,128)S(1)}, u32[]{:S(2)}, u32[]{:S(2)}) async-start(f32[16,264,128]{2,1,0:T(8,128)} %pack.1), calls=%async_computation | async-start | bytes 4325376 | tf_op jit(solution)/shard_map/all_to_all | solution.py:334
  51.6 0.6 collective-permute-start.9
  52.2 1.5 collective-permute-start.11
  53.6 0.0 collective-permute-start.7
  53.6 0.5 collective-permute-start.8
  54.1 64.5 %collective-permute-done.9.refs_10_ = f32[14,128,128]{2,1,0:T(8,128)} collective-permute-done((f32[14,128,128]{2,1,0:T(8,128)}, f32[14,128,128]{2,1,0:T(8,128)}, u32[]{:S(2)}, u32[]{:S(2)}) %collective-permute-start.9) | collective-permute-done | bytes 917536 | tf_op jit(solution)/shard_map/ppermute | solution.py:18
  118.7 0.5 collective-permute-start.10
  119.2 0.4 collective-permute-done.11.refs_12_
  119.6 0.0 collective-permute-start.12
  119.6 0.0 all-to-all-done.t_ref.refs_2_
  119.6 2.1 collective-permute-start.13
  121.7 0.3 fusion
  122.0 0.6 convert_element_type.8.drops_ref
  122.7 0.0 collective-permute-done.7.refs_7_
  122.7 0.0 collective-permute-done.8.refs_9_
  122.7 0.0 collective-permute-done.10.refs_11_
  122.7 0.3 collective-permute-done.12.refs_13_
  123.0 15.0 %first.2 = (bf16[14,256,2048]{2,1,0:T(8,128)(2,1)}, f32[16,128,128]{2,1,0:T(8,128)}, bf16[2048,256]{1,0:T(8,128)(2,1)}) custom-call(s32[32]{0:T(128)} %convert_element_type.8.drops_ref, s32[1]{0:T(128)} %bitcast.1.me_ref, s32[256]{0:T(256)} %constant.40.table_ref, f32[16,264,128]{2,1,0:T(8,128)} %copy-done.2, f32[14,128,128]{2,1,0:T(8,128)} %bitcast.16, ...), custom_call_target="tpu_custom_call" | custom-call | tf_op jit(solution)/shard_map/first/pallas_call | solution.py:319
  137.9 0.0 collective-permute-done.13.refs_0_
  137.9 0.4 collective-permute-start.14
  138.3 2.2 collective-permute-done.14.refs_1_
  140.5 3.3 %first.3 = (bf16[2,256,2048]{2,1,0:T(8,128)(2,1)}, f32[16,128,128]{2,1,0:T(8,128)}) custom-call(s32[32]{0:T(128)S(1)} %copy-done.1, s32[1]{0:T(128)} %bitcast.1.me_ref, s32[256]{0:T(256)S(1)} %copy-done, f32[16,264,128]{2,1,0:T(8,128)} %copy-done.2, f32[14,128,128]{2,1,0:T(8,128)S(1)} %collective-permute-done.13.refs_0_, ...), custom_call_target="tpu_custom_call", output_to_operand_aliasing={{1}: (7, {})} | custom-call | tf_op jit(solution)/shard_map/first/pallas_call | solution.py:319
  143.8 6.0 %all-to-all-start.1 = ((f32[16,128,128]{2,1,0:T(8,128)}), f32[16,128,128]{2,1,0:T(8,128)S(1)}, u32[]{:S(2)}, u32[]{:S(2)}) async-start(f32[16,128,128]{2,1,0:T(8,128)} %get-tuple-element.22.refs_3_), calls=%async_computation.1 | async-start | bytes 2097152 | tf_op jit(solution)/shard_map/all_to_all | solution.py:334
  149.8 17.8 %later.1 = f32[16,2,128,128]{3,2,1,0:T(8,128)} custom-call(s32[32]{0:T(128)} %convert_element_type.8.drops_ref, s32[1]{0:T(128)} %bitcast.1.me_ref, s32[256]{0:T(256)} %constant.40.table_ref, bf16[14,256,2048]{2,1,0:T(8,128)(2,1)} %get-tuple-element.16.refs_0_, bf16[2,256,2048]{2,1,0:T(8,128)(2,1)} %get-tuple-element.21.refs_1_, f32[16,264,128]{2,1,0:T(8,128)} %copy-done.2, ...), custom_call_target="tpu_custom_call" | custom-call | tf_op jit(solution)/shard_map/later/pallas_call | solution.py:319
  167.6 5.6 %all-to-all-done.1.first_ref = f32[16,128,128]{2,1,0:T(8,128)S(1)} async-done(((f32[16,128,128]{2,1,0:T(8,128)}), f32[16,128,128]{2,1,0:T(8,128)S(1)}, u32[]{:S(2)}, u32[]{:S(2)}) %all-to-all-start.1) | async-done | bytes 1048608 | tf_op jit(solution)/shard_map/all_to_all | solution.py:334
  173.2 6.4 %all-to-all-start.2 = ((f32[16,2,128,128]{3,2,1,0:T(8,128)}), f32[16,2,128,128]{3,2,1,0:T(8,128)S(1)}, u32[]{:S(2)}, u32[]{:S(2)}) async-start(f32[16,2,128,128]{3,2,1,0:T(8,128)} %later.1), calls=%async_computation.2 | async-start | bytes 4194304 | tf_op jit(solution)/shard_map/all_to_all | solution.py:334
  179.7 3.1 %unpack_first.1.sum_ref = f32[14,128,128]{2,1,0:T(8,128)} custom-call(s32[14]{0:T(128)} %bitcast.19, f32[3]{0:T(128)} %coefs_ref.3, f32[16,128,128]{2,1,0:T(8,128)} %copy-done.4, f32[14,128,128]{2,1,0:T(8,128)} %bitcast.17), custom_call_target="tpu_custom_call" | custom-call | tf_op jit(solution)/shard_map/unpack_first/pallas_call | solution.py:319
  182.7 42.8 %all-to-all-done.2.held_ref = f32[16,2,128,128]{3,2,1,0:T(8,128)S(1)} async-done(((f32[16,2,128,128]{3,2,1,0:T(8,128)}), f32[16,2,128,128]{3,2,1,0:T(8,128)S(1)}, u32[]{:S(2)}, u32[]{:S(2)}) %all-to-all-start.2) | async-done | bytes 2097184 | tf_op jit(solution)/shard_map/all_to_all | solution.py:334
  225.6 1.3 copy-done.3
  226.9 3.6 %unpack_last.1 = (f32[14,128,128]{2,1,0:T(8,128)}, f32[14,128,128]{2,1,0:T(8,128)}, f32[14,128,128]{2,1,0:T(8,128)}) custom-call(s32[14]{0:T(128)} %bitcast.20, f32[3]{0:T(128)} %coefs_ref.3, f32[16,2,128,128]{3,2,1,0:T(8,128)} %copy-done.3, f32[14,128,128]{2,1,0:T(8,128)} %unpack_first.1.sum_ref), custom_call_target="tpu_custom_call" | custom-call | tf_op jit(solution)/shard_map/unpack_last/pallas_call | solution.py:319
  (14 shorter events, 0.0 us)
Async XLA Ops:
  0.6 23.3 %collective-permute-start = (f32[14,128,128]{2,1,0:T(8,128)}, f32[14,128,128]{2,1,0:T(8,128)S(1)}, u32[]{:S(2)}, u32[]{:S(2)}) collective-permute-start(f32[14,128,128]{2,1,0:T(8,128)} %bitcast.13), channel_id=1, source_target_pairs={{0,4},{1,3},{2,0},{3,7},{4,8},{5,1},{6,2},{7,11},{8,12},{9,5},{10,... | collective-permute-start | bytes 2752520 | tf_op jit(solution)/shard_map/ppermute | solution.py:18
  1.1 23.3 %collective-permute-start.2 = (f32[14,128,128]{2,1,0:T(8,128)}, f32[14,128,128]{2,1,0:T(8,128)S(1)}, u32[]{:S(2)}, u32[]{:S(2)}) collective-permute-start(f32[14,128,128]{2,1,0:T(8,128)} %bitcast.14), channel_id=1, source_target_pairs={{0,2},{1,5},{2,6},{3,1},{4,0},{5,9},{6,10},{7,3},{8,4},{9,13},{10,... | collective-permute-start | bytes 2752520 | tf_op jit(solution)/shard_map/ppermute | solution.py:18
  2.7 30.4 %collective-permute-start.4 = (f32[14,128,128]{2,1,0:T(8,128)}, f32[14,128,128]{2,1,0:T(8,128)S(1)}, u32[]{:S(2)}, u32[]{:S(2)}) collective-permute-start(f32[14,128,128]{2,1,0:T(8,128)} %bitcast.15), channel_id=1, source_target_pairs={{0,1},{1,0},{2,3},{3,2},{4,5},{5,4},{6,7},{7,6},{8,9},{9,8},{10,11... | collective-permute-start | bytes 2752520 | tf_op jit(solution)/shard_map/ppermute | solution.py:18
  24.0 22.5 %copy-start.5 = (f32[14,128,128]{2,1,0:T(8,128)}, f32[14,128,128]{2,1,0:T(8,128)S(1)}, u32[]{:S(2)}) copy-start(f32[14,128,128]{2,1,0:T(8,128)S(1)} %collective-permute-done.refs_2_) | copy-start | bytes 2752516
  24.0 22.5 %collective-permute-start.1 = (f32[14,128,128]{2,1,0:T(8,128)S(1)}, f32[14,128,128]{2,1,0:T(8,128)}, u32[]{:S(2)}, u32[]{:S(2)}) collective-permute-start(f32[14,128,128]{2,1,0:T(8,128)S(1)} %collective-permute-done.refs_2_), channel_id=1, source_target_pairs={{0,4},{1,3},{2,0},{3,7},{4,8},{5,1},{6,2},{7,11},{8,12},{9,5},{10,... | collective-permute-start | bytes 2752520 | tf_op jit(solution)/shard_map/ppermute | solution.py:18
  24.4 22.0 %copy-start.6 = (f32[14,128,128]{2,1,0:T(8,128)}, f32[14,128,128]{2,1,0:T(8,128)S(1)}, u32[]{:S(2)}) copy-start(f32[14,128,128]{2,1,0:T(8,128)S(1)} %collective-permute-done.2.refs_4_) | copy-start | bytes 2752516
  24.4 22.0 %collective-permute-start.3 = (f32[14,128,128]{2,1,0:T(8,128)S(1)}, f32[14,128,128]{2,1,0:T(8,128)}, u32[]{:S(2)}, u32[]{:S(2)}) collective-permute-start(f32[14,128,128]{2,1,0:T(8,128)S(1)} %collective-permute-done.2.refs_4_), channel_id=1, source_target_pairs={{0,2},{1,5},{2,6},{3,1},{4,0},{5,9},{6,10},{7,3},{8,4},{9,13},{10,... | collective-permute-start | bytes 2752520 | tf_op jit(solution)/shard_map/ppermute | solution.py:18
  26.0 20.4 %collective-permute-start.5 = (f32[14,128,128]{2,1,0:T(8,128)S(1)}, f32[14,128,128]{2,1,0:T(8,128)}, u32[]{:S(2)}, u32[]{:S(2)}) collective-permute-start(f32[14,128,128]{2,1,0:T(8,128)S(1)} %collective-permute-done.refs_2_), channel_id=1, source_target_pairs={{0,1},{1,0},{2,3},{3,2},{4,5},{5,4},{6,7},{7,6},{8,9},{9,8},{10,11... | collective-permute-start | bytes 2752520 | tf_op jit(solution)/shard_map/ppermute | solution.py:18
  26.0 20.4 %collective-permute-start.6 = (f32[14,128,128]{2,1,0:T(8,128)S(1)}, f32[14,128,128]{2,1,0:T(8,128)}, u32[]{:S(2)}, u32[]{:S(2)}) collective-permute-start(f32[14,128,128]{2,1,0:T(8,128)S(1)} %collective-permute-done.2.refs_4_), channel_id=1, source_target_pairs={{0,1},{1,0},{2,3},{3,2},{4,5},{5,4},{6,7},{7,6},{8,9},{9,8},{10,11... | collective-permute-start | bytes 2752520 | tf_op jit(solution)/shard_map/ppermute | solution.py:18
  33.1 13.4 %copy-start.7 = (f32[14,128,128]{2,1,0:T(8,128)}, f32[14,128,128]{2,1,0:T(8,128)S(1)}, u32[]{:S(2)}) copy-start(f32[14,128,128]{2,1,0:T(8,128)S(1)} %collective-permute-done.4.refs_1_) | copy-start | bytes 2752516
  46.5 73.1 %all-to-all-start = ((f32[16,264,128]{2,1,0:T(8,128)}), f32[16,264,128]{2,1,0:T(8,128)S(1)}, u32[]{:S(2)}, u32[]{:S(2)}) async-start(f32[16,264,128]{2,1,0:T(8,128)} %pack.1), calls=%async_computation | async-start | bytes 4325376 | tf_op jit(solution)/shard_map/all_to_all | solution.py:334
  51.6 67.1 %collective-permute-start.9 = (f32[14,128,128]{2,1,0:T(8,128)}, f32[14,128,128]{2,1,0:T(8,128)}, u32[]{:S(2)}, u32[]{:S(2)}) collective-permute-start(f32[14,128,128]{2,1,0:T(8,128)} %collective-permute-done.1.refs_6_), channel_id=1, source_target_pairs={{0,4},{1,3},{2,0},{3,7},{4,8},{5,1},{6,2},{7,11},{8,12},{9,5},{10,... | collective-permute-start | bytes 2752520 | tf_op jit(solution)/shard_map/ppermute | solution.py:18
  52.2 67.4 %collective-permute-start.11 = (f32[14,128,128]{2,1,0:T(8,128)}, f32[14,128,128]{2,1,0:T(8,128)}, u32[]{:S(2)}, u32[]{:S(2)}) collective-permute-start(f32[14,128,128]{2,1,0:T(8,128)} %collective-permute-done.3.refs_8_), channel_id=1, source_target_pairs={{0,2},{1,5},{2,6},{3,1},{4,0},{5,9},{6,10},{7,3},{8,4},{9,13},{10,... | collective-permute-start | bytes 2752520 | tf_op jit(solution)/shard_map/ppermute | solution.py:18
  53.6 69.0 %collective-permute-start.7 = (f32[14,128,128]{2,1,0:T(8,128)}, f32[14,128,128]{2,1,0:T(8,128)}, u32[]{:S(2)}, u32[]{:S(2)}) collective-permute-start(f32[14,128,128]{2,1,0:T(8,128)} %collective-permute-done.1.refs_6_), channel_id=1, source_target_pairs={{0,1},{1,0},{2,3},{3,2},{4,5},{5,4},{6,7},{7,6},{8,9},{9,8},{10,11... | collective-permute-start | bytes 2752520 | tf_op jit(solution)/shard_map/ppermute | solution.py:18
  53.6 69.0 %collective-permute-start.8 = (f32[14,128,128]{2,1,0:T(8,128)}, f32[14,128,128]{2,1,0:T(8,128)}, u32[]{:S(2)}, u32[]{:S(2)}) collective-permute-start(f32[14,128,128]{2,1,0:T(8,128)} %collective-permute-done.3.refs_8_), channel_id=1, source_target_pairs={{0,1},{1,0},{2,3},{3,2},{4,5},{5,4},{6,7},{7,6},{8,9},{9,8},{10,11... | collective-permute-start | bytes 2752520 | tf_op jit(solution)/shard_map/ppermute | solution.py:18
  118.7 4.0 %collective-permute-start.10 = (f32[14,128,128]{2,1,0:T(8,128)}, f32[14,128,128]{2,1,0:T(8,128)}, u32[]{:S(2)}, u32[]{:S(2)}) collective-permute-start(f32[14,128,128]{2,1,0:T(8,128)} %collective-permute-done.9.refs_10_), channel_id=1, source_target_pairs={{0,1},{1,0},{2,3},{3,2},{4,5},{5,4},{6,7},{7,6},{8,9},{9,8},{10,11... | collective-permute-start | bytes 2752520 | tf_op jit(solution)/shard_map/ppermute | solution.py:18
  119.6 3.4 %collective-permute-start.12 = (f32[14,128,128]{2,1,0:T(8,128)}, f32[14,128,128]{2,1,0:T(8,128)}, u32[]{:S(2)}, u32[]{:S(2)}) collective-permute-start(f32[14,128,128]{2,1,0:T(8,128)} %collective-permute-done.11.refs_12_), channel_id=1, source_target_pairs={{0,1},{1,0},{2,3},{3,2},{4,5},{5,4},{6,7},{7,6},{8,9},{9,8},{10,11... | collective-permute-start | bytes 2752520 | tf_op jit(solution)/shard_map/ppermute | solution.py:18
  119.6 3.4 %copy-start.2 = (f32[16,264,128]{2,1,0:T(8,128)}, f32[16,264,128]{2,1,0:T(8,128)S(1)}, u32[]{:S(2)}) copy-start(f32[16,264,128]{2,1,0:T(8,128)S(1)} %all-to-all-done.t_ref.refs_2_) | copy-start | bytes 6488068
  119.6 18.4 %collective-permute-start.13 = (f32[14,128,128]{2,1,0:T(8,128)}, f32[14,128,128]{2,1,0:T(8,128)S(1)}, u32[]{:S(2)}, u32[]{:S(2)}) collective-permute-start(f32[14,128,128]{2,1,0:T(8,128)} %collective-permute-done.9.refs_10_), channel_id=1, source_target_pairs={{0,4},{1,3},{2,0},{3,7},{4,8},{5,1},{6,2},{7,11},{8,12},{9,5},{10,... | collective-permute-start | bytes 2752520 | tf_op jit(solution)/shard_map/ppermute | solution.py:18
  122.7 17.8 %copy-start = (s32[256]{0:T(256)S(1)}, s32[256]{0:T(256)}, u32[]{:S(2)}) copy-start(s32[256]{0:T(256)} %constant.40.table_ref) | copy-start | bytes 3076
  122.7 17.8 %copy-start.1 = (s32[32]{0:T(128)S(1)}, s32[32]{0:T(128)}, u32[]{:S(2)}) copy-start(s32[32]{0:T(128)} %convert_element_type.8.drops_ref) | copy-start | bytes 388
  137.9 2.5 %collective-permute-start.14 = (f32[14,128,128]{2,1,0:T(8,128)S(1)}, f32[14,128,128]{2,1,0:T(8,128)S(1)}, u32[]{:S(2)}, u32[]{:S(2)}) collective-permute-start(f32[14,128,128]{2,1,0:T(8,128)S(1)} %collective-permute-done.13.refs_0_), channel_id=1, source_target_pairs={{0,1},{1,0},{2,3},{3,2},{4,5},{5,4},{6,7},{7,6},{8,9},{9,8},{10,11... | collective-permute-start | bytes 2752520 | tf_op jit(solution)/shard_map/ppermute | solution.py:18
  143.8 29.4 %all-to-all-start.1 = ((f32[16,128,128]{2,1,0:T(8,128)}), f32[16,128,128]{2,1,0:T(8,128)S(1)}, u32[]{:S(2)}, u32[]{:S(2)}) async-start(f32[16,128,128]{2,1,0:T(8,128)} %get-tuple-element.22.refs_3_), calls=%async_computation.1 | async-start | bytes 2097152 | tf_op jit(solution)/shard_map/all_to_all | solution.py:334
  173.2 6.4 %copy-start.4 = (f32[16,128,128]{2,1,0:T(8,128)}, f32[16,128,128]{2,1,0:T(8,128)S(1)}, u32[]{:S(2)}) copy-start(f32[16,128,128]{2,1,0:T(8,128)S(1)} %all-to-all-done.1.first_ref) | copy-start | bytes 3145732
  173.2 52.4 %all-to-all-start.2 = ((f32[16,2,128,128]{3,2,1,0:T(8,128)}), f32[16,2,128,128]{3,2,1,0:T(8,128)S(1)}, u32[]{:S(2)}, u32[]{:S(2)}) async-start(f32[16,2,128,128]{3,2,1,0:T(8,128)} %later.1), calls=%async_computation.2 | async-start | bytes 4194304 | tf_op jit(solution)/shard_map/all_to_all | solution.py:334
  225.6 1.3 copy-start.3

commit v21 on v18

--- a/solution.py
+++ b/solution.py
@@ -135,7 +135,7 @@
 def kept_rows(total, rows, drops_ref, w):
     row = rows[w]
     offset = lax.rem(rows.me - row + REACH + total, total)
-    _, named = place_of(offset, drops_ref[2 * row + 1])
+    _, named = place_of(offset, drops_ref[row, 1])
     return named
 
 
@@ -186,7 +186,7 @@
 
     def densify(r, slot, place):
         row = rows[start + r]
-        drop = drops_ref[2 * row]
+        drop = drops_ref[row, 0]
         for p in range(window):
             offset = lax.rem(rows[p] - row + REACH + total, total)
             k, named = place_of(offset, drop)
@@ -358,7 +358,7 @@
     table, parts = window_table(total)
     gathered = gathered_rows(h_blocks[0], total, lambda *others: exchange(after(send, *others)))
     column = next(gathered)
-    drops = column[:, 2 * size:2 * size + 2, 0].astype(jnp.int32).reshape(-1)
+    drops = column[:, 2 * size:2 * size + 2, 0].astype(jnp.int32)
     rows = jnp.array(table, jnp.int32).reshape(-1)
     window = sum(parts)
     dense_shape = (window, 2 * size, window * size)
@@ -367,7 +367,7 @@
     start = 0
     for part in parts:
         h_rows = gathered.send(dense[-1] if start else None)
-        group = max(g for g in (2, 7, 13) if part % g == 0)
+        group = max(g for g in (2, 13, 14) if part % g == 0)
         scratch = [
             pltpu.VMEM((part, count, size, size), f32),
             pltpu.VMEM((min(2, part // group), group) + dense_shape[1:], bf16),

time: 233 us -> 233 us (level)
  no operation moved by 1% of the time
where the time goes in v21:
time: 233 us; the launch traced here: 231 us
  waiting for transfers between devices  150 us (64%)
  Pallas kernels  46.4 us (20%)
  starting transfers between devices  27.8 us (12%)
    ppermute x15, waiting for transfers between devices, permute(): return lax.ppermute(x, 'row', [(i, target(i)) for i in range(devices)])  102 us
    all_to_all x3, waiting for transfers between devices, exchange(): return lax.all_to_all(x, 'row', 0, 0, tiled=True)  48.3 us
    pallas_call x6, Pallas kernels, call(): pl.pallas_call(kernel, out_shape=[pltpu.HBM(out.shape, out.dtype) for out...  46.4 us
    all_to_all x3, starting transfers between devices, exchange(): return lax.all_to_all(x, 'row', 0, 0, tiled=True)  17.5 us
    ppermute x15, starting transfers between devices, permute(): return lax.ppermute(x, 'row', [(i, target(i)) for i in range(devices)])  10.2 us
  transfers between devices with their start and end apart: 18, of which 8 were waited for; matrix products, arithmetic and copies ran while one was open for 1% of the time, Pallas kernels for 17%

profile of v21, /device:TPU:22, one launch (start us, length us, event | category | flops | bytes accessed | tf_op | source)
XLA Modules:
  0.0 230.8 jit_solution(221719282670556512)
XLA Ops:
  0.6 0.5 collective-permute-start
  1.1 1.6 collective-permute-start.2
  2.7 0.0 collective-permute-start.4
  2.7 21.2 %collective-permute-done.refs_2_ = f32[14,128,128]{2,1,0:T(8,128)S(1)} collective-permute-done((f32[14,128,128]{2,1,0:T(8,128)}, f32[14,128,128]{2,1,0:T(8,128)S(1)}, u32[]{:S(2)}, u32[]{:S(2)}) %collective-permute-start) | collective-permute-done | bytes 917536 | tf_op jit(solution)/shard_map/ppermute | solution.py:18
  24.0 0.4 collective-permute-start.1
  24.4 0.0 collective-permute-done.2.refs_4_
  24.4 1.6 collective-permute-start.3
  26.0 0.0 collective-permute-start.5
  26.0 0.5 collective-permute-start.6
  26.5 1.3 fusion
  29.1 0.6 pad_add_fusion.info_ref
  29.7 3.3 %pack.1 = f32[16,264,128]{2,1,0:T(8,128)} custom-call(s32[3]{0:T(128)} %pad_add_fusion.info_ref, s32[14]{0:T(128)} %bitcast.19, f32[14,128,128]{2,1,0:T(8,128)} %bitcast.12, f32[14,128,128]{2,1,0:T(8,128)} %bitcast.13), custom_call_target="tpu_custom_call" | custom-call | tf_op jit(solution)/shard_map/pack/pallas_call | solution.py:326
  33.0 0.0 collective-permute-done.4.refs_1_
  33.0 0.0 copy-start.7
  33.1 13.4 %collective-permute-done.1.refs_6_ = f32[14,128,128]{2,1,0:T(8,128)} collective-permute-done((f32[14,128,128]{2,1,0:T(8,128)S(1)}, f32[14,128,128]{2,1,0:T(8,128)}, u32[]{:S(2)}, u32[]{:S(2)}) %collective-permute-start.1) | collective-permute-done | bytes 917536 | tf_op jit(solution)/shard_map/ppermute | solution.py:18
  46.4 0.0 collective-permute-done.3.refs_8_
  46.4 0.0 collective-permute-done.5.refs_3_
  46.4 0.0 collective-permute-done.6.refs_5_
  46.5 5.1 %all-to-all-start = ((f32[16,264,128]{2,1,0:T(8,128)}), f32[16,264,128]{2,1,0:T(8,128)S(1)}, u32[]{:S(2)}, u32[]{:S(2)}) async-start(f32[16,264,128]{2,1,0:T(8,128)} %pack.1), calls=%async_computation | async-start | bytes 4325376 | tf_op jit(solution)/shard_map/all_to_all | solution.py:341
  51.6 0.6 collective-permute-start.9
  52.2 1.5 collective-permute-start.11
  53.6 0.0 collective-permute-start.7
  53.6 0.5 collective-permute-start.8
  54.1 64.5 %collective-permute-done.9.refs_10_ = f32[14,128,128]{2,1,0:T(8,128)} collective-permute-done((f32[14,128,128]{2,1,0:T(8,128)}, f32[14,128,128]{2,1,0:T(8,128)}, u32[]{:S(2)}, u32[]{:S(2)}) %collective-permute-start.9) | collective-permute-done | bytes 917536 | tf_op jit(solution)/shard_map/ppermute | solution.py:18
  118.7 0.5 collective-permute-start.10
  119.2 0.4 collective-permute-done.11.refs_12_
  119.6 0.0 collective-permute-start.12
  119.6 0.0 all-to-all-done.t_ref.refs_2_
  119.6 2.1 collective-permute-start.13
  121.7 0.1 copy.16
  121.8 0.7 copy.19.drops_ref
  122.5 0.0 collective-permute-done.7.refs_7_
  122.5 0.0 collective-permute-done.8.refs_9_
  122.5 0.0 collective-permute-done.10.refs_11_
  122.5 0.5 collective-permute-done.12.refs_13_
  123.0 15.1 %first.2 = (bf16[14,256,2048]{2,1,0:T(8,128)(2,1)}, f32[16,128,128]{2,1,0:T(8,128)}, bf16[2048,256]{1,0:T(8,128)(2,1)}) custom-call(s32[16,2]{1,0:T(8,128)} %copy.19.drops_ref, s32[1]{0:T(128)} %bitcast.1.me_ref, s32[256]{0:T(256)} %constant.40.table_ref, f32[16,264,128]{2,1,0:T(8,128)} %copy-done.2, f32[14,128,128]{2,1,0:T(8,128)} %bitcast.17, ...), custom_call_target="tpu_custom_call" | custom-call | tf_op jit(solution)/shard_map/first/pallas_call | solution.py:326
  138.1 0.0 collective-permute-done.13.refs_0_
  138.1 0.4 collective-permute-start.14
  138.5 2.1 collective-permute-done.14.refs_1_
  140.6 3.5 %first.3 = (bf16[2,256,2048]{2,1,0:T(8,128)(2,1)}, f32[16,128,128]{2,1,0:T(8,128)}) custom-call(s32[16,2]{1,0:T(8,128)S(1)} %copy-done, s32[1]{0:T(128)} %bitcast.1.me_ref, s32[256]{0:T(256)S(1)} %copy-done.1, f32[16,264,128]{2,1,0:T(8,128)} %copy-done.2, f32[14,128,128]{2,1,0:T(8,128)S(1)} %collective-permute-done.13.refs_0_, ...), custom_call_target="tpu_custom_call", output_to_operand_aliasing={{1}: (7, {})} | custom-call | tf_op jit(solution)/shard_map/first/pallas_call | solution.py:326
  144.1 6.0 %all-to-all-start.1 = ((f32[16,128,128]{2,1,0:T(8,128)}), f32[16,128,128]{2,1,0:T(8,128)S(1)}, u32[]{:S(2)}, u32[]{:S(2)}) async-start(f32[16,128,128]{2,1,0:T(8,128)} %get-tuple-element.22.refs_3_), calls=%async_computation.1 | async-start | bytes 2097152 | tf_op jit(solution)/shard_map/all_to_all | solution.py:341
  150.1 17.9 %later.1 = f32[16,2,128,128]{3,2,1,0:T(8,128)} custom-call(s32[16,2]{1,0:T(8,128)} %copy.19.drops_ref, s32[1]{0:T(128)} %bitcast.1.me_ref, s32[256]{0:T(256)} %constant.40.table_ref, bf16[14,256,2048]{2,1,0:T(8,128)(2,1)} %get-tuple-element.16.refs_0_, bf16[2,256,2048]{2,1,0:T(8,128)(2,1)} %get-tuple-element.21.refs_1_, f32[16,264,128]{2,1,0:T(8,128)} %copy-done.2, ...), custom_call_target="tpu_custom_call" | custom-call | tf_op jit(solution)/shard_map/later/pallas_call | solution.py:326
  168.0 5.5 %all-to-all-done.1.first_ref = f32[16,128,128]{2,1,0:T(8,128)S(1)} async-done(((f32[16,128,128]{2,1,0:T(8,128)}), f32[16,128,128]{2,1,0:T(8,128)S(1)}, u32[]{:S(2)}, u32[]{:S(2)}) %all-to-all-start.1) | async-done | bytes 1048608 | tf_op jit(solution)/shard_map/all_to_all | solution.py:341
  173.5 6.4 %all-to-all-start.2 = ((f32[16,2,128,128]{3,2,1,0:T(8,128)}), f32[16,2,128,128]{3,2,1,0:T(8,128)S(1)}, u32[]{:S(2)}, u32[]{:S(2)}) async-start(f32[16,2,128,128]{3,2,1,0:T(8,128)} %later.1), calls=%async_computation.2 | async-start | bytes 4194304 | tf_op jit(solution)/shard_map/all_to_all | solution.py:341
  179.9 3.1 %unpack_first.1.sum_ref = f32[14,128,128]{2,1,0:T(8,128)} custom-call(s32[14]{0:T(128)} %bitcast.20, f32[3]{0:T(128)} %coefs_ref.3, f32[16,128,128]{2,1,0:T(8,128)} %copy-done.4, f32[14,128,128]{2,1,0:T(8,128)} %bitcast.18), custom_call_target="tpu_custom_call" | custom-call | tf_op jit(solution)/shard_map/unpack_first/pallas_call | solution.py:326
  183.0 42.8 %all-to-all-done.2.held_ref = f32[16,2,128,128]{3,2,1,0:T(8,128)S(1)} async-done(((f32[16,2,128,128]{3,2,1,0:T(8,128)}), f32[16,2,128,128]{3,2,1,0:T(8,128)S(1)}, u32[]{:S(2)}, u32[]{:S(2)}) %all-to-all-start.2) | async-done | bytes 2097184 | tf_op jit(solution)/shard_map/all_to_all | solution.py:341
  225.8 1.3 copy-done.3
  227.2 3.6 %unpack_last.1 = (f32[14,128,128]{2,1,0:T(8,128)}, f32[14,128,128]{2,1,0:T(8,128)}, f32[14,128,128]{2,1,0:T(8,128)}) custom-call(s32[14]{0:T(128)} %bitcast.21, f32[3]{0:T(128)} %coefs_ref.3, f32[16,2,128,128]{3,2,1,0:T(8,128)} %copy-done.3, f32[14,128,128]{2,1,0:T(8,128)} %unpack_first.1.sum_ref), custom_call_target="tpu_custom_call" | custom-call | tf_op jit(solution)/shard_map/unpack_last/pallas_call | solution.py:326
  (15 shorter events, 0.0 us)
Async XLA Ops:
  0.6 23.3 %collective-permute-start = (f32[14,128,128]{2,1,0:T(8,128)}, f32[14,128,128]{2,1,0:T(8,128)S(1)}, u32[]{:S(2)}, u32[]{:S(2)}) collective-permute-start(f32[14,128,128]{2,1,0:T(8,128)} %bitcast.14), channel_id=1, source_target_pairs={{0,4},{1,3},{2,0},{3,7},{4,8},{5,1},{6,2},{7,11},{8,12},{9,5},{10,... | collective-permute-start | bytes 2752520 | tf_op jit(solution)/shard_map/ppermute | solution.py:18
  1.1 23.3 %collective-permute-start.2 = (f32[14,128,128]{2,1,0:T(8,128)}, f32[14,128,128]{2,1,0:T(8,128)S(1)}, u32[]{:S(2)}, u32[]{:S(2)}) collective-permute-start(f32[14,128,128]{2,1,0:T(8,128)} %bitcast.15), channel_id=1, source_target_pairs={{0,2},{1,5},{2,6},{3,1},{4,0},{5,9},{6,10},{7,3},{8,4},{9,13},{10,... | collective-permute-start | bytes 2752520 | tf_op jit(solution)/shard_map/ppermute | solution.py:18
  2.7 30.3 %collective-permute-start.4 = (f32[14,128,128]{2,1,0:T(8,128)}, f32[14,128,128]{2,1,0:T(8,128)S(1)}, u32[]{:S(2)}, u32[]{:S(2)}) collective-permute-start(f32[14,128,128]{2,1,0:T(8,128)} %bitcast.16), channel_id=1, source_target_pairs={{0,1},{1,0},{2,3},{3,2},{4,5},{5,4},{6,7},{7,6},{8,9},{9,8},{10,11... | collective-permute-start | bytes 2752520 | tf_op jit(solution)/shard_map/ppermute | solution.py:18
  24.0 22.5 %copy-start.5 = (f32[14,128,128]{2,1,0:T(8,128)}, f32[14,128,128]{2,1,0:T(8,128)S(1)}, u32[]{:S(2)}) copy-start(f32[14,128,128]{2,1,0:T(8,128)S(1)} %collective-permute-done.refs_2_) | copy-start | bytes 2752516
  24.0 22.5 %collective-permute-start.1 = (f32[14,128,128]{2,1,0:T(8,128)S(1)}, f32[14,128,128]{2,1,0:T(8,128)}, u32[]{:S(2)}, u32[]{:S(2)}) collective-permute-start(f32[14,128,128]{2,1,0:T(8,128)S(1)} %collective-permute-done.refs_2_), channel_id=1, source_target_pairs={{0,4},{1,3},{2,0},{3,7},{4,8},{5,1},{6,2},{7,11},{8,12},{9,5},{10,... | collective-permute-start | bytes 2752520 | tf_op jit(solution)/shard_map/ppermute | solution.py:18
  24.4 22.0 %copy-start.6 = (f32[14,128,128]{2,1,0:T(8,128)}, f32[14,128,128]{2,1,0:T(8,128)S(1)}, u32[]{:S(2)}) copy-start(f32[14,128,128]{2,1,0:T(8,128)S(1)} %collective-permute-done.2.refs_4_) | copy-start | bytes 2752516
  24.4 22.0 %collective-permute-start.3 = (f32[14,128,128]{2,1,0:T(8,128)S(1)}, f32[14,128,128]{2,1,0:T(8,128)}, u32[]{:S(2)}, u32[]{:S(2)}) collective-permute-start(f32[14,128,128]{2,1,0:T(8,128)S(1)} %collective-permute-done.2.refs_4_), channel_id=1, source_target_pairs={{0,2},{1,5},{2,6},{3,1},{4,0},{5,9},{6,10},{7,3},{8,4},{9,13},{10,... | collective-permute-start | bytes 2752520 | tf_op jit(solution)/shard_map/ppermute | solution.py:18
  26.0 20.4 %collective-permute-start.5 = (f32[14,128,128]{2,1,0:T(8,128)S(1)}, f32[14,128,128]{2,1,0:T(8,128)}, u32[]{:S(2)}, u32[]{:S(2)}) collective-permute-start(f32[14,128,128]{2,1,0:T(8,128)S(1)} %collective-permute-done.refs_2_), channel_id=1, source_target_pairs={{0,1},{1,0},{2,3},{3,2},{4,5},{5,4},{6,7},{7,6},{8,9},{9,8},{10,11... | collective-permute-start | bytes 2752520 | tf_op jit(solution)/shard_map/ppermute | solution.py:18
  26.0 20.4 %collective-permute-start.6 = (f32[14,128,128]{2,1,0:T(8,128)S(1)}, f32[14,128,128]{2,1,0:T(8,128)}, u32[]{:S(2)}, u32[]{:S(2)}) collective-permute-start(f32[14,128,128]{2,1,0:T(8,128)S(1)} %collective-permute-done.2.refs_4_), channel_id=1, source_target_pairs={{0,1},{1,0},{2,3},{3,2},{4,5},{5,4},{6,7},{7,6},{8,9},{9,8},{10,11... | collective-permute-start | bytes 2752520 | tf_op jit(solution)/shard_map/ppermute | solution.py:18
  33.0 13.4 %copy-start.7 = (f32[14,128,128]{2,1,0:T(8,128)}, f32[14,128,128]{2,1,0:T(8,128)S(1)}, u32[]{:S(2)}) copy-start(f32[14,128,128]{2,1,0:T(8,128)S(1)} %collective-permute-done.4.refs_1_) | copy-start | bytes 2752516
  46.5 73.1 %all-to-all-start = ((f32[16,264,128]{2,1,0:T(8,128)}), f32[16,264,128]{2,1,0:T(8,128)S(1)}, u32[]{:S(2)}, u32[]{:S(2)}) async-start(f32[16,264,128]{2,1,0:T(8,128)} %pack.1), calls=%async_computation | async-start | bytes 4325376 | tf_op jit(solution)/shard_map/all_to_all | solution.py:341
  51.6 67.1 %collective-permute-start.9 = (f32[14,128,128]{2,1,0:T(8,128)}, f32[14,128,128]{2,1,0:T(8,128)}, u32[]{:S(2)}, u32[]{:S(2)}) collective-permute-start(f32[14,128,128]{2,1,0:T(8,128)} %collective-permute-done.1.refs_6_), channel_id=1, source_target_pairs={{0,4},{1,3},{2,0},{3,7},{4,8},{5,1},{6,2},{7,11},{8,12},{9,5},{10,... | collective-permute-start | bytes 2752520 | tf_op jit(solution)/shard_map/ppermute | solution.py:18
  52.2 67.4 %collective-permute-start.11 = (f32[14,128,128]{2,1,0:T(8,128)}, f32[14,128,128]{2,1,0:T(8,128)}, u32[]{:S(2)}, u32[]{:S(2)}) collective-permute-start(f32[14,128,128]{2,1,0:T(8,128)} %collective-permute-done.3.refs_8_), channel_id=1, source_target_pairs={{0,2},{1,5},{2,6},{3,1},{4,0},{5,9},{6,10},{7,3},{8,4},{9,13},{10,... | collective-permute-start | bytes 2752520 | tf_op jit(solution)/shard_map/ppermute | solution.py:18
  53.6 68.8 %collective-permute-start.7 = (f32[14,128,128]{2,1,0:T(8,128)}, f32[14,128,128]{2,1,0:T(8,128)}, u32[]{:S(2)}, u32[]{:S(2)}) collective-permute-start(f32[14,128,128]{2,1,0:T(8,128)} %collective-permute-done.1.refs_6_), channel_id=1, source_target_pairs={{0,1},{1,0},{2,3},{3,2},{4,5},{5,4},{6,7},{7,6},{8,9},{9,8},{10,11... | collective-permute-start | bytes 2752520 | tf_op jit(solution)/shard_map/ppermute | solution.py:18
  53.6 68.8 %collective-permute-start.8 = (f32[14,128,128]{2,1,0:T(8,128)}, f32[14,128,128]{2,1,0:T(8,128)}, u32[]{:S(2)}, u32[]{:S(2)}) collective-permute-start(f32[14,128,128]{2,1,0:T(8,128)} %collective-permute-done.3.refs_8_), channel_id=1, source_target_pairs={{0,1},{1,0},{2,3},{3,2},{4,5},{5,4},{6,7},{7,6},{8,9},{9,8},{10,11... | collective-permute-start | bytes 2752520 | tf_op jit(solution)/shard_map/ppermute | solution.py:18
  118.7 3.8 %collective-permute-start.10 = (f32[14,128,128]{2,1,0:T(8,128)}, f32[14,128,128]{2,1,0:T(8,128)}, u32[]{:S(2)}, u32[]{:S(2)}) collective-permute-start(f32[14,128,128]{2,1,0:T(8,128)} %collective-permute-done.9.refs_10_), channel_id=1, source_target_pairs={{0,1},{1,0},{2,3},{3,2},{4,5},{5,4},{6,7},{7,6},{8,9},{9,8},{10,11... | collective-permute-start | bytes 2752520 | tf_op jit(solution)/shard_map/ppermute | solution.py:18
  119.6 3.4 %collective-permute-start.12 = (f32[14,128,128]{2,1,0:T(8,128)}, f32[14,128,128]{2,1,0:T(8,128)}, u32[]{:S(2)}, u32[]{:S(2)}) collective-permute-start(f32[14,128,128]{2,1,0:T(8,128)} %collective-permute-done.11.refs_12_), channel_id=1, source_target_pairs={{0,1},{1,0},{2,3},{3,2},{4,5},{5,4},{6,7},{7,6},{8,9},{9,8},{10,11... | collective-permute-start | bytes 2752520 | tf_op jit(solution)/shard_map/ppermute | solution.py:18
  119.6 3.4 %copy-start.2 = (f32[16,264,128]{2,1,0:T(8,128)}, f32[16,264,128]{2,1,0:T(8,128)S(1)}, u32[]{:S(2)}) copy-start(f32[16,264,128]{2,1,0:T(8,128)S(1)} %all-to-all-done.t_ref.refs_2_) | copy-start | bytes 6488068
  119.6 18.5 %collective-permute-start.13 = (f32[14,128,128]{2,1,0:T(8,128)}, f32[14,128,128]{2,1,0:T(8,128)S(1)}, u32[]{:S(2)}, u32[]{:S(2)}) collective-permute-start(f32[14,128,128]{2,1,0:T(8,128)} %collective-permute-done.9.refs_10_), channel_id=1, source_target_pairs={{0,4},{1,3},{2,0},{3,7},{4,8},{5,1},{6,2},{7,11},{8,12},{9,5},{10,... | collective-permute-start | bytes 2752520 | tf_op jit(solution)/shard_map/ppermute | solution.py:18
  122.5 18.2 %copy-start = (s32[16,2]{1,0:T(8,128)S(1)}, s32[16,2]{1,0:T(8,128)}, u32[]{:S(2)}) copy-start(s32[16,2]{1,0:T(8,128)} %copy.19.drops_ref) | copy-start | bytes 388
  122.5 18.2 %copy-start.1 = (s32[256]{0:T(256)S(1)}, s32[256]{0:T(256)}, u32[]{:S(2)}) copy-start(s32[256]{0:T(256)} %constant.40.table_ref) | copy-start | bytes 3076
  138.1 2.5 %collective-permute-start.14 = (f32[14,128,128]{2,1,0:T(8,128)S(1)}, f32[14,128,128]{2,1,0:T(8,128)S(1)}, u32[]{:S(2)}, u32[]{:S(2)}) collective-permute-start(f32[14,128,128]{2,1,0:T(8,128)S(1)} %collective-permute-done.13.refs_0_), channel_id=1, source_target_pairs={{0,1},{1,0},{2,3},{3,2},{4,5},{5,4},{6,7},{7,6},{8,9},{9,8},{10,11... | collective-permute-start | bytes 2752520 | tf_op jit(solution)/shard_map/ppermute | solution.py:18
  144.1 29.4 %all-to-all-start.1 = ((f32[16,128,128]{2,1,0:T(8,128)}), f32[16,128,128]{2,1,0:T(8,128)S(1)}, u32[]{:S(2)}, u32[]{:S(2)}) async-start(f32[16,128,128]{2,1,0:T(8,128)} %get-tuple-element.22.refs_3_), calls=%async_computation.1 | async-start | bytes 2097152 | tf_op jit(solution)/shard_map/all_to_all | solution.py:341
  173.5 6.4 %copy-start.4 = (f32[16,128,128]{2,1,0:T(8,128)}, f32[16,128,128]{2,1,0:T(8,128)S(1)}, u32[]{:S(2)}) copy-start(f32[16,128,128]{2,1,0:T(8,128)S(1)} %all-to-all-done.1.first_ref) | copy-start | bytes 3145732
  173.5 52.4 %all-to-all-start.2 = ((f32[16,2,128,128]{3,2,1,0:T(8,128)}), f32[16,2,128,128]{3,2,1,0:T(8,128)S(1)}, u32[]{:S(2)}, u32[]{:S(2)}) async-start(f32[16,2,128,128]{3,2,1,0:T(8,128)} %later.1), calls=%async_computation.2 | async-start | bytes 4194304 | tf_op jit(solution)/shard_map/all_to_all | solution.py:341
  225.8 1.3 copy-start.3

commit v22 on v18

--- a/solution.py
+++ b/solution.py
@@ -62,7 +62,7 @@
     rows = [x, other_core(x)]
     ahead, behind, first = round_of(x, x)
     ahead, behind, second = round_of(ahead, behind)
-    column = exchange(ahead, behind, rows[1], first[1], first[3])
+    column = exchange(ahead, behind)
     yield column
     ahead, behind, third = round_of(ahead, behind)
     far = permute(after(ahead, column), lambda i: along_ring(i, 1))

time: 233 us -> 236 us (1.013)
  waiting for transfers between devices: 150 us -> 153 us
    ppermute x15, waiting for transfers between devices: 102 us -> 104 us  [permute(): return lax.ppermute(x, 'row', [(i, target(i)) for i in range(devices)])]
where the time goes in v22:
time: 236 us; the launch traced here: 234 us
  waiting for transfers between devices  153 us (65%)
  Pallas kernels  46 us (19%)
  starting transfers between devices  27.9 us (12%)
  local copies, waits for them, and re-layouts  2.89 us (1%)
    ppermute x15, waiting for transfers between devices, permute(): return lax.ppermute(x, 'row', [(i, target(i)) for i in range(devices)])  104 us
    all_to_all x3, waiting for transfers between devices, exchange(): return lax.all_to_all(x, 'row', 0, 0, tiled=True)  48.4 us
    pallas_call x6, Pallas kernels, call(): pl.pallas_call(kernel, out_shape=[pltpu.HBM(out.shape, out.dtype) for out...  46 us
    all_to_all x3, starting transfers between devices, exchange(): return lax.all_to_all(x, 'row', 0, 0, tiled=True)  17.5 us
    ppermute x15, starting transfers between devices, permute(): return lax.ppermute(x, 'row', [(i, target(i)) for i in range(devices)])  10.4 us
  transfers between devices with their start and end apart: 18, of which 8 were waited for; matrix products, arithmetic and copies ran while one was open for 1% of the time, Pallas kernels for 17%

profile of v22, /device:TPU:22, one launch (start us, length us, event | category | flops | bytes accessed | tf_op | source)
XLA Modules:
  0.0 233.8 jit_solution(15871092643493187626)
XLA Ops:
  0.6 0.5 collective-permute-start
  1.1 1.6 collective-permute-start.2
  2.7 21.2 %collective-permute-done.refs_2_ = f32[14,128,128]{2,1,0:T(8,128)S(1)} collective-permute-done((f32[14,128,128]{2,1,0:T(8,128)}, f32[14,128,128]{2,1,0:T(8,128)S(1)}, u32[]{:S(2)}, u32[]{:S(2)}) %collective-permute-start) | collective-permute-done | bytes 917536 | tf_op jit(solution)/shard_map/ppermute | solution.py:18
  24.0 0.4 collective-permute-start.1
  24.4 0.0 collective-permute-done.2.refs_4_
  24.4 1.6 collective-permute-start.3
  26.0 1.4 fusion.1
  28.7 0.6 pad_add_fusion.info_ref
  29.3 3.2 %pack.1 = f32[16,264,128]{2,1,0:T(8,128)} custom-call(s32[3]{0:T(128)} %pad_add_fusion.info_ref, s32[14]{0:T(128)} %bitcast.18, f32[14,128,128]{2,1,0:T(8,128)} %bitcast.11, f32[14,128,128]{2,1,0:T(8,128)} %bitcast.12), custom_call_target="tpu_custom_call" | custom-call | tf_op jit(solution)/shard_map/pack/pallas_call | solution.py:326
  32.5 0.0 copy-start.5
  32.5 13.9 %collective-permute-done.1.refs_6_ = f32[14,128,128]{2,1,0:T(8,128)} collective-permute-done((f32[14,128,128]{2,1,0:T(8,128)S(1)}, f32[14,128,128]{2,1,0:T(8,128)}, u32[]{:S(2)}, u32[]{:S(2)}) %collective-permute-start.1) | collective-permute-done | bytes 917536 | tf_op jit(solution)/shard_map/ppermute | solution.py:18
  46.4 0.0 collective-permute-done.3.refs_8_
  46.4 5.1 %all-to-all-start = ((f32[16,264,128]{2,1,0:T(8,128)}), f32[16,264,128]{2,1,0:T(8,128)S(1)}, u32[]{:S(2)}, u32[]{:S(2)}) async-start(f32[16,264,128]{2,1,0:T(8,128)} %pack.1), calls=%async_computation | async-start | bytes 4325376 | tf_op jit(solution)/shard_map/all_to_all | solution.py:341
  51.6 0.6 collective-permute-start.9
  52.1 0.8 collective-permute-start.4
  52.9 0.0 collective-permute-start.5
  52.9 1.2 collective-permute-start.11
  54.1 0.0 collective-permute-start.6
  54.1 64.5 %collective-permute-done.9.refs_10_ = f32[14,128,128]{2,1,0:T(8,128)S(1)} collective-permute-done((f32[14,128,128]{2,1,0:T(8,128)}, f32[14,128,128]{2,1,0:T(8,128)S(1)}, u32[]{:S(2)}, u32[]{:S(2)}) %collective-permute-start.9) | collective-permute-done | bytes 917536 | tf_op jit(solution)/shard_map/ppermute | solution.py:18
  118.7 0.9 copy-done.8
  119.6 0.5 collective-permute-start.7
  120.1 0.0 all-to-all-done.t_ref.refs_2_
  120.1 0.0 collective-permute-done.4.refs_1_
  120.1 0.1 collective-permute-start.8
  120.2 0.0 collective-permute-done.5.refs_3_
  120.2 0.5 collective-permute-start.10
  120.7 0.0 collective-permute-done.11.refs_12_
  120.7 0.1 collective-permute-start.12
  120.8 0.0 collective-permute-done.6.refs_5_
  120.8 2.3 collective-permute-start.13
  123.1 0.3 fusion
  123.4 0.6 convert_element_type.8.drops_ref
  124.0 0.0 collective-permute-done.7.refs_7_
  124.1 0.0 collective-permute-done.8.refs_9_
  124.1 1.1 collective-permute-done.10.refs_11_
  125.2 1.3 collective-permute-done.12.refs_13_
  126.5 14.9 %first.2 = (bf16[14,256,2048]{2,1,0:T(8,128)(2,1)}, f32[16,128,128]{2,1,0:T(8,128)}, bf16[2048,256]{1,0:T(8,128)(2,1)}) custom-call(s32[32]{0:T(128)} %convert_element_type.8.drops_ref, s32[1]{0:T(128)} %bitcast.1.me_ref, s32[256]{0:T(256)} %constant.40.table_ref, f32[16,264,128]{2,1,0:T(8,128)} %copy-done.2, f32[14,128,128]{2,1,0:T(8,128)} %bitcast.15, ...), custom_call_target="tpu_custom_call" | custom-call | tf_op jit(solution)/shard_map/first/pallas_call | solution.py:326
  141.4 0.3 collective-permute-start.14
  141.7 2.2 collective-permute-done.14.refs_1_
  143.9 3.3 %first.3 = (bf16[2,256,2048]{2,1,0:T(8,128)(2,1)}, f32[16,128,128]{2,1,0:T(8,128)}) custom-call(s32[32]{0:T(128)S(1)} %copy-done.1, s32[1]{0:T(128)} %bitcast.1.me_ref, s32[256]{0:T(256)S(1)} %copy-done, f32[16,264,128]{2,1,0:T(8,128)} %copy-done.2, f32[14,128,128]{2,1,0:T(8,128)S(1)} %collective-permute-done.13.refs_0_, ...), custom_call_target="tpu_custom_call", output_to_operand_aliasing={{1}: (7, {})} | custom-call | tf_op jit(solution)/shard_map/first/pallas_call | solution.py:326
  147.3 5.9 %all-to-all-start.1 = ((f32[16,128,128]{2,1,0:T(8,128)}), f32[16,128,128]{2,1,0:T(8,128)S(1)}, u32[]{:S(2)}, u32[]{:S(2)}) async-start(f32[16,128,128]{2,1,0:T(8,128)} %get-tuple-element.22.refs_3_), calls=%async_computation.1 | async-start | bytes 2097152 | tf_op jit(solution)/shard_map/all_to_all | solution.py:341
  153.2 17.8 %later.1 = f32[16,2,128,128]{3,2,1,0:T(8,128)} custom-call(s32[32]{0:T(128)} %convert_element_type.8.drops_ref, s32[1]{0:T(128)} %bitcast.1.me_ref, s32[256]{0:T(256)} %constant.40.table_ref, bf16[14,256,2048]{2,1,0:T(8,128)(2,1)} %get-tuple-element.16.refs_0_, bf16[2,256,2048]{2,1,0:T(8,128)(2,1)} %get-tuple-element.21.refs_1_, f32[16,264,128]{2,1,0:T(8,128)} %copy-done.2, ...), custom_call_target="tpu_custom_call" | custom-call | tf_op jit(solution)/shard_map/later/pallas_call | solution.py:326
  171.0 5.6 %all-to-all-done.1.first_ref = f32[16,128,128]{2,1,0:T(8,128)S(1)} async-done(((f32[16,128,128]{2,1,0:T(8,128)}), f32[16,128,128]{2,1,0:T(8,128)S(1)}, u32[]{:S(2)}, u32[]{:S(2)}) %all-to-all-start.1) | async-done | bytes 1048608 | tf_op jit(solution)/shard_map/all_to_all | solution.py:341
  176.6 6.4 %all-to-all-start.2 = ((f32[16,2,128,128]{3,2,1,0:T(8,128)}), f32[16,2,128,128]{3,2,1,0:T(8,128)S(1)}, u32[]{:S(2)}, u32[]{:S(2)}) async-start(f32[16,2,128,128]{3,2,1,0:T(8,128)} %later.1), calls=%async_computation.2 | async-start | bytes 4194304 | tf_op jit(solution)/shard_map/all_to_all | solution.py:341
  183.0 3.1 %unpack_first.1.sum_ref = f32[14,128,128]{2,1,0:T(8,128)} custom-call(s32[14]{0:T(128)} %bitcast.19, f32[3]{0:T(128)} %coefs_ref.3, f32[16,128,128]{2,1,0:T(8,128)} %copy-done.4, f32[14,128,128]{2,1,0:T(8,128)} %bitcast.17), custom_call_target="tpu_custom_call" | custom-call | tf_op jit(solution)/shard_map/unpack_first/pallas_call | solution.py:326
  186.1 42.8 %all-to-all-done.2.held_ref = f32[16,2,128,128]{3,2,1,0:T(8,128)S(1)} async-done(((f32[16,2,128,128]{3,2,1,0:T(8,128)}), f32[16,2,128,128]{3,2,1,0:T(8,128)S(1)}, u32[]{:S(2)}, u32[]{:S(2)}) %all-to-all-start.2) | async-done | bytes 2097184 | tf_op jit(solution)/shard_map/all_to_all | solution.py:341
  228.9 1.3 copy-done.3
  230.2 3.6 %unpack_last.1 = (f32[14,128,128]{2,1,0:T(8,128)}, f32[14,128,128]{2,1,0:T(8,128)}, f32[14,128,128]{2,1,0:T(8,128)}) custom-call(s32[14]{0:T(128)} %bitcast.20, f32[3]{0:T(128)} %coefs_ref.3, f32[16,2,128,128]{3,2,1,0:T(8,128)} %copy-done.3, f32[14,128,128]{2,1,0:T(8,128)} %unpack_first.1.sum_ref), custom_call_target="tpu_custom_call" | custom-call | tf_op jit(solution)/shard_map/unpack_last/pallas_call | solution.py:326
  (16 shorter events, 0.0 us)
Async XLA Ops:
  0.6 23.3 %collective-permute-start = (f32[14,128,128]{2,1,0:T(8,128)}, f32[14,128,128]{2,1,0:T(8,128)S(1)}, u32[]{:S(2)}, u32[]{:S(2)}) collective-permute-start(f32[14,128,128]{2,1,0:T(8,128)} %bitcast.13), channel_id=1, source_target_pairs={{0,4},{1,3},{2,0},{3,7},{4,8},{5,1},{6,2},{7,11},{8,12},{9,5},{10,... | collective-permute-start | bytes 2752520 | tf_op jit(solution)/shard_map/ppermute | solution.py:18
  1.1 23.3 %collective-permute-start.2 = (f32[14,128,128]{2,1,0:T(8,128)}, f32[14,128,128]{2,1,0:T(8,128)S(1)}, u32[]{:S(2)}, u32[]{:S(2)}) collective-permute-start(f32[14,128,128]{2,1,0:T(8,128)} %bitcast.14), channel_id=1, source_target_pairs={{0,2},{1,5},{2,6},{3,1},{4,0},{5,9},{6,10},{7,3},{8,4},{9,13},{10,... | collective-permute-start | bytes 2752520 | tf_op jit(solution)/shard_map/ppermute | solution.py:18
  24.0 22.5 %copy-start.6 = (f32[14,128,128]{2,1,0:T(8,128)}, f32[14,128,128]{2,1,0:T(8,128)S(1)}, u32[]{:S(2)}) copy-start(f32[14,128,128]{2,1,0:T(8,128)S(1)} %collective-permute-done.refs_2_) | copy-start | bytes 2752516
  24.0 22.5 %collective-permute-start.1 = (f32[14,128,128]{2,1,0:T(8,128)S(1)}, f32[14,128,128]{2,1,0:T(8,128)}, u32[]{:S(2)}, u32[]{:S(2)}) collective-permute-start(f32[14,128,128]{2,1,0:T(8,128)S(1)} %collective-permute-done.refs_2_), channel_id=1, source_target_pairs={{0,4},{1,3},{2,0},{3,7},{4,8},{5,1},{6,2},{7,11},{8,12},{9,5},{10,... | collective-permute-start | bytes 2752520 | tf_op jit(solution)/shard_map/ppermute | solution.py:18
  24.4 22.0 %copy-start.7 = (f32[14,128,128]{2,1,0:T(8,128)}, f32[14,128,128]{2,1,0:T(8,128)S(1)}, u32[]{:S(2)}) copy-start(f32[14,128,128]{2,1,0:T(8,128)S(1)} %collective-permute-done.2.refs_4_) | copy-start | bytes 2752516
  24.4 22.0 %collective-permute-start.3 = (f32[14,128,128]{2,1,0:T(8,128)S(1)}, f32[14,128,128]{2,1,0:T(8,128)}, u32[]{:S(2)}, u32[]{:S(2)}) collective-permute-start(f32[14,128,128]{2,1,0:T(8,128)S(1)} %collective-permute-done.2.refs_4_), channel_id=1, source_target_pairs={{0,2},{1,5},{2,6},{3,1},{4,0},{5,9},{6,10},{7,3},{8,4},{9,13},{10,... | collective-permute-start | bytes 2752520 | tf_op jit(solution)/shard_map/ppermute | solution.py:18
  32.5 19.6 %copy-start.5 = (f32[1,14,128,128]{3,2,1,0:T(8,128)S(1)}, f32[1,14,128,128]{3,2,1,0:T(8,128)}, u32[]{:S(2)}) copy-start(f32[1,14,128,128]{3,2,1,0:T(8,128)} %param.8) | copy-start | bytes 2752516
  46.4 73.7 %all-to-all-start = ((f32[16,264,128]{2,1,0:T(8,128)}), f32[16,264,128]{2,1,0:T(8,128)S(1)}, u32[]{:S(2)}, u32[]{:S(2)}) async-start(f32[16,264,128]{2,1,0:T(8,128)} %pack.1), calls=%async_computation | async-start | bytes 4325376 | tf_op jit(solution)/shard_map/all_to_all | solution.py:341
  51.6 67.1 %collective-permute-start.9 = (f32[14,128,128]{2,1,0:T(8,128)}, f32[14,128,128]{2,1,0:T(8,128)S(1)}, u32[]{:S(2)}, u32[]{:S(2)}) collective-permute-start(f32[14,128,128]{2,1,0:T(8,128)} %collective-permute-done.1.refs_6_), channel_id=1, source_target_pairs={{0,4},{1,3},{2,0},{3,7},{4,8},{5,1},{6,2},{7,11},{8,12},{9,5},{10,... | collective-permute-start | bytes 2752520 | tf_op jit(solution)/shard_map/ppermute | solution.py:18
  52.1 68.0 %collective-permute-start.4 = (f32[14,128,128]{2,1,0:T(8,128)S(1)}, f32[14,128,128]{2,1,0:T(8,128)}, u32[]{:S(2)}, u32[]{:S(2)}) collective-permute-start(f32[14,128,128]{2,1,0:T(8,128)S(1)} %bitcast.16), channel_id=1, source_target_pairs={{0,1},{1,0},{2,3},{3,2},{4,5},{5,4},{6,7},{7,6},{8,9},{9,8},{10,11... | collective-permute-start | bytes 2752520 | tf_op jit(solution)/shard_map/ppermute | solution.py:18
  52.9 67.3 %collective-permute-start.5 = (f32[14,128,128]{2,1,0:T(8,128)}, f32[14,128,128]{2,1,0:T(8,128)}, u32[]{:S(2)}, u32[]{:S(2)}) collective-permute-start(f32[14,128,128]{2,1,0:T(8,128)} %copy-done.6), channel_id=1, source_target_pairs={{0,1},{1,0},{2,3},{3,2},{4,5},{5,4},{6,7},{7,6},{8,9},{9,8},{10,11... | collective-permute-start | bytes 2752520 | tf_op jit(solution)/shard_map/ppermute | solution.py:18
  52.9 67.8 %collective-permute-start.11 = (f32[14,128,128]{2,1,0:T(8,128)}, f32[14,128,128]{2,1,0:T(8,128)}, u32[]{:S(2)}, u32[]{:S(2)}) collective-permute-start(f32[14,128,128]{2,1,0:T(8,128)} %collective-permute-done.3.refs_8_), channel_id=1, source_target_pairs={{0,2},{1,5},{2,6},{3,1},{4,0},{5,9},{6,10},{7,3},{8,4},{9,13},{10,... | collective-permute-start | bytes 2752520 | tf_op jit(solution)/shard_map/ppermute | solution.py:18
  54.1 66.7 %collective-permute-start.6 = (f32[14,128,128]{2,1,0:T(8,128)}, f32[14,128,128]{2,1,0:T(8,128)}, u32[]{:S(2)}, u32[]{:S(2)}) collective-permute-start(f32[14,128,128]{2,1,0:T(8,128)} %copy-done.7), channel_id=1, source_target_pairs={{0,1},{1,0},{2,3},{3,2},{4,5},{5,4},{6,7},{7,6},{8,9},{9,8},{10,11... | collective-permute-start | bytes 2752520 | tf_op jit(solution)/shard_map/ppermute | solution.py:18
  118.7 0.9 copy-start.8
  119.6 4.5 %collective-permute-start.7 = (f32[14,128,128]{2,1,0:T(8,128)}, f32[14,128,128]{2,1,0:T(8,128)}, u32[]{:S(2)}, u32[]{:S(2)}) collective-permute-start(f32[14,128,128]{2,1,0:T(8,128)} %collective-permute-done.1.refs_6_), channel_id=1, source_target_pairs={{0,1},{1,0},{2,3},{3,2},{4,5},{5,4},{6,7},{7,6},{8,9},{9,8},{10,11... | collective-permute-start | bytes 2752520 | tf_op jit(solution)/shard_map/ppermute | solution.py:18
  120.1 6.4 %copy-start.2 = (f32[16,264,128]{2,1,0:T(8,128)}, f32[16,264,128]{2,1,0:T(8,128)S(1)}, u32[]{:S(2)}) copy-start(f32[16,264,128]{2,1,0:T(8,128)S(1)} %all-to-all-done.t_ref.refs_2_) | copy-start | bytes 6488068
  120.1 3.9 %collective-permute-start.8 = (f32[14,128,128]{2,1,0:T(8,128)}, f32[14,128,128]{2,1,0:T(8,128)}, u32[]{:S(2)}, u32[]{:S(2)}) collective-permute-start(f32[14,128,128]{2,1,0:T(8,128)} %collective-permute-done.3.refs_8_), channel_id=1, source_target_pairs={{0,1},{1,0},{2,3},{3,2},{4,5},{5,4},{6,7},{7,6},{8,9},{9,8},{10,11... | collective-permute-start | bytes 2752520 | tf_op jit(solution)/shard_map/ppermute | solution.py:18
  120.2 5.0 %collective-permute-start.10 = (f32[14,128,128]{2,1,0:T(8,128)}, f32[14,128,128]{2,1,0:T(8,128)}, u32[]{:S(2)}, u32[]{:S(2)}) collective-permute-start(f32[14,128,128]{2,1,0:T(8,128)} %copy-done.8), channel_id=1, source_target_pairs={{0,1},{1,0},{2,3},{3,2},{4,5},{5,4},{6,7},{7,6},{8,9},{9,8},{10,11... | collective-permute-start | bytes 2752520 | tf_op jit(solution)/shard_map/ppermute | solution.py:18
  120.7 5.8 %collective-permute-start.12 = (f32[14,128,128]{2,1,0:T(8,128)}, f32[14,128,128]{2,1,0:T(8,128)}, u32[]{:S(2)}, u32[]{:S(2)}) collective-permute-start(f32[14,128,128]{2,1,0:T(8,128)} %collective-permute-done.11.refs_12_), channel_id=1, source_target_pairs={{0,1},{1,0},{2,3},{3,2},{4,5},{5,4},{6,7},{7,6},{8,9},{9,8},{10,11... | collective-permute-start | bytes 2752520 | tf_op jit(solution)/shard_map/ppermute | solution.py:18
  120.8 20.6 %collective-permute-start.13 = (f32[14,128,128]{2,1,0:T(8,128)}, f32[14,128,128]{2,1,0:T(8,128)S(1)}, u32[]{:S(2)}, u32[]{:S(2)}) collective-permute-start(f32[14,128,128]{2,1,0:T(8,128)} %copy-done.8), channel_id=1, source_target_pairs={{0,4},{1,3},{2,0},{3,7},{4,8},{5,1},{6,2},{7,11},{8,12},{9,5},{10,... | collective-permute-start | bytes 2752520 | tf_op jit(solution)/shard_map/ppermute | solution.py:18
  124.0 19.9 %copy-start = (s32[256]{0:T(256)S(1)}, s32[256]{0:T(256)}, u32[]{:S(2)}) copy-start(s32[256]{0:T(256)} %constant.40.table_ref) | copy-start | bytes 3076
  124.0 19.9 %copy-start.1 = (s32[32]{0:T(128)S(1)}, s32[32]{0:T(128)}, u32[]{:S(2)}) copy-start(s32[32]{0:T(128)} %convert_element_type.8.drops_ref) | copy-start | bytes 388
  141.4 2.5 %collective-permute-start.14 = (f32[14,128,128]{2,1,0:T(8,128)S(1)}, f32[14,128,128]{2,1,0:T(8,128)S(1)}, u32[]{:S(2)}, u32[]{:S(2)}) collective-permute-start(f32[14,128,128]{2,1,0:T(8,128)S(1)} %collective-permute-done.13.refs_0_), channel_id=1, source_target_pairs={{0,1},{1,0},{2,3},{3,2},{4,5},{5,4},{6,7},{7,6},{8,9},{9,8},{10,11... | collective-permute-start | bytes 2752520 | tf_op jit(solution)/shard_map/ppermute | solution.py:18
  147.3 29.3 %all-to-all-start.1 = ((f32[16,128,128]{2,1,0:T(8,128)}), f32[16,128,128]{2,1,0:T(8,128)S(1)}, u32[]{:S(2)}, u32[]{:S(2)}) async-start(f32[16,128,128]{2,1,0:T(8,128)} %get-tuple-element.22.refs_3_), calls=%async_computation.1 | async-start | bytes 2097152 | tf_op jit(solution)/shard_map/all_to_all | solution.py:341
  176.6 6.4 %copy-start.4 = (f32[16,128,128]{2,1,0:T(8,128)}, f32[16,128,128]{2,1,0:T(8,128)S(1)}, u32[]{:S(2)}) copy-start(f32[16,128,128]{2,1,0:T(8,128)S(1)} %all-to-all-done.1.first_ref) | copy-start | bytes 3145732
  176.6 52.4 %all-to-all-start.2 = ((f32[16,2,128,128]{3,2,1,0:T(8,128)}), f32[16,2,128,128]{3,2,1,0:T(8,128)S(1)}, u32[]{:S(2)}, u32[]{:S(2)}) async-start(f32[16,2,128,128]{3,2,1,0:T(8,128)} %later.1), calls=%async_computation.2 | async-start | bytes 4194304 | tf_op jit(solution)/shard_map/all_to_all | solution.py:341
  228.9 1.3 copy-start.3
